TPU v7x, 32 devices: a whole 2x2x4 slice. The times are simulated.
32 devices in a mesh: grp: 2 (over y), pb: 16 (over z, x, core).
Axes of the slice: x: 2, y: 2, z: 4, core: 2. Of those that a mesh axis runs over, the one named last changes fastest.
Arguments:
- queries: bfloat16 [4096, 2048], P('pb', 'grp'), parts along dimension 1, may hold values from -150 to 150
- keys: bfloat16 [4096, 256], P('pb', 'grp'), parts along dimension 1, may hold values from -6 to 6
- values: bfloat16 [4096, 256], P('pb', 'grp'), parts along dimension 1, may hold values from -6 to 6
- basis: bfloat16 [256, 128], P('grp'), parts along dimension 0, may hold values from -0.5 to 0.5
- picks: int32 [64, 16], P('grp'), parts along dimension 0, may hold values from -1 to 7, as said below
Outputs:
- attended: bfloat16 [4096, 2048], P('pb', 'grp'), parts along dimension 1
There are 2 independent parts, one for each index of `grp`. A program takes and returns all parts, laid end to end along the dimension named above; each array names one. Nothing has to cross between parts.
Inputs may be any that keep to these rules, and one draw needn't show every extreme that they name: picks[b, s] is -1 when neither block of device s (blocks s and 31 - s) ends before block b - 1 begins; else it names a sub-block of one of those blocks that lies wholly before block b - 1.
All inputs are finite; a program needn't handle non-finite values.
Results may differ from a plain program's by a relative error of at most 0.011.
Values may be sent and summed in bfloat16 or wider, within the bound.
No kernel may reach another device: no remote copies, remote signals or barrier semaphores. Data moves between devices by JAX's collectives and lax.ppermute only.
A program may use at most 64 MiB of HBM per device.

v0:
```python
import jax
import jax.numpy as jnp
from jax import lax
from jax.sharding import PartitionSpec as P

KB = 32


def passed_along(value, axis, steps):
    count = lax.axis_size(axis)
    leading, last = (max(0, -steps), min(count, count - steps))
    return lax.ppermute(value, axis, [(source, source + steps) for source in range(leading, last)])


def attend(q_rot, chosen, chosen_ok, own):
    nq = q_rot.shape[0]
    dim = q_rot.shape[2]
    keys_all = jnp.concatenate([chosen[:, :dim], own[:, :dim]], axis=0)
    vals_all = jnp.concatenate([chosen[:, dim:], own[:, dim:]], axis=0)
    causal = jnp.arange(nq)[:, None] >= jnp.arange(nq)[None, :]
    usable = jnp.concatenate(
        [jnp.broadcast_to(chosen_ok[None, :], (nq, chosen.shape[0])), causal], axis=1
    )
    scores = jnp.einsum(
        "qhd,kd->hqk", q_rot, keys_all, preferred_element_type=jnp.float32
    ) * dim ** (-0.5)
    scores = jnp.where(usable[None], scores, jnp.float32(-1e30))
    top = jnp.max(scores, axis=-1, keepdims=True)
    weight = jnp.exp(scores - top)
    total = jnp.sum(weight, axis=-1)
    weight_b = weight.astype(jnp.bfloat16)
    summed = jnp.einsum("hqk,kd->qhd", weight_b, vals_all, preferred_element_type=jnp.float32)
    result = summed / jnp.transpose(total)[:, :, None]
    return result.astype(jnp.bfloat16).reshape(nq, -1)


def per_device(queries, keys, values, basis, picks):
    rows_dev = queries.shape[0]
    half = rows_dev // 2
    dim = basis.shape[0]
    heads = queries.shape[1] // dim
    count = lax.axis_size("pb")
    me = lax.axis_index("pb")
    nblk = 2 * count
    kv_rows = jnp.concatenate([keys, values], axis=1)
    width = kv_rows.shape[1]
    q_rot = jnp.einsum(
        "shd,de->she",
        queries.reshape(rows_dev, heads, dim),
        basis,
        preferred_element_type=jnp.float32,
    ).astype(jnp.bfloat16)
    mine = jnp.take(picks, jnp.stack([me, nblk - 1 - me]), axis=0)
    ok_pick = jnp.repeat(mine >= 0, KB, axis=1)
    ok_before = jnp.stack([jnp.broadcast_to(me >= 1, (half,)), jnp.ones((half,), dtype=bool)])
    chosen_ok = jnp.concatenate([ok_pick, ok_before], axis=1)
    sub_blocks = kv_rows.reshape(rows_dev // KB, KB, width)
    column = jnp.take(picks, me, axis=1)
    wanted_by = jnp.stack([column[:count], column[count:][::-1]], axis=1)
    outgoing = jnp.take(sub_blocks, jnp.maximum(wanted_by, 0), axis=0)
    outgoing = jnp.where((wanted_by >= 0)[:, :, None, None], outgoing, jnp.zeros_like(outgoing))
    incoming = lax.all_to_all(outgoing, "pb", split_axis=0, concat_axis=0, tiled=True)
    picked = jnp.transpose(incoming, (1, 0, 2, 3)).reshape(2, count * KB, width)
    earlier = passed_along(kv_rows[:half], "pb", 1)
    later = passed_along(kv_rows[half:], "pb", -1)
    later = jnp.where(me == count - 1, kv_rows[:half], later)
    chosen = jnp.concatenate([picked, jnp.stack([earlier, later])], axis=1)
    leading_out = attend(q_rot[:half], chosen[0], chosen_ok[0], kv_rows[:half])
    trailing_out = attend(q_rot[half:], chosen[1], chosen_ok[1], kv_rows[half:])
    return jnp.concatenate([leading_out, trailing_out], axis=0)


def solution(mesh):
    in_specs = (P("pb", "grp"), P("pb", "grp"), P("pb", "grp"), P("grp", None), P("grp", None))
    out_specs = P("pb", "grp")
    return jax.shard_map(
        per_device, mesh=mesh, in_specs=in_specs, out_specs=out_specs, check_vma=False
    )
```

profile of v0, /device:TPU:0, one launch (start us, length us, event | category | flops | bytes accessed | tf_op | source)
XLA Modules:
  0.0 34.2 jit_solution(14715687914329215323)
XLA Ops:
  0.0 0.9 %constant_dynamic-update-slice_fusion.1 = bf16[256,256]{1,0:T(8,128)(2,1)S(1)} fusion(bf16[256,128]{1,0:T(8,128)(2,1)} %param.6), kind=kLoop, calls=%fused_computation.57 | loop fusion | bytes 131072
  0.9 0.9 %constant_dynamic-update-slice_fusion = bf16[256,256]{1,0:T(8,128)(2,1)S(1)} fusion(bf16[256,256]{1,0:T(8,128)(2,1)S(1)} %constant_dynamic-update-slice_fusion.1, bf16[256,128]{1,0:T(8,128)(2,1)} %param.7), kind=kLoop, calls=%fused_computation.56 | loop fusion | bytes 131072 | tf_op jit(solution)/shard_map/concatenate | solution.py:45
  1.8 1.3 %collective-permute-start.1 = (bf16[128,256]{1,0:T(8,128)(2,1)S(1)}, bf16[128,256]{1,0:T(8,128)(2,1)S(1)}, u32[]{:S(2)}, u32[]{:S(2)}) collective-permute-start(bf16[128,256]{1,0:T(8,128)(2,1)S(1)} %slice.97), channel_id=1, source_target_pairs={{1,0},{2,1},{3,2},{4,3},{5,4},{6,5},{7,6},{8,7},{9,8},{10,9},{11,1... | collective-permute-start | bytes 196616 | tf_op jit(solution)/shard_map/ppermute | solution.py:12
  3.1 0.7 %fusion.46 = s32[1,32]{1,0:T(1,128)S(1)} fusion(pred[]{:T(512)S(6)} %and.19, s32[32,16]{0,1:T(8,128)} %param.9, s32[]{:T(128)S(6)} %select_n.55), kind=kLoop, calls=%fused_computation.66 | loop fusion | flops 32 | bytes 261 | tf_op jit(solution)/shard_map/jit(_take)/select_n | solution.py:58
  3.9 0.1 rev.3
  4.0 0.1 copy.38
  4.1 0.1 copy.39
  4.5 0.6 %gather_fusion = bf16[32,32,256]{2,1,0:T(8,128)(2,1)S(1)} fusion(bf16[8,32,256]{2,1,0:T(8,128)(2,1)S(1)} %bitcast.106, s32[1024]{0:T(1024)S(1)} %get-tuple-element.42), kind=kCustom, calls=%fused_computation | custom fusion | bytes 1048704 | tf_op jit(solution)/shard_map/jit(_take)/gather | solution.py:60
  5.1 0.9 %select_select_fusion = bf16[16,2,32,256]{3,2,1,0:T(8,128)(2,1)} fusion(bf16[16,2,32,256]{3,2,1,0:T(8,128)(2,1)S(1)} %bitcast.109, pred[16,2]{1,0:T(8,128)(4,1)S(1)} %copy.39, pred[16,2]{1,0:T(8,128)(4,1)S(1)} %copy.38), kind=kLoop, calls=%fused_computation.27 | loop fusion | flops 524288 | bytes 1048640 | tf_op jit(solution)/shard_map/jit(_where)/select_n | solution.py:61
  6.0 8.1 %all-to-all-start = ((bf16[16,2,32,256]{3,2,1,0:T(8,128)(2,1)}), bf16[16,2,32,256]{3,2,1,0:T(8,128)(2,1)S(1)}, u32[]{:S(2)}, u32[]{:S(2)}) async-start(bf16[16,2,32,256]{3,2,1,0:T(8,128)(2,1)} %select_select_fusion), calls=%async_computation | async-start | bytes 1048576 | tf_op jit(solution)/shard_map/all_to_all | solution.py:62
  14.3 0.6 %gather_fusion.1 = s32[2,16]{1,0:T(2,128)S(1)} fusion(s32[32,16]{1,0:T(8,128)S(1)} %copy.44, s32[1024]{0:T(1024)S(1)} %get-tuple-element.41), kind=kCustom, calls=%fused_computation.1 | custom fusion | bytes 264 | tf_op jit(solution)/shard_map/jit(_take)/gather | solution.py:53
  15.2 0.3 pad_add_fusion.1
  15.5 0.3 convolution_convert_fusion
  15.9 2.3 %collective-permute-start = (bf16[128,256]{1,0:T(8,128)(2,1)S(1)}, bf16[128,256]{1,0:T(8,128)(2,1)S(1)}, u32[]{:S(2)}, u32[]{:S(2)}) collective-permute-start(bf16[128,256]{1,0:T(8,128)(2,1)S(1)} %get-tuple-element.24), channel_id=1, source_target_pairs={{0,1},{1,2},{2,3},{3,4},{4,5},{5,6},{6,7},{7,8},{8,9},{9,10},{10,1... | collective-permute-start | bytes 196616 | tf_op jit(solution)/shard_map/ppermute | solution.py:12
  18.2 10.3 %all-to-all-done = bf16[16,2,32,256]{3,2,1,0:T(8,128)(2,1)S(1)} async-done(((bf16[16,2,32,256]{3,2,1,0:T(8,128)(2,1)}), bf16[16,2,32,256]{3,2,1,0:T(8,128)(2,1)S(1)}, u32[]{:S(2)}, u32[]{:S(2)}) %all-to-all-start) | async-done | bytes 524320 | tf_op jit(solution)/shard_map/all_to_all | solution.py:62
  28.8 0.6 %fusion.5 = (f32[8,128]{1,0:T(8,128)S(1)}, f32[768,128,8]{1,0,2:T(8,128)S(1)}) fusion(pred[128,768]{0,1:T(8,128)(4,1)S(1)} %get-tuple-element.31, bf16[256,8,128]{2,0,1:T(8,128)(2,1)S(1)} %convolution_convert_fusion, bf16[128,128]{1,0:T(8,128)(2,1)S(1)} %get-tuple-element.29, bf16[640,128]{1,0:T(8,128)(2,1)S(1)} %get-tuple-element.23), kind=kOutput, calls=%fused_computation.11 | convolution fusion | flops 204078080 | bytes 3706880 | tf_op jit(solution)/shard_map/qhd,kd->hqk/dot_general | solution.py:24
  29.4 0.7 %fusion.2 = f32[8,128]{1,0:T(8,128)S(1)} fusion(f32[768,128,8]{1,0,2:T(8,128)S(1)} %get-tuple-element.38, f32[8,128]{1,0:T(8,128)S(1)} %get-tuple-element.37, pred[128,768]{0,1:T(8,128)(4,1)S(1)} %get-tuple-element.31), kind=kLoop, calls=%fused_computation.8 | loop fusion | flops 3144704 | bytes 3252224 | tf_op jit(solution)/shard_map/reduce_sum | solution.py:30
  30.1 0.9 %fusion.21 = bf16[128,8,128]{0,2,1:T(8,128)(2,1)S(1)} fusion(f32[768,128,8]{1,0,2:T(8,128)S(1)} %get-tuple-element.38, f32[8,128]{1,0:T(8,128)S(1)} %get-tuple-element.37, pred[128,768]{0,1:T(8,128)(4,1)S(1)} %get-tuple-element.31, f32[128,8]{0,1:T(8,128)S(1)} %bitcast.114, bf16[128,128]{1,0:T(8,128)(2,1)S(1)} %get-tuple-element.27, ...), kind=kOutput, calls=%fused_computation.20 | convolution fusion | flops 205127680 | bytes 3710976 | tf_op jit(solution)/shard_map/hqk,kd->qhd/dot_general | solution.py:32
  31.0 0.1 copy.51
  31.1 0.6 %fusion.4 = (f32[8,128]{1,0:T(8,128)S(1)}, f32[768,128,8]{1,0,2:T(8,128)S(1)}) fusion(pred[128,768]{0,1:T(8,128)(4,1)S(1)} %get-tuple-element.30, bf16[256,8,128]{2,0,1:T(8,128)(2,1)S(1)} %convolution_convert_fusion, bf16[128,128]{1,0:T(8,128)(2,1)S(1)} %get-tuple-element.28, bf16[640,128]{1,0:T(8,128)(2,1)S(1)} %get-tuple-element.21), kind=kOutput, calls=%fused_computation.10 | convolution fusion | flops 204078080 | bytes 3706880 | tf_op jit(solution)/shard_map/qhd,kd->hqk/dot_general | solution.py:24
  31.7 0.7 %fusion = f32[8,128]{1,0:T(8,128)S(1)} fusion(f32[768,128,8]{1,0,2:T(8,128)S(1)} %get-tuple-element.40, f32[8,128]{1,0:T(8,128)S(1)} %get-tuple-element.39, pred[128,768]{0,1:T(8,128)(4,1)S(1)} %get-tuple-element.30), kind=kLoop, calls=%fused_computation.6 | loop fusion | flops 3144704 | bytes 3252224 | tf_op jit(solution)/shard_map/reduce_sum | solution.py:30
  32.4 0.9 %fusion.27 = bf16[128,8,128]{0,2,1:T(8,128)(2,1)S(1)} fusion(f32[768,128,8]{1,0,2:T(8,128)S(1)} %get-tuple-element.40, f32[8,128]{1,0:T(8,128)S(1)} %get-tuple-element.39, pred[128,768]{0,1:T(8,128)(4,1)S(1)} %get-tuple-element.30, f32[128,8]{0,1:T(8,128)S(1)} %bitcast.113, bf16[128,128]{1,0:T(8,128)(2,1)S(1)} %get-tuple-element.26, ...), kind=kOutput, calls=%fused_computation.22 | convolution fusion | flops 205127680 | bytes 3710976 | tf_op jit(solution)/shard_map/hqk,kd->qhd/dot_general | solution.py:32
  33.3 0.1 copy.50
  33.4 0.8 %pad_maximum_fusion = bf16[256,1024]{1,0:T(8,128)(2,1)} fusion(bf16[128,1024]{1,0:T(8,128)(2,1)S(1)} %copy.51, bf16[128,1024]{1,0:T(8,128)(2,1)S(1)} %copy.50), kind=kLoop, calls=%fused_computation.26 | loop fusion | flops 1048576 | bytes 1048576 | tf_op jit(solution)/shard_map/concatenate | solution.py:70
  (39 shorter events, 1.1 us)
Async XLA Ops:
  0.0 15.5 %copy-start = (bf16[256,1024]{1,0:T(8,128)(2,1)S(1)}, bf16[256,1024]{1,0:T(8,128)(2,1)}, u32[]{:S(2)}) copy-start(bf16[256,1024]{1,0:T(8,128)(2,1)} %param.5) | copy-start | bytes 1572868
  0.0 15.8 %copy-start.1 = (bf16[256,128]{1,0:T(8,128)(2,1)S(1)}, bf16[256,128]{1,0:T(8,128)(2,1)}, u32[]{:S(2)}) copy-start(bf16[256,128]{1,0:T(8,128)(2,1)} %param.6) | copy-start | bytes 196612
  0.0 18.2 %copy-start.2 = (bf16[256,128]{1,0:T(8,128)(2,1)S(1)}, bf16[256,128]{1,0:T(8,128)(2,1)}, u32[]{:S(2)}) copy-start(bf16[256,128]{1,0:T(8,128)(2,1)} %param.7) | copy-start | bytes 196612
  0.0 14.1 %copy-start.4 = (s32[32,16]{0,1:T(8,128)S(1)}, s32[32,16]{0,1:T(8,128)}, u32[]{:S(2)}) copy-start(s32[32,16]{0,1:T(8,128)} %param.9) | copy-start | bytes 6148
  0.0 15.5 %copy-start.3 = (bf16[128,128]{1,0:T(8,128)(2,1)S(1)}, bf16[128,128]{1,0:T(8,128)(2,1)}, u32[]{:S(2)}) copy-start(bf16[128,128]{1,0:T(8,128)(2,1)} %param.8) | copy-start | bytes 98308
  1.8 14.1 %collective-permute-start.1 = (bf16[128,256]{1,0:T(8,128)(2,1)S(1)}, bf16[128,256]{1,0:T(8,128)(2,1)S(1)}, u32[]{:S(2)}, u32[]{:S(2)}) collective-permute-start(bf16[128,256]{1,0:T(8,128)(2,1)S(1)} %slice.97), channel_id=1, source_target_pairs={{1,0},{2,1},{3,2},{4,3},{5,4},{6,5},{7,6},{8,7},{9,8},{10,9},{11,1... | collective-permute-start | bytes 196616 | tf_op jit(solution)/shard_map/ppermute | solution.py:12
  6.0 22.6 %all-to-all-start = ((bf16[16,2,32,256]{3,2,1,0:T(8,128)(2,1)}), bf16[16,2,32,256]{3,2,1,0:T(8,128)(2,1)S(1)}, u32[]{:S(2)}, u32[]{:S(2)}) async-start(bf16[16,2,32,256]{3,2,1,0:T(8,128)(2,1)} %select_select_fusion), calls=%async_computation | async-start | bytes 1048576 | tf_op jit(solution)/shard_map/all_to_all | solution.py:62
  15.9 12.7 %collective-permute-start = (bf16[128,256]{1,0:T(8,128)(2,1)S(1)}, bf16[128,256]{1,0:T(8,128)(2,1)S(1)}, u32[]{:S(2)}, u32[]{:S(2)}) collective-permute-start(bf16[128,256]{1,0:T(8,128)(2,1)S(1)} %get-tuple-element.24), channel_id=1, source_target_pairs={{0,1},{1,2},{2,3},{3,4},{4,5},{5,6},{6,7},{7,8},{8,9},{9,10},{10,1... | collective-permute-start | bytes 196616 | tf_op jit(solution)/shard_map/ppermute | solution.py:12
where the time goes:
time: 34.6 us; the launch traced here: 34.2 us
  starting transfers between devices  11.7 us (34%)
  waiting for transfers between devices  10.3 us (30%)
  other arithmetic  4.42 us (13%)
  local copies, waits for them, and re-layouts  4.25 us (12%)
  matrix products  3.25 us (9%)
    all_to_all x1, waiting for transfers between devices, per_device(): lax.all_to_all(outgoing, 'pb', split_axis=0, concat_axis=0, tiled=True)  10.3 us
    all_to_all x1, starting transfers between devices, per_device(): lax.all_to_all(outgoing, 'pb', split_axis=0, concat_axis=0, tiled=True)  8.1 us
    ppermute x2, starting transfers between devices, passed_along(): lax.ppermute(value, axis, [(source, source + steps) for source in range(l...  3.6 us
    dot_general x2, matrix products, attend(): jnp.einsum('hqk,kd->qhd', weight_b, vals_all, preferred_element_type=jnp....  1.77 us
    reduce_sum x2, other arithmetic, attend(): total = jnp.sum(weight, axis=-1)  1.31 us
    dot_general x2, matrix products, attend(): jnp.einsum('qhd,kd->hqk', q_rot, keys_all, preferred_element_type=jnp.flo...  1.2 us
    unnamed x12, local copies, waits for them, and re-layouts  1.01 us
    select_n x1, other arithmetic, per_device(): jnp.where((wanted_by >= 0)[:, :, None, None], outgoing, jnp.zeros_like(ou...  0.93 us
  transfers between devices with their start and end apart: 3, of which 1 were waited for; matrix products, arithmetic and copies ran while one was open for 13% of the time, Pallas kernels for 0%

commit v1 on v0

v1 whole, which is shorter than its diff:
```python
import functools
import math

import jax
import jax.numpy as jnp
from jax import lax
from jax.experimental import pallas as pl
from jax.experimental.pallas import tpu as pltpu
from jax.sharding import PartitionSpec as P

KB = 32
NEG = -1e30
VMEM_BYTES = 40 * 1024 * 1024


def passed_along(value, axis, steps):
    count = lax.axis_size(axis)
    leading, last = (max(0, -steps), min(count, count - steps))
    return lax.ppermute(value, axis, [(source, source + steps) for source in range(leading, last)])


def scores_of(k, q):
    return lax.dot_general(k, q, (((1,), (1,)), ((), ())), preferred_element_type=jnp.float32)


def pack_kernel(count, picks_ref, k_ref, v_ref, out_ref, first_ref, second_ref):
    me = lax.axis_index("pb")
    dim = k_ref.shape[1]
    half = k_ref.shape[0] // 2
    first_ref[:, :dim] = k_ref[:half]
    first_ref[:, dim:] = v_ref[:half]
    second_ref[:, :dim] = k_ref[half:]
    second_ref[:, dim:] = v_ref[half:]

    def one(dest, carry):
        for slot in range(2):
            block = dest if slot == 0 else 2 * count - 1 - dest
            pick = jnp.maximum(picks_ref[block, me], 0)
            rows = pl.ds(pl.multiple_of(pick * KB, KB), KB)
            out_ref[dest, slot, :, :dim] = k_ref[rows, :]
            out_ref[dest, slot, :, dim:] = v_ref[rows, :]
        return carry

    lax.fori_loop(0, count, one, 0, unroll=min(count, 16))


def near_kernel(count, scale, q_ref, basis_ref, k_ref, v_ref, earlier_ref, later_ref, rot_ref, m_ref, l_ref, acc_ref):
    me = lax.axis_index("pb")
    dim = basis_ref.shape[0]
    half = q_ref.shape[0] // 2
    heads = q_ref.shape[1] // dim
    basis = basis_ref[...]
    step = 2 * half
    key_row = lax.broadcasted_iota(jnp.int32, (half, step), 0)
    query = lax.broadcasted_iota(jnp.int32, (half, step), 1) % half
    causal = key_row <= query
    for block in range(2):
        rows = slice(block * half, (block + 1) * half)
        k_own, v_own = k_ref[rows], v_ref[rows]
        if block == 0:
            k_prev, v_prev = earlier_ref[:, :dim], earlier_ref[:, dim:]
            usable = me >= 1
        else:
            last = me == count - 1
            k_prev = jnp.where(last, k_ref[:half], later_ref[:, :dim])
            v_prev = jnp.where(last, v_ref[:half], later_ref[:, dim:])
        k_all = jnp.concatenate([k_prev, k_own], axis=0)
        v_t = jnp.concatenate([v_prev, v_own], axis=0).T
        for pair in range(heads // 2):
            q = [
                jnp.dot(
                    q_ref[rows, (2 * pair + h) * dim : (2 * pair + h + 1) * dim], basis, preferred_element_type=jnp.float32
                ).astype(jnp.bfloat16)
                for h in range(2)
            ]
            q = jnp.concatenate(q, axis=0)
            cols = slice(pair * step, (pair + 1) * step)
            rot_ref[block, cols, :] = q
            s = scores_of(k_all, q) * scale
            s_prev, s_own = s[:half], jnp.where(causal, s[half:], NEG)
            if block == 0:
                s_prev = jnp.where(usable, s_prev, NEG)
            s = jnp.concatenate([s_prev, s_own], axis=0)
            m = jnp.max(s, axis=0, keepdims=True)
            w = jnp.exp2(s - m)
            m_ref[block, :, cols] = m
            l_ref[block, :, cols] = jnp.sum(w, axis=0, keepdims=True)
            acc_ref[block, :, cols] = jnp.dot(v_t, w.astype(jnp.bfloat16), preferred_element_type=jnp.float32)


def far_kernel(count, chunk, scale, kv_ref, rot_ref, m_ref, l_ref, acc_ref, out_ref):
    me = lax.axis_index("pb")
    dim = rot_ref.shape[2]
    half = out_ref.shape[0] // 2
    heads = out_ref.shape[1] // dim
    step = 2 * half
    nk = chunk * KB

    def finish(block, pair, l, acc):
        done = acc / l
        for h in range(2):
            head = 2 * pair + h
            out_ref[block * half : (block + 1) * half, head * dim : (head + 1) * dim] = (
                done[:, h * half : (h + 1) * half].T.astype(out_ref.dtype)
            )

    def run(block):
        def part(c, m_all, l_all, acc_all):
            source = c * chunk + lax.broadcasted_iota(jnp.int32, (nk, step), 0) // KB
            if block == 0:
                usable = source < me - 1
            else:
                usable = (source < 2 * count - 2 - me) | (source > me + 1)
            k = kv_ref[pl.ds(c * chunk, chunk), block, :, :dim].reshape(nk, dim)
            v_t = kv_ref[pl.ds(c * chunk, chunk), block, :, dim:].reshape(nk, dim).T
            ms, ls, accs = [], [], []
            for pair in range(heads // 2):
                cols = slice(pair * step, (pair + 1) * step)
                s = scores_of(k, rot_ref[block, cols, :]) * scale
                s = jnp.where(usable, s, NEG)
                m_old = m_all[pair]
                m = jnp.maximum(m_old, jnp.max(s, axis=0, keepdims=True))
                w = jnp.exp2(s - m)
                old = jnp.exp2(m_old - m)
                ms.append(m)
                ls.append(l_all[pair] * old + jnp.sum(w, axis=0, keepdims=True))
                accs.append(acc_all[pair] * old + jnp.dot(v_t, w.astype(jnp.bfloat16), preferred_element_type=jnp.float32))
            return ms, ls, accs

        pairs = range(heads // 2)
        state = tuple(
            [ref[block, :, pair * step : (pair + 1) * step] for pair in pairs] for ref in (m_ref, l_ref, acc_ref)
        )
        if count == chunk:
            state = part(0, *state)
        else:
            state = lax.fori_loop(0, count // chunk, lambda c, carry: part(c, *carry), state)
        for pair in pairs:
            finish(block, pair, state[1][pair], state[2][pair])

    run(1)

    @pl.when(me >= 2)
    def _():
        run(0)

    @pl.when(me < 2)
    def _():
        for pair in range(heads // 2):
            cols = slice(pair * step, (pair + 1) * step)
            finish(0, pair, l_ref[0, :, cols], acc_ref[0, :, cols])


def per_device(queries, keys, values, basis, picks):
    rows_dev, dim = keys.shape
    half = rows_dev // 2
    count = lax.axis_size("pb")
    wide = queries.shape[1] // dim * half
    scale = dim**-0.5 * math.log2(math.e)
    vmem = pl.BlockSpec(memory_space=pltpu.VMEM)
    smem = pl.BlockSpec(memory_space=pltpu.SMEM)
    params = pltpu.CompilerParams(vmem_limit_bytes=VMEM_BYTES)
    bf16, f32 = jnp.bfloat16, jnp.float32

    outgoing, first, second = pl.pallas_call(
        functools.partial(pack_kernel, count),
        out_shape=[
            jax.ShapeDtypeStruct((count, 2, KB, 2 * dim), bf16),
            jax.ShapeDtypeStruct((half, 2 * dim), bf16),
            jax.ShapeDtypeStruct((half, 2 * dim), bf16),
        ],
        in_specs=[smem, vmem, vmem],
        out_specs=[vmem] * 3,
        compiler_params=params,
        name="pack",
    )(picks, keys, values)
    incoming = lax.all_to_all(outgoing, "pb", split_axis=0, concat_axis=0, tiled=True)
    earlier = passed_along(first, "pb", 1)
    later = passed_along(second, "pb", -1)
    near = pl.pallas_call(
        functools.partial(near_kernel, count, scale),
        out_shape=[
            jax.ShapeDtypeStruct((2, wide, dim), bf16),
            jax.ShapeDtypeStruct((2, 1, wide), f32),
            jax.ShapeDtypeStruct((2, 1, wide), f32),
            jax.ShapeDtypeStruct((2, dim, wide), f32),
        ],
        in_specs=[vmem] * 6,
        out_specs=[vmem] * 4,
        compiler_params=params,
        cost_estimate=pl.CostEstimate(flops=700_000_000, bytes_accessed=2_500_000, transcendentals=600_000),
        name="near",
    )(queries, basis, keys, values, earlier, later)
    return pl.pallas_call(
        functools.partial(far_kernel, count, min(count, 16), scale),
        out_shape=jax.ShapeDtypeStruct(queries.shape, bf16),
        in_specs=[vmem] * 5,
        out_specs=vmem,
        compiler_params=params,
        name="far",
    )(incoming, *near)


def solution(mesh):
    in_specs = (P("pb", "grp"), P("pb", "grp"), P("pb", "grp"), P("grp", None), P("grp", None))
    out_specs = P("pb", "grp")
    return jax.shard_map(
        per_device, mesh=mesh, in_specs=in_specs, out_specs=out_specs, check_vma=False
    )
```

time: 34.6 us -> 33.7 us (0.974)
  the two profiles are of different devices: /device:TPU:0 before, /device:TPU:11 now
where the time goes in v1:
time: 33.7 us; the launch traced here: 33.4 us
  starting transfers between devices  11.9 us (35%)
  Pallas kernels  9.86 us (29%)
  waiting for transfers between devices  9.03 us (27%)
  local copies, waits for them, and re-layouts  2.46 us (7%)
    ppermute x2, waiting for transfers between devices, passed_along(): lax.ppermute(value, axis, [(source, source + steps) for source in range(l...  9.03 us
    all_to_all x1, starting transfers between devices, per_device(): lax.all_to_all(outgoing, 'pb', split_axis=0, concat_axis=0, tiled=True)  6.7 us
    ppermute x2, starting transfers between devices, passed_along(): lax.ppermute(value, axis, [(source, source + steps) for source in range(l...  5.25 us
    pallas_call x1, Pallas kernels, per_device(): pl.pallas_call(functools.partial(far_kernel, count, min(count, 16), scale...  4.41 us
    pallas_call x1, Pallas kernels, per_device(): pl.pallas_call(functools.partial(near_kernel, count, scale), out_shape=[j...  3.69 us
    unnamed x13, local copies, waits for them, and re-layouts  2.46 us
    pallas_call x1, Pallas kernels, per_device(): pl.pallas_call(functools.partial(pack_kernel, count), out_shape=[jax.Shap...  1.76 us
  transfers between devices with their start and end apart: 3, of which 2 were waited for; matrix products, arithmetic and copies ran while one was open for 0% of the time, Pallas kernels for 11%

profile of v1, /device:TPU:11, one launch (start us, length us, event | category | flops | bytes accessed | tf_op | source)
XLA Modules:
  0.0 33.4 jit_solution(2304455912309058)
XLA Ops:
  0.0 0.8 %copy.6.picks_ref = s32[32,16]{1,0:T(8,128)S(1)} copy(s32[32,16]{0,1:T(8,128)} %param.9) | data formatting | bytes 4096 | tf_op args[4]
  0.8 0.0 copy-start
  0.8 0.8 %copy-done = bf16[256,128]{1,0:T(8,128)(2,1)S(1)} copy-done((bf16[256,128]{1,0:T(8,128)(2,1)S(1)}, bf16[256,128]{1,0:T(8,128)(2,1)}, u32[]{:S(2)}) %copy-start) | copy-done | bytes 65560
  1.6 0.0 copy-start.2
  1.6 0.8 %copy-done.2 = bf16[256,128]{1,0:T(8,128)(2,1)S(1)} copy-done((bf16[256,128]{1,0:T(8,128)(2,1)S(1)}, bf16[256,128]{1,0:T(8,128)(2,1)}, u32[]{:S(2)}) %copy-start.2) | copy-done | bytes 65560
  2.5 1.8 %pack.1 = (bf16[16,2,32,256]{3,2,1,0:T(8,128)(2,1)}, bf16[128,256]{1,0:T(8,128)(2,1)S(1)}, bf16[128,256]{1,0:T(8,128)(2,1)S(1)}) custom-call(s32[32,16]{1,0:T(8,128)S(1)} %copy.6.picks_ref, bf16[256,128]{1,0:T(8,128)(2,1)S(1)} %copy-done, bf16[256,128]{1,0:T(8,128)(2,1)S(1)} %copy-done.2), custom_call_target="tpu_custom_call" | custom-call | tf_op jit(solution)/shard_map/pack/pallas_call | solution.py:165
  4.2 0.0 copy-start.1
  4.2 0.0 copy-start.3
  4.2 0.0 copy-start.4
  4.2 0.0 copy-start.5
  4.2 6.7 %all-to-all-start = ((bf16[16,2,32,256]{3,2,1,0:T(8,128)(2,1)}), bf16[16,2,32,256]{3,2,1,0:T(8,128)(2,1)S(1)}, u32[]{:S(2)}, u32[]{:S(2)}) async-start(bf16[16,2,32,256]{3,2,1,0:T(8,128)(2,1)} %get-tuple-element.12), calls=%async_computation | async-start | bytes 1048576 | tf_op jit(solution)/shard_map/all_to_all | solution.py:177
  10.9 3.3 %collective-permute-start = (bf16[128,256]{1,0:T(8,128)(2,1)S(1)}, bf16[128,256]{1,0:T(8,128)(2,1)S(1)}, u32[]{:S(2)}, u32[]{:S(2)}) collective-permute-start(bf16[128,256]{1,0:T(8,128)(2,1)S(1)} %get-tuple-element.13), channel_id=1, source_target_pairs={{0,1},{1,2},{2,3},{3,4},{4,5},{5,6},{6,7},{7,8},{8,9},{9,10},{10,1... | collective-permute-start | bytes 196616 | tf_op jit(solution)/shard_map/ppermute | solution.py:19
  14.3 1.9 %collective-permute-start.1 = (bf16[128,256]{1,0:T(8,128)(2,1)S(1)}, bf16[128,256]{1,0:T(8,128)(2,1)S(1)}, u32[]{:S(2)}, u32[]{:S(2)}) collective-permute-start(bf16[128,256]{1,0:T(8,128)(2,1)S(1)} %get-tuple-element.14), channel_id=1, source_target_pairs={{1,0},{2,1},{3,2},{4,3},{5,4},{6,5},{7,6},{8,7},{9,8},{10,9},{11,1... | collective-permute-start | bytes 196616 | tf_op jit(solution)/shard_map/ppermute | solution.py:19
  16.2 7.4 %collective-permute-done.earlier_ref = bf16[128,256]{1,0:T(8,128)(2,1)S(1)} collective-permute-done((bf16[128,256]{1,0:T(8,128)(2,1)S(1)}, bf16[128,256]{1,0:T(8,128)(2,1)S(1)}, u32[]{:S(2)}, u32[]{:S(2)}) %collective-permute-start) | collective-permute-done | bytes 65568 | tf_op jit(solution)/shard_map/ppermute | solution.py:19
  23.6 1.6 %collective-permute-done.1.later_ref = bf16[128,256]{1,0:T(8,128)(2,1)S(1)} collective-permute-done((bf16[128,256]{1,0:T(8,128)(2,1)S(1)}, bf16[128,256]{1,0:T(8,128)(2,1)S(1)}, u32[]{:S(2)}, u32[]{:S(2)}) %collective-permute-start.1) | collective-permute-done | bytes 65568 | tf_op jit(solution)/shard_map/ppermute | solution.py:19
  25.2 0.0 copy-done.1
  25.2 0.0 copy-done.3
  25.2 0.0 copy-done.4
  25.2 0.0 copy-done.5
  25.2 3.7 %near.1 = (bf16[2,1024,128]{2,1,0:T(8,128)(2,1)S(1)}, f32[2,1,1024]{2,1,0:T(1,128)S(1)}, f32[2,1,1024]{2,1,0:T(1,128)S(1)}, f32[2,128,1024]{2,1,0:T(8,128)S(1)}) custom-call(bf16[256,1024]{1,0:T(8,128)(2,1)S(1)} %copy-done.4, bf16[128,128]{1,0:T(8,128)(2,1)S(1)} %copy-done.5, bf16[256,128]{1,0:T(8,128)(2,1)S(1)} %copy-done.1, ...), custom_call_target="tpu_custom_call" | custom-call | flops 700000000 | bytes 2500000 | tf_op jit(solution)/shard_map/near/pallas_call | solution.py:180
  28.9 0.0 all-to-all-done.kv_ref
  28.9 4.4 %far.1 = bf16[256,1024]{1,0:T(8,128)(2,1)} custom-call(bf16[16,2,32,256]{3,2,1,0:T(8,128)(2,1)S(1)} %all-to-all-done.kv_ref, bf16[2,1024,128]{2,1,0:T(8,128)(2,1)S(1)} %get-tuple-element.15.rot_ref, f32[2,1,1024]{2,1,0:T(1,128)S(1)} %get-tuple-element.16.m_ref, f32[2,1,1024]{2,1,0:T(1,128)S(1)} %get-tuple-element.17.l_ref, ...), custom_call_target="tpu_custom_call" | custom-call | tf_op jit(solution)/shard_map/far/pallas_call | solution.py:194
Async XLA Ops:
  0.8 0.8 %copy-start = (bf16[256,128]{1,0:T(8,128)(2,1)S(1)}, bf16[256,128]{1,0:T(8,128)(2,1)}, u32[]{:S(2)}) copy-start(bf16[256,128]{1,0:T(8,128)(2,1)} %k_ref.3) | copy-start | bytes 196612
  1.6 0.8 %copy-start.2 = (bf16[256,128]{1,0:T(8,128)(2,1)S(1)}, bf16[256,128]{1,0:T(8,128)(2,1)}, u32[]{:S(2)}) copy-start(bf16[256,128]{1,0:T(8,128)(2,1)} %v_ref.3) | copy-start | bytes 196612
  4.2 21.0 %copy-start.1 = (bf16[256,128]{1,0:T(8,128)(2,1)S(1)}, bf16[256,128]{1,0:T(8,128)(2,1)}, u32[]{:S(2)}) copy-start(bf16[256,128]{1,0:T(8,128)(2,1)} %k_ref.3) | copy-start | bytes 196612
  4.2 21.0 %copy-start.3 = (bf16[256,128]{1,0:T(8,128)(2,1)S(1)}, bf16[256,128]{1,0:T(8,128)(2,1)}, u32[]{:S(2)}) copy-start(bf16[256,128]{1,0:T(8,128)(2,1)} %v_ref.3) | copy-start | bytes 196612
  4.2 21.0 %copy-start.4 = (bf16[256,1024]{1,0:T(8,128)(2,1)S(1)}, bf16[256,1024]{1,0:T(8,128)(2,1)}, u32[]{:S(2)}) copy-start(bf16[256,1024]{1,0:T(8,128)(2,1)} %q_ref.1) | copy-start | bytes 1572868
  4.2 21.0 %copy-start.5 = (bf16[128,128]{1,0:T(8,128)(2,1)S(1)}, bf16[128,128]{1,0:T(8,128)(2,1)}, u32[]{:S(2)}) copy-start(bf16[128,128]{1,0:T(8,128)(2,1)} %basis_ref.1) | copy-start | bytes 98308
  4.2 24.7 %all-to-all-start = ((bf16[16,2,32,256]{3,2,1,0:T(8,128)(2,1)}), bf16[16,2,32,256]{3,2,1,0:T(8,128)(2,1)S(1)}, u32[]{:S(2)}, u32[]{:S(2)}) async-start(bf16[16,2,32,256]{3,2,1,0:T(8,128)(2,1)} %get-tuple-element.12), calls=%async_computation | async-start | bytes 1048576 | tf_op jit(solution)/shard_map/all_to_all | solution.py:177
  10.9 12.6 %collective-permute-start = (bf16[128,256]{1,0:T(8,128)(2,1)S(1)}, bf16[128,256]{1,0:T(8,128)(2,1)S(1)}, u32[]{:S(2)}, u32[]{:S(2)}) collective-permute-start(bf16[128,256]{1,0:T(8,128)(2,1)S(1)} %get-tuple-element.13), channel_id=1, source_target_pairs={{0,1},{1,2},{2,3},{3,4},{4,5},{5,6},{6,7},{7,8},{8,9},{9,10},{10,1... | collective-permute-start | bytes 196616 | tf_op jit(solution)/shard_map/ppermute | solution.py:19
  14.3 11.0 %collective-permute-start.1 = (bf16[128,256]{1,0:T(8,128)(2,1)S(1)}, bf16[128,256]{1,0:T(8,128)(2,1)S(1)}, u32[]{:S(2)}, u32[]{:S(2)}) collective-permute-start(bf16[128,256]{1,0:T(8,128)(2,1)S(1)} %get-tuple-element.14), channel_id=1, source_target_pairs={{1,0},{2,1},{3,2},{4,3},{5,4},{6,5},{7,6},{8,7},{9,8},{10,9},{11,1... | collective-permute-start | bytes 196616 | tf_op jit(solution)/shard_map/ppermute | solution.py:19

commit v2 on v1

v2 whole, which is shorter than its diff:
```python
import functools
import math

import jax
import jax.numpy as jnp
from jax import lax
from jax.experimental import pallas as pl
from jax.experimental.pallas import tpu as pltpu
from jax.sharding import PartitionSpec as P

KB = 32
PLANE = 4
NEG = -1e30
VMEM_BYTES = 40 * 1024 * 1024


def place(count):
    me = lax.axis_index("pb")
    return me, me // PLANE, me % PLANE


def sub(index):
    return pl.ds(pl.multiple_of(index * KB, KB), KB)


def scores_of(k, q):
    return lax.dot_general(k, q, (((1,), (1,)), ((), ())), preferred_element_type=jnp.float32)


def pack_kernel(count, picks_ref, k_ref, v_ref, *refs):
    planes = count // PLANE
    kv_ref, cross_ref, own_refs, packet_refs, sems = refs[0], refs[1], refs[2:5], refs[5:-1], refs[-1]
    me, z, r = place(count)
    dim = k_ref.shape[1]
    half = k_ref.shape[0] // 2
    per_half = half // KB
    copies = [
        pltpu.make_async_copy(k_ref, kv_ref.at[:, :dim], sems.at[0]),
        pltpu.make_async_copy(v_ref, kv_ref.at[:, dim:], sems.at[1]),
    ]
    for copy in copies:
        copy.start()
    for copy in copies:
        copy.wait()

    def late_pick(dest):
        return jnp.maximum(picks_ref[me, 2 * count - 1 - dest], 0)

    for j, ref in enumerate(packet_refs, 1):
        up = z + j < planes
        to = jnp.where(up, 0, (z + j - planes) * PLANE)
        for t in range(PLANE):
            index = jnp.where(up, t, late_pick(to + t))
            ref[t * KB : (t + 1) * KB] = kv_ref[sub(index)]
    for m, ref in enumerate(own_refs, 1):
        peer = r ^ m
        late = kv_ref[sub(late_pick(z * PLANE + peer))]
        if m == 2:
            ref[:KB] = late
            ref[KB:] = kv_ref[sub(jnp.maximum(picks_ref[me, z * PLANE + peer], 0))]
        else:
            ref[:KB] = late
            start = jnp.where(r < peer, 0, per_half)
            for t in range(per_half):
                ref[(t + 1) * KB : (t + 2) * KB] = kv_ref[sub(start + t)]
    start = jnp.where(r == PLANE - 1, 0, per_half)
    for t in range(per_half):
        cross_ref[t * KB : (t + 1) * KB] = kv_ref[sub(start + t)]


def select_kernel(count, picks_ref, *refs):
    planes = count // PLANE
    packet_refs, late_refs, early_refs = refs[: planes - 1], refs[planes - 1 : planes + 2], refs[planes + 2 :]
    me, z, r = place(count)
    for j, ref in enumerate(packet_refs, 1):
        up = z >= j
        source = jnp.where(up, z - j, z - j + planes) * PLANE + r
        for m, (late_ref, early_ref) in enumerate(zip(late_refs, early_refs, strict=True), 1):
            peer = r ^ m
            dest = z * PLANE + peer
            late = jnp.where(up, jnp.maximum(picks_ref[source, 2 * count - 1 - dest], 0), peer)
            early = jnp.where(up, jnp.maximum(picks_ref[source, dest], 0), 0)
            late_ref[(j - 1) * KB : j * KB] = ref[sub(late)]
            early_ref[(j - 1) * KB : j * KB] = ref[sub(early)]


def near_kernel(count, scale, q_ref, basis_ref, kv_ref, cross_ref, own1_ref, own3_ref, rot_ref, m_ref, l_ref, acc_ref):
    me, z, r = place(count)
    dim = basis_ref.shape[0]
    half = q_ref.shape[0] // 2
    heads = q_ref.shape[1] // dim
    basis = basis_ref[...]
    step = 2 * half
    key_row = lax.broadcasted_iota(jnp.int32, (half, step), 0)
    query = lax.broadcasted_iota(jnp.int32, (half, step), 1) % half
    causal = key_row <= query
    cross, own1, own3 = cross_ref[...], own1_ref[KB:], own3_ref[KB:]
    for block in range(2):
        rows = slice(block * half, (block + 1) * half)
        if block == 0:
            prev = jnp.where(r == 0, cross, jnp.where(r == 2, own3, own1))
        else:
            prev = jnp.where(r == PLANE - 1, cross, jnp.where(r == 1, own3, own1))
            prev = jnp.where(me == count - 1, kv_ref[:half], prev)
        kv = jnp.concatenate([prev, kv_ref[rows]], axis=0)
        k_all, v_t = kv[:, :dim], kv[:, dim:].T
        for pair in range(heads // 2):
            q = [
                jnp.dot(
                    q_ref[rows, (2 * pair + h) * dim : (2 * pair + h + 1) * dim], basis, preferred_element_type=jnp.float32
                ).astype(jnp.bfloat16)
                for h in range(2)
            ]
            q = jnp.concatenate(q, axis=0)
            cols = slice(pair * step, (pair + 1) * step)
            rot_ref[block, cols, :] = q
            s = scores_of(k_all, q) * scale
            s_prev, s_own = s[:half], jnp.where(causal, s[half:], NEG)
            if block == 0:
                s_prev = jnp.where(me >= 1, s_prev, NEG)
            s = jnp.concatenate([s_prev, s_own], axis=0)
            m = jnp.max(s, axis=0, keepdims=True)
            w = jnp.exp2(s - m)
            m_ref[block, :, cols] = m
            l_ref[block, :, cols] = jnp.sum(w, axis=0, keepdims=True)
            acc_ref[block, :, cols] = jnp.dot(v_t, w.astype(jnp.bfloat16), preferred_element_type=jnp.float32)


def far_kernel(count, chunk, scale, picks_ref, *refs):
    planes = count // PLANE
    packet_refs, refs = refs[: planes - 1], refs[planes - 1 :]
    late_refs, early_refs, own_refs = refs[0:3], refs[3:6], refs[6:9]
    kv_ref, rot_ref, m_ref, l_ref, acc_ref, out_ref, keys_ref = refs[9:]
    me, z, r = place(count)
    dim = rot_ref.shape[2]
    half = out_ref.shape[0] // 2
    heads = out_ref.shape[1] // dim
    step = 2 * half
    nk = chunk * KB
    pairs = range(heads // 2)

    def put(m, j, value):
        keys_ref[(m * planes + j) * KB : (m * planes + j + 1) * KB] = value

    def gather(block):
        mine = me if block == 0 else 2 * count - 1 - me
        put(0, 0, kv_ref[sub(jnp.maximum(picks_ref[me, mine], 0))])
        for j, ref in enumerate(packet_refs, 1):
            up = z >= j
            source = jnp.where(up, z - j, z - j + planes) * PLANE + r
            put(0, j, ref[sub(jnp.where(up, jnp.maximum(picks_ref[source, mine], 0), r))])
        for m in range(1, PLANE):
            own = own_refs[m - 1]
            if block == 1:
                put(m, 0, own[:KB])
            elif m == 2:
                put(m, 0, own[KB:])
            else:
                put(m, 0, own[sub(jnp.maximum(picks_ref[z * PLANE + (r ^ m), mine], 0) % (half // KB) + 1)])
            moved = late_refs if block == 1 else early_refs
            keys_ref[(m * planes + 1) * KB : (m + 1) * planes * KB] = moved[m - 1][...]

    def finish(block, pair, l, acc):
        done = acc / l
        for h in range(2):
            head = 2 * pair + h
            out_ref[block * half : (block + 1) * half, head * dim : (head + 1) * dim] = (
                done[:, h * half : (h + 1) * half].T.astype(out_ref.dtype)
            )

    def usable(block, g):
        m, j = g // planes, g % planes
        home = z - j
        source = jnp.where(home < 0, home + planes, home) * PLANE + (r ^ m)
        if block == 0:
            return source < me - 1
        return (source < 2 * count - 2 - me) | (source > me + 1)

    def run(block):
        gather(block)

        def part(c, m_all, l_all, acc_all):
            rows = slice(None) if count == chunk else pl.ds(pl.multiple_of(c * nk, nk), nk)
            k = keys_ref[rows, :dim]
            v_t = keys_ref[rows, dim:].T
            ok = [usable(block, c * chunk + g) for g in range(chunk)]
            ms, ls, accs = [], [], []
            for pair in pairs:
                cols = slice(pair * step, (pair + 1) * step)
                s = scores_of(k, rot_ref[block, cols, :]) * scale
                s = jnp.concatenate([jnp.where(ok[g], s[g * KB : (g + 1) * KB], NEG) for g in range(chunk)], axis=0)
                m_old = m_all[pair]
                m = jnp.maximum(m_old, jnp.max(s, axis=0, keepdims=True))
                w = jnp.exp2(s - m)
                old = jnp.exp2(m_old - m)
                ms.append(m)
                ls.append(l_all[pair] * old + jnp.sum(w, axis=0, keepdims=True))
                accs.append(acc_all[pair] * old + jnp.dot(v_t, w.astype(jnp.bfloat16), preferred_element_type=jnp.float32))
            return ms, ls, accs

        state = tuple([ref[block, :, pair * step : (pair + 1) * step] for pair in pairs] for ref in (m_ref, l_ref, acc_ref))
        if count == chunk:
            state = part(0, *state)
        else:
            state = lax.fori_loop(0, count // chunk, lambda c, carry: part(c, *carry), state)
        for pair in pairs:
            finish(block, pair, state[1][pair], state[2][pair])

    run(1)

    @pl.when(me >= 2)
    def _():
        run(0)

    @pl.when(me < 2)
    def _():
        for pair in pairs:
            cols = slice(pair * step, (pair + 1) * step)
            finish(0, pair, l_ref[0, :, cols], acc_ref[0, :, cols])


def per_device(queries, keys, values, basis, picks):
    rows_dev, dim = keys.shape
    half = rows_dev // 2
    count = lax.axis_size("pb")
    planes = count // PLANE
    wide = queries.shape[1] // dim * half
    scale = dim**-0.5 * math.log2(math.e)
    vmem = pl.BlockSpec(memory_space=pltpu.VMEM)
    smem = pl.BlockSpec(memory_space=pltpu.SMEM)
    hbm = pl.BlockSpec(memory_space=pltpu.HBM)
    params = pltpu.CompilerParams(vmem_limit_bytes=VMEM_BYTES)
    bf16, f32 = jnp.bfloat16, jnp.float32
    by_source = picks.T

    def rows(n):
        return jax.ShapeDtypeStruct((n, 2 * dim), bf16)

    def permute(value, pairs):
        return lax.ppermute(value, "pb", pairs)

    kv, cross, *rest = pl.pallas_call(
        functools.partial(pack_kernel, count),
        out_shape=[rows(rows_dev), rows(half), rows(half + KB), rows(2 * KB), rows(half + KB)]
        + [rows(PLANE * KB)] * (planes - 1),
        in_specs=[smem, hbm, hbm],
        out_specs=[vmem] * (4 + planes),
        scratch_shapes=[pltpu.SemaphoreType.DMA((2,))],
        compiler_params=params,
        name="pack",
    )(by_source, keys, values)
    own, packets = rest[:3], rest[3:]

    packets = [
        permute(packet, [(s, (s + j * PLANE) % count) for s in range(count)]) for j, packet in enumerate(packets, 1)
    ]
    borders = range(PLANE - 1, count - 1, PLANE)
    cross = permute(cross, [(s, s + 1) for s in borders] + [(s + 1, s) for s in borders])
    own = [permute(value, [(s, s ^ m) for s in range(count)]) for m, value in enumerate(own, 1)]

    near = pl.pallas_call(
        functools.partial(near_kernel, count, scale),
        out_shape=[
            jax.ShapeDtypeStruct((2, wide, dim), bf16),
            jax.ShapeDtypeStruct((2, 1, wide), f32),
            jax.ShapeDtypeStruct((2, 1, wide), f32),
            jax.ShapeDtypeStruct((2, dim, wide), f32),
        ],
        in_specs=[vmem] * 6,
        out_specs=[vmem] * 4,
        compiler_params=params,
        cost_estimate=pl.CostEstimate(flops=700_000_000, bytes_accessed=2_500_000, transcendentals=600_000),
        name="near",
    )(queries, basis, kv, cross, own[0], own[2])

    moved = pl.pallas_call(
        functools.partial(select_kernel, count),
        out_shape=[rows((planes - 1) * KB)] * 6,
        in_specs=[smem] + [vmem] * (planes - 1),
        out_specs=[vmem] * 6,
        compiler_params=params,
        name="select",
    )(by_source, *packets)
    late = [permute(moved[m - 1], [(s, s ^ m) for s in range(count)]) for m in range(1, PLANE)]
    early = [permute(moved[m + 2], [(s, s ^ m) for s in range(PLANE, count)]) for m in range(1, PLANE)]

    return pl.pallas_call(
        functools.partial(far_kernel, count, min(count, 16), scale),
        out_shape=jax.ShapeDtypeStruct(queries.shape, bf16),
        in_specs=[smem] + [vmem] * (planes + 13),
        out_specs=vmem,
        scratch_shapes=[pltpu.VMEM((count * KB, 2 * dim), bf16)],
        compiler_params=params,
        name="far",
    )(by_source, *packets, *late, *early, *own, kv, *near)


def solution(mesh):
    in_specs = (P("pb", "grp"), P("pb", "grp"), P("pb", "grp"), P("grp", None), P("grp", None))
    out_specs = P("pb", "grp")
    return jax.shard_map(
        per_device, mesh=mesh, in_specs=in_specs, out_specs=out_specs, check_vma=False
    )
```

time: 33.7 us -> 37.8 us (1.12)
  starting transfers between devices: 11.9 us -> 21.3 us
  waiting for transfers between devices: 9.03 us -> 2.23 us
  local copies, waits for them, and re-layouts: 2.46 us -> 3.41 us
  Pallas kernels: 9.86 us -> 10.3 us
    ppermute x2 -> x13, starting transfers between devices: 5.25 us -> 21.3 us  [permute(): return lax.ppermute(value, 'pb', pairs)]
    ppermute x2 -> x13, waiting for transfers between devices: 9.03 us -> 2.23 us  [permute(): return lax.ppermute(value, 'pb', pairs)]
    all_to_all x1 -> x0, starting transfers between devices: 6.7 us -> none  [per_device(): lax.all_to_all(outgoing, 'pb', split_axis=0, concat_axis=0, tiled=True)]
    unnamed x13 -> x10, local copies, waits for them, and re-layouts: 2.46 us -> 3.41 us
    pallas_call x1, Pallas kernels: 4.41 us -> 5.04 us  [per_device(): pl.pallas_call(functools.partial(far_kernel, count, min(count, 16), scale...]
    pallas_call x1 -> x2, Pallas kernels: 1.76 us -> 1.54 us  [the longest x1 0.79 us: per_device(): pl.pallas_call(functools.partial(pack_kernel, count), out_shape=[rows(row...]
  transfers between devices with their start and end apart: 3 -> 13, of which waited for: 2 -> 1; matrix products, arithmetic and copies ran while one was open for 0% -> 0% of each run, Pallas kernels for 11% -> 12%
where the time goes in v2:
time: 37.8 us; the launch traced here: 37.4 us
  starting transfers between devices  21.3 us (56%)
  Pallas kernels  10.3 us (27%)
  local copies, waits for them, and re-layouts  3.41 us (9%)
  waiting for transfers between devices  2.23 us (6%)
    ppermute x13, starting transfers between devices, permute(): return lax.ppermute(value, 'pb', pairs)  21.3 us
    pallas_call x1, Pallas kernels, per_device(): pl.pallas_call(functools.partial(far_kernel, count, min(count, 16), scale...  5.04 us
    pallas_call x1, Pallas kernels, per_device(): pl.pallas_call(functools.partial(near_kernel, count, scale), out_shape=[j...  3.7 us
    unnamed x10, local copies, waits for them, and re-layouts  3.41 us
    ppermute x13, waiting for transfers between devices, permute(): return lax.ppermute(value, 'pb', pairs)  2.23 us
    pallas_call x1, Pallas kernels, per_device(): pl.pallas_call(functools.partial(pack_kernel, count), out_shape=[rows(row...  0.79 us
  transfers between devices with their start and end apart: 13, of which 1 were waited for; matrix products, arithmetic and copies ran while one was open for 0% of the time, Pallas kernels for 12%

profile of v2, /device:TPU:11, one launch (start us, length us, event | category | flops | bytes accessed | tf_op | source)
XLA Modules:
  0.0 37.4 jit_solution(564797550714370022)
XLA Ops:
  0.0 0.7 %copy-done = s32[32,16]{0,1:T(8,128)S(1)} copy-done((s32[32,16]{0,1:T(8,128)S(1)}, s32[32,16]{0,1:T(8,128)}, u32[]{:S(2)}) %copy-start) | copy-done | bytes 2072
  0.7 0.8 %copy-done.1 = bf16[256,128]{1,0:T(8,128)(2,1)S(1)} copy-done((bf16[256,128]{1,0:T(8,128)(2,1)S(1)}, bf16[256,128]{1,0:T(8,128)(2,1)}, u32[]{:S(2)}) %copy-start.1) | copy-done | bytes 65560
  1.5 0.8 %copy-done.2 = bf16[256,128]{1,0:T(8,128)(2,1)S(1)} copy-done((bf16[256,128]{1,0:T(8,128)(2,1)S(1)}, bf16[256,128]{1,0:T(8,128)(2,1)}, u32[]{:S(2)}) %copy-start.2) | copy-done | bytes 65560
  2.4 0.8 %pack.1 = (bf16[256,256]{1,0:T(8,128)(2,1)S(1)}, bf16[128,256]{1,0:T(8,128)(2,1)S(1)}, bf16[160,256]{1,0:T(8,128)(2,1)S(1)}, bf16[64,256]{1,0:T(8,128)(2,1)S(1)}...) custom-call(s32[16,32]{1,0:T(8,128)S(1)} %bitcast.1, ...), custom_call_target="tpu_custom_call" | custom-call | tf_op jit(solution)/shard_map/pack/pallas_call | solution.py:242
  3.2 1.3 %collective-permute-start = (bf16[128,256]{1,0:T(8,128)(2,1)S(1)}, bf16[128,256]{1,0:T(8,128)(2,1)S(1)}, u32[]{:S(2)}, u32[]{:S(2)}) collective-permute-start(bf16[128,256]{1,0:T(8,128)(2,1)S(1)} %get-tuple-element.23), channel_id=1, source_target_pairs={{0,4},{1,5},{2,6},{3,7},{4,8},{5,9},{6,10},{7,11},{8,12},{9,13},{1... | collective-permute-start | bytes 196616 | tf_op jit(solution)/shard_map/ppermute | solution.py:240
  4.5 1.1 %collective-permute-start.1 = (bf16[128,256]{1,0:T(8,128)(2,1)S(1)}, bf16[128,256]{1,0:T(8,128)(2,1)S(1)}, u32[]{:S(2)}, u32[]{:S(2)}) collective-permute-start(bf16[128,256]{1,0:T(8,128)(2,1)S(1)} %get-tuple-element.24), channel_id=1, source_target_pairs={{0,8},{1,9},{2,10},{3,11},{4,12},{5,13},{6,14},{7,15},{8,0},{9,1},... | collective-permute-start | bytes 196616 | tf_op jit(solution)/shard_map/ppermute | solution.py:240
  5.6 1.4 %collective-permute-start.2 = (bf16[128,256]{1,0:T(8,128)(2,1)S(1)}, bf16[128,256]{1,0:T(8,128)(2,1)S(1)}, u32[]{:S(2)}, u32[]{:S(2)}) collective-permute-start(bf16[128,256]{1,0:T(8,128)(2,1)S(1)} %get-tuple-element.25), channel_id=1, source_target_pairs={{0,12},{1,13},{2,14},{3,15},{4,0},{5,1},{6,2},{7,3},{8,4},{9,5},{1... | collective-permute-start | bytes 196616 | tf_op jit(solution)/shard_map/ppermute | solution.py:240
  7.0 1.5 %collective-permute-start.9 = (bf16[160,256]{1,0:T(8,128)(2,1)S(1)}, bf16[160,256]{1,0:T(8,128)(2,1)S(1)}, u32[]{:S(2)}, u32[]{:S(2)}) collective-permute-start(bf16[160,256]{1,0:T(8,128)(2,1)S(1)} %get-tuple-element.32), channel_id=1, source_target_pairs={{0,1},{1,0},{2,3},{3,2},{4,5},{5,4},{6,7},{7,6},{8,9},{9,8},{10,11... | collective-permute-start | bytes 245768 | tf_op jit(solution)/shard_map/ppermute | solution.py:240
  8.5 0.1 collective-permute-start.11
  8.7 4.0 %collective-permute-start.12 = (bf16[128,256]{1,0:T(8,128)(2,1)S(1)}, bf16[128,256]{1,0:T(8,128)(2,1)S(1)}, u32[]{:S(2)}, u32[]{:S(2)}) collective-permute-start(bf16[128,256]{1,0:T(8,128)(2,1)S(1)} %get-tuple-element.36), channel_id=1, source_target_pairs={{3,4},{7,8},{11,12},{4,3},{8,7},{12,11},{19,20},{23,24},{27,28},{2... | collective-permute-start | bytes 196616 | tf_op jit(solution)/shard_map/ppermute | solution.py:240
  12.7 0.0 collective-permute-done.2.refs_2_
  12.7 0.8 %select.1 = (bf16[96,256]{1,0:T(8,128)(2,1)S(1)}, bf16[96,256]{1,0:T(8,128)(2,1)S(1)}, bf16[96,256]{1,0:T(8,128)(2,1)S(1)}, bf16[96,256]{1,0:T(8,128)(2,1)S(1)},...) custom-call(s32[16,32]{1,0:T(8,128)S(1)} %bitcast.2, bf16[128,256]{1,0:T(8,128)(2,1)S(1)} %collective-permute-done.refs_0_, ...), custom_call_target="tpu_custom_call" | custom-call | tf_op jit(solution)/shard_map/select/pallas_call | solution.py:276
  13.5 0.1 collective-permute-start.3
  13.6 0.6 %collective-permute-start.10 = (bf16[64,256]{1,0:T(8,128)(2,1)S(1)}, bf16[64,256]{1,0:T(8,128)(2,1)S(1)}, u32[]{:S(2)}, u32[]{:S(2)}) collective-permute-start(bf16[64,256]{1,0:T(8,128)(2,1)S(1)} %get-tuple-element.33), channel_id=1, source_target_pairs={{0,2},{1,3},{2,0},{3,1},{4,6},{5,7},{6,4},{7,5},{8,10},{9,11},{10,... | collective-permute-start | bytes 98312 | tf_op jit(solution)/shard_map/ppermute | solution.py:240
  14.2 2.2 %collective-permute-done.10.refs_10_ = bf16[64,256]{1,0:T(8,128)(2,1)S(1)} collective-permute-done((bf16[64,256]{1,0:T(8,128)(2,1)S(1)}, bf16[64,256]{1,0:T(8,128)(2,1)S(1)}, u32[]{:S(2)}, u32[]{:S(2)}) %collective-permute-start.10) | collective-permute-done | bytes 32800 | tf_op jit(solution)/shard_map/ppermute | solution.py:240
  16.4 0.6 %collective-permute-start.4 = (bf16[96,256]{1,0:T(8,128)(2,1)S(1)}, bf16[96,256]{1,0:T(8,128)(2,1)S(1)}, u32[]{:S(2)}, u32[]{:S(2)}) collective-permute-start(bf16[96,256]{1,0:T(8,128)(2,1)S(1)} %get-tuple-element.27), channel_id=1, source_target_pairs={{0,2},{1,3},{2,0},{3,1},{4,6},{5,7},{6,4},{7,5},{8,10},{9,11},{10,... | collective-permute-start | bytes 147464 | tf_op jit(solution)/shard_map/ppermute | solution.py:240
  17.0 2.6 %collective-permute-start.5 = (bf16[96,256]{1,0:T(8,128)(2,1)S(1)}, bf16[96,256]{1,0:T(8,128)(2,1)S(1)}, u32[]{:S(2)}, u32[]{:S(2)}) collective-permute-start(bf16[96,256]{1,0:T(8,128)(2,1)S(1)} %get-tuple-element.28), channel_id=1, source_target_pairs={{0,3},{1,2},{2,1},{3,0},{4,7},{5,6},{6,5},{7,4},{8,11},{9,10},{10,... | collective-permute-start | bytes 147464 | tf_op jit(solution)/shard_map/ppermute | solution.py:240
  19.6 1.9 %collective-permute-start.6 = (bf16[96,256]{1,0:T(8,128)(2,1)S(1)}, bf16[96,256]{1,0:T(8,128)(2,1)S(1)}, u32[]{:S(2)}, u32[]{:S(2)}) collective-permute-start(bf16[96,256]{1,0:T(8,128)(2,1)S(1)} %get-tuple-element.29), channel_id=1, source_target_pairs={{4,5},{5,4},{6,7},{7,6},{8,9},{9,8},{10,11},{11,10},{12,13},{13,12... | collective-permute-start | bytes 147464 | tf_op jit(solution)/shard_map/ppermute | solution.py:240
  21.6 2.1 %collective-permute-start.7 = (bf16[96,256]{1,0:T(8,128)(2,1)S(1)}, bf16[96,256]{1,0:T(8,128)(2,1)S(1)}, u32[]{:S(2)}, u32[]{:S(2)}) collective-permute-start(bf16[96,256]{1,0:T(8,128)(2,1)S(1)} %get-tuple-element.30), channel_id=1, source_target_pairs={{4,6},{5,7},{6,4},{7,5},{8,10},{9,11},{10,8},{11,9},{12,14},{13,15... | collective-permute-start | bytes 147464 | tf_op jit(solution)/shard_map/ppermute | solution.py:240
  23.7 3.8 %collective-permute-start.8 = (bf16[96,256]{1,0:T(8,128)(2,1)S(1)}, bf16[96,256]{1,0:T(8,128)(2,1)S(1)}, u32[]{:S(2)}, u32[]{:S(2)}) collective-permute-start(bf16[96,256]{1,0:T(8,128)(2,1)S(1)} %get-tuple-element.31), channel_id=1, source_target_pairs={{4,7},{5,6},{6,5},{7,4},{8,11},{9,10},{10,9},{11,8},{12,15},{13,14... | collective-permute-start | bytes 147464 | tf_op jit(solution)/shard_map/ppermute | solution.py:240
  27.5 0.0 copy-start.3
  27.6 1.0 %copy-done.3 = bf16[256,1024]{1,0:T(8,128)(2,1)S(1)} copy-done((bf16[256,1024]{1,0:T(8,128)(2,1)S(1)}, bf16[256,1024]{1,0:T(8,128)(2,1)}, u32[]{:S(2)}) %copy-start.3) | copy-done | bytes 524312
  28.6 3.7 %near.1 = (bf16[2,1024,128]{2,1,0:T(8,128)(2,1)S(1)}, f32[2,1,1024]{2,1,0:T(1,128)S(1)}, f32[2,1,1024]{2,1,0:T(1,128)S(1)}, f32[2,128,1024]{2,1,0:T(8,128)S(1)}) custom-call(bf16[256,1024]{1,0:T(8,128)(2,1)S(1)} %copy-done.3, bf16[128,128]{1,0:T(8,128)(2,1)S(1)} %copy-done.4, bf16[256,256]{1,0:T(8,128)(2,1)S(1)} %get-tuple-element.35.kv_ref.refs_12_, ...), custom_call_target="tpu_custom_call" | custom-call | flops 700000000 | bytes 2500000 | tf_op jit(solution)/shard_map/near/pallas_call | solution.py:261
  32.3 5.0 %far.1 = bf16[256,1024]{1,0:T(8,128)(2,1)} custom-call(s32[16,32]{1,0:T(8,128)S(1)} %bitcast.3, bf16[128,256]{1,0:T(8,128)(2,1)S(1)} %collective-permute-done.refs_0_, bf16[128,256]{1,0:T(8,128)(2,1)S(1)} %collective-permute-done.1.refs_1_, bf16[128,256]{1,0:T(8,128)(2,1)S(1)} %collective-permute-done.2.refs_2_, ...), custom_call_target="tpu_custom_call" | custom-call | tf_op jit(solution)/shard_map/far/pallas_call | solution.py:287
  (16 shorter events, 0.0 us)
Async XLA Ops:
  0.0 0.7 %copy-start = (s32[32,16]{0,1:T(8,128)S(1)}, s32[32,16]{0,1:T(8,128)}, u32[]{:S(2)}) copy-start(s32[32,16]{0,1:T(8,128)} %param.9) | copy-start | bytes 6148
  0.7 0.8 %copy-start.1 = (bf16[256,128]{1,0:T(8,128)(2,1)S(1)}, bf16[256,128]{1,0:T(8,128)(2,1)}, u32[]{:S(2)}) copy-start(bf16[256,128]{1,0:T(8,128)(2,1)} %k_ref.1) | copy-start | bytes 196612
  1.5 0.8 %copy-start.2 = (bf16[256,128]{1,0:T(8,128)(2,1)S(1)}, bf16[256,128]{1,0:T(8,128)(2,1)}, u32[]{:S(2)}) copy-start(bf16[256,128]{1,0:T(8,128)(2,1)} %v_ref.1) | copy-start | bytes 196612
  3.2 5.5 %collective-permute-start = (bf16[128,256]{1,0:T(8,128)(2,1)S(1)}, bf16[128,256]{1,0:T(8,128)(2,1)S(1)}, u32[]{:S(2)}, u32[]{:S(2)}) collective-permute-start(bf16[128,256]{1,0:T(8,128)(2,1)S(1)} %get-tuple-element.23), channel_id=1, source_target_pairs={{0,4},{1,5},{2,6},{3,7},{4,8},{5,9},{6,10},{7,11},{8,12},{9,13},{1... | collective-permute-start | bytes 196616 | tf_op jit(solution)/shard_map/ppermute | solution.py:240
  4.5 8.2 %collective-permute-start.1 = (bf16[128,256]{1,0:T(8,128)(2,1)S(1)}, bf16[128,256]{1,0:T(8,128)(2,1)S(1)}, u32[]{:S(2)}, u32[]{:S(2)}) collective-permute-start(bf16[128,256]{1,0:T(8,128)(2,1)S(1)} %get-tuple-element.24), channel_id=1, source_target_pairs={{0,8},{1,9},{2,10},{3,11},{4,12},{5,13},{6,14},{7,15},{8,0},{9,1},... | collective-permute-start | bytes 196616 | tf_op jit(solution)/shard_map/ppermute | solution.py:240
  5.6 7.1 %collective-permute-start.2 = (bf16[128,256]{1,0:T(8,128)(2,1)S(1)}, bf16[128,256]{1,0:T(8,128)(2,1)S(1)}, u32[]{:S(2)}, u32[]{:S(2)}) collective-permute-start(bf16[128,256]{1,0:T(8,128)(2,1)S(1)} %get-tuple-element.25), channel_id=1, source_target_pairs={{0,12},{1,13},{2,14},{3,15},{4,0},{5,1},{6,2},{7,3},{8,4},{9,5},{1... | collective-permute-start | bytes 196616 | tf_op jit(solution)/shard_map/ppermute | solution.py:240
  7.0 12.6 %collective-permute-start.9 = (bf16[160,256]{1,0:T(8,128)(2,1)S(1)}, bf16[160,256]{1,0:T(8,128)(2,1)S(1)}, u32[]{:S(2)}, u32[]{:S(2)}) collective-permute-start(bf16[160,256]{1,0:T(8,128)(2,1)S(1)} %get-tuple-element.32), channel_id=1, source_target_pairs={{0,1},{1,0},{2,3},{3,2},{4,5},{5,4},{6,7},{7,6},{8,9},{9,8},{10,11... | collective-permute-start | bytes 245768 | tf_op jit(solution)/shard_map/ppermute | solution.py:240
  8.5 13.0 %collective-permute-start.11 = (bf16[160,256]{1,0:T(8,128)(2,1)S(1)}, bf16[160,256]{1,0:T(8,128)(2,1)S(1)}, u32[]{:S(2)}, u32[]{:S(2)}) collective-permute-start(bf16[160,256]{1,0:T(8,128)(2,1)S(1)} %get-tuple-element.34), channel_id=1, source_target_pairs={{0,3},{1,2},{2,1},{3,0},{4,7},{5,6},{6,5},{7,4},{8,11},{9,10},{10,... | collective-permute-start | bytes 245768 | tf_op jit(solution)/shard_map/ppermute | solution.py:240
  8.7 18.9 %copy-start.4 = (bf16[128,128]{1,0:T(8,128)(2,1)S(1)}, bf16[128,128]{1,0:T(8,128)(2,1)}, u32[]{:S(2)}) copy-start(bf16[128,128]{1,0:T(8,128)(2,1)} %basis_ref.1) | copy-start | bytes 98308
  8.7 8.3 %collective-permute-start.12 = (bf16[128,256]{1,0:T(8,128)(2,1)S(1)}, bf16[128,256]{1,0:T(8,128)(2,1)S(1)}, u32[]{:S(2)}, u32[]{:S(2)}) collective-permute-start(bf16[128,256]{1,0:T(8,128)(2,1)S(1)} %get-tuple-element.36), channel_id=1, source_target_pairs={{3,4},{7,8},{11,12},{4,3},{8,7},{12,11},{19,20},{23,24},{27,28},{2... | collective-permute-start | bytes 196616 | tf_op jit(solution)/shard_map/ppermute | solution.py:240
  13.5 10.2 %collective-permute-start.3 = (bf16[96,256]{1,0:T(8,128)(2,1)S(1)}, bf16[96,256]{1,0:T(8,128)(2,1)S(1)}, u32[]{:S(2)}, u32[]{:S(2)}) collective-permute-start(bf16[96,256]{1,0:T(8,128)(2,1)S(1)} %get-tuple-element.26), channel_id=1, source_target_pairs={{0,1},{1,0},{2,3},{3,2},{4,5},{5,4},{6,7},{7,6},{8,9},{9,8},{10,11... | collective-permute-start | bytes 147464 | tf_op jit(solution)/shard_map/ppermute | solution.py:240
  13.6 2.8 %collective-permute-start.10 = (bf16[64,256]{1,0:T(8,128)(2,1)S(1)}, bf16[64,256]{1,0:T(8,128)(2,1)S(1)}, u32[]{:S(2)}, u32[]{:S(2)}) collective-permute-start(bf16[64,256]{1,0:T(8,128)(2,1)S(1)} %get-tuple-element.33), channel_id=1, source_target_pairs={{0,2},{1,3},{2,0},{3,1},{4,6},{5,7},{6,4},{7,5},{8,10},{9,11},{10,... | collective-permute-start | bytes 98312 | tf_op jit(solution)/shard_map/ppermute | solution.py:240
  16.4 15.9 %collective-permute-start.4 = (bf16[96,256]{1,0:T(8,128)(2,1)S(1)}, bf16[96,256]{1,0:T(8,128)(2,1)S(1)}, u32[]{:S(2)}, u32[]{:S(2)}) collective-permute-start(bf16[96,256]{1,0:T(8,128)(2,1)S(1)} %get-tuple-element.27), channel_id=1, source_target_pairs={{0,2},{1,3},{2,0},{3,1},{4,6},{5,7},{6,4},{7,5},{8,10},{9,11},{10,... | collective-permute-start | bytes 147464 | tf_op jit(solution)/shard_map/ppermute | solution.py:240
  17.0 15.3 %collective-permute-start.5 = (bf16[96,256]{1,0:T(8,128)(2,1)S(1)}, bf16[96,256]{1,0:T(8,128)(2,1)S(1)}, u32[]{:S(2)}, u32[]{:S(2)}) collective-permute-start(bf16[96,256]{1,0:T(8,128)(2,1)S(1)} %get-tuple-element.28), channel_id=1, source_target_pairs={{0,3},{1,2},{2,1},{3,0},{4,7},{5,6},{6,5},{7,4},{8,11},{9,10},{10,... | collective-permute-start | bytes 147464 | tf_op jit(solution)/shard_map/ppermute | solution.py:240
  19.6 12.7 %collective-permute-start.6 = (bf16[96,256]{1,0:T(8,128)(2,1)S(1)}, bf16[96,256]{1,0:T(8,128)(2,1)S(1)}, u32[]{:S(2)}, u32[]{:S(2)}) collective-permute-start(bf16[96,256]{1,0:T(8,128)(2,1)S(1)} %get-tuple-element.29), channel_id=1, source_target_pairs={{4,5},{5,4},{6,7},{7,6},{8,9},{9,8},{10,11},{11,10},{12,13},{13,12... | collective-permute-start | bytes 147464 | tf_op jit(solution)/shard_map/ppermute | solution.py:240
  21.6 10.8 %collective-permute-start.7 = (bf16[96,256]{1,0:T(8,128)(2,1)S(1)}, bf16[96,256]{1,0:T(8,128)(2,1)S(1)}, u32[]{:S(2)}, u32[]{:S(2)}) collective-permute-start(bf16[96,256]{1,0:T(8,128)(2,1)S(1)} %get-tuple-element.30), channel_id=1, source_target_pairs={{4,6},{5,7},{6,4},{7,5},{8,10},{9,11},{10,8},{11,9},{12,14},{13,15... | collective-permute-start | bytes 147464 | tf_op jit(solution)/shard_map/ppermute | solution.py:240
  23.7 8.7 %collective-permute-start.8 = (bf16[96,256]{1,0:T(8,128)(2,1)S(1)}, bf16[96,256]{1,0:T(8,128)(2,1)S(1)}, u32[]{:S(2)}, u32[]{:S(2)}) collective-permute-start(bf16[96,256]{1,0:T(8,128)(2,1)S(1)} %get-tuple-element.31), channel_id=1, source_target_pairs={{4,7},{5,6},{6,5},{7,4},{8,11},{9,10},{10,9},{11,8},{12,15},{13,14... | collective-permute-start | bytes 147464 | tf_op jit(solution)/shard_map/ppermute | solution.py:240
  27.5 1.0 %copy-start.3 = (bf16[256,1024]{1,0:T(8,128)(2,1)S(1)}, bf16[256,1024]{1,0:T(8,128)(2,1)}, u32[]{:S(2)}) copy-start(bf16[256,1024]{1,0:T(8,128)(2,1)} %q_ref.1) | copy-start | bytes 1572868

commit v3 on v0

v3 whole, which is shorter than its diff:
```python
import functools
import math

import jax
import jax.numpy as jnp
from jax import lax
from jax.experimental import pallas as pl
from jax.experimental.pallas import tpu as pltpu
from jax.sharding import PartitionSpec as P

KB = 32
PLANE = 4
NEG = -1e30
VMEM_BYTES = 40 * 1024 * 1024
CHUNK = 16


def place(count):
    me = lax.axis_index("pb")
    return me, me // PLANE, me % PLANE


def sub(index):
    return pl.ds(pl.multiple_of(index * KB, KB), KB)


def at(n):
    return slice(n * KB, (n + 1) * KB)


def scores_of(k, q):
    return lax.dot_general(k, q, (((1,), (1,)), ((), ())), preferred_element_type=jnp.float32)


def pack_kernel(count, picks_ref, k_ref, v_ref, *refs):
    planes = count // PLANE
    kv_ref, table_ref, mine_ref, cross_ref, own_refs, packet_refs = refs[0], refs[1], refs[2], refs[3], refs[4:7], refs[7:]
    me, z, r = place(count)
    dim = k_ref.shape[1]
    per_half = k_ref.shape[0] // 2 // KB
    kv_ref[:, :dim] = k_ref[...]
    kv_ref[:, dim:] = v_ref[...]

    def late_pick(source, dest):
        return jnp.maximum(picks_ref[source, 2 * count - 1 - dest], 0)

    for j, ref in enumerate(packet_refs, 1):
        up = z + j < planes
        to = jnp.where(up, 0, (z + j - planes) * PLANE)
        for t in range(PLANE):
            ref[at(t)] = kv_ref[sub(jnp.where(up, t, late_pick(me, to + t)))]
    mine_ref[...] = kv_ref[sub(late_pick(me, me))]
    for m, ref in enumerate(own_refs, 1):
        peer = r ^ m
        dest = z * PLANE + peer
        ref[at(0)] = kv_ref[sub(late_pick(me, dest))]
        ref[at(1)] = kv_ref[sub(jnp.maximum(picks_ref[me, dest], 0))]
        if m != 2:
            start = jnp.where(r < peer, 0, per_half)
            for t in range(per_half):
                ref[at(t + 2)] = kv_ref[sub(start + t)]
    start = jnp.where(r == PLANE - 1, 0, per_half)
    for t in range(per_half):
        cross_ref[at(t)] = kv_ref[sub(start + t)]
    for j in range(1, planes):
        up = z >= j
        source = jnp.where(up, z - j, z - j + planes) * PLANE + r
        for m in range(PLANE):
            peer = r ^ m
            dest = z * PLANE + peer
            row = ((j - 1) * PLANE + m) * 2
            late = jnp.where(up, late_pick(source, dest), peer)
            early = jnp.where(up, jnp.maximum(picks_ref[source, dest], 0), 0)
            table_ref[row : row + 1] = jnp.full((1, dim), late, jnp.int32)
            table_ref[row + 1 : row + 2] = jnp.full((1, dim), early, jnp.int32)


def select_kernel(count, table_ref, own2_ref, *refs):
    planes = count // PLANE
    packet_refs, moved_refs = refs[: planes - 1], refs[planes - 1 :]
    dim = table_ref.shape[1]
    moved_refs[2][at(2 * planes - 2)] = own2_ref[at(0)]
    moved_refs[2][at(2 * planes - 1)] = own2_ref[at(1)]
    for j, packet in enumerate(packet_refs):
        for part in (slice(0, dim), slice(dim, 2 * dim)):
            choices = [packet[at(t), part] for t in range(PLANE)]
            for m in range(PLANE):
                for kind in range(2):
                    row = (j * PLANE + m) * 2 + kind
                    index = jnp.broadcast_to(table_ref[row : row + 1], (KB, dim))
                    value = choices[0]
                    for t in range(1, PLANE):
                        value = jnp.where(index == t, choices[t], value)
                    moved_refs[m][at(j + kind * (planes - 1)), part] = value


def attend_all(n_cols, score, v_ts, state, save):
    ahead = score(0)
    for step in range(n_cols):
        s = ahead
        if step + 1 < n_cols:
            ahead = score(step + 1)
        m = jnp.max(s, axis=0, keepdims=True)
        if state is not None:
            m_old, l_old, acc_old = state(step)
            m = jnp.maximum(m, m_old)
        w = jnp.exp2(s - m)
        l = jnp.sum(w, axis=0, keepdims=True)
        acc = jnp.dot(v_ts, w.astype(jnp.bfloat16), preferred_element_type=jnp.float32)
        if state is not None:
            old = jnp.exp2(m_old - m)
            l = l + l_old * old
            acc = acc + acc_old * old
        save(step, m, l, acc)


def fold(kv, masks, scale, width, block, rot_ref, old_refs, save):
    dim = rot_ref.shape[2]
    total = len(masks)
    steps = rot_ref.shape[1] // width
    carried = [tuple(ref[block, :, step * width : (step + 1) * width] for ref in old_refs) for step in range(steps)]
    for first in range(0, total, CHUNK):
        last = min(first + CHUNK, total)
        k = kv[first * KB : last * KB, :dim]
        v_t = kv[first * KB : last * KB, dim:].T

        def score(step, k=k, first=first, last=last):
            s = scores_of(k, rot_ref[block, step * width : (step + 1) * width, :]) * scale
            if all(ok is None for ok in masks[first:last]):
                return s
            return jnp.concatenate(
                [s[at(g - first)] if masks[g] is None else jnp.where(masks[g], s[at(g - first)], NEG) for g in range(first, last)]
            )

        def keep(step, *values):
            carried[step] = values

        attend_all(steps, score, v_t, carried.__getitem__, save if last == total else keep)


def near_kernel(scale, width, q_ref, basis_ref, kv_ref, rot_ref, m_ref, l_ref, acc_ref):
    dim = basis_ref.shape[0]
    half = q_ref.shape[0] // 2
    heads = q_ref.shape[1] // dim
    basis = basis_ref[...]
    key_row = lax.broadcasted_iota(jnp.int32, (half, width), 0)
    query = lax.broadcasted_iota(jnp.int32, (half, width), 1) % half
    causal = key_row <= query
    for block in range(2):
        rows = slice(block * half, (block + 1) * half)
        for h in range(heads):
            q = jnp.dot(q_ref[rows, h * dim : (h + 1) * dim], basis, preferred_element_type=jnp.float32)
            rot_ref[block, h * half : (h + 1) * half, :] = q.astype(jnp.bfloat16)
    for block in range(2):
        rows = slice(block * half, (block + 1) * half)
        k, v_t = kv_ref[rows, :dim], kv_ref[rows, dim:].T

        def score(step, block=block, k=k):
            s = scores_of(k, rot_ref[block, step * width : (step + 1) * width, :]) * scale
            return jnp.where(causal, s, NEG)

        def save(step, m, l, acc, block=block):
            for ref, value in zip((m_ref, l_ref, acc_ref), (m, l, acc), strict=True):
                ref[block, :, step * width : (step + 1) * width] = value

        attend_all(heads * half // width, score, v_t, None, save)


def mid_kernel(count, scale, width, *refs):
    kv_ref, cross_ref, own1_ref, own3_ref, mine_ref, moved_ref = refs[:6]
    rot_ref, old, new = refs[6], refs[7:10], refs[10:13]
    me, z, r = place(count)
    planes = count // PLANE
    half = cross_ref.shape[0]
    cross, own1, own3 = cross_ref[...], own1_ref[2 * KB :], own3_ref[2 * KB :]
    for block in range(2):
        if block == 0:
            prev = jnp.where(r == 0, cross, jnp.where(r == 2, own3, own1))
            kv = [prev, own3_ref[at(1)], moved_ref[(planes - 1) * KB :]]
            masks = [me >= 1] * (half // KB) + [(r ^ 3) < r - 1] + [z >= j for j in range(1, planes)]
        else:
            prev = jnp.where(r == PLANE - 1, cross, jnp.where(r == 1, own3, own1))
            prev = jnp.where(me == count - 1, kv_ref[:half], prev)
            kv = [prev, own1_ref[at(0)], own3_ref[at(0)], mine_ref[...], moved_ref[: (planes - 1) * KB]]
            masks = [None] * (half // KB + 2) + [me < count - 1] + [None] * (planes - 1)

        def save(step, m, l, acc, block=block):
            for ref, value in zip(new, (m, l, acc), strict=True):
                ref[block, :, step * width : (step + 1) * width] = value

        fold(jnp.concatenate(kv, axis=0), masks, scale, width, block, rot_ref, old, save)


def far_kernel(count, scale, width, *refs):
    moved_refs, rot_ref, old, out_ref = refs[0:3], refs[3], refs[4:7], refs[7]
    me, z, r = place(count)
    planes = count // PLANE
    dim = rot_ref.shape[2]
    half = out_ref.shape[0] // 2

    def finish(block, step, l, acc):
        done = acc / l
        for h in range(width // half):
            head = step * (width // half) + h
            out_ref[block * half : (block + 1) * half, head * dim : (head + 1) * dim] = (
                done[:, h * half : (h + 1) * half].T.astype(out_ref.dtype)
            )

    def run(block):
        parts, masks = [], []
        for m, ref in enumerate(moved_refs, 1):
            first = (1 - block) * (planes - 1)
            parts.append(ref[first * KB : (first + planes - 1) * KB])
            masks += [None if block else (z >= j) & ((z - j) * PLANE + (r ^ m) < me - 1) for j in range(1, planes)]
        parts.append(moved_refs[1][at(2 * planes - 1 - block)])
        masks.append(None if block else (r ^ 2) < r - 1)
        kv = jnp.concatenate(parts, axis=0)
        fold(kv, masks, scale, width, block, rot_ref, old, lambda step, m, l, acc: finish(block, step, l, acc))

    run(1)

    @pl.when(me >= 2)
    def _():
        run(0)

    @pl.when(me < 2)
    def _():
        for step in range(rot_ref.shape[1] // width):
            cols = slice(step * width, (step + 1) * width)
            finish(0, step, old[1][0, :, cols], old[2][0, :, cols])


def per_device(queries, keys, values, basis, picks):
    rows_dev, dim = keys.shape
    half = rows_dev // 2
    count = lax.axis_size("pb")
    planes = count // PLANE
    wide = queries.shape[1] // dim * half
    width = 2 * half
    scale = dim**-0.5 * math.log2(math.e)
    vmem = pl.BlockSpec(memory_space=pltpu.VMEM)
    smem = pl.BlockSpec(memory_space=pltpu.SMEM)
    params = pltpu.CompilerParams(vmem_limit_bytes=VMEM_BYTES)
    bf16, f32 = jnp.bfloat16, jnp.float32
    state = [
        jax.ShapeDtypeStruct((2, 1, wide), f32),
        jax.ShapeDtypeStruct((2, 1, wide), f32),
        jax.ShapeDtypeStruct((2, dim, wide), f32),
    ]

    def rows(n):
        return jax.ShapeDtypeStruct((n * KB, 2 * dim), bf16)

    def permute(value, pairs):
        return lax.ppermute(value, "pb", pairs)

    def cost(keys_each):
        return pl.CostEstimate(
            flops=8 * wide * keys_each * dim, bytes_accessed=4_000_000, transcendentals=2 * wide * keys_each
        )

    by_source = picks.T
    per_half = half // KB
    table = jax.ShapeDtypeStruct(((planes - 1) * PLANE * 2, dim), jnp.int32)
    kv, table, mine, cross, *rest = pl.pallas_call(
        functools.partial(pack_kernel, count),
        out_shape=[rows(2 * per_half), table, rows(1), rows(per_half), rows(2 + per_half), rows(2), rows(2 + per_half)]
        + [rows(PLANE)] * (planes - 1),
        in_specs=[smem, vmem, vmem],
        out_specs=[vmem] * (6 + planes),
        compiler_params=pltpu.CompilerParams(vmem_limit_bytes=62 * 1024 * 1024),
        name="pack",
    )(by_source, keys, values)
    own, packets = rest[:3], rest[3:]

    packets = [
        permute(packet, [(s, (s + j * PLANE) % count) for s in range(count)]) for j, packet in enumerate(packets, 1)
    ]

    near = pl.pallas_call(
        functools.partial(near_kernel, scale, width),
        out_shape=[jax.ShapeDtypeStruct((2, wide, dim), bf16)] + state,
        in_specs=[vmem] * 3,
        out_specs=[vmem] * 4,
        compiler_params=params,
        cost_estimate=cost(half),
        name="near",
    )(queries, basis, kv)
    packets, near = lax.optimization_barrier((packets, near))
    direct = [permute(own[m - 1], [(s, s ^ m) for s in range(count)]) for m in (1, 3)]
    borders = range(PLANE - 1, count - 1, PLANE)
    cross = permute(cross, [(s, s + 1) for s in borders] + [(s + 1, s) for s in borders])

    moved = list(
        pl.pallas_call(
            functools.partial(select_kernel, count),
            out_shape=[rows(2 * planes - 2 + 2 * (m == 2)) for m in range(PLANE)],
            in_specs=[vmem] * (planes + 1),
            out_specs=[vmem] * PLANE,
            compiler_params=params,
            name="select",
        )(table, own[1], *packets)
    )
    for m in (2, 3):
        moved[m] = permute(moved[m], [(s, s ^ m) for s in range(count)])

    mid = pl.pallas_call(
        functools.partial(mid_kernel, count, scale, width),
        out_shape=state,
        in_specs=[vmem] * 10,
        out_specs=[vmem] * 3,
        compiler_params=params,
        cost_estimate=cost(2 * half),
        name="mid",
    )(kv, cross, *direct, mine, moved[0], *near)
    moved[1], mid = lax.optimization_barrier((moved[1], mid))
    moved[1] = permute(moved[1], [(s, s ^ 1) for s in range(count)])

    return pl.pallas_call(
        functools.partial(far_kernel, count, scale, width),
        out_shape=jax.ShapeDtypeStruct(queries.shape, bf16),
        in_specs=[vmem] * 7,
        out_specs=vmem,
        compiler_params=params,
        cost_estimate=cost(3 * half),
        name="far",
    )(*moved[1:], near[0], *mid)


def solution(mesh):
    in_specs = (P("pb", "grp"), P("pb", "grp"), P("pb", "grp"), P("grp", None), P("grp", None))
    out_specs = P("pb", "grp")
    return jax.shard_map(
        per_device, mesh=mesh, in_specs=in_specs, out_specs=out_specs, check_vma=False
    )
```

time: 34.6 us -> 24.7 us (0.71)
  waiting for transfers between devices: 10.3 us -> 3.72 us
  Pallas kernels: 0 us -> 6.05 us
  other arithmetic: 4.42 us -> 0 us
  matrix products: 3.25 us -> 0 us
  local copies, waits for them, and re-layouts: 4.25 us -> 1.96 us
  starting transfers between devices: 11.7 us -> 12.6 us
    all_to_all x1 -> x0, waiting for transfers between devices: 10.3 us -> none  [per_device(): lax.all_to_all(outgoing, 'pb', split_axis=0, concat_axis=0, tiled=True)]
    ppermute x2 -> x9, starting transfers between devices: 3.6 us -> 12.6 us  [permute(): return lax.ppermute(value, 'pb', pairs)]
    all_to_all x1 -> x0, starting transfers between devices: 8.1 us -> none  [per_device(): lax.all_to_all(outgoing, 'pb', split_axis=0, concat_axis=0, tiled=True)]
    pallas_call x0 -> x5, Pallas kernels: none -> 6.05 us  [the longest x1 1.84 us: per_device(): pl.pallas_call(functools.partial(pack_kernel, count), out_shape=[rows(2 *...]
    ppermute x2 -> x9, waiting for transfers between devices: 0.01 us -> 3.72 us  [permute(): return lax.ppermute(value, 'pb', pairs)]
    dot_general x5 -> x0, matrix products: 3.25 us -> none  [the longest x2 1.77 us: attend(): jnp.einsum('hqk,kd->qhd', weight_b, vals_all, preferred_element_type=jnp....]
    select_n x3 -> x0, other arithmetic: 1.71 us -> none  [the longest x1 0.93 us: per_device(): jnp.where((wanted_by >= 0)[:, :, None, None], outgoing, jnp.zeros_like(ou...]
    reduce_sum x2 -> x0, other arithmetic: 1.31 us -> none  [attend(): total = jnp.sum(weight, axis=-1)]
  transfers between devices with their start and end apart: 3 -> 9, of which waited for: 1 -> 1; matrix products, arithmetic and copies ran while one was open for 13% -> 0% of each run, Pallas kernels for 0% -> 10%
where the time goes in v3:
time: 24.7 us; the launch traced here: 24.4 us
  starting transfers between devices  12.6 us (51%)
  Pallas kernels  6.05 us (24%)
  waiting for transfers between devices  3.72 us (15%)
  local copies, waits for them, and re-layouts  1.96 us (8%)
    ppermute x9, starting transfers between devices, permute(): return lax.ppermute(value, 'pb', pairs)  12.6 us
    ppermute x9, waiting for transfers between devices, permute(): return lax.ppermute(value, 'pb', pairs)  3.72 us
    unnamed x14, local copies, waits for them, and re-layouts  1.96 us
    pallas_call x1, Pallas kernels, per_device(): pl.pallas_call(functools.partial(pack_kernel, count), out_shape=[rows(2 *...  1.84 us
    pallas_call x1, Pallas kernels, per_device(): pl.pallas_call(functools.partial(far_kernel, count, scale, width), out_sh...  1.78 us
    pallas_call x1, Pallas kernels, per_device(): pl.pallas_call(functools.partial(mid_kernel, count, scale, width), out_sh...  1.35 us
    pallas_call x1, Pallas kernels, per_device(): pl.pallas_call(functools.partial(near_kernel, scale, width), out_shape=[j...  0.97 us
  transfers between devices with their start and end apart: 9, of which 1 were waited for; matrix products, arithmetic and copies ran while one was open for 0% of the time, Pallas kernels for 10%

profile of v3, /device:TPU:0, one launch (start us, length us, event | category | flops | bytes accessed | tf_op | source)
XLA Modules:
  0.0 24.4 jit_solution(4751383608930918156)
XLA Ops:
  0.0 1.8 %pack.1 = (bf16[256,256]{1,0:T(8,128)(2,1)}, s32[24,128]{1,0:T(8,128)}, bf16[32,256]{1,0:T(8,128)(2,1)}, bf16[128,256]{1,0:T(8,128)(2,1)}, bf16[192,256]{1,0:T(8...) custom-call(s32[16,32]{1,0:T(8,128)} %bitcast.1, ...), custom_call_target="tpu_custom_call" | custom-call | tf_op jit(solution)/shard_map/pack/pallas_call | solution.py:265
  1.8 3.0 %collective-permute-start = (bf16[128,256]{1,0:T(8,128)(2,1)}, bf16[128,256]{1,0:T(8,128)(2,1)S(1)}, u32[]{:S(2)}, u32[]{:S(2)}) collective-permute-start(bf16[128,256]{1,0:T(8,128)(2,1)} %get-tuple-element.39), channel_id=1, source_target_pairs={{0,4},{1,5},{2,6},{3,7},{4,8},{5,9},{6,10},{7,11},{8,12},{9,13},{1... | collective-permute-start | bytes 196616 | tf_op jit(solution)/shard_map/ppermute | solution.py:255
  4.9 0.0 collective-permute-start.4
  4.9 1.6 %collective-permute-start.5 = (bf16[192,256]{1,0:T(8,128)(2,1)}, bf16[192,256]{1,0:T(8,128)(2,1)S(1)}, u32[]{:S(2)}, u32[]{:S(2)}) collective-permute-start(bf16[192,256]{1,0:T(8,128)(2,1)} %get-tuple-element.53), channel_id=1, source_target_pairs={{0,3},{1,2},{2,1},{3,0},{4,7},{5,6},{6,5},{7,4},{8,11},{9,10},{10,... | collective-permute-start | bytes 294920 | tf_op jit(solution)/shard_map/ppermute | solution.py:255
  6.5 2.6 %collective-permute-start.1 = (bf16[128,256]{1,0:T(8,128)(2,1)}, bf16[128,256]{1,0:T(8,128)(2,1)S(1)}, u32[]{:S(2)}, u32[]{:S(2)}) collective-permute-start(bf16[128,256]{1,0:T(8,128)(2,1)} %get-tuple-element.40), channel_id=1, source_target_pairs={{0,8},{1,9},{2,10},{3,11},{4,12},{5,13},{6,14},{7,15},{8,0},{9,1},... | collective-permute-start | bytes 196616 | tf_op jit(solution)/shard_map/ppermute | solution.py:255
  9.1 1.3 %collective-permute-start.2 = (bf16[128,256]{1,0:T(8,128)(2,1)}, bf16[128,256]{1,0:T(8,128)(2,1)S(1)}, u32[]{:S(2)}, u32[]{:S(2)}) collective-permute-start(bf16[128,256]{1,0:T(8,128)(2,1)} %get-tuple-element.41), channel_id=1, source_target_pairs={{0,12},{1,13},{2,14},{3,15},{4,0},{5,1},{6,2},{7,3},{8,4},{9,5},{1... | collective-permute-start | bytes 196616 | tf_op jit(solution)/shard_map/ppermute | solution.py:255
  10.4 0.0 collective-permute-done.refs_0_
  10.4 0.7 %collective-permute-start.3 = (bf16[128,256]{1,0:T(8,128)(2,1)}, bf16[128,256]{1,0:T(8,128)(2,1)S(1)}, u32[]{:S(2)}, u32[]{:S(2)}) collective-permute-start(bf16[128,256]{1,0:T(8,128)(2,1)} %get-tuple-element.51), channel_id=1, source_target_pairs={{3,4},{7,8},{11,12},{4,3},{8,7},{12,11},{19,20},{23,24},{27,28},{2... | collective-permute-start | bytes 196616 | tf_op jit(solution)/shard_map/ppermute | solution.py:255
  11.1 0.0 copy-start
  11.1 1.0 %copy-done = bf16[256,1024]{1,0:T(8,128)(2,1)S(1)} copy-done((bf16[256,1024]{1,0:T(8,128)(2,1)S(1)}, bf16[256,1024]{1,0:T(8,128)(2,1)}, u32[]{:S(2)}) %copy-start) | copy-done | bytes 524312
  12.1 0.9 %copy-done.1 = bf16[256,256]{1,0:T(8,128)(2,1)S(1)} copy-done((bf16[256,256]{1,0:T(8,128)(2,1)S(1)}, bf16[256,256]{1,0:T(8,128)(2,1)}, u32[]{:S(2)}) %copy-start.1) | copy-done | bytes 131096
  13.0 1.0 %near.1 = (bf16[2,1024,128]{2,1,0:T(8,128)(2,1)S(1)}, f32[2,1,1024]{2,1,0:T(1,128)S(1)}, f32[2,1,1024]{2,1,0:T(1,128)S(1)}, f32[2,128,1024]{2,1,0:T(8,128)S(1)}) custom-call(bf16[256,1024]{1,0:T(8,128)(2,1)S(1)} %copy-done, bf16[128,128]{1,0:T(8,128)(2,1)S(1)} %copy-done.4, bf16[256,256]{1,0:T(8,128)(2,1)S(1)} %copy-done.1), custom_call_target="tpu_custom_call" | custom-call | flops 134217728 | bytes 4000000 | tf_op jit(solution)/shard_map/near/pallas_call | solution.py:280
  14.0 0.0 copy-start.2
  14.0 0.0 collective-permute-done.2.refs_2_
  14.1 0.1 select.1
  14.2 0.7 %collective-permute-start.7 = (bf16[256,256]{1,0:T(8,128)(2,1)S(1)}, bf16[256,256]{1,0:T(8,128)(2,1)S(1)}, u32[]{:S(2)}, u32[]{:S(2)}) collective-permute-start(bf16[256,256]{1,0:T(8,128)(2,1)S(1)} %get-tuple-element.64), channel_id=1, source_target_pairs={{0,2},{1,3},{2,0},{3,1},{4,6},{5,7},{6,4},{7,5},{8,10},{9,11},{10,... | collective-permute-start | bytes 393224 | tf_op jit(solution)/shard_map/ppermute | solution.py:255
  14.9 2.5 %collective-permute-start.8 = (bf16[192,256]{1,0:T(8,128)(2,1)S(1)}, bf16[192,256]{1,0:T(8,128)(2,1)S(1)}, u32[]{:S(2)}, u32[]{:S(2)}) collective-permute-start(bf16[192,256]{1,0:T(8,128)(2,1)S(1)} %get-tuple-element.65), channel_id=1, source_target_pairs={{0,3},{1,2},{2,1},{3,0},{4,7},{5,6},{6,5},{7,4},{8,11},{9,10},{10,... | collective-permute-start | bytes 294920 | tf_op jit(solution)/shard_map/ppermute | solution.py:255
  17.4 0.0 collective-permute-done.3.refs_1_
  17.5 1.3 %mid.1 = (f32[2,1,1024]{2,1,0:T(1,128)S(1)}, f32[2,1,1024]{2,1,0:T(1,128)S(1)}, f32[2,128,1024]{2,1,0:T(8,128)S(1)}) custom-call(bf16[256,256]{1,0:T(8,128)(2,1)S(1)} %copy-done.2, bf16[128,256]{1,0:T(8,128)(2,1)S(1)} %collective-permute-done.3.refs_1_, bf16[192,256]{1,0:T(8,128)(2,1)S(1)} %collective-permute-done.4.refs_2_, ...), custom_call_target="tpu_custom_call" | custom-call | flops 268435456 | bytes 4000000 | tf_op jit(solution)/shard_map/mid/pallas_call | solution.py:307
  18.8 0.1 collective-permute-start.6
  18.9 3.7 %collective-permute-done.8.refs_2_ = bf16[192,256]{1,0:T(8,128)(2,1)S(1)} collective-permute-done((bf16[192,256]{1,0:T(8,128)(2,1)S(1)}, bf16[192,256]{1,0:T(8,128)(2,1)S(1)}, u32[]{:S(2)}, u32[]{:S(2)}) %collective-permute-start.8) | collective-permute-done | bytes 98336 | tf_op jit(solution)/shard_map/ppermute | solution.py:255
  22.7 0.0 collective-permute-done.7.refs_1_
  22.7 0.0 collective-permute-done.6.refs_0_
  22.7 1.8 %far.1 = bf16[256,1024]{1,0:T(8,128)(2,1)} custom-call(bf16[192,256]{1,0:T(8,128)(2,1)S(1)} %collective-permute-done.6.refs_0_, bf16[256,256]{1,0:T(8,128)(2,1)S(1)} %collective-permute-done.7.refs_1_, bf16[192,256]{1,0:T(8,128)(2,1)S(1)} %collective-permute-done.8.refs_2_, bf16[2,1024,128]{2,1,0:T(8,128)(2,1)S(1)} %get-tuple-element.56.refs_6_.refs_3_, ...), custom_call_target="tpu_custom_call" | custom-call | flops 402653184 | bytes 4000000 | tf_op jit(solution)/shard_map/far/pallas_call | solution.py:319
  (13 shorter events, 0.0 us)
Async XLA Ops:
  0.0 11.1 %copy-start.4 = (bf16[128,128]{1,0:T(8,128)(2,1)S(1)}, bf16[128,128]{1,0:T(8,128)(2,1)}, u32[]{:S(2)}) copy-start(bf16[128,128]{1,0:T(8,128)(2,1)} %basis_ref.1) | copy-start | bytes 98308
  1.8 8.6 %collective-permute-start = (bf16[128,256]{1,0:T(8,128)(2,1)}, bf16[128,256]{1,0:T(8,128)(2,1)S(1)}, u32[]{:S(2)}, u32[]{:S(2)}) collective-permute-start(bf16[128,256]{1,0:T(8,128)(2,1)} %get-tuple-element.39), channel_id=1, source_target_pairs={{0,4},{1,5},{2,6},{3,7},{4,8},{5,9},{6,10},{7,11},{8,12},{9,13},{1... | collective-permute-start | bytes 196616 | tf_op jit(solution)/shard_map/ppermute | solution.py:255
  4.9 12.6 %collective-permute-start.4 = (bf16[192,256]{1,0:T(8,128)(2,1)}, bf16[192,256]{1,0:T(8,128)(2,1)S(1)}, u32[]{:S(2)}, u32[]{:S(2)}) collective-permute-start(bf16[192,256]{1,0:T(8,128)(2,1)} %get-tuple-element.52), channel_id=1, source_target_pairs={{0,1},{1,0},{2,3},{3,2},{4,5},{5,4},{6,7},{7,6},{8,9},{9,8},{10,11... | collective-permute-start | bytes 294920 | tf_op jit(solution)/shard_map/ppermute | solution.py:255
  4.9 12.6 %collective-permute-start.5 = (bf16[192,256]{1,0:T(8,128)(2,1)}, bf16[192,256]{1,0:T(8,128)(2,1)S(1)}, u32[]{:S(2)}, u32[]{:S(2)}) collective-permute-start(bf16[192,256]{1,0:T(8,128)(2,1)} %get-tuple-element.53), channel_id=1, source_target_pairs={{0,3},{1,2},{2,1},{3,0},{4,7},{5,6},{6,5},{7,4},{8,11},{9,10},{10,... | collective-permute-start | bytes 294920 | tf_op jit(solution)/shard_map/ppermute | solution.py:255
  6.5 7.6 %collective-permute-start.1 = (bf16[128,256]{1,0:T(8,128)(2,1)}, bf16[128,256]{1,0:T(8,128)(2,1)S(1)}, u32[]{:S(2)}, u32[]{:S(2)}) collective-permute-start(bf16[128,256]{1,0:T(8,128)(2,1)} %get-tuple-element.40), channel_id=1, source_target_pairs={{0,8},{1,9},{2,10},{3,11},{4,12},{5,13},{6,14},{7,15},{8,0},{9,1},... | collective-permute-start | bytes 196616 | tf_op jit(solution)/shard_map/ppermute | solution.py:255
  9.1 5.0 %collective-permute-start.2 = (bf16[128,256]{1,0:T(8,128)(2,1)}, bf16[128,256]{1,0:T(8,128)(2,1)S(1)}, u32[]{:S(2)}, u32[]{:S(2)}) collective-permute-start(bf16[128,256]{1,0:T(8,128)(2,1)} %get-tuple-element.41), channel_id=1, source_target_pairs={{0,12},{1,13},{2,14},{3,15},{4,0},{5,1},{6,2},{7,3},{8,4},{9,5},{1... | collective-permute-start | bytes 196616 | tf_op jit(solution)/shard_map/ppermute | solution.py:255
  10.4 7.0 %collective-permute-start.3 = (bf16[128,256]{1,0:T(8,128)(2,1)}, bf16[128,256]{1,0:T(8,128)(2,1)S(1)}, u32[]{:S(2)}, u32[]{:S(2)}) collective-permute-start(bf16[128,256]{1,0:T(8,128)(2,1)} %get-tuple-element.51), channel_id=1, source_target_pairs={{3,4},{7,8},{11,12},{4,3},{8,7},{12,11},{19,20},{23,24},{27,28},{2... | collective-permute-start | bytes 196616 | tf_op jit(solution)/shard_map/ppermute | solution.py:255
  11.1 1.0 %copy-start = (bf16[256,1024]{1,0:T(8,128)(2,1)S(1)}, bf16[256,1024]{1,0:T(8,128)(2,1)}, u32[]{:S(2)}) copy-start(bf16[256,1024]{1,0:T(8,128)(2,1)} %q_ref.1) | copy-start | bytes 1572868
  12.1 0.9 %copy-start.1 = (bf16[256,256]{1,0:T(8,128)(2,1)S(1)}, bf16[256,256]{1,0:T(8,128)(2,1)}, u32[]{:S(2)}) copy-start(bf16[256,256]{1,0:T(8,128)(2,1)} %get-tuple-element.42.kv_ref.refs_0_) | copy-start | bytes 393220
  13.0 1.0 %copy-start.3 = (bf16[64,256]{1,0:T(8,128)(2,1)S(1)}, bf16[64,256]{1,0:T(8,128)(2,1)}, u32[]{:S(2)}) copy-start(bf16[64,256]{1,0:T(8,128)(2,1)} %get-tuple-element.38.own2_ref) | copy-start | bytes 98308
  13.0 1.0 %copy-start.6 = (s32[24,128]{1,0:T(8,128)S(1)}, s32[24,128]{1,0:T(8,128)}, u32[]{:S(2)}) copy-start(s32[24,128]{1,0:T(8,128)} %get-tuple-element.37.table_ref) | copy-start | bytes 36868
  14.0 3.4 %copy-start.2 = (bf16[256,256]{1,0:T(8,128)(2,1)S(1)}, bf16[256,256]{1,0:T(8,128)(2,1)}, u32[]{:S(2)}) copy-start(bf16[256,256]{1,0:T(8,128)(2,1)} %get-tuple-element.42.kv_ref.refs_0_) | copy-start | bytes 393220
  14.1 3.4 %copy-start.5 = (bf16[32,256]{1,0:T(8,128)(2,1)S(1)}, bf16[32,256]{1,0:T(8,128)(2,1)}, u32[]{:S(2)}) copy-start(bf16[32,256]{1,0:T(8,128)(2,1)} %get-tuple-element.54.refs_4_) | copy-start | bytes 49156
  14.2 8.5 %collective-permute-start.7 = (bf16[256,256]{1,0:T(8,128)(2,1)S(1)}, bf16[256,256]{1,0:T(8,128)(2,1)S(1)}, u32[]{:S(2)}, u32[]{:S(2)}) collective-permute-start(bf16[256,256]{1,0:T(8,128)(2,1)S(1)} %get-tuple-element.64), channel_id=1, source_target_pairs={{0,2},{1,3},{2,0},{3,1},{4,6},{5,7},{6,4},{7,5},{8,10},{9,11},{10,... | collective-permute-start | bytes 393224 | tf_op jit(solution)/shard_map/ppermute | solution.py:255
  14.9 7.7 %collective-permute-start.8 = (bf16[192,256]{1,0:T(8,128)(2,1)S(1)}, bf16[192,256]{1,0:T(8,128)(2,1)S(1)}, u32[]{:S(2)}, u32[]{:S(2)}) collective-permute-start(bf16[192,256]{1,0:T(8,128)(2,1)S(1)} %get-tuple-element.65), channel_id=1, source_target_pairs={{0,3},{1,2},{2,1},{3,0},{4,7},{5,6},{6,5},{7,4},{8,11},{9,10},{10,... | collective-permute-start | bytes 294920 | tf_op jit(solution)/shard_map/ppermute | solution.py:255
  18.8 3.8 %collective-permute-start.6 = (bf16[192,256]{1,0:T(8,128)(2,1)S(1)}, bf16[192,256]{1,0:T(8,128)(2,1)S(1)}, u32[]{:S(2)}, u32[]{:S(2)}) collective-permute-start(bf16[192,256]{1,0:T(8,128)(2,1)S(1)} %get-tuple-element.63), channel_id=1, source_target_pairs={{0,1},{1,0},{2,3},{3,2},{4,5},{5,4},{6,7},{7,6},{8,9},{9,8},{10,11... | collective-permute-start | bytes 294920 | tf_op jit(solution)/shard_map/ppermute | solution.py:255

commit v4 on v3

--- a/solution.py
+++ b/solution.py
@@ -34,7 +34,7 @@
 
 def pack_kernel(count, picks_ref, k_ref, v_ref, *refs):
     planes = count // PLANE
-    kv_ref, table_ref, mine_ref, cross_ref, own_refs, packet_refs = refs[0], refs[1], refs[2], refs[3], refs[4:7], refs[7:]
+    kv_ref, table_ref, own_ref, inner_ref, cross_ref, packet_refs = *refs[:5], refs[5:]
     me, z, r = place(count)
     dim = k_ref.shape[1]
     per_half = k_ref.shape[0] // 2 // KB
@@ -44,24 +44,24 @@
     def late_pick(source, dest):
         return jnp.maximum(picks_ref[source, 2 * count - 1 - dest], 0)
 
+    def early_pick(source, dest):
+        return jnp.maximum(picks_ref[source, dest], 0)
+
     for j, ref in enumerate(packet_refs, 1):
         up = z + j < planes
         to = jnp.where(up, 0, (z + j - planes) * PLANE)
         for t in range(PLANE):
             ref[at(t)] = kv_ref[sub(jnp.where(up, t, late_pick(me, to + t)))]
-    mine_ref[...] = kv_ref[sub(late_pick(me, me))]
-    for m, ref in enumerate(own_refs, 1):
-        peer = r ^ m
-        dest = z * PLANE + peer
-        ref[at(0)] = kv_ref[sub(late_pick(me, dest))]
-        ref[at(1)] = kv_ref[sub(jnp.maximum(picks_ref[me, dest], 0))]
-        if m != 2:
-            start = jnp.where(r < peer, 0, per_half)
-            for t in range(per_half):
-                ref[at(t + 2)] = kv_ref[sub(start + t)]
-    start = jnp.where(r == PLANE - 1, 0, per_half)
+    for m in range(PLANE):
+        dest = z * PLANE + (r ^ m)
+        own_ref[at(2 * m)] = kv_ref[sub(late_pick(me, dest))]
+        own_ref[at(2 * m + 1)] = kv_ref[sub(early_pick(me, dest))]
     for t in range(per_half):
-        cross_ref[at(t)] = kv_ref[sub(start + t)]
+        index = jnp.where(r == 1, t, per_half + t)
+        if t == 0:
+            index = jnp.where(r == 0, early_pick(me, me + PLANE - 1), index)
+        inner_ref[at(t)] = kv_ref[sub(index)]
+        cross_ref[at(t)] = kv_ref[sub(jnp.where(r == PLANE - 1, t, per_half + t))]
     for j in range(1, planes):
         up = z >= j
         source = jnp.where(up, z - j, z - j + planes) * PLANE + r
@@ -70,28 +70,41 @@
             dest = z * PLANE + peer
             row = ((j - 1) * PLANE + m) * 2
             late = jnp.where(up, late_pick(source, dest), peer)
-            early = jnp.where(up, jnp.maximum(picks_ref[source, dest], 0), 0)
+            early = jnp.where(up, early_pick(source, dest), 0)
             table_ref[row : row + 1] = jnp.full((1, dim), late, jnp.int32)
             table_ref[row + 1 : row + 2] = jnp.full((1, dim), early, jnp.int32)
 
 
-def select_kernel(count, table_ref, own2_ref, *refs):
+def select_kernel(count, table_ref, own_ref, kv_ref, *refs):
     planes = count // PLANE
     packet_refs, moved_refs = refs[: planes - 1], refs[planes - 1 :]
     dim = table_ref.shape[1]
-    moved_refs[2][at(2 * planes - 2)] = own2_ref[at(0)]
-    moved_refs[2][at(2 * planes - 1)] = own2_ref[at(1)]
-    for j, packet in enumerate(packet_refs):
+    per_half = kv_ref.shape[0] // 2 // KB
+    for t in range(per_half):
+        moved_refs[1][at(2 * planes + t)] = kv_ref[sub(lax.axis_index("pb") % 2 * per_half + t)]
+    for m, ref in enumerate(moved_refs):
+        ref[at(0)] = own_ref[at(2 * m)]
+        if m < PLANE - 1:
+            ref[at(planes)] = own_ref[at(2 * m + 1)]
+    for j, packet in enumerate(packet_refs, 1):
         for part in (slice(0, dim), slice(dim, 2 * dim)):
             choices = [packet[at(t), part] for t in range(PLANE)]
-            for m in range(PLANE):
+            for m, ref in enumerate(moved_refs):
                 for kind in range(2):
-                    row = (j * PLANE + m) * 2 + kind
+                    row = ((j - 1) * PLANE + m) * 2 + kind
                     index = jnp.broadcast_to(table_ref[row : row + 1], (KB, dim))
                     value = choices[0]
                     for t in range(1, PLANE):
                         value = jnp.where(index == t, choices[t], value)
-                    moved_refs[m][at(j + kind * (planes - 1)), part] = value
+                    ref[at(kind * (planes - (m == PLANE - 1)) + j), part] = value
+
+
+def usable(count, block, m):
+    me, z, r = place(count)
+    planes = count // PLANE
+    if block == 1:
+        return [me < count - 1 if m == 0 else None] + [None] * (planes - 1)
+    return [(r ^ m) < r - 1] + [(z >= j) & ((z - j) * PLANE + (r ^ m) < me - 1) for j in range(1, planes)]
 
 
 def attend_all(n_cols, score, v_ts, state, save):
@@ -166,35 +179,51 @@
         attend_all(heads * half // width, score, v_t, None, save)
 
 
+def gathered(count, moved_refs, first_m, block, inner_ref, prev):
+    planes = count // PLANE
+    kv, masks = [], []
+    for i, ref in enumerate(moved_refs):
+        ok = usable(count, block, first_m + i)
+        if first_m + i == PLANE - 1 and block == 0:
+            kv += [inner_ref[at(0)], ref[planes * KB :]]
+        else:
+            first = (1 - block) * planes * KB
+            kv.append(ref[first : first + planes * KB])
+        masks += ok
+    if prev is not None:
+        kv.append(prev)
+        masks += [lax.axis_index("pb") >= 1 if block == 0 else None] * (prev.shape[0] // KB)
+    return jnp.concatenate(kv, axis=0), masks
+
+
 def mid_kernel(count, scale, width, *refs):
-    kv_ref, cross_ref, own1_ref, own3_ref, mine_ref, moved_ref = refs[:6]
-    rot_ref, old, new = refs[6], refs[7:10], refs[10:13]
-    me, z, r = place(count)
-    planes = count // PLANE
-    half = cross_ref.shape[0]
-    cross, own1, own3 = cross_ref[...], own1_ref[2 * KB :], own3_ref[2 * KB :]
-    for block in range(2):
-        if block == 0:
-            prev = jnp.where(r == 0, cross, jnp.where(r == 2, own3, own1))
-            kv = [prev, own3_ref[at(1)], moved_ref[(planes - 1) * KB :]]
-            masks = [me >= 1] * (half // KB) + [(r ^ 3) < r - 1] + [z >= j for j in range(1, planes)]
-        else:
-            prev = jnp.where(r == PLANE - 1, cross, jnp.where(r == 1, own3, own1))
-            prev = jnp.where(me == count - 1, kv_ref[:half], prev)
-            kv = [prev, own1_ref[at(0)], own3_ref[at(0)], mine_ref[...], moved_ref[: (planes - 1) * KB]]
-            masks = [None] * (half // KB + 2) + [me < count - 1] + [None] * (planes - 1)
-
-        def save(step, m, l, acc, block=block):
+    moved_refs, rot_ref, old, new = refs[0:2], refs[2], refs[3:6], refs[6:9]
+    odd = lax.axis_index("pb") % 2 == 1
+    after = 2 * (count // PLANE) * KB
+
+    def run(block, with_prev):
+        def save(step, m, l, acc):
             for ref, value in zip(new, (m, l, acc), strict=True):
                 ref[block, :, step * width : (step + 1) * width] = value
 
-        fold(jnp.concatenate(kv, axis=0), masks, scale, width, block, rot_ref, old, save)
+        kv, masks = gathered(count, moved_refs, 0, block, None, moved_refs[1][after:] if with_prev else None)
+        fold(kv, masks, scale, width, block, rot_ref, old, save)
+
+    @pl.when(odd)
+    def _():
+        run(0, True)
+        run(1, False)
+
+    @pl.when(jnp.logical_not(odd))
+    def _():
+        run(0, False)
+        run(1, True)
 
 
 def far_kernel(count, scale, width, *refs):
-    moved_refs, rot_ref, old, out_ref = refs[0:3], refs[3], refs[4:7], refs[7]
-    me, z, r = place(count)
-    planes = count // PLANE
+    kv_ref, inner_ref, cross_ref, moved_refs, rot_ref, old, out_ref = *refs[:3], refs[3:5], refs[5], refs[6:9], refs[9]
+    me, _, r = place(count)
+    odd = me % 2 == 1
     dim = rot_ref.shape[2]
     half = out_ref.shape[0] // 2
 
@@ -206,22 +235,30 @@
                 done[:, h * half : (h + 1) * half].T.astype(out_ref.dtype)
             )
 
-    def run(block):
-        parts, masks = [], []
-        for m, ref in enumerate(moved_refs, 1):
-            first = (1 - block) * (planes - 1)
-            parts.append(ref[first * KB : (first + planes - 1) * KB])
-            masks += [None if block else (z >= j) & ((z - j) * PLANE + (r ^ m) < me - 1) for j in range(1, planes)]
-        parts.append(moved_refs[1][at(2 * planes - 1 - block)])
-        masks.append(None if block else (r ^ 2) < r - 1)
-        kv = jnp.concatenate(parts, axis=0)
+    def run(block, with_prev):
+        prev = None
+        if with_prev:
+            prev = jnp.where((r == 0) | (r == PLANE - 1), cross_ref[...], inner_ref[...])
+            if block == 1:
+                prev = jnp.where(me == count - 1, kv_ref[:half], prev)
+        kv, masks = gathered(count, moved_refs, 2, block, inner_ref, prev)
         fold(kv, masks, scale, width, block, rot_ref, old, lambda step, m, l, acc: finish(block, step, l, acc))
 
-    run(1)
-
-    @pl.when(me >= 2)
-    def _():
-        run(0)
+    @pl.when(odd)
+    def _():
+        run(1, True)
+
+    @pl.when(jnp.logical_not(odd))
+    def _():
+        run(1, False)
+
+    @pl.when((me >= 2) & odd)
+    def _():
+        run(0, False)
+
+    @pl.when((me >= 2) & jnp.logical_not(odd))
+    def _():
+        run(0, True)
 
     @pl.when(me < 2)
     def _():
@@ -262,16 +299,15 @@
     by_source = picks.T
     per_half = half // KB
     table = jax.ShapeDtypeStruct(((planes - 1) * PLANE * 2, dim), jnp.int32)
-    kv, table, mine, cross, *rest = pl.pallas_call(
+    kv, table, own, inner, cross, *packets = pl.pallas_call(
         functools.partial(pack_kernel, count),
-        out_shape=[rows(2 * per_half), table, rows(1), rows(per_half), rows(2 + per_half), rows(2), rows(2 + per_half)]
+        out_shape=[rows(2 * per_half), table, rows(2 * PLANE), rows(per_half), rows(per_half)]
         + [rows(PLANE)] * (planes - 1),
         in_specs=[smem, vmem, vmem],
-        out_specs=[vmem] * (6 + planes),
-        compiler_params=pltpu.CompilerParams(vmem_limit_bytes=62 * 1024 * 1024),
+        out_specs=[vmem] * (4 + planes),
+        compiler_params=pltpu.CompilerParams(vmem_limit_bytes=60 * 1024 * 1024),
         name="pack",
     )(by_source, keys, values)
-    own, packets = rest[:3], rest[3:]
 
     packets = [
         permute(packet, [(s, (s + j * PLANE) % count) for s in range(count)]) for j, packet in enumerate(packets, 1)
@@ -287,44 +323,43 @@
         name="near",
     )(queries, basis, kv)
     packets, near = lax.optimization_barrier((packets, near))
-    direct = [permute(own[m - 1], [(s, s ^ m) for s in range(count)]) for m in (1, 3)]
-    borders = range(PLANE - 1, count - 1, PLANE)
-    cross = permute(cross, [(s, s + 1) for s in borders] + [(s + 1, s) for s in borders])
-
+    inner = permute(inner, [(s, s ^ (PLANE - 1)) for s in range(count)])
+    packets, inner = lax.optimization_barrier((packets, inner))
+
+    sizes = [2 * planes, 2 * planes + per_half, 2 * planes, 2 * planes - 1]
     moved = list(
         pl.pallas_call(
             functools.partial(select_kernel, count),
-            out_shape=[rows(2 * planes - 2 + 2 * (m == 2)) for m in range(PLANE)],
-            in_specs=[vmem] * (planes + 1),
+            out_shape=[rows(size) for size in sizes],
+            in_specs=[vmem] * (planes + 2),
             out_specs=[vmem] * PLANE,
             compiler_params=params,
             name="select",
-        )(table, own[1], *packets)
+        )(table, own, kv, *packets)
     )
-    for m in (2, 3):
-        moved[m] = permute(moved[m], [(s, s ^ m) for s in range(count)])
+    moved[1:] = [permute(moved[m], [(s, s ^ m) for s in range(count)]) for m in range(1, PLANE)]
+    borders = range(PLANE - 1, count - 1, PLANE)
+    cross = permute(cross, [(s, s + 1) for s in borders] + [(s + 1, s) for s in borders])
 
     mid = pl.pallas_call(
         functools.partial(mid_kernel, count, scale, width),
         out_shape=state,
-        in_specs=[vmem] * 10,
+        in_specs=[vmem] * 6,
         out_specs=[vmem] * 3,
         compiler_params=params,
-        cost_estimate=cost(2 * half),
+        cost_estimate=cost(3 * half),
         name="mid",
-    )(kv, cross, *direct, mine, moved[0], *near)
-    moved[1], mid = lax.optimization_barrier((moved[1], mid))
-    moved[1] = permute(moved[1], [(s, s ^ 1) for s in range(count)])
+    )(*moved[:2], *near)
 
     return pl.pallas_call(
         functools.partial(far_kernel, count, scale, width),
         out_shape=jax.ShapeDtypeStruct(queries.shape, bf16),
-        in_specs=[vmem] * 7,
+        in_specs=[vmem] * 9,
         out_specs=vmem,
         compiler_params=params,
-        cost_estimate=cost(3 * half),
+        cost_estimate=cost(2 * half),
         name="far",
-    )(*moved[1:], near[0], *mid)
+    )(kv, inner, cross, *moved[2:], near[0], *mid)
 
 
 def solution(mesh):

time: 24.7 us -> 23.5 us (0.951)
  starting transfers between devices: 12.6 us -> 9.63 us
  waiting for transfers between devices: 3.72 us -> 5.37 us
    ppermute x9 -> x8, starting transfers between devices: 12.6 us -> 9.63 us  [permute(): return lax.ppermute(value, 'pb', pairs)]
    ppermute x9 -> x8, waiting for transfers between devices: 3.72 us -> 5.37 us  [permute(): return lax.ppermute(value, 'pb', pairs)]
  transfers between devices with their start and end apart: 9 -> 8, of which waited for: 1 -> 4; matrix products, arithmetic and copies ran while one was open for 0% -> 0% of each run, Pallas kernels for 10% -> 10%
where the time goes in v4:
time: 23.5 us; the launch traced here: 23.2 us
  starting transfers between devices  9.63 us (41%)
  Pallas kernels  6.2 us (26%)
  waiting for transfers between devices  5.37 us (23%)
  local copies, waits for them, and re-layouts  1.97 us (8%)
    ppermute x8, starting transfers between devices, permute(): return lax.ppermute(value, 'pb', pairs)  9.63 us
    ppermute x8, waiting for transfers between devices, permute(): return lax.ppermute(value, 'pb', pairs)  5.37 us
    unnamed x14, local copies, waits for them, and re-layouts  1.97 us
    pallas_call x1, Pallas kernels, per_device(): pl.pallas_call(functools.partial(pack_kernel, count), out_shape=[rows(2 *...  1.85 us
    pallas_call x1, Pallas kernels, per_device(): pl.pallas_call(functools.partial(far_kernel, count, scale, width), out_sh...  1.84 us
    pallas_call x1, Pallas kernels, per_device(): pl.pallas_call(functools.partial(mid_kernel, count, scale, width), out_sh...  1.42 us
    pallas_call x1, Pallas kernels, per_device(): pl.pallas_call(functools.partial(near_kernel, scale, width), out_shape=[j...  0.97 us
  transfers between devices with their start and end apart: 8, of which 4 were waited for; matrix products, arithmetic and copies ran while one was open for 0% of the time, Pallas kernels for 10%

profile of v4, /device:TPU:0, one launch (start us, length us, event | category | flops | bytes accessed | tf_op | source)
XLA Modules:
  0.0 23.2 jit_solution(10470513329028109149)
XLA Ops:
  0.0 1.8 %pack.1 = (bf16[256,256]{1,0:T(8,128)(2,1)}, s32[24,128]{1,0:T(8,128)}, bf16[256,256]{1,0:T(8,128)(2,1)}, bf16[128,256]{1,0:T(8,128)(2,1)}, bf16[128,256]{1,0:T(...) custom-call(s32[16,32]{1,0:T(8,128)} %bitcast.1, ...), custom_call_target="tpu_custom_call" | custom-call | tf_op jit(solution)/shard_map/pack/pallas_call | solution.py:302
  1.9 3.0 %collective-permute-start = (bf16[128,256]{1,0:T(8,128)(2,1)}, bf16[128,256]{1,0:T(8,128)(2,1)S(1)}, u32[]{:S(2)}, u32[]{:S(2)}) collective-permute-start(bf16[128,256]{1,0:T(8,128)(2,1)} %get-tuple-element.36), channel_id=1, source_target_pairs={{0,4},{1,5},{2,6},{3,7},{4,8},{5,9},{6,10},{7,11},{8,12},{9,13},{1... | collective-permute-start | bytes 196616 | tf_op jit(solution)/shard_map/ppermute | solution.py:292
  4.9 2.6 %collective-permute-start.1 = (bf16[128,256]{1,0:T(8,128)(2,1)}, bf16[128,256]{1,0:T(8,128)(2,1)S(1)}, u32[]{:S(2)}, u32[]{:S(2)}) collective-permute-start(bf16[128,256]{1,0:T(8,128)(2,1)} %get-tuple-element.37), channel_id=1, source_target_pairs={{0,8},{1,9},{2,10},{3,11},{4,12},{5,13},{6,14},{7,15},{8,0},{9,1},... | collective-permute-start | bytes 196616 | tf_op jit(solution)/shard_map/ppermute | solution.py:292
  7.5 1.3 %collective-permute-start.2 = (bf16[128,256]{1,0:T(8,128)(2,1)}, bf16[128,256]{1,0:T(8,128)(2,1)S(1)}, u32[]{:S(2)}, u32[]{:S(2)}) collective-permute-start(bf16[128,256]{1,0:T(8,128)(2,1)} %get-tuple-element.38), channel_id=1, source_target_pairs={{0,12},{1,13},{2,14},{3,15},{4,0},{5,1},{6,2},{7,3},{8,4},{9,5},{1... | collective-permute-start | bytes 196616 | tf_op jit(solution)/shard_map/ppermute | solution.py:292
  8.8 0.1 collective-permute-start.3
  8.9 0.9 %copy-done = bf16[256,256]{1,0:T(8,128)(2,1)S(1)} copy-done((bf16[256,256]{1,0:T(8,128)(2,1)S(1)}, bf16[256,256]{1,0:T(8,128)(2,1)}, u32[]{:S(2)}) %copy-start) | copy-done | bytes 131096
  9.8 1.0 %copy-done.2 = bf16[256,1024]{1,0:T(8,128)(2,1)S(1)} copy-done((bf16[256,1024]{1,0:T(8,128)(2,1)S(1)}, bf16[256,1024]{1,0:T(8,128)(2,1)}, u32[]{:S(2)}) %copy-start.2) | copy-done | bytes 524312
  10.9 1.0 %near.1 = (bf16[2,1024,128]{2,1,0:T(8,128)(2,1)S(1)}, f32[2,1,1024]{2,1,0:T(1,128)S(1)}, f32[2,1,1024]{2,1,0:T(1,128)S(1)}, f32[2,128,1024]{2,1,0:T(8,128)S(1)}) custom-call(bf16[256,1024]{1,0:T(8,128)(2,1)S(1)} %copy-done.2, bf16[128,128]{1,0:T(8,128)(2,1)S(1)} %copy-done.4, bf16[256,256]{1,0:T(8,128)(2,1)S(1)} %copy-done), custom_call_target="tpu_custom_call" | custom-call | flops 134217728 | bytes 4000000 | tf_op jit(solution)/shard_map/near/pallas_call | solution.py:316
  11.8 0.0 collective-permute-done.refs_0_
  11.8 0.3 %collective-permute-done.1.refs_1_ = bf16[128,256]{1,0:T(8,128)(2,1)S(1)} collective-permute-done((bf16[128,256]{1,0:T(8,128)(2,1)}, bf16[128,256]{1,0:T(8,128)(2,1)S(1)}, u32[]{:S(2)}, u32[]{:S(2)}) %collective-permute-start.1) | collective-permute-done | bytes 65568 | tf_op jit(solution)/shard_map/ppermute | solution.py:292
  12.2 0.2 collective-permute-done.2.refs_2_
  12.4 1.0 %collective-permute-done.3.refs_1_ = bf16[128,256]{1,0:T(8,128)(2,1)S(1)} collective-permute-done((bf16[128,256]{1,0:T(8,128)(2,1)}, bf16[128,256]{1,0:T(8,128)(2,1)S(1)}, u32[]{:S(2)}, u32[]{:S(2)}) %collective-permute-start.3) | collective-permute-done | bytes 65568 | tf_op jit(solution)/shard_map/ppermute | solution.py:292
  13.4 0.1 select.1
  13.5 0.2 collective-permute-start.7
  13.7 0.8 %collective-permute-start.5 = (bf16[256,256]{1,0:T(8,128)(2,1)S(1)}, bf16[256,256]{1,0:T(8,128)(2,1)S(1)}, u32[]{:S(2)}, u32[]{:S(2)}) collective-permute-start(bf16[256,256]{1,0:T(8,128)(2,1)S(1)} %get-tuple-element.54), channel_id=1, source_target_pairs={{0,2},{1,3},{2,0},{3,1},{4,6},{5,7},{6,4},{7,5},{8,10},{9,11},{10,... | collective-permute-start | bytes 393224 | tf_op jit(solution)/shard_map/ppermute | solution.py:292
  14.5 0.9 %collective-permute-start.6 = (bf16[224,256]{1,0:T(8,128)(2,1)S(1)}, bf16[224,256]{1,0:T(8,128)(2,1)S(1)}, u32[]{:S(2)}, u32[]{:S(2)}) collective-permute-start(bf16[224,256]{1,0:T(8,128)(2,1)S(1)} %get-tuple-element.55), channel_id=1, source_target_pairs={{0,3},{1,2},{2,1},{3,0},{4,7},{5,6},{6,5},{7,4},{8,11},{9,10},{10,... | collective-permute-start | bytes 344072 | tf_op jit(solution)/shard_map/ppermute | solution.py:292
  15.4 0.7 %collective-permute-start.4 = (bf16[128,256]{1,0:T(8,128)(2,1)S(1)}, bf16[128,256]{1,0:T(8,128)(2,1)S(1)}, u32[]{:S(2)}, u32[]{:S(2)}) collective-permute-start(bf16[128,256]{1,0:T(8,128)(2,1)S(1)} %copy-done.6), channel_id=1, source_target_pairs={{3,4},{7,8},{11,12},{4,3},{8,7},{12,11},{19,20},{23,24},{27,28},{2... | collective-permute-start | bytes 196616 | tf_op jit(solution)/shard_map/ppermute | solution.py:292
  16.1 0.0 collective-permute-done.7.refs_1_
  16.1 0.0 copy-start.1
  16.1 1.4 %mid.1 = (f32[2,1,1024]{2,1,0:T(1,128)S(1)}, f32[2,1,1024]{2,1,0:T(1,128)S(1)}, f32[2,128,1024]{2,1,0:T(8,128)S(1)}) custom-call(bf16[256,256]{1,0:T(8,128)(2,1)S(1)} %get-tuple-element.57.refs_0_, bf16[384,256]{1,0:T(8,128)(2,1)S(1)} %collective-permute-done.7.refs_1_, bf16[2,1024,128]{2,1,0:T(8,128)(2,1)S(1)} %get-tuple-element.56.refs_2_.refs_5_, ...), custom_call_target="tpu_custom_call" | custom-call | flops 402653184 | bytes 4000000 | tf_op jit(solution)/shard_map/mid/pallas_call | solution.py:344
  17.5 0.0 collective-permute-done.4.refs_2_
  17.6 3.8 %collective-permute-done.6.refs_4_ = bf16[224,256]{1,0:T(8,128)(2,1)S(1)} collective-permute-done((bf16[224,256]{1,0:T(8,128)(2,1)S(1)}, bf16[224,256]{1,0:T(8,128)(2,1)S(1)}, u32[]{:S(2)}, u32[]{:S(2)}) %collective-permute-start.6) | collective-permute-done | bytes 114720 | tf_op jit(solution)/shard_map/ppermute | solution.py:292
  21.4 0.0 collective-permute-done.5.refs_3_
  21.4 1.8 %far.1 = bf16[256,1024]{1,0:T(8,128)(2,1)} custom-call(bf16[256,256]{1,0:T(8,128)(2,1)S(1)} %copy-done.1, bf16[128,256]{1,0:T(8,128)(2,1)S(1)} %collective-permute-done.3.refs_1_, bf16[128,256]{1,0:T(8,128)(2,1)S(1)} %collective-permute-done.4.refs_2_, bf16[256,256]{1,0:T(8,128)(2,1)S(1)} %collective-permute-done.5.refs_3_, ...), custom_call_target="tpu_custom_call" | custom-call | flops 268435456 | bytes 4000000 | tf_op jit(solution)/shard_map/far/pallas_call | solution.py:354
  (11 shorter events, 0.0 us)
Async XLA Ops:
  0.0 8.9 %copy-start.4 = (bf16[128,128]{1,0:T(8,128)(2,1)S(1)}, bf16[128,128]{1,0:T(8,128)(2,1)}, u32[]{:S(2)}) copy-start(bf16[128,128]{1,0:T(8,128)(2,1)} %basis_ref.1) | copy-start | bytes 98308
  1.9 10.0 %collective-permute-start = (bf16[128,256]{1,0:T(8,128)(2,1)}, bf16[128,256]{1,0:T(8,128)(2,1)S(1)}, u32[]{:S(2)}, u32[]{:S(2)}) collective-permute-start(bf16[128,256]{1,0:T(8,128)(2,1)} %get-tuple-element.36), channel_id=1, source_target_pairs={{0,4},{1,5},{2,6},{3,7},{4,8},{5,9},{6,10},{7,11},{8,12},{9,13},{1... | collective-permute-start | bytes 196616 | tf_op jit(solution)/shard_map/ppermute | solution.py:292
  4.9 7.3 %collective-permute-start.1 = (bf16[128,256]{1,0:T(8,128)(2,1)}, bf16[128,256]{1,0:T(8,128)(2,1)S(1)}, u32[]{:S(2)}, u32[]{:S(2)}) collective-permute-start(bf16[128,256]{1,0:T(8,128)(2,1)} %get-tuple-element.37), channel_id=1, source_target_pairs={{0,8},{1,9},{2,10},{3,11},{4,12},{5,13},{6,14},{7,15},{8,0},{9,1},... | collective-permute-start | bytes 196616 | tf_op jit(solution)/shard_map/ppermute | solution.py:292
  7.5 4.9 %collective-permute-start.2 = (bf16[128,256]{1,0:T(8,128)(2,1)}, bf16[128,256]{1,0:T(8,128)(2,1)S(1)}, u32[]{:S(2)}, u32[]{:S(2)}) collective-permute-start(bf16[128,256]{1,0:T(8,128)(2,1)} %get-tuple-element.38), channel_id=1, source_target_pairs={{0,12},{1,13},{2,14},{3,15},{4,0},{5,1},{6,2},{7,3},{8,4},{9,5},{1... | collective-permute-start | bytes 196616 | tf_op jit(solution)/shard_map/ppermute | solution.py:292
  8.8 4.6 %collective-permute-start.3 = (bf16[128,256]{1,0:T(8,128)(2,1)}, bf16[128,256]{1,0:T(8,128)(2,1)S(1)}, u32[]{:S(2)}, u32[]{:S(2)}) collective-permute-start(bf16[128,256]{1,0:T(8,128)(2,1)} %get-tuple-element.46), channel_id=1, source_target_pairs={{0,3},{1,2},{2,1},{3,0},{4,7},{5,6},{6,5},{7,4},{8,11},{9,10},{10,... | collective-permute-start | bytes 196616 | tf_op jit(solution)/shard_map/ppermute | solution.py:292
  8.9 0.9 %copy-start = (bf16[256,256]{1,0:T(8,128)(2,1)S(1)}, bf16[256,256]{1,0:T(8,128)(2,1)}, u32[]{:S(2)}) copy-start(bf16[256,256]{1,0:T(8,128)(2,1)} %get-tuple-element.35.kv_ref.refs_0_) | copy-start | bytes 393220
  9.8 1.0 %copy-start.2 = (bf16[256,1024]{1,0:T(8,128)(2,1)S(1)}, bf16[256,1024]{1,0:T(8,128)(2,1)}, u32[]{:S(2)}) copy-start(bf16[256,1024]{1,0:T(8,128)(2,1)} %q_ref.1) | copy-start | bytes 1572868
  10.9 2.5 %copy-start.3 = (bf16[256,256]{1,0:T(8,128)(2,1)S(1)}, bf16[256,256]{1,0:T(8,128)(2,1)}, u32[]{:S(2)}) copy-start(bf16[256,256]{1,0:T(8,128)(2,1)} %get-tuple-element.50.own_ref) | copy-start | bytes 393220
  10.9 2.5 %copy-start.5 = (s32[24,128]{1,0:T(8,128)S(1)}, s32[24,128]{1,0:T(8,128)}, u32[]{:S(2)}) copy-start(s32[24,128]{1,0:T(8,128)} %get-tuple-element.49.table_ref) | copy-start | bytes 36868
  13.4 2.1 %copy-start.6 = (bf16[128,256]{1,0:T(8,128)(2,1)S(1)}, bf16[128,256]{1,0:T(8,128)(2,1)}, u32[]{:S(2)}) copy-start(bf16[128,256]{1,0:T(8,128)(2,1)} %get-tuple-element.48) | copy-start | bytes 196612
  13.5 2.6 %collective-permute-start.7 = (bf16[384,256]{1,0:T(8,128)(2,1)S(1)}, bf16[384,256]{1,0:T(8,128)(2,1)S(1)}, u32[]{:S(2)}, u32[]{:S(2)}) collective-permute-start(bf16[384,256]{1,0:T(8,128)(2,1)S(1)} %get-tuple-element.58), channel_id=1, source_target_pairs={{0,1},{1,0},{2,3},{3,2},{4,5},{5,4},{6,7},{7,6},{8,9},{9,8},{10,11... | collective-permute-start | bytes 589832 | tf_op jit(solution)/shard_map/ppermute | solution.py:292
  13.7 7.7 %collective-permute-start.5 = (bf16[256,256]{1,0:T(8,128)(2,1)S(1)}, bf16[256,256]{1,0:T(8,128)(2,1)S(1)}, u32[]{:S(2)}, u32[]{:S(2)}) collective-permute-start(bf16[256,256]{1,0:T(8,128)(2,1)S(1)} %get-tuple-element.54), channel_id=1, source_target_pairs={{0,2},{1,3},{2,0},{3,1},{4,6},{5,7},{6,4},{7,5},{8,10},{9,11},{10,... | collective-permute-start | bytes 393224 | tf_op jit(solution)/shard_map/ppermute | solution.py:292
  14.5 6.9 %collective-permute-start.6 = (bf16[224,256]{1,0:T(8,128)(2,1)S(1)}, bf16[224,256]{1,0:T(8,128)(2,1)S(1)}, u32[]{:S(2)}, u32[]{:S(2)}) collective-permute-start(bf16[224,256]{1,0:T(8,128)(2,1)S(1)} %get-tuple-element.55), channel_id=1, source_target_pairs={{0,3},{1,2},{2,1},{3,0},{4,7},{5,6},{6,5},{7,4},{8,11},{9,10},{10,... | collective-permute-start | bytes 344072 | tf_op jit(solution)/shard_map/ppermute | solution.py:292
  15.4 2.1 %collective-permute-start.4 = (bf16[128,256]{1,0:T(8,128)(2,1)S(1)}, bf16[128,256]{1,0:T(8,128)(2,1)S(1)}, u32[]{:S(2)}, u32[]{:S(2)}) collective-permute-start(bf16[128,256]{1,0:T(8,128)(2,1)S(1)} %copy-done.6), channel_id=1, source_target_pairs={{3,4},{7,8},{11,12},{4,3},{8,7},{12,11},{19,20},{23,24},{27,28},{2... | collective-permute-start | bytes 196616 | tf_op jit(solution)/shard_map/ppermute | solution.py:292
  16.1 5.3 %copy-start.1 = (bf16[256,256]{1,0:T(8,128)(2,1)S(1)}, bf16[256,256]{1,0:T(8,128)(2,1)}, u32[]{:S(2)}) copy-start(bf16[256,256]{1,0:T(8,128)(2,1)} %get-tuple-element.35.kv_ref.refs_0_) | copy-start | bytes 393220

commit v5 on v4

v5 whole, which is shorter than its diff:
```python
import functools
import math

import jax
import jax.numpy as jnp
from jax import lax
from jax.experimental import pallas as pl
from jax.experimental.pallas import tpu as pltpu
from jax.sharding import PartitionSpec as P

KB = 32
PLANE = 4
NEG = -1e30
VMEM_BYTES = 40 * 1024 * 1024
CHUNK = 16


def place(count):
    me = lax.axis_index("pb")
    return me, me // PLANE, me % PLANE


def sub(index):
    return pl.ds(pl.multiple_of(index * KB, KB), KB)


def at(n):
    return slice(n * KB, (n + 1) * KB)


def scores_of(k, q):
    return lax.dot_general(k, q, (((1,), (1,)), ((), ())), preferred_element_type=jnp.float32)


def splat(picks_ref, wanted, width):
    lane = lax.broadcasted_iota(jnp.int32, (1, picks_ref.shape[1]), 1)
    rows = [jnp.where(lane == block, picks_ref[pl.ds(source, 1), :], 0) for source, block in wanted]
    total = jnp.sum(jnp.concatenate(rows, axis=0), axis=1, keepdims=True)
    return jnp.broadcast_to(jnp.maximum(total, 0), (len(wanted), width))


def chosen(index, choices):
    index = jnp.broadcast_to(index, choices[0].shape)
    value = choices[0]
    for t, choice in enumerate(choices[1:], 1):
        value = jnp.where(index == t, choice, value)
    return value


def pack_kernel(count, picks_ref, both_ref, *refs):
    planes = count // PLANE
    kv_ref, table_ref, own_ref, inner_ref, cross_ref, packet_refs = *refs[:5], refs[5:]
    me, z, r = place(count)
    dim = both_ref.shape[1]
    total = both_ref.shape[0] // 2 // KB
    per_half = total // 2
    for part in range(2):
        kv_ref[:, part * dim : (part + 1) * dim] = both_ref[part * total * KB : (part + 1) * total * KB]
    wanted, down = [], []
    for j in range(1, planes):
        up = z + j < planes
        to = jnp.where(up, 0, (z + j - planes) * PLANE)
        wanted += [(me, 2 * count - 1 - (to + t)) for t in range(PLANE)]
        down += [up] * PLANE
    for m in range(PLANE):
        dest = z * PLANE + (r ^ m)
        wanted += [(me, 2 * count - 1 - dest), (me, dest)]
    wanted.append((me, jnp.minimum(me + PLANE - 1, count - 1)))
    index = splat(picks_ref, wanted, dim)
    for part in range(2):
        cols = slice(part * dim, (part + 1) * dim)
        subs = [both_ref[at(part * total + t)] for t in range(total)]
        for g, up in enumerate(down):
            j, t = g // PLANE, g % PLANE
            packet_refs[j][at(t), cols] = jnp.where(up, subs[t], chosen(index[g : g + 1], subs))
        for g in range(2 * PLANE):
            i = len(down) + g
            own_ref[at(g), cols] = chosen(index[i : i + 1], subs)
        for t in range(per_half):
            inner = jnp.where(r == 1, subs[t], subs[per_half + t])
            if t == 0:
                inner = jnp.where(r == 0, chosen(index[len(wanted) - 1 :], subs), inner)
            inner_ref[at(t), cols] = inner
            cross_ref[at(t), cols] = jnp.where(r == PLANE - 1, subs[t], subs[per_half + t])
    wanted, fixed = [], []
    for j in range(1, planes):
        up = z >= j
        source = jnp.where(up, z - j, z - j + planes) * PLANE + r
        for m in range(PLANE):
            dest = z * PLANE + (r ^ m)
            wanted += [(source, 2 * count - 1 - dest), (source, dest)]
            fixed += [(up, r ^ m), (up, 0)]
    index = splat(picks_ref, wanted, dim)
    for g, (up, other) in enumerate(fixed):
        table_ref[g : g + 1] = jnp.where(up, index[g : g + 1], other)


def select_kernel(count, table_ref, own_ref, kv_ref, *refs):
    planes = count // PLANE
    packet_refs, moved_refs = refs[: planes - 1], refs[planes - 1 :]
    dim = table_ref.shape[1]
    per_half = kv_ref.shape[0] // 2 // KB
    for t in range(per_half):
        moved_refs[1][at(2 * planes + t)] = kv_ref[sub(lax.axis_index("pb") % 2 * per_half + t)]
    for m in range(PLANE):
        moved_refs[m][at(0)] = own_ref[at(2 * m)]
        if m < PLANE - 1:
            moved_refs[m][at(planes)] = own_ref[at(2 * m + 1)]
    for j, packet in enumerate(packet_refs, 1):
        for part in (slice(0, dim), slice(dim, 2 * dim)):
            choices = [packet[at(t), part] for t in range(PLANE)]
            for m in range(PLANE):
                row = ((j - 1) * PLANE + m) * 2
                moved_refs[m][at(j), part] = chosen(table_ref[row : row + 1], choices)
                early = chosen(table_ref[row + 1 : row + 2], choices)
                if m < 2:
                    moved_refs[m][at(planes + j), part] = early
                else:
                    moved_refs[m][at(planes + j - (m == 3)), part] = early


def usable(count, block, m):
    me, z, r = place(count)
    planes = count // PLANE
    if block == 1:
        return [me < count - 1 if m == 0 else None] + [None] * (planes - 1)
    return [(r ^ m) < r - 1] + [(z >= j) & ((z - j) * PLANE + (r ^ m) < me - 1) for j in range(1, planes)]


def attend_all(n_cols, score, v_ts, state, save):
    ahead = score(0)
    for step in range(n_cols):
        s = ahead
        if step + 1 < n_cols:
            ahead = score(step + 1)
        m = jnp.max(s, axis=0, keepdims=True)
        if state is not None:
            m_old, l_old, acc_old = state(step)
            m = jnp.maximum(m, m_old)
        w = jnp.exp2(s - m)
        l = jnp.sum(w, axis=0, keepdims=True)
        acc = jnp.dot(v_ts, w.astype(jnp.bfloat16), preferred_element_type=jnp.float32)
        if state is not None:
            old = jnp.exp2(m_old - m)
            l = l + l_old * old
            acc = acc + acc_old * old
        save(step, m, l, acc)


def fold(kv, masks, scale, width, block, rot_ref, old_refs, save):
    dim = rot_ref.shape[2]
    total = len(masks)
    steps = rot_ref.shape[1] // width
    carried = [tuple(ref[block, :, step * width : (step + 1) * width] for ref in old_refs) for step in range(steps)]
    for first in range(0, total, CHUNK):
        last = min(first + CHUNK, total)
        k = kv[first * KB : last * KB, :dim]
        v_t = kv[first * KB : last * KB, dim:].T

        def score(step, k=k, first=first, last=last):
            s = scores_of(k, rot_ref[block, step * width : (step + 1) * width, :]) * scale
            if all(ok is None for ok in masks[first:last]):
                return s
            return jnp.concatenate(
                [s[at(g - first)] if masks[g] is None else jnp.where(masks[g], s[at(g - first)], NEG) for g in range(first, last)]
            )

        def keep(step, *values):
            carried[step] = values

        attend_all(steps, score, v_t, carried.__getitem__, save if last == total else keep)


def near_kernel(scale, width, q_ref, basis_ref, kv_ref, rot_ref, m_ref, l_ref, acc_ref):
    dim = basis_ref.shape[0]
    half = q_ref.shape[0] // 2
    heads = q_ref.shape[1] // dim
    basis = basis_ref[...]
    key_row = lax.broadcasted_iota(jnp.int32, (half, width), 0)
    query = lax.broadcasted_iota(jnp.int32, (half, width), 1) % half
    causal = key_row <= query
    for block in range(2):
        rows = slice(block * half, (block + 1) * half)
        for h in range(heads):
            q = jnp.dot(q_ref[rows, h * dim : (h + 1) * dim], basis, preferred_element_type=jnp.float32)
            rot_ref[block, h * half : (h + 1) * half, :] = q.astype(jnp.bfloat16)
    for block in range(2):
        rows = slice(block * half, (block + 1) * half)
        k, v_t = kv_ref[rows, :dim], kv_ref[rows, dim:].T

        def score(step, block=block, k=k):
            s = scores_of(k, rot_ref[block, step * width : (step + 1) * width, :]) * scale
            return jnp.where(causal, s, NEG)

        def save(step, m, l, acc, block=block):
            for ref, value in zip((m_ref, l_ref, acc_ref), (m, l, acc), strict=True):
                ref[block, :, step * width : (step + 1) * width] = value

        attend_all(heads * half // width, score, v_t, None, save)


def fold_kernel(count, scale, width, first_m, *refs):
    inner_ref, moved_refs, rot_ref, old, new = refs[0], refs[1:-7], refs[-7], refs[-6:-3], refs[-3:]
    me, _, r = place(count)
    even = me % 2 == 0
    late = (count // PLANE) * KB

    def run(block):
        parts, masks = [], []
        for i, ref in enumerate(moved_refs):
            m = first_m + i
            masks += usable(count, block, m)
            if block == 1:
                parts.append(ref[:late])
            elif m == PLANE - 1:
                parts += [inner_ref[at(0)], ref[late : 2 * late - KB]]
            else:
                parts.append(ref[late : 2 * late])
        if first_m == 0:
            beside = even if block == 1 else jnp.logical_not(even)
            parts.append(jnp.where(beside, moved_refs[1][2 * late :], inner_ref[...]))
            masks += [beside | (r == 1 + (1 - block))] * (inner_ref.shape[0] // KB)

        def save(step, m, l, acc):
            for ref, value in zip(new, (m, l, acc), strict=True):
                ref[block, :, step * width : (step + 1) * width] = value

        fold(jnp.concatenate(parts, axis=0), masks, scale, width, block, rot_ref, old, save)

    run(1)
    pl.when(me >= (1 if first_m == 0 else 2))(lambda: run(0))


def last_kernel(count, scale, width, kv_ref, cross_ref, rot_ref, m_ref, l_ref, acc_ref, out_ref):
    me, z, r = place(count)
    half = out_ref.shape[0] // 2
    dim = rot_ref.shape[2]
    old = (m_ref, l_ref, acc_ref)

    def finish(block, step, l, acc):
        done = acc / l
        for h in range(width // half):
            head = step * (width // half) + h
            out_ref[block * half : (block + 1) * half, head * dim : (head + 1) * dim] = (
                done[:, h * half : (h + 1) * half].T.astype(out_ref.dtype)
            )

    def add(block):
        prev = cross_ref[...]
        if block == 1:
            prev = jnp.where(me == count - 1, kv_ref[:half], prev)
        masks = [None] * (half // KB)
        fold(prev, masks, scale, width, block, rot_ref, old, lambda step, m, l, acc: finish(block, step, l, acc))

    def close(block):
        for step in range(rot_ref.shape[1] // width):
            cols = slice(step * width, (step + 1) * width)
            finish(block, step, l_ref[block, :, cols], acc_ref[block, :, cols])

    for block, outer in enumerate(((r == 0) & (z > 0), r == PLANE - 1)):
        pl.when(outer)(functools.partial(add, block))
        pl.when(jnp.logical_not(outer))(functools.partial(close, block))


def per_device(queries, keys, values, basis, picks):
    rows_dev, dim = keys.shape
    half = rows_dev // 2
    count = lax.axis_size("pb")
    planes = count // PLANE
    wide = queries.shape[1] // dim * half
    width = 2 * half
    scale = dim**-0.5 * math.log2(math.e)
    vmem = pl.BlockSpec(memory_space=pltpu.VMEM)
    params = pltpu.CompilerParams(vmem_limit_bytes=VMEM_BYTES)
    bf16, f32 = jnp.bfloat16, jnp.float32
    shapes = [
        jax.ShapeDtypeStruct((2, 1, wide), f32),
        jax.ShapeDtypeStruct((2, 1, wide), f32),
        jax.ShapeDtypeStruct((2, dim, wide), f32),
    ]

    def rows(n):
        return jax.ShapeDtypeStruct((n * KB, 2 * dim), bf16)

    def permute(value, pairs):
        return lax.ppermute(value, "pb", pairs)

    def cost(keys_each):
        return pl.CostEstimate(
            flops=8 * wide * keys_each * dim, bytes_accessed=4_000_000, transcendentals=2 * wide * keys_each
        )

    per_half = half // KB
    table = jax.ShapeDtypeStruct(((planes - 1) * PLANE * 2, dim), jnp.int32)
    kv, table, own, inner, cross, *packets = pl.pallas_call(
        functools.partial(pack_kernel, count),
        out_shape=[rows(2 * per_half), table, rows(2 * PLANE), rows(per_half), rows(per_half)]
        + [rows(PLANE)] * (planes - 1),
        in_specs=[vmem] * 2,
        out_specs=[vmem] * (4 + planes),
        compiler_params=params,
        name="pack",
    )(picks.T, jnp.concatenate([keys, values]))

    packets = [
        permute(packet, [(s, (s + j * PLANE) % count) for s in range(count)]) for j, packet in enumerate(packets, 1)
    ]

    near = pl.pallas_call(
        functools.partial(near_kernel, scale, width),
        out_shape=[jax.ShapeDtypeStruct((2, wide, dim), bf16)] + shapes,
        in_specs=[vmem] * 3,
        out_specs=[vmem] * 4,
        compiler_params=params,
        cost_estimate=cost(half),
        name="near",
    )(queries, basis, kv)
    packets, near = lax.optimization_barrier((packets, near))
    inner = permute(inner, [(s, s ^ (PLANE - 1)) for s in range(count)])

    sizes = [2 * planes, 2 * planes + per_half, 2 * planes, 2 * planes - 1]
    moved = list(
        pl.pallas_call(
            functools.partial(select_kernel, count),
            out_shape=[rows(size) for size in sizes],
            in_specs=[vmem] * (planes + 2),
            out_specs=[vmem] * len(sizes),
            compiler_params=params,
            name="select",
        )(table, own, kv, *packets)
    )
    moved[1], inner = lax.optimization_barrier((moved[1], inner))
    for m in range(1, PLANE):
        moved[m] = permute(moved[m], [(s, s ^ m) for s in range(count)])

    rotated, *state = near

    def folded(state, first_m, messages):
        return pl.pallas_call(
            functools.partial(fold_kernel, count, scale, width, first_m),
            out_shape=shapes,
            in_specs=[vmem] * (5 + len(messages)),
            out_specs=[vmem] * 3,
            input_output_aliases={2 + len(messages) + i: i for i in range(3)},
            compiler_params=params,
            cost_estimate=cost(half * len(messages)),
            name=f"fold{first_m}",
        )(inner, *messages, rotated, *state)

    state = folded(state, 0, moved[:2])
    borders = range(PLANE - 1, count - 1, PLANE)
    cross = permute(cross, [(s, s + 1) for s in borders] + [(s + 1, s) for s in borders])
    state = folded(state, 2, moved[2:3])
    state = folded(state, 3, moved[3:4])
    return pl.pallas_call(
        functools.partial(last_kernel, count, scale, width),
        out_shape=jax.ShapeDtypeStruct(queries.shape, bf16),
        in_specs=[vmem] * 6,
        out_specs=vmem,
        compiler_params=params,
        cost_estimate=cost(half),
        name="last",
    )(kv, cross, rotated, *state)


def solution(mesh):
    in_specs = (P("pb", "grp"), P("pb", "grp"), P("pb", "grp"), P("grp", None), P("grp", None))
    out_specs = P("pb", "grp")
    return jax.shard_map(
        per_device, mesh=mesh, in_specs=in_specs, out_specs=out_specs, check_vma=False
    )
```

time: 23.5 us -> 22.7 us (0.966)
  Pallas kernels: 6.2 us -> 4.8 us
  local copies, waits for them, and re-layouts: 1.97 us -> 1.05 us
  other arithmetic: 0 us -> 0.89 us
  waiting for transfers between devices: 5.37 us -> 5.87 us
    pallas_call x1, Pallas kernels: 1.85 us -> 0.47 us  [per_device(): pl.pallas_call(functools.partial(pack_kernel, count), out_shape=[rows(2 *...]
    unnamed x14 -> x6, local copies, waits for them, and re-layouts: 1.97 us -> 1.05 us
    concatenate x0 -> x1, other arithmetic: none -> 0.89 us  [per_device(): jnp.concatenate([keys, values])]
    ppermute x8, waiting for transfers between devices: 5.37 us -> 5.87 us  [permute(): return lax.ppermute(value, 'pb', pairs)]
    pallas_call x2 -> x4, Pallas kernels: 3.26 us -> 3.24 us  [the longest x3 2.13 us: folded(): pl.pallas_call(functools.partial(fold_kernel, count, scale, width, first_...]
  transfers between devices with their start and end apart: 8 -> 8, of which waited for: 4 -> 5; matrix products, arithmetic and copies ran while one was open for 0% -> 0% of each run, Pallas kernels for 10% -> 14%
where the time goes in v5:
time: 22.7 us; the launch traced here: 22.3 us
  starting transfers between devices  9.62 us (42%)
  waiting for transfers between devices  5.87 us (26%)
  Pallas kernels  4.8 us (21%)
  local copies, waits for them, and re-layouts  1.05 us (5%)
  other arithmetic  0.89 us (4%)
    ppermute x8, starting transfers between devices, permute(): return lax.ppermute(value, 'pb', pairs)  9.62 us
    ppermute x8, waiting for transfers between devices, permute(): return lax.ppermute(value, 'pb', pairs)  5.87 us
    pallas_call x3, Pallas kernels, folded(): pl.pallas_call(functools.partial(fold_kernel, count, scale, width, first_...  2.13 us
    pallas_call x1, Pallas kernels, per_device(): pl.pallas_call(functools.partial(last_kernel, count, scale, width), out_s...  1.11 us
    unnamed x6, local copies, waits for them, and re-layouts  1.05 us
    pallas_call x1, Pallas kernels, per_device(): pl.pallas_call(functools.partial(near_kernel, scale, width), out_shape=[j...  0.97 us
    concatenate x1, other arithmetic, per_device(): jnp.concatenate([keys, values])  0.89 us
    pallas_call x1, Pallas kernels, per_device(): pl.pallas_call(functools.partial(pack_kernel, count), out_shape=[rows(2 *...  0.47 us
  transfers between devices with their start and end apart: 8, of which 5 were waited for; matrix products, arithmetic and copies ran while one was open for 0% of the time, Pallas kernels for 14%

profile of v5, /device:TPU:0, one launch (start us, length us, event | category | flops | bytes accessed | tf_op | source)
XLA Modules:
  0.0 22.3 jit_solution(17014486744644710041)
XLA Ops:
  0.0 0.9 %pad_maximum_fusion.both_ref = bf16[512,128]{1,0:T(8,128)(2,1)S(1)} fusion(bf16[256,128]{1,0:T(8,128)(2,1)} %param.7, bf16[256,128]{1,0:T(8,128)(2,1)} %param.6), kind=kLoop, calls=%fused_computation | loop fusion | flops 262144 | bytes 262144 | tf_op jit(solution)/shard_map/concatenate | solution.py:303
  0.9 0.0 copy-start.1
  0.9 0.5 %pack.1 = (bf16[256,256]{1,0:T(8,128)(2,1)S(1)}, s32[24,128]{1,0:T(8,128)S(1)}, bf16[256,256]{1,0:T(8,128)(2,1)S(1)}, bf16[128,256]{1,0:T(8,128)(2,1)S(1)}, bf16...) custom-call(s32[16,32]{1,0:T(8,128)S(1)} %bitcast.1, ...), custom_call_target="tpu_custom_call" | custom-call | tf_op jit(solution)/shard_map/pack/pallas_call | solution.py:295
  1.4 3.1 %collective-permute-start.1 = (bf16[128,256]{1,0:T(8,128)(2,1)S(1)}, bf16[128,256]{1,0:T(8,128)(2,1)S(1)}, u32[]{:S(2)}, u32[]{:S(2)}) collective-permute-start(bf16[128,256]{1,0:T(8,128)(2,1)S(1)} %get-tuple-element.41), channel_id=1, source_target_pairs={{0,4},{1,5},{2,6},{3,7},{4,8},{5,9},{6,10},{7,11},{8,12},{9,13},{1... | collective-permute-start | bytes 196616 | tf_op jit(solution)/shard_map/ppermute | solution.py:286
  4.5 2.6 %collective-permute-start.2 = (bf16[128,256]{1,0:T(8,128)(2,1)S(1)}, bf16[128,256]{1,0:T(8,128)(2,1)S(1)}, u32[]{:S(2)}, u32[]{:S(2)}) collective-permute-start(bf16[128,256]{1,0:T(8,128)(2,1)S(1)} %get-tuple-element.42), channel_id=1, source_target_pairs={{0,8},{1,9},{2,10},{3,11},{4,12},{5,13},{6,14},{7,15},{8,0},{9,1},... | collective-permute-start | bytes 196616 | tf_op jit(solution)/shard_map/ppermute | solution.py:286
  7.1 1.3 %collective-permute-start.3 = (bf16[128,256]{1,0:T(8,128)(2,1)S(1)}, bf16[128,256]{1,0:T(8,128)(2,1)S(1)}, u32[]{:S(2)}, u32[]{:S(2)}) collective-permute-start(bf16[128,256]{1,0:T(8,128)(2,1)S(1)} %get-tuple-element.43), channel_id=1, source_target_pairs={{0,12},{1,13},{2,14},{3,15},{4,0},{5,1},{6,2},{7,3},{8,4},{9,5},{1... | collective-permute-start | bytes 196616 | tf_op jit(solution)/shard_map/ppermute | solution.py:286
  8.4 0.1 collective-permute-start.4
  8.5 1.0 %copy-done = bf16[256,1024]{1,0:T(8,128)(2,1)S(1)} copy-done((bf16[256,1024]{1,0:T(8,128)(2,1)S(1)}, bf16[256,1024]{1,0:T(8,128)(2,1)}, u32[]{:S(2)}) %copy-start) | copy-done | bytes 524312
  9.5 1.0 %near.1 = (bf16[2,1024,128]{2,1,0:T(8,128)(2,1)S(1)}, f32[2,1,1024]{2,1,0:T(1,128)S(1)}, f32[2,1,1024]{2,1,0:T(1,128)S(1)}, f32[2,128,1024]{2,1,0:T(8,128)S(1)}) custom-call(bf16[256,1024]{1,0:T(8,128)(2,1)S(1)} %copy-done, bf16[128,128]{1,0:T(8,128)(2,1)S(1)} %copy-done.1, bf16[256,256]{1,0:T(8,128)(2,1)S(1)} %get-tuple-element.39.kv_ref), custom_call_target="tpu_custom_call" | custom-call | flops 134217728 | bytes 4000000 | tf_op jit(solution)/shard_map/near/pallas_call | solution.py:309
  10.5 0.0 collective-permute-done.1.refs_0_
  10.5 1.0 %collective-permute-done.2.refs_1_ = bf16[128,256]{1,0:T(8,128)(2,1)S(1)} collective-permute-done((bf16[128,256]{1,0:T(8,128)(2,1)S(1)}, bf16[128,256]{1,0:T(8,128)(2,1)S(1)}, u32[]{:S(2)}, u32[]{:S(2)}) %collective-permute-start.2) | collective-permute-done | bytes 65568 | tf_op jit(solution)/shard_map/ppermute | solution.py:286
  11.5 0.2 %collective-permute-done.3.refs_2_ = bf16[128,256]{1,0:T(8,128)(2,1)S(1)} collective-permute-done((bf16[128,256]{1,0:T(8,128)(2,1)S(1)}, bf16[128,256]{1,0:T(8,128)(2,1)S(1)}, u32[]{:S(2)}, u32[]{:S(2)}) %collective-permute-start.3) | collective-permute-done | bytes 65568 | tf_op jit(solution)/shard_map/ppermute | solution.py:286
  11.8 0.1 select.1
  11.9 0.9 %collective-permute-done.4.refs_0_ = bf16[128,256]{1,0:T(8,128)(2,1)S(1)} collective-permute-done((bf16[128,256]{1,0:T(8,128)(2,1)S(1)}, bf16[128,256]{1,0:T(8,128)(2,1)S(1)}, u32[]{:S(2)}, u32[]{:S(2)}) %collective-permute-start.4) | collective-permute-done | bytes 65568 | tf_op jit(solution)/shard_map/ppermute | solution.py:286
  12.8 0.1 collective-permute-start.7
  12.9 0.7 %collective-permute-start.6 = (bf16[256,256]{1,0:T(8,128)(2,1)S(1)}, bf16[256,256]{1,0:T(8,128)(2,1)S(1)}, u32[]{:S(2)}, u32[]{:S(2)}) collective-permute-start(bf16[256,256]{1,0:T(8,128)(2,1)S(1)} %get-tuple-element.58), channel_id=1, source_target_pairs={{0,2},{1,3},{2,0},{3,1},{4,6},{5,7},{6,4},{7,5},{8,10},{9,11},{10,... | collective-permute-start | bytes 393224 | tf_op jit(solution)/shard_map/ppermute | solution.py:286
  13.6 1.0 %collective-permute-start.5 = (bf16[224,256]{1,0:T(8,128)(2,1)S(1)}, bf16[224,256]{1,0:T(8,128)(2,1)S(1)}, u32[]{:S(2)}, u32[]{:S(2)}) collective-permute-start(bf16[224,256]{1,0:T(8,128)(2,1)S(1)} %get-tuple-element.57), channel_id=1, source_target_pairs={{0,3},{1,2},{2,1},{3,0},{4,7},{5,6},{6,5},{7,4},{8,11},{9,10},{10,... | collective-permute-start | bytes 344072 | tf_op jit(solution)/shard_map/ppermute | solution.py:286
  14.6 0.7 %collective-permute-start = (bf16[128,256]{1,0:T(8,128)(2,1)S(1)}, bf16[128,256]{1,0:T(8,128)(2,1)S(1)}, u32[]{:S(2)}, u32[]{:S(2)}) collective-permute-start(bf16[128,256]{1,0:T(8,128)(2,1)S(1)} %get-tuple-element.40), channel_id=1, source_target_pairs={{3,4},{7,8},{11,12},{4,3},{8,7},{12,11},{19,20},{23,24},{27,28},{2... | collective-permute-start | bytes 196616 | tf_op jit(solution)/shard_map/ppermute | solution.py:286
  15.3 0.9 %fold0.1 = (f32[2,1,1024]{2,1,0:T(1,128)S(1)}, f32[2,1,1024]{2,1,0:T(1,128)S(1)}, f32[2,128,1024]{2,1,0:T(8,128)S(1)}) custom-call(bf16[128,256]{1,0:T(8,128)(2,1)S(1)} %collective-permute-done.4.refs_0_, bf16[256,256]{1,0:T(8,128)(2,1)S(1)} %get-tuple-element.59.refs_1_, ...), custom_call_target="tpu_custom_call", output_to_operand_aliasing={{0}: (4, {}), {1}: (5, {}), {2}: (6, {})} | custom-call | flops 268435456 | bytes 4000000 | tf_op jit(solution)/shard_map/fold0/pallas_call | solution.py:339
  16.2 3.0 %collective-permute-done.6.refs_1_ = bf16[256,256]{1,0:T(8,128)(2,1)S(1)} collective-permute-done((bf16[256,256]{1,0:T(8,128)(2,1)S(1)}, bf16[256,256]{1,0:T(8,128)(2,1)S(1)}, u32[]{:S(2)}, u32[]{:S(2)}) %collective-permute-start.6) | collective-permute-done | bytes 131104 | tf_op jit(solution)/shard_map/ppermute | solution.py:286
  19.2 0.6 %fold2.1 = (f32[2,1,1024]{2,1,0:T(1,128)S(1)}, f32[2,1,1024]{2,1,0:T(1,128)S(1)}, f32[2,128,1024]{2,1,0:T(8,128)S(1)}) custom-call(bf16[128,256]{1,0:T(8,128)(2,1)S(1)} %collective-permute-done.4.refs_0_, bf16[256,256]{1,0:T(8,128)(2,1)S(1)} %collective-permute-done.6.refs_1_, ...), custom_call_target="tpu_custom_call", output_to_operand_aliasing={{0}: (3, {}), {1}: (4, {}), {2}: (5, {})} | custom-call | flops 134217728 | bytes 4000000 | tf_op jit(solution)/shard_map/fold2/pallas_call | solution.py:339
  19.9 0.7 %collective-permute-done.5.refs_1_ = bf16[224,256]{1,0:T(8,128)(2,1)S(1)} collective-permute-done((bf16[224,256]{1,0:T(8,128)(2,1)S(1)}, bf16[224,256]{1,0:T(8,128)(2,1)S(1)}, u32[]{:S(2)}, u32[]{:S(2)}) %collective-permute-start.5) | collective-permute-done | bytes 114720 | tf_op jit(solution)/shard_map/ppermute | solution.py:286
  20.6 0.6 %fold3.1 = (f32[2,1,1024]{2,1,0:T(1,128)S(1)}, f32[2,1,1024]{2,1,0:T(1,128)S(1)}, f32[2,128,1024]{2,1,0:T(8,128)S(1)}) custom-call(bf16[128,256]{1,0:T(8,128)(2,1)S(1)} %collective-permute-done.4.refs_0_, bf16[224,256]{1,0:T(8,128)(2,1)S(1)} %collective-permute-done.5.refs_1_, ...), custom_call_target="tpu_custom_call", output_to_operand_aliasing={{0}: (3, {}), {1}: (4, {}), {2}: (5, {})} | custom-call | flops 134217728 | bytes 4000000 | tf_op jit(solution)/shard_map/fold3/pallas_call | solution.py:339
  21.2 1.1 %last.1 = bf16[256,1024]{1,0:T(8,128)(2,1)} custom-call(bf16[256,256]{1,0:T(8,128)(2,1)S(1)} %get-tuple-element.39.kv_ref, bf16[128,256]{1,0:T(8,128)(2,1)S(1)} %collective-permute-done.cross_ref, bf16[2,1024,128]{2,1,0:T(8,128)(2,1)S(1)} %get-tuple-element.48.refs_3_.refs_2_.rot_ref, f32[2,1,1024]{2,1,0:T(1,128)S(1)} %get-tuple-element.70.m_ref, ...), custom_call_target="tpu_custom_call" | custom-call | flops 134217728 | bytes 4000000 | tf_op jit(solution)/shard_map/last/pallas_call | solution.py:355
  (6 shorter events, 0.0 us)
Async XLA Ops:
  0.0 0.9 %copy-start.2 = (s32[32,16]{0,1:T(8,128)S(1)}, s32[32,16]{0,1:T(8,128)}, u32[]{:S(2)}) copy-start(s32[32,16]{0,1:T(8,128)} %param.9) | copy-start | bytes 6148
  0.9 7.6 %copy-start.1 = (bf16[128,128]{1,0:T(8,128)(2,1)S(1)}, bf16[128,128]{1,0:T(8,128)(2,1)}, u32[]{:S(2)}) copy-start(bf16[128,128]{1,0:T(8,128)(2,1)} %basis_ref.1) | copy-start | bytes 98308
  1.4 9.1 %collective-permute-start.1 = (bf16[128,256]{1,0:T(8,128)(2,1)S(1)}, bf16[128,256]{1,0:T(8,128)(2,1)S(1)}, u32[]{:S(2)}, u32[]{:S(2)}) collective-permute-start(bf16[128,256]{1,0:T(8,128)(2,1)S(1)} %get-tuple-element.41), channel_id=1, source_target_pairs={{0,4},{1,5},{2,6},{3,7},{4,8},{5,9},{6,10},{7,11},{8,12},{9,13},{1... | collective-permute-start | bytes 196616 | tf_op jit(solution)/shard_map/ppermute | solution.py:286
  4.5 7.1 %collective-permute-start.2 = (bf16[128,256]{1,0:T(8,128)(2,1)S(1)}, bf16[128,256]{1,0:T(8,128)(2,1)S(1)}, u32[]{:S(2)}, u32[]{:S(2)}) collective-permute-start(bf16[128,256]{1,0:T(8,128)(2,1)S(1)} %get-tuple-element.42), channel_id=1, source_target_pairs={{0,8},{1,9},{2,10},{3,11},{4,12},{5,13},{6,14},{7,15},{8,0},{9,1},... | collective-permute-start | bytes 196616 | tf_op jit(solution)/shard_map/ppermute | solution.py:286
  7.1 4.7 %collective-permute-start.3 = (bf16[128,256]{1,0:T(8,128)(2,1)S(1)}, bf16[128,256]{1,0:T(8,128)(2,1)S(1)}, u32[]{:S(2)}, u32[]{:S(2)}) collective-permute-start(bf16[128,256]{1,0:T(8,128)(2,1)S(1)} %get-tuple-element.43), channel_id=1, source_target_pairs={{0,12},{1,13},{2,14},{3,15},{4,0},{5,1},{6,2},{7,3},{8,4},{9,5},{1... | collective-permute-start | bytes 196616 | tf_op jit(solution)/shard_map/ppermute | solution.py:286
  8.4 4.3 %collective-permute-start.4 = (bf16[128,256]{1,0:T(8,128)(2,1)S(1)}, bf16[128,256]{1,0:T(8,128)(2,1)S(1)}, u32[]{:S(2)}, u32[]{:S(2)}) collective-permute-start(bf16[128,256]{1,0:T(8,128)(2,1)S(1)} %get-tuple-element.55), channel_id=1, source_target_pairs={{0,3},{1,2},{2,1},{3,0},{4,7},{5,6},{6,5},{7,4},{8,11},{9,10},{10,... | collective-permute-start | bytes 196616 | tf_op jit(solution)/shard_map/ppermute | solution.py:286
  8.5 1.0 %copy-start = (bf16[256,1024]{1,0:T(8,128)(2,1)S(1)}, bf16[256,1024]{1,0:T(8,128)(2,1)}, u32[]{:S(2)}) copy-start(bf16[256,1024]{1,0:T(8,128)(2,1)} %q_ref.1) | copy-start | bytes 1572868
  12.8 2.5 %collective-permute-start.7 = (bf16[384,256]{1,0:T(8,128)(2,1)S(1)}, bf16[384,256]{1,0:T(8,128)(2,1)S(1)}, u32[]{:S(2)}, u32[]{:S(2)}) collective-permute-start(bf16[384,256]{1,0:T(8,128)(2,1)S(1)} %get-tuple-element.60), channel_id=1, source_target_pairs={{0,1},{1,0},{2,3},{3,2},{4,5},{5,4},{6,7},{7,6},{8,9},{9,8},{10,11... | collective-permute-start | bytes 589832 | tf_op jit(solution)/shard_map/ppermute | solution.py:286
  12.9 6.3 %collective-permute-start.6 = (bf16[256,256]{1,0:T(8,128)(2,1)S(1)}, bf16[256,256]{1,0:T(8,128)(2,1)S(1)}, u32[]{:S(2)}, u32[]{:S(2)}) collective-permute-start(bf16[256,256]{1,0:T(8,128)(2,1)S(1)} %get-tuple-element.58), channel_id=1, source_target_pairs={{0,2},{1,3},{2,0},{3,1},{4,6},{5,7},{6,4},{7,5},{8,10},{9,11},{10,... | collective-permute-start | bytes 393224 | tf_op jit(solution)/shard_map/ppermute | solution.py:286
  13.6 7.0 %collective-permute-start.5 = (bf16[224,256]{1,0:T(8,128)(2,1)S(1)}, bf16[224,256]{1,0:T(8,128)(2,1)S(1)}, u32[]{:S(2)}, u32[]{:S(2)}) collective-permute-start(bf16[224,256]{1,0:T(8,128)(2,1)S(1)} %get-tuple-element.57), channel_id=1, source_target_pairs={{0,3},{1,2},{2,1},{3,0},{4,7},{5,6},{6,5},{7,4},{8,11},{9,10},{10,... | collective-permute-start | bytes 344072 | tf_op jit(solution)/shard_map/ppermute | solution.py:286
  14.6 6.6 %collective-permute-start = (bf16[128,256]{1,0:T(8,128)(2,1)S(1)}, bf16[128,256]{1,0:T(8,128)(2,1)S(1)}, u32[]{:S(2)}, u32[]{:S(2)}) collective-permute-start(bf16[128,256]{1,0:T(8,128)(2,1)S(1)} %get-tuple-element.40), channel_id=1, source_target_pairs={{3,4},{7,8},{11,12},{4,3},{8,7},{12,11},{19,20},{23,24},{27,28},{2... | collective-permute-start | bytes 196616 | tf_op jit(solution)/shard_map/ppermute | solution.py:286

commit v6 on v5

--- a/solution.py
+++ b/solution.py
@@ -49,7 +49,7 @@
 
 def pack_kernel(count, picks_ref, both_ref, *refs):
     planes = count // PLANE
-    kv_ref, table_ref, own_ref, inner_ref, cross_ref, packet_refs = *refs[:5], refs[5:]
+    kv_ref, table_ref, own_ref, side_ref, packet_refs = *refs[:4], refs[4:]
     me, z, r = place(count)
     dim = both_ref.shape[1]
     total = both_ref.shape[0] // 2 // KB
@@ -65,7 +65,6 @@
     for m in range(PLANE):
         dest = z * PLANE + (r ^ m)
         wanted += [(me, 2 * count - 1 - dest), (me, dest)]
-    wanted.append((me, jnp.minimum(me + PLANE - 1, count - 1)))
     index = splat(picks_ref, wanted, dim)
     for part in range(2):
         cols = slice(part * dim, (part + 1) * dim)
@@ -77,11 +76,7 @@
             i = len(down) + g
             own_ref[at(g), cols] = chosen(index[i : i + 1], subs)
         for t in range(per_half):
-            inner = jnp.where(r == 1, subs[t], subs[per_half + t])
-            if t == 0:
-                inner = jnp.where(r == 0, chosen(index[len(wanted) - 1 :], subs), inner)
-            inner_ref[at(t), cols] = inner
-            cross_ref[at(t), cols] = jnp.where(r == PLANE - 1, subs[t], subs[per_half + t])
+            side_ref[at(t), cols] = jnp.where(me % 2 == 1, subs[t], subs[per_half + t])
     wanted, fixed = [], []
     for j in range(1, planes):
         up = z >= j
@@ -97,15 +92,14 @@
 
 def select_kernel(count, table_ref, own_ref, kv_ref, *refs):
     planes = count // PLANE
-    packet_refs, moved_refs = refs[: planes - 1], refs[planes - 1 :]
+    packet_refs, moved_refs, early_ref = refs[: planes - 1], refs[planes - 1 : planes + 3], refs[planes + 3]
     dim = table_ref.shape[1]
     per_half = kv_ref.shape[0] // 2 // KB
     for t in range(per_half):
         moved_refs[1][at(2 * planes + t)] = kv_ref[sub(lax.axis_index("pb") % 2 * per_half + t)]
     for m in range(PLANE):
         moved_refs[m][at(0)] = own_ref[at(2 * m)]
-        if m < PLANE - 1:
-            moved_refs[m][at(planes)] = own_ref[at(2 * m + 1)]
+        moved_refs[m][at(planes)] = own_ref[at(2 * m + 1)]
     for j, packet in enumerate(packet_refs, 1):
         for part in (slice(0, dim), slice(dim, 2 * dim)):
             choices = [packet[at(t), part] for t in range(PLANE)]
@@ -113,10 +107,10 @@
                 row = ((j - 1) * PLANE + m) * 2
                 moved_refs[m][at(j), part] = chosen(table_ref[row : row + 1], choices)
                 early = chosen(table_ref[row + 1 : row + 2], choices)
-                if m < 2:
+                if m < PLANE - 1:
                     moved_refs[m][at(planes + j), part] = early
                 else:
-                    moved_refs[m][at(planes + j - (m == 3)), part] = early
+                    early_ref[at(j - 1), part] = early
 
 
 def usable(count, block, m):
@@ -199,27 +193,24 @@
         attend_all(heads * half // width, score, v_t, None, save)
 
 
-def fold_kernel(count, scale, width, first_m, *refs):
-    inner_ref, moved_refs, rot_ref, old, new = refs[0], refs[1:-7], refs[-7], refs[-6:-3], refs[-3:]
-    me, _, r = place(count)
-    even = me % 2 == 0
+def fold_kernel(count, scale, width, stage, *refs):
+    come, rot_ref, old, new = refs[:-7], refs[-7], refs[-6:-3], refs[-3:]
+    me, z, _ = place(count)
     late = (count // PLANE) * KB
 
     def run(block):
-        parts, masks = [], []
-        for i, ref in enumerate(moved_refs):
-            m = first_m + i
-            masks += usable(count, block, m)
+        if stage == 0:
+            mine_ref, next_ref, side_ref, kv_ref = come
+            half = side_ref.shape[0]
+            masks = usable(count, block, 0) + usable(count, block, 1) + [None] * (half // KB)
+            parts = [ref[(1 - block) * late : (2 - block) * late] for ref in (mine_ref, next_ref)]
+            side = side_ref[...]
             if block == 1:
-                parts.append(ref[:late])
-            elif m == PLANE - 1:
-                parts += [inner_ref[at(0)], ref[late : 2 * late - KB]]
-            else:
-                parts.append(ref[late : 2 * late])
-        if first_m == 0:
-            beside = even if block == 1 else jnp.logical_not(even)
-            parts.append(jnp.where(beside, moved_refs[1][2 * late :], inner_ref[...]))
-            masks += [beside | (r == 1 + (1 - block))] * (inner_ref.shape[0] // KB)
+                side = jnp.where(me == count - 1, kv_ref[:half], side)
+            parts.append(jnp.where(me % 2 == block, side, next_ref[2 * late :]))
+        else:
+            first = (1 - block) * late
+            parts, masks = [come[0][first : first + late]], usable(count, block, stage)
 
         def save(step, m, l, acc):
             for ref, value in zip(new, (m, l, acc), strict=True):
@@ -227,15 +218,22 @@
 
         fold(jnp.concatenate(parts, axis=0), masks, scale, width, block, rot_ref, old, save)
 
-    run(1)
-    pl.when(me >= (1 if first_m == 0 else 2))(lambda: run(0))
-
-
-def last_kernel(count, scale, width, kv_ref, cross_ref, rot_ref, m_ref, l_ref, acc_ref, out_ref):
-    me, z, r = place(count)
+    if stage == 0:
+        run(1)
+        pl.when(me >= 1)(lambda: run(0))
+    elif stage == 2:
+        run(1)
+        pl.when(me >= 2)(lambda: run(0))
+    else:
+        pl.when(z >= 1)(lambda: run(1))
+
+
+def last_kernel(count, scale, width, third_ref, early_ref, rot_ref, *refs):
+    old, out_ref = refs[:3], refs[3]
+    me, z, _ = place(count)
+    late = (count // PLANE) * KB
     half = out_ref.shape[0] // 2
     dim = rot_ref.shape[2]
-    old = (m_ref, l_ref, acc_ref)
 
     def finish(block, step, l, acc):
         done = acc / l
@@ -245,21 +243,30 @@
                 done[:, h * half : (h + 1) * half].T.astype(out_ref.dtype)
             )
 
-    def add(block):
-        prev = cross_ref[...]
-        if block == 1:
-            prev = jnp.where(me == count - 1, kv_ref[:half], prev)
-        masks = [None] * (half // KB)
-        fold(prev, masks, scale, width, block, rot_ref, old, lambda step, m, l, acc: finish(block, step, l, acc))
+    def add(block, parts, masks):
+        kv = jnp.concatenate(parts, axis=0)
+        fold(kv, masks, scale, width, block, rot_ref, old, lambda step, m, l, acc: finish(block, step, l, acc))
 
     def close(block):
         for step in range(rot_ref.shape[1] // width):
             cols = slice(step * width, (step + 1) * width)
-            finish(block, step, l_ref[block, :, cols], acc_ref[block, :, cols])
-
-    for block, outer in enumerate(((r == 0) & (z > 0), r == PLANE - 1)):
-        pl.when(outer)(functools.partial(add, block))
-        pl.when(jnp.logical_not(outer))(functools.partial(close, block))
+            finish(block, step, old[1][block, :, cols], old[2][block, :, cols])
+
+    @pl.when(z == 0)
+    def _():
+        add(1, [third_ref[:late]], usable(count, 1, 3))
+
+    @pl.when(z > 0)
+    def _():
+        close(1)
+
+    @pl.when(me >= 2)
+    def _():
+        add(0, [third_ref[late:], early_ref[...]], usable(count, 0, 3))
+
+    @pl.when(me < 2)
+    def _():
+        close(0)
 
 
 def per_device(queries, keys, values, basis, picks):
@@ -292,12 +299,12 @@
 
     per_half = half // KB
     table = jax.ShapeDtypeStruct(((planes - 1) * PLANE * 2, dim), jnp.int32)
-    kv, table, own, inner, cross, *packets = pl.pallas_call(
+    kv, table, own, side, *packets = pl.pallas_call(
         functools.partial(pack_kernel, count),
-        out_shape=[rows(2 * per_half), table, rows(2 * PLANE), rows(per_half), rows(per_half)]
+        out_shape=[rows(2 * per_half), table, rows(2 * PLANE), rows(per_half)]
         + [rows(PLANE)] * (planes - 1),
         in_specs=[vmem] * 2,
-        out_specs=[vmem] * (4 + planes),
+        out_specs=[vmem] * (3 + planes),
         compiler_params=params,
         name="pack",
     )(picks.T, jnp.concatenate([keys, values]))
@@ -316,9 +323,17 @@
         name="near",
     )(queries, basis, kv)
     packets, near = lax.optimization_barrier((packets, near))
-    inner = permute(inner, [(s, s ^ (PLANE - 1)) for s in range(count)])
-
-    sizes = [2 * planes, 2 * planes + per_half, 2 * planes, 2 * planes - 1]
+    groups = lax.axis_size("grp")
+    pairs = []
+    for g in range(groups):
+        pairs += [(g * count + s, g * count + s + (1 if s % 2 else -1)) for s in range(1, count - 1)]
+        pairs += [(g * count + s, (g + 1) % groups * count + s) for s in (0, count - 1)]
+    side = lax.ppermute(side, ("grp", "pb"), pairs)
+
+    def swap(value, m):
+        return permute(value, [(s, s ^ m) for s in range(count)])
+
+    sizes = [2 * planes, 2 * planes + per_half, 2 * planes, planes + 1, planes - 1]
     moved = list(
         pl.pallas_call(
             functools.partial(select_kernel, count),
@@ -329,29 +344,28 @@
             name="select",
         )(table, own, kv, *packets)
     )
-    moved[1], inner = lax.optimization_barrier((moved[1], inner))
-    for m in range(1, PLANE):
-        moved[m] = permute(moved[m], [(s, s ^ m) for s in range(count)])
+    moved[1], side = lax.optimization_barrier((moved[1], side))
+    for m in (1, 2, 3):
+        moved[m] = swap(moved[m], m)
+    early = permute(moved[PLANE], [(s, s ^ (PLANE - 1 if s >= PLANE else 1)) for s in range(count)])
 
     rotated, *state = near
 
-    def folded(state, first_m, messages):
+    def folded(state, stage, messages):
         return pl.pallas_call(
-            functools.partial(fold_kernel, count, scale, width, first_m),
+            functools.partial(fold_kernel, count, scale, width, stage),
             out_shape=shapes,
-            in_specs=[vmem] * (5 + len(messages)),
+            in_specs=[vmem] * (4 + len(messages)),
             out_specs=[vmem] * 3,
-            input_output_aliases={2 + len(messages) + i: i for i in range(3)},
+            input_output_aliases={1 + len(messages) + i: i for i in range(3)},
             compiler_params=params,
-            cost_estimate=cost(half * len(messages)),
-            name=f"fold{first_m}",
-        )(inner, *messages, rotated, *state)
-
-    state = folded(state, 0, moved[:2])
-    borders = range(PLANE - 1, count - 1, PLANE)
-    cross = permute(cross, [(s, s + 1) for s in borders] + [(s + 1, s) for s in borders])
-    state = folded(state, 2, moved[2:3])
-    state = folded(state, 3, moved[3:4])
+            cost_estimate=cost(half),
+            name=f"fold{stage}",
+        )(*messages, rotated, *state)
+
+    state = folded(state, 0, [moved[0], moved[1], side, kv])
+    state = folded(state, 2, [moved[2]])
+    state = folded(state, 3, [moved[3]])
     return pl.pallas_call(
         functools.partial(last_kernel, count, scale, width),
         out_shape=jax.ShapeDtypeStruct(queries.shape, bf16),
@@ -360,7 +374,7 @@
         compiler_params=params,
         cost_estimate=cost(half),
         name="last",
-    )(kv, cross, rotated, *state)
+    )(moved[3], early, rotated, *state)
 
 
 def solution(mesh):

time: 22.7 us -> 22.2 us (0.978)
  the two profiles are of different devices: /device:TPU:0 before, /device:TPU:17 now
where the time goes in v6:
time: 22.2 us; the launch traced here: 22 us
  starting transfers between devices  10.3 us (46%)
  Pallas kernels  6.59 us (30%)
  waiting for transfers between devices  3.01 us (14%)
  local copies, waits for them, and re-layouts  1.05 us (5%)
  other arithmetic  0.89 us (4%)
    ppermute x7, starting transfers between devices, permute(): return lax.ppermute(value, 'pb', pairs)  7.85 us
    pallas_call x3, Pallas kernels, folded(): pl.pallas_call(functools.partial(fold_kernel, count, scale, width, stage)...  3.54 us
    ppermute x7, waiting for transfers between devices, permute(): return lax.ppermute(value, 'pb', pairs)  2.95 us
    ppermute x1, starting transfers between devices, per_device(): side = lax.ppermute(side, ('grp', 'pb'), pairs)  2.48 us
    pallas_call x1, Pallas kernels, per_device(): pl.pallas_call(functools.partial(last_kernel, count, scale, width), out_s...  1.51 us
    unnamed x6, local copies, waits for them, and re-layouts  1.05 us
    pallas_call x1, Pallas kernels, per_device(): pl.pallas_call(functools.partial(near_kernel, scale, width), out_shape=[j...  0.97 us
    concatenate x1, other arithmetic, per_device(): jnp.concatenate([keys, values])  0.89 us
  transfers between devices with their start and end apart: 8, of which 3 were waited for; matrix products, arithmetic and copies ran while one was open for 0% of the time, Pallas kernels for 21%

profile of v6, /device:TPU:17, one launch (start us, length us, event | category | flops | bytes accessed | tf_op | source)
XLA Modules:
  0.0 22.0 jit_solution(883394742552143444)
XLA Ops:
  0.0 0.9 %pad_maximum_fusion.both_ref = bf16[512,128]{1,0:T(8,128)(2,1)S(1)} fusion(bf16[256,128]{1,0:T(8,128)(2,1)} %param.7, bf16[256,128]{1,0:T(8,128)(2,1)} %param.6), kind=kLoop, calls=%fused_computation | loop fusion | flops 262144 | bytes 262144 | tf_op jit(solution)/shard_map/concatenate | solution.py:310
  0.9 0.0 copy-start.1
  0.9 0.4 %pack.1 = (bf16[256,256]{1,0:T(8,128)(2,1)S(1)}, s32[24,128]{1,0:T(8,128)S(1)}, bf16[256,256]{1,0:T(8,128)(2,1)S(1)}, bf16[128,256]{1,0:T(8,128)(2,1)S(1)}, bf16...) custom-call(s32[16,32]{1,0:T(8,128)S(1)} %bitcast.1, ...), custom_call_target="tpu_custom_call" | custom-call | tf_op jit(solution)/shard_map/pack/pallas_call | solution.py:302
  1.4 1.3 %collective-permute-start = (bf16[128,256]{1,0:T(8,128)(2,1)S(1)}, bf16[128,256]{1,0:T(8,128)(2,1)S(1)}, u32[]{:S(2)}, u32[]{:S(2)}) collective-permute-start(bf16[128,256]{1,0:T(8,128)(2,1)S(1)} %get-tuple-element.42), channel_id=1, source_target_pairs={{0,4},{1,5},{2,6},{3,7},{4,8},{5,9},{6,10},{7,11},{8,12},{9,13},{1... | collective-permute-start | bytes 196616 | tf_op jit(solution)/shard_map/ppermute | solution.py:293
  2.7 0.1 collective-permute-start.1
  2.8 1.2 %collective-permute-start.2 = (bf16[128,256]{1,0:T(8,128)(2,1)S(1)}, bf16[128,256]{1,0:T(8,128)(2,1)S(1)}, u32[]{:S(2)}, u32[]{:S(2)}) collective-permute-start(bf16[128,256]{1,0:T(8,128)(2,1)S(1)} %get-tuple-element.44), channel_id=1, source_target_pairs={{0,12},{1,13},{2,14},{3,15},{4,0},{5,1},{6,2},{7,3},{8,4},{9,5},{1... | collective-permute-start | bytes 196616 | tf_op jit(solution)/shard_map/ppermute | solution.py:293
  4.0 2.5 %collective-permute-start.6 = (bf16[128,256]{1,0:T(8,128)(2,1)S(1)}, bf16[128,256]{1,0:T(8,128)(2,1)S(1)}, u32[]{:S(2)}, u32[]{:S(2)}) collective-permute-start(bf16[128,256]{1,0:T(8,128)(2,1)S(1)} %get-tuple-element.58), channel_id=1, source_target_pairs={{1,2},{2,1},{3,4},{4,3},{5,6},{6,5},{7,8},{8,7},{9,10},{10,9},{11,... | collective-permute-start | bytes 196616 | tf_op jit(solution)/shard_map/ppermute | solution.py:331
  6.5 1.0 %copy-done = bf16[256,1024]{1,0:T(8,128)(2,1)S(1)} copy-done((bf16[256,1024]{1,0:T(8,128)(2,1)S(1)}, bf16[256,1024]{1,0:T(8,128)(2,1)}, u32[]{:S(2)}) %copy-start) | copy-done | bytes 524312
  7.5 1.0 %near.1 = (bf16[2,1024,128]{2,1,0:T(8,128)(2,1)S(1)}, f32[2,1,1024]{2,1,0:T(1,128)S(1)}, f32[2,1,1024]{2,1,0:T(1,128)S(1)}, f32[2,128,1024]{2,1,0:T(8,128)S(1)}) custom-call(bf16[256,1024]{1,0:T(8,128)(2,1)S(1)} %copy-done, bf16[128,128]{1,0:T(8,128)(2,1)S(1)} %copy-done.1, bf16[256,256]{1,0:T(8,128)(2,1)S(1)} %get-tuple-element.41.kv_ref.refs_3_), custom_call_target="tpu_custom_call" | custom-call | flops 134217728 | bytes 4000000 | tf_op jit(solution)/shard_map/near/pallas_call | solution.py:316
  8.5 0.0 collective-permute-done.1.refs_1_
  8.5 0.0 collective-permute-done.2.refs_2_
  8.5 0.1 select.1
  8.6 0.1 collective-permute-done.6.refs_2_
  8.7 3.5 %collective-permute-start.7 = (bf16[384,256]{1,0:T(8,128)(2,1)S(1)}, bf16[384,256]{1,0:T(8,128)(2,1)S(1)}, u32[]{:S(2)}, u32[]{:S(2)}) collective-permute-start(bf16[384,256]{1,0:T(8,128)(2,1)S(1)} %get-tuple-element.59), channel_id=1, source_target_pairs={{0,1},{1,0},{2,3},{3,2},{4,5},{5,4},{6,7},{7,6},{8,9},{9,8},{10,11... | collective-permute-start | bytes 589832 | tf_op jit(solution)/shard_map/ppermute | solution.py:293
  12.2 1.6 %collective-permute-start.3 = (bf16[160,256]{1,0:T(8,128)(2,1)S(1)}, bf16[160,256]{1,0:T(8,128)(2,1)S(1)}, u32[]{:S(2)}, u32[]{:S(2)}) collective-permute-start(bf16[160,256]{1,0:T(8,128)(2,1)S(1)} %get-tuple-element.52), channel_id=1, source_target_pairs={{0,3},{1,2},{2,1},{3,0},{4,7},{5,6},{6,5},{7,4},{8,11},{9,10},{10,... | collective-permute-start | bytes 245768 | tf_op jit(solution)/shard_map/ppermute | solution.py:293
  13.8 0.1 collective-permute-start.4
  13.9 0.0 collective-permute-done.7.refs_1_
  13.9 1.7 %fold0.1 = (f32[2,1,1024]{2,1,0:T(1,128)S(1)}, f32[2,1,1024]{2,1,0:T(1,128)S(1)}, f32[2,128,1024]{2,1,0:T(8,128)S(1)}) custom-call(bf16[256,256]{1,0:T(8,128)(2,1)S(1)} %get-tuple-element.56.refs_0_, bf16[384,256]{1,0:T(8,128)(2,1)S(1)} %collective-permute-done.7.refs_1_, ...), custom_call_target="tpu_custom_call", output_to_operand_aliasing={{0}: (5, {}), {1}: (6, {}), {2}: (7, {})} | custom-call | flops 134217728 | bytes 4000000 | tf_op jit(solution)/shard_map/fold0/pallas_call | solution.py:355
  15.7 1.6 %collective-permute-done.5.refs_0_ = bf16[256,256]{1,0:T(8,128)(2,1)S(1)} collective-permute-done((bf16[256,256]{1,0:T(8,128)(2,1)S(1)}, bf16[256,256]{1,0:T(8,128)(2,1)S(1)}, u32[]{:S(2)}, u32[]{:S(2)}) %collective-permute-start.5) | collective-permute-done | bytes 131104 | tf_op jit(solution)/shard_map/ppermute | solution.py:293
  17.3 1.2 %fold2.1 = (f32[2,1,1024]{2,1,0:T(1,128)S(1)}, f32[2,1,1024]{2,1,0:T(1,128)S(1)}, f32[2,128,1024]{2,1,0:T(8,128)S(1)}) custom-call(bf16[256,256]{1,0:T(8,128)(2,1)S(1)} %collective-permute-done.5.refs_0_, bf16[2,1024,128]{2,1,0:T(8,128)(2,1)S(1)} %get-tuple-element.54.refs_4_.refs_1_.rot_ref, ...), custom_call_target="tpu_custom_call", output_to_operand_aliasing={{0}: (2, {}), {1}: (3, {}), {2}: (4, {})} | custom-call | flops 134217728 | bytes 4000000 | tf_op jit(solution)/shard_map/fold2/pallas_call | solution.py:355
  18.5 1.3 %collective-permute-done.3.refs_0_.third_ref = bf16[160,256]{1,0:T(8,128)(2,1)S(1)} collective-permute-done((bf16[160,256]{1,0:T(8,128)(2,1)S(1)}, bf16[160,256]{1,0:T(8,128)(2,1)S(1)}, u32[]{:S(2)}, u32[]{:S(2)}) %collective-permute-start.3) | collective-permute-done | bytes 81952 | tf_op jit(solution)/shard_map/ppermute | solution.py:293
  19.8 0.6 %fold3.1 = (f32[2,1,1024]{2,1,0:T(1,128)S(1)}, f32[2,1,1024]{2,1,0:T(1,128)S(1)}, f32[2,128,1024]{2,1,0:T(8,128)S(1)}) custom-call(bf16[160,256]{1,0:T(8,128)(2,1)S(1)} %collective-permute-done.3.refs_0_.third_ref, bf16[2,1024,128]{2,1,0:T(8,128)(2,1)S(1)} %get-tuple-element.54.refs_4_.refs_1_.rot_ref, ...), custom_call_target="tpu_custom_call", output_to_operand_aliasing={{0}: (2, {}), {1}: (3, {}), {2}: (4, {})} | custom-call | flops 134217728 | bytes 4000000 | tf_op jit(solution)/shard_map/fold3/pallas_call | solution.py:355
  20.4 0.0 collective-permute-done.4.early_ref
  20.5 1.5 %last.1 = bf16[256,1024]{1,0:T(8,128)(2,1)} custom-call(bf16[160,256]{1,0:T(8,128)(2,1)S(1)} %collective-permute-done.3.refs_0_.third_ref, bf16[96,256]{1,0:T(8,128)(2,1)S(1)} %collective-permute-done.4.early_ref, bf16[2,1024,128]{2,1,0:T(8,128)(2,1)S(1)} %get-tuple-element.54.refs_4_.refs_1_.rot_ref, f32[2,1,1024]{2,1,0:T(1,128)S(1)} %get-tuple-element.70.refs_0_, ...), custom_call_target="tpu_custom_call" | custom-call | flops 134217728 | bytes 4000000 | tf_op jit(solution)/shard_map/last/pallas_call | solution.py:369
  (6 shorter events, 0.0 us)
Async XLA Ops:
  0.0 0.9 %copy-start.2 = (s32[32,16]{0,1:T(8,128)S(1)}, s32[32,16]{0,1:T(8,128)}, u32[]{:S(2)}) copy-start(s32[32,16]{0,1:T(8,128)} %param.9) | copy-start | bytes 6148
  0.9 5.5 %copy-start.1 = (bf16[128,128]{1,0:T(8,128)(2,1)S(1)}, bf16[128,128]{1,0:T(8,128)(2,1)}, u32[]{:S(2)}) copy-start(bf16[128,128]{1,0:T(8,128)(2,1)} %basis_ref.1) | copy-start | bytes 98308
  1.4 7.1 %collective-permute-start = (bf16[128,256]{1,0:T(8,128)(2,1)S(1)}, bf16[128,256]{1,0:T(8,128)(2,1)S(1)}, u32[]{:S(2)}, u32[]{:S(2)}) collective-permute-start(bf16[128,256]{1,0:T(8,128)(2,1)S(1)} %get-tuple-element.42), channel_id=1, source_target_pairs={{0,4},{1,5},{2,6},{3,7},{4,8},{5,9},{6,10},{7,11},{8,12},{9,13},{1... | collective-permute-start | bytes 196616 | tf_op jit(solution)/shard_map/ppermute | solution.py:293
  2.7 5.8 %collective-permute-start.1 = (bf16[128,256]{1,0:T(8,128)(2,1)S(1)}, bf16[128,256]{1,0:T(8,128)(2,1)S(1)}, u32[]{:S(2)}, u32[]{:S(2)}) collective-permute-start(bf16[128,256]{1,0:T(8,128)(2,1)S(1)} %get-tuple-element.43), channel_id=1, source_target_pairs={{0,8},{1,9},{2,10},{3,11},{4,12},{5,13},{6,14},{7,15},{8,0},{9,1},... | collective-permute-start | bytes 196616 | tf_op jit(solution)/shard_map/ppermute | solution.py:293
  2.8 5.7 %collective-permute-start.2 = (bf16[128,256]{1,0:T(8,128)(2,1)S(1)}, bf16[128,256]{1,0:T(8,128)(2,1)S(1)}, u32[]{:S(2)}, u32[]{:S(2)}) collective-permute-start(bf16[128,256]{1,0:T(8,128)(2,1)S(1)} %get-tuple-element.44), channel_id=1, source_target_pairs={{0,12},{1,13},{2,14},{3,15},{4,0},{5,1},{6,2},{7,3},{8,4},{9,5},{1... | collective-permute-start | bytes 196616 | tf_op jit(solution)/shard_map/ppermute | solution.py:293
  4.0 4.7 %collective-permute-start.6 = (bf16[128,256]{1,0:T(8,128)(2,1)S(1)}, bf16[128,256]{1,0:T(8,128)(2,1)S(1)}, u32[]{:S(2)}, u32[]{:S(2)}) collective-permute-start(bf16[128,256]{1,0:T(8,128)(2,1)S(1)} %get-tuple-element.58), channel_id=1, source_target_pairs={{1,2},{2,1},{3,4},{4,3},{5,6},{6,5},{7,8},{8,7},{9,10},{10,9},{11,... | collective-permute-start | bytes 196616 | tf_op jit(solution)/shard_map/ppermute | solution.py:331
  6.5 1.0 %copy-start = (bf16[256,1024]{1,0:T(8,128)(2,1)S(1)}, bf16[256,1024]{1,0:T(8,128)(2,1)}, u32[]{:S(2)}) copy-start(bf16[256,1024]{1,0:T(8,128)(2,1)} %q_ref.1) | copy-start | bytes 1572868
  8.7 5.2 %collective-permute-start.7 = (bf16[384,256]{1,0:T(8,128)(2,1)S(1)}, bf16[384,256]{1,0:T(8,128)(2,1)S(1)}, u32[]{:S(2)}, u32[]{:S(2)}) collective-permute-start(bf16[384,256]{1,0:T(8,128)(2,1)S(1)} %get-tuple-element.59), channel_id=1, source_target_pairs={{0,1},{1,0},{2,3},{3,2},{4,5},{5,4},{6,7},{7,6},{8,9},{9,8},{10,11... | collective-permute-start | bytes 589832 | tf_op jit(solution)/shard_map/ppermute | solution.py:293
  12.2 5.1 %collective-permute-start.5 = (bf16[256,256]{1,0:T(8,128)(2,1)S(1)}, bf16[256,256]{1,0:T(8,128)(2,1)S(1)}, u32[]{:S(2)}, u32[]{:S(2)}) collective-permute-start(bf16[256,256]{1,0:T(8,128)(2,1)S(1)} %get-tuple-element.55), channel_id=1, source_target_pairs={{0,2},{1,3},{2,0},{3,1},{4,6},{5,7},{6,4},{7,5},{8,10},{9,11},{10,... | collective-permute-start | bytes 393224 | tf_op jit(solution)/shard_map/ppermute | solution.py:293
  12.2 7.7 %collective-permute-start.3 = (bf16[160,256]{1,0:T(8,128)(2,1)S(1)}, bf16[160,256]{1,0:T(8,128)(2,1)S(1)}, u32[]{:S(2)}, u32[]{:S(2)}) collective-permute-start(bf16[160,256]{1,0:T(8,128)(2,1)S(1)} %get-tuple-element.52), channel_id=1, source_target_pairs={{0,3},{1,2},{2,1},{3,0},{4,7},{5,6},{6,5},{7,4},{8,11},{9,10},{10,... | collective-permute-start | bytes 245768 | tf_op jit(solution)/shard_map/ppermute | solution.py:293
  13.8 6.7 %collective-permute-start.4 = (bf16[96,256]{1,0:T(8,128)(2,1)S(1)}, bf16[96,256]{1,0:T(8,128)(2,1)S(1)}, u32[]{:S(2)}, u32[]{:S(2)}) collective-permute-start(bf16[96,256]{1,0:T(8,128)(2,1)S(1)} %get-tuple-element.53), channel_id=1, source_target_pairs={{0,1},{1,0},{2,3},{3,2},{4,7},{5,6},{6,5},{7,4},{8,11},{9,10},{10,... | collective-permute-start | bytes 147464 | tf_op jit(solution)/shard_map/ppermute | solution.py:293

commit v7 on v6

--- a/solution.py
+++ b/solution.py
@@ -49,7 +49,7 @@
 
 def pack_kernel(count, picks_ref, both_ref, *refs):
     planes = count // PLANE
-    kv_ref, table_ref, own_ref, side_ref, packet_refs = *refs[:4], refs[4:]
+    kv_ref, table_ref, own_ref, over_ref, side_ref, packet_refs = *refs[:5], refs[5:]
     me, z, r = place(count)
     dim = both_ref.shape[1]
     total = both_ref.shape[0] // 2 // KB
@@ -62,7 +62,9 @@
         to = jnp.where(up, 0, (z + j - planes) * PLANE)
         wanted += [(me, 2 * count - 1 - (to + t)) for t in range(PLANE)]
         down += [up] * PLANE
-    for m in range(PLANE):
+    for m in (0, 1):
+        wanted.append((me, 2 * count - 1 - (z * PLANE + (r ^ m))))
+    for m in (2, 3):
         dest = z * PLANE + (r ^ m)
         wanted += [(me, 2 * count - 1 - dest), (me, dest)]
     index = splat(picks_ref, wanted, dim)
@@ -72,9 +74,9 @@
         for g, up in enumerate(down):
             j, t = g // PLANE, g % PLANE
             packet_refs[j][at(t), cols] = jnp.where(up, subs[t], chosen(index[g : g + 1], subs))
-        for g in range(2 * PLANE):
-            i = len(down) + g
-            own_ref[at(g), cols] = chosen(index[i : i + 1], subs)
+        for g in range(6):
+            ref, t = (own_ref, g) if g < 2 else (over_ref, g - 2)
+            ref[at(t), cols] = chosen(index[len(down) + g : len(down) + g + 1], subs)
         for t in range(per_half):
             side_ref[at(t), cols] = jnp.where(me % 2 == 1, subs[t], subs[per_half + t])
     wanted, fixed = [], []
@@ -90,27 +92,28 @@
         table_ref[g : g + 1] = jnp.where(up, index[g : g + 1], other)
 
 
-def select_kernel(count, table_ref, own_ref, kv_ref, *refs):
+def select_kernel(count, table_ref, own_ref, over_ref, kv_ref, *refs):
     planes = count // PLANE
-    packet_refs, moved_refs, early_ref = refs[: planes - 1], refs[planes - 1 : planes + 3], refs[planes + 3]
+    packet_refs, moved_refs, early_refs = refs[: planes - 1], refs[planes - 1 : planes + 3], refs[planes + 3 :]
     dim = table_ref.shape[1]
     per_half = kv_ref.shape[0] // 2 // KB
+    for m in (0, 1):
+        moved_refs[m][at(0)] = own_ref[at(m)]
+    moved_refs[1][(2 * planes - 1) * KB : (2 * planes + 1) * KB] = over_ref[2 * KB :]
     for t in range(per_half):
-        moved_refs[1][at(2 * planes + t)] = kv_ref[sub(lax.axis_index("pb") % 2 * per_half + t)]
-    for m in range(PLANE):
-        moved_refs[m][at(0)] = own_ref[at(2 * m)]
-        moved_refs[m][at(planes)] = own_ref[at(2 * m + 1)]
+        moved_refs[1][at(2 * planes + 1 + t)] = kv_ref[sub(lax.axis_index("pb") % 2 * per_half + t)]
     for j, packet in enumerate(packet_refs, 1):
         for part in (slice(0, dim), slice(dim, 2 * dim)):
             choices = [packet[at(t), part] for t in range(PLANE)]
-            for m in range(PLANE):
+            for m, ref in enumerate(moved_refs):
                 row = ((j - 1) * PLANE + m) * 2
-                moved_refs[m][at(j), part] = chosen(table_ref[row : row + 1], choices)
+                first = j - (m > 1)
+                ref[at(first), part] = chosen(table_ref[row : row + 1], choices)
                 early = chosen(table_ref[row + 1 : row + 2], choices)
-                if m < PLANE - 1:
-                    moved_refs[m][at(planes + j), part] = early
+                if m < 2:
+                    ref[at(first + planes - 1), part] = early
                 else:
-                    early_ref[at(j - 1), part] = early
+                    early_refs[m - 2][at(first), part] = early
 
 
 def usable(count, block, m):
@@ -195,22 +198,24 @@
 
 def fold_kernel(count, scale, width, stage, *refs):
     come, rot_ref, old, new = refs[:-7], refs[-7], refs[-6:-3], refs[-3:]
-    me, z, _ = place(count)
-    late = (count // PLANE) * KB
+    me = lax.axis_index("pb")
+    rest = (count // PLANE - 1) * KB
 
     def run(block):
+        masks = [usable(count, block, m) for m in range(PLANE)]
         if stage == 0:
-            mine_ref, next_ref, side_ref, kv_ref = come
+            mine_ref, next_ref, over_ref, side_ref, kv_ref = come
             half = side_ref.shape[0]
-            masks = usable(count, block, 0) + usable(count, block, 1) + [None] * (half // KB)
-            parts = [ref[(1 - block) * late : (2 - block) * late] for ref in (mine_ref, next_ref)]
+            far = slice(0, rest + KB) if block == 1 else slice(rest + KB, 2 * rest + KB)
             side = side_ref[...]
             if block == 1:
                 side = jnp.where(me == count - 1, kv_ref[:half], side)
-            parts.append(jnp.where(me % 2 == block, side, next_ref[2 * late :]))
+            third = 2 * rest + (2 - block) * KB
+            parts = [mine_ref[far], next_ref[far], over_ref[at(1 - block)], next_ref[third : third + KB]]
+            parts.append(jnp.where(me % 2 == block, side, next_ref[2 * rest + 3 * KB :]))
+            masks = masks[0][1 - block :] + masks[1][1 - block :] + masks[2][:1] + masks[3][:1] + [None] * (half // KB)
         else:
-            first = (1 - block) * late
-            parts, masks = [come[0][first : first + late]], usable(count, block, stage)
+            parts, masks = [come[0][...]], masks[stage][1:]
 
         def save(step, m, l, acc):
             for ref, value in zip(new, (m, l, acc), strict=True):
@@ -218,20 +223,14 @@
 
         fold(jnp.concatenate(parts, axis=0), masks, scale, width, block, rot_ref, old, save)
 
+    run(1)
     if stage == 0:
-        run(1)
         pl.when(me >= 1)(lambda: run(0))
-    elif stage == 2:
-        run(1)
-        pl.when(me >= 2)(lambda: run(0))
-    else:
-        pl.when(z >= 1)(lambda: run(1))
-
-
-def last_kernel(count, scale, width, third_ref, early_ref, rot_ref, *refs):
+
+
+def last_kernel(count, scale, width, third_ref, early2_ref, early3_ref, rot_ref, *refs):
     old, out_ref = refs[:3], refs[3]
-    me, z, _ = place(count)
-    late = (count // PLANE) * KB
+    _, z, _ = place(count)
     half = out_ref.shape[0] // 2
     dim = rot_ref.shape[2]
 
@@ -243,30 +242,22 @@
                 done[:, h * half : (h + 1) * half].T.astype(out_ref.dtype)
             )
 
-    def add(block, parts, masks):
-        kv = jnp.concatenate(parts, axis=0)
+    def add(block):
+        masks = usable(count, block, PLANE - 1)[1:]
+        kv = third_ref[...]
+        if block == 0:
+            kv = jnp.concatenate([early2_ref[...], early3_ref[...]], axis=0)
+            masks = usable(count, block, 2)[1:] + masks
         fold(kv, masks, scale, width, block, rot_ref, old, lambda step, m, l, acc: finish(block, step, l, acc))
 
-    def close(block):
+    add(1)
+    pl.when(z >= 1)(lambda: add(0))
+
+    @pl.when(z < 1)
+    def _():
         for step in range(rot_ref.shape[1] // width):
             cols = slice(step * width, (step + 1) * width)
-            finish(block, step, old[1][block, :, cols], old[2][block, :, cols])
-
-    @pl.when(z == 0)
-    def _():
-        add(1, [third_ref[:late]], usable(count, 1, 3))
-
-    @pl.when(z > 0)
-    def _():
-        close(1)
-
-    @pl.when(me >= 2)
-    def _():
-        add(0, [third_ref[late:], early_ref[...]], usable(count, 0, 3))
-
-    @pl.when(me < 2)
-    def _():
-        close(0)
+            finish(0, step, old[1][0, :, cols], old[2][0, :, cols])
 
 
 def per_device(queries, keys, values, basis, picks):
@@ -299,13 +290,14 @@
 
     per_half = half // KB
     table = jax.ShapeDtypeStruct(((planes - 1) * PLANE * 2, dim), jnp.int32)
-    kv, table, own, side, *packets = pl.pallas_call(
+    kv, table, own, over, side, *packets = pl.pallas_call(
         functools.partial(pack_kernel, count),
-        out_shape=[rows(2 * per_half), table, rows(2 * PLANE), rows(per_half)]
+        out_shape=[rows(2 * per_half), table, rows(2), rows(4), rows(per_half)]
         + [rows(PLANE)] * (planes - 1),
         in_specs=[vmem] * 2,
-        out_specs=[vmem] * (3 + planes),
+        out_specs=[vmem] * (4 + planes),
         compiler_params=params,
+        cost_estimate=pl.CostEstimate(flops=4000000000, bytes_accessed=1_000_000, transcendentals=0),
         name="pack",
     )(picks.T, jnp.concatenate([keys, values]))
 
@@ -323,6 +315,7 @@
         name="near",
     )(queries, basis, kv)
     packets, near = lax.optimization_barrier((packets, near))
+    over = permute(over, [(s, s ^ 2) for s in range(count)])
     groups = lax.axis_size("grp")
     pairs = []
     for g in range(groups):
@@ -333,21 +326,23 @@
     def swap(value, m):
         return permute(value, [(s, s ^ m) for s in range(count)])
 
-    sizes = [2 * planes, 2 * planes + per_half, 2 * planes, planes + 1, planes - 1]
+    sizes = [2 * planes - 1, 2 * planes + 1 + per_half, planes - 1, planes - 1, planes - 1, planes - 1]
     moved = list(
         pl.pallas_call(
             functools.partial(select_kernel, count),
             out_shape=[rows(size) for size in sizes],
-            in_specs=[vmem] * (planes + 2),
+            in_specs=[vmem] * (planes + 3),
             out_specs=[vmem] * len(sizes),
             compiler_params=params,
             name="select",
-        )(table, own, kv, *packets)
+        )(table, own, over, kv, *packets)
     )
     moved[1], side = lax.optimization_barrier((moved[1], side))
     for m in (1, 2, 3):
         moved[m] = swap(moved[m], m)
-    early = permute(moved[PLANE], [(s, s ^ (PLANE - 1 if s >= PLANE else 1)) for s in range(count)])
+    for i in range(PLANE, len(moved)):
+        m = PLANE - len(moved) + i
+        moved[i] = permute(moved[i], [(s, s ^ (m if s >= PLANE else 1)) for s in range(count)])
 
     rotated, *state = near
 
@@ -363,18 +358,17 @@
             name=f"fold{stage}",
         )(*messages, rotated, *state)
 
-    state = folded(state, 0, [moved[0], moved[1], side, kv])
+    state = folded(state, 0, [moved[0], moved[1], over, side, kv])
     state = folded(state, 2, [moved[2]])
-    state = folded(state, 3, [moved[3]])
     return pl.pallas_call(
         functools.partial(last_kernel, count, scale, width),
         out_shape=jax.ShapeDtypeStruct(queries.shape, bf16),
-        in_specs=[vmem] * 6,
+        in_specs=[vmem] * 7,
         out_specs=vmem,
         compiler_params=params,
         cost_estimate=cost(half),
         name="last",
-    )(moved[3], early, rotated, *state)
+    )(*moved[3:], rotated, *state)
 
 
 def solution(mesh):

time: 22.2 us -> 21.7 us (0.977)
  the two profiles are of different devices: /device:TPU:17 before, /device:TPU:13 now
where the time goes in v7:
time: 21.7 us; the launch traced here: 21.6 us
  starting transfers between devices  12.3 us (57%)
  Pallas kernels  5.89 us (27%)
  waiting for transfers between devices  2.38 us (11%)
  other arithmetic  0.89 us (4%)
    ppermute x9, starting transfers between devices, permute(): return lax.ppermute(value, 'pb', pairs)  10.3 us
    pallas_call x2, Pallas kernels, folded(): pl.pallas_call(functools.partial(fold_kernel, count, scale, width, stage)...  2.43 us
    pallas_call x1, Pallas kernels, per_device(): pl.pallas_call(functools.partial(last_kernel, count, scale, width), out_s...  1.96 us
    ppermute x1, starting transfers between devices, per_device(): side = lax.ppermute(side, ('grp', 'pb'), pairs)  1.94 us
    ppermute x9, waiting for transfers between devices, permute(): return lax.ppermute(value, 'pb', pairs)  1.68 us
    pallas_call x1, Pallas kernels, per_device(): pl.pallas_call(functools.partial(near_kernel, scale, width), out_shape=[j...  0.98 us
    concatenate x1, other arithmetic, per_device(): jnp.concatenate([keys, values])  0.89 us
    ppermute x1, waiting for transfers between devices, per_device(): side = lax.ppermute(side, ('grp', 'pb'), pairs)  0.7 us
  transfers between devices with their start and end apart: 10, of which 3 were waited for; matrix products, arithmetic and copies ran while one was open for 0% of the time, Pallas kernels for 16%

profile of v7, /device:TPU:13, one launch (start us, length us, event | category | flops | bytes accessed | tf_op | source)
XLA Modules:
  0.0 21.6 jit_solution(785453182261826145)
XLA Ops:
  0.0 0.9 %pad_maximum_fusion.both_ref = bf16[512,128]{1,0:T(8,128)(2,1)S(1)} fusion(bf16[256,128]{1,0:T(8,128)(2,1)} %param.7, bf16[256,128]{1,0:T(8,128)(2,1)} %param.6), kind=kLoop, calls=%fused_computation | loop fusion | flops 262144 | bytes 262144 | tf_op jit(solution)/shard_map/concatenate | solution.py:302
  0.9 0.0 copy-start
  0.9 0.0 copy-start.1
  0.9 0.4 %pack.1 = (bf16[256,256]{1,0:T(8,128)(2,1)S(1)}, s32[24,128]{1,0:T(8,128)S(1)}, bf16[64,256]{1,0:T(8,128)(2,1)S(1)}, bf16[128,256]{1,0:T(8,128)(2,1)S(1)}, bf16[...) custom-call(s32[16,32]{1,0:T(8,128)S(1)} %bitcast.1, ...), custom_call_target="tpu_custom_call" | custom-call | flops 4000000000 | bytes 1000000 | tf_op jit(solution)/shard_map/pack/pallas_call | solution.py:293
  1.3 1.3 %collective-permute-start.1 = (bf16[128,256]{1,0:T(8,128)(2,1)S(1)}, bf16[128,256]{1,0:T(8,128)(2,1)S(1)}, u32[]{:S(2)}, u32[]{:S(2)}) collective-permute-start(bf16[128,256]{1,0:T(8,128)(2,1)S(1)} %get-tuple-element.42), channel_id=1, source_target_pairs={{0,4},{1,5},{2,6},{3,7},{4,8},{5,9},{6,10},{7,11},{8,12},{9,13},{1... | collective-permute-start | bytes 196616 | tf_op jit(solution)/shard_map/ppermute | solution.py:284
  2.7 1.1 %collective-permute-start.2 = (bf16[128,256]{1,0:T(8,128)(2,1)S(1)}, bf16[128,256]{1,0:T(8,128)(2,1)S(1)}, u32[]{:S(2)}, u32[]{:S(2)}) collective-permute-start(bf16[128,256]{1,0:T(8,128)(2,1)S(1)} %get-tuple-element.43), channel_id=1, source_target_pairs={{0,8},{1,9},{2,10},{3,11},{4,12},{5,13},{6,14},{7,15},{8,0},{9,1},... | collective-permute-start | bytes 196616 | tf_op jit(solution)/shard_map/ppermute | solution.py:284
  3.8 1.4 %collective-permute-start.3 = (bf16[128,256]{1,0:T(8,128)(2,1)S(1)}, bf16[128,256]{1,0:T(8,128)(2,1)S(1)}, u32[]{:S(2)}, u32[]{:S(2)}) collective-permute-start(bf16[128,256]{1,0:T(8,128)(2,1)S(1)} %get-tuple-element.44), channel_id=1, source_target_pairs={{0,12},{1,13},{2,14},{3,15},{4,0},{5,1},{6,2},{7,3},{8,4},{9,5},{1... | collective-permute-start | bytes 196616 | tf_op jit(solution)/shard_map/ppermute | solution.py:284
  5.2 1.2 %collective-permute-start = (bf16[128,256]{1,0:T(8,128)(2,1)S(1)}, bf16[128,256]{1,0:T(8,128)(2,1)S(1)}, u32[]{:S(2)}, u32[]{:S(2)}) collective-permute-start(bf16[128,256]{1,0:T(8,128)(2,1)S(1)} %get-tuple-element.40), channel_id=1, source_target_pairs={{0,2},{1,3},{2,0},{3,1},{4,6},{5,7},{6,4},{7,5},{8,10},{9,11},{10,... | collective-permute-start | bytes 196616 | tf_op jit(solution)/shard_map/ppermute | solution.py:284
  6.4 1.9 %collective-permute-start.8 = (bf16[128,256]{1,0:T(8,128)(2,1)S(1)}, bf16[128,256]{1,0:T(8,128)(2,1)S(1)}, u32[]{:S(2)}, u32[]{:S(2)}) collective-permute-start(bf16[128,256]{1,0:T(8,128)(2,1)S(1)} %get-tuple-element.59), channel_id=1, source_target_pairs={{1,2},{2,1},{3,4},{4,3},{5,6},{6,5},{7,8},{8,7},{9,10},{10,9},{11,... | collective-permute-start | bytes 196616 | tf_op jit(solution)/shard_map/ppermute | solution.py:324
  8.3 1.0 %near.1 = (bf16[2,1024,128]{2,1,0:T(8,128)(2,1)S(1)}, f32[2,1,1024]{2,1,0:T(1,128)S(1)}, f32[2,1,1024]{2,1,0:T(1,128)S(1)}, f32[2,128,1024]{2,1,0:T(8,128)S(1)}) custom-call(bf16[256,1024]{1,0:T(8,128)(2,1)S(1)} %copy-done, bf16[128,128]{1,0:T(8,128)(2,1)S(1)} %copy-done.1, bf16[256,256]{1,0:T(8,128)(2,1)S(1)} %get-tuple-element.41.kv_ref.refs_4_), custom_call_target="tpu_custom_call" | custom-call | flops 134217728 | bytes 4000000 | tf_op jit(solution)/shard_map/near/pallas_call | solution.py:308
  9.3 0.0 collective-permute-done.1.refs_0_
  9.3 0.8 %collective-permute-done.3.refs_2_ = bf16[128,256]{1,0:T(8,128)(2,1)S(1)} collective-permute-done((bf16[128,256]{1,0:T(8,128)(2,1)S(1)}, bf16[128,256]{1,0:T(8,128)(2,1)S(1)}, u32[]{:S(2)}, u32[]{:S(2)}) %collective-permute-start.3) | collective-permute-done | bytes 65568 | tf_op jit(solution)/shard_map/ppermute | solution.py:284
  10.1 0.0 collective-permute-done.over_ref.refs_2_
  10.2 0.1 select.1
  10.3 0.7 %collective-permute-done.8.refs_3_ = bf16[128,256]{1,0:T(8,128)(2,1)S(1)} collective-permute-done((bf16[128,256]{1,0:T(8,128)(2,1)S(1)}, bf16[128,256]{1,0:T(8,128)(2,1)S(1)}, u32[]{:S(2)}, u32[]{:S(2)}) %collective-permute-start.8) | collective-permute-done | bytes 65568 | tf_op jit(solution)/shard_map/ppermute | solution.py:324
  11.0 1.8 %collective-permute-start.9 = (bf16[416,256]{1,0:T(8,128)(2,1)S(1)}, bf16[416,256]{1,0:T(8,128)(2,1)S(1)}, u32[]{:S(2)}, u32[]{:S(2)}) collective-permute-start(bf16[416,256]{1,0:T(8,128)(2,1)S(1)} %get-tuple-element.60), channel_id=1, source_target_pairs={{0,1},{1,0},{2,3},{3,2},{4,5},{5,4},{6,7},{7,6},{8,9},{9,8},{10,11... | collective-permute-start | bytes 638984 | tf_op jit(solution)/shard_map/ppermute | solution.py:284
  12.8 1.0 %collective-permute-start.7 = (bf16[96,256]{1,0:T(8,128)(2,1)S(1)}, bf16[96,256]{1,0:T(8,128)(2,1)S(1)}, u32[]{:S(2)}, u32[]{:S(2)}) collective-permute-start(bf16[96,256]{1,0:T(8,128)(2,1)S(1)} %get-tuple-element.56), channel_id=1, source_target_pairs={{0,2},{1,3},{2,0},{3,1},{4,6},{5,7},{6,4},{7,5},{8,10},{9,11},{10,... | collective-permute-start | bytes 147464 | tf_op jit(solution)/shard_map/ppermute | solution.py:284
  13.7 0.7 %collective-permute-start.4 = (bf16[96,256]{1,0:T(8,128)(2,1)S(1)}, bf16[96,256]{1,0:T(8,128)(2,1)S(1)}, u32[]{:S(2)}, u32[]{:S(2)}) collective-permute-start(bf16[96,256]{1,0:T(8,128)(2,1)S(1)} %get-tuple-element.52), channel_id=1, source_target_pairs={{0,3},{1,2},{2,1},{3,0},{4,7},{5,6},{6,5},{7,4},{8,11},{9,10},{10,... | collective-permute-start | bytes 147464 | tf_op jit(solution)/shard_map/ppermute | solution.py:284
  14.4 1.0 %collective-permute-start.5 = (bf16[96,256]{1,0:T(8,128)(2,1)S(1)}, bf16[96,256]{1,0:T(8,128)(2,1)S(1)}, u32[]{:S(2)}, u32[]{:S(2)}) collective-permute-start(bf16[96,256]{1,0:T(8,128)(2,1)S(1)} %get-tuple-element.53), channel_id=1, source_target_pairs={{0,1},{1,0},{2,3},{3,2},{4,6},{5,7},{6,4},{7,5},{8,10},{9,11},{10,... | collective-permute-start | bytes 147464 | tf_op jit(solution)/shard_map/ppermute | solution.py:284
  15.4 0.8 %collective-permute-start.6 = (bf16[96,256]{1,0:T(8,128)(2,1)S(1)}, bf16[96,256]{1,0:T(8,128)(2,1)S(1)}, u32[]{:S(2)}, u32[]{:S(2)}) collective-permute-start(bf16[96,256]{1,0:T(8,128)(2,1)S(1)} %get-tuple-element.54), channel_id=1, source_target_pairs={{0,1},{1,0},{2,3},{3,2},{4,7},{5,6},{6,5},{7,4},{8,11},{9,10},{10,... | collective-permute-start | bytes 147464 | tf_op jit(solution)/shard_map/ppermute | solution.py:284
  16.3 1.9 %fold0.1 = (f32[2,1,1024]{2,1,0:T(1,128)S(1)}, f32[2,1,1024]{2,1,0:T(1,128)S(1)}, f32[2,128,1024]{2,1,0:T(8,128)S(1)}) custom-call(bf16[224,256]{1,0:T(8,128)(2,1)S(1)} %get-tuple-element.57.refs_0_, bf16[416,256]{1,0:T(8,128)(2,1)S(1)} %collective-permute-done.9.refs_1_, ...), custom_call_target="tpu_custom_call", output_to_operand_aliasing={{0}: (6, {}), {1}: (7, {}), {2}: (8, {})} | custom-call | flops 134217728 | bytes 4000000 | tf_op jit(solution)/shard_map/fold0/pallas_call | solution.py:350
  18.1 0.6 %fold2.1 = (f32[2,1,1024]{2,1,0:T(1,128)S(1)}, f32[2,1,1024]{2,1,0:T(1,128)S(1)}, f32[2,128,1024]{2,1,0:T(8,128)S(1)}) custom-call(bf16[96,256]{1,0:T(8,128)(2,1)S(1)} %collective-permute-done.7.refs_0_, bf16[2,1024,128]{2,1,0:T(8,128)(2,1)S(1)} %get-tuple-element.55.refs_5_.refs_1_.rot_ref, ...), custom_call_target="tpu_custom_call", output_to_operand_aliasing={{0}: (2, {}), {1}: (3, {}), {2}: (4, {})} | custom-call | flops 134217728 | bytes 4000000 | tf_op jit(solution)/shard_map/fold2/pallas_call | solution.py:350
  18.7 0.8 %collective-permute-done.6.early3_ref = bf16[96,256]{1,0:T(8,128)(2,1)S(1)} collective-permute-done((bf16[96,256]{1,0:T(8,128)(2,1)S(1)}, bf16[96,256]{1,0:T(8,128)(2,1)S(1)}, u32[]{:S(2)}, u32[]{:S(2)}) %collective-permute-start.6) | collective-permute-done | bytes 49184 | tf_op jit(solution)/shard_map/ppermute | solution.py:284
  19.6 2.0 %last.1 = bf16[256,1024]{1,0:T(8,128)(2,1)} custom-call(bf16[96,256]{1,0:T(8,128)(2,1)S(1)} %collective-permute-done.4.third_ref, bf16[96,256]{1,0:T(8,128)(2,1)S(1)} %collective-permute-done.5.early2_ref, bf16[96,256]{1,0:T(8,128)(2,1)S(1)} %collective-permute-done.6.early3_ref, bf16[2,1024,128]{2,1,0:T(8,128)(2,1)S(1)} %get-tuple-element.55.refs_5_.refs_1_.rot_ref, ...), custom_call_target="tpu_custom_call" | custom-call | flops 134217728 | bytes 4000000 | tf_op jit(solution)/shard_map/last/pallas_call | solution.py:363
  (9 shorter events, 0.0 us)
Async XLA Ops:
  0.0 0.9 %copy-start.2 = (s32[32,16]{0,1:T(8,128)S(1)}, s32[32,16]{0,1:T(8,128)}, u32[]{:S(2)}) copy-start(s32[32,16]{0,1:T(8,128)} %param.9) | copy-start | bytes 6148
  0.9 7.4 %copy-start = (bf16[256,1024]{1,0:T(8,128)(2,1)S(1)}, bf16[256,1024]{1,0:T(8,128)(2,1)}, u32[]{:S(2)}) copy-start(bf16[256,1024]{1,0:T(8,128)(2,1)} %q_ref.1) | copy-start | bytes 1572868
  0.9 7.4 %copy-start.1 = (bf16[128,128]{1,0:T(8,128)(2,1)S(1)}, bf16[128,128]{1,0:T(8,128)(2,1)}, u32[]{:S(2)}) copy-start(bf16[128,128]{1,0:T(8,128)(2,1)} %basis_ref.1) | copy-start | bytes 98308
  1.3 8.0 %collective-permute-start.1 = (bf16[128,256]{1,0:T(8,128)(2,1)S(1)}, bf16[128,256]{1,0:T(8,128)(2,1)S(1)}, u32[]{:S(2)}, u32[]{:S(2)}) collective-permute-start(bf16[128,256]{1,0:T(8,128)(2,1)S(1)} %get-tuple-element.42), channel_id=1, source_target_pairs={{0,4},{1,5},{2,6},{3,7},{4,8},{5,9},{6,10},{7,11},{8,12},{9,13},{1... | collective-permute-start | bytes 196616 | tf_op jit(solution)/shard_map/ppermute | solution.py:284
  2.7 6.6 %collective-permute-start.2 = (bf16[128,256]{1,0:T(8,128)(2,1)S(1)}, bf16[128,256]{1,0:T(8,128)(2,1)S(1)}, u32[]{:S(2)}, u32[]{:S(2)}) collective-permute-start(bf16[128,256]{1,0:T(8,128)(2,1)S(1)} %get-tuple-element.43), channel_id=1, source_target_pairs={{0,8},{1,9},{2,10},{3,11},{4,12},{5,13},{6,14},{7,15},{8,0},{9,1},... | collective-permute-start | bytes 196616 | tf_op jit(solution)/shard_map/ppermute | solution.py:284
  3.8 6.4 %collective-permute-start.3 = (bf16[128,256]{1,0:T(8,128)(2,1)S(1)}, bf16[128,256]{1,0:T(8,128)(2,1)S(1)}, u32[]{:S(2)}, u32[]{:S(2)}) collective-permute-start(bf16[128,256]{1,0:T(8,128)(2,1)S(1)} %get-tuple-element.44), channel_id=1, source_target_pairs={{0,12},{1,13},{2,14},{3,15},{4,0},{5,1},{6,2},{7,3},{8,4},{9,5},{1... | collective-permute-start | bytes 196616 | tf_op jit(solution)/shard_map/ppermute | solution.py:284
  5.2 5.0 %collective-permute-start = (bf16[128,256]{1,0:T(8,128)(2,1)S(1)}, bf16[128,256]{1,0:T(8,128)(2,1)S(1)}, u32[]{:S(2)}, u32[]{:S(2)}) collective-permute-start(bf16[128,256]{1,0:T(8,128)(2,1)S(1)} %get-tuple-element.40), channel_id=1, source_target_pairs={{0,2},{1,3},{2,0},{3,1},{4,6},{5,7},{6,4},{7,5},{8,10},{9,11},{10,... | collective-permute-start | bytes 196616 | tf_op jit(solution)/shard_map/ppermute | solution.py:284
  6.4 4.6 %collective-permute-start.8 = (bf16[128,256]{1,0:T(8,128)(2,1)S(1)}, bf16[128,256]{1,0:T(8,128)(2,1)S(1)}, u32[]{:S(2)}, u32[]{:S(2)}) collective-permute-start(bf16[128,256]{1,0:T(8,128)(2,1)S(1)} %get-tuple-element.59), channel_id=1, source_target_pairs={{1,2},{2,1},{3,4},{4,3},{5,6},{6,5},{7,8},{8,7},{9,10},{10,9},{11,... | collective-permute-start | bytes 196616 | tf_op jit(solution)/shard_map/ppermute | solution.py:324
  11.0 5.3 %collective-permute-start.9 = (bf16[416,256]{1,0:T(8,128)(2,1)S(1)}, bf16[416,256]{1,0:T(8,128)(2,1)S(1)}, u32[]{:S(2)}, u32[]{:S(2)}) collective-permute-start(bf16[416,256]{1,0:T(8,128)(2,1)S(1)} %get-tuple-element.60), channel_id=1, source_target_pairs={{0,1},{1,0},{2,3},{3,2},{4,5},{5,4},{6,7},{7,6},{8,9},{9,8},{10,11... | collective-permute-start | bytes 638984 | tf_op jit(solution)/shard_map/ppermute | solution.py:284
  12.8 5.4 %collective-permute-start.7 = (bf16[96,256]{1,0:T(8,128)(2,1)S(1)}, bf16[96,256]{1,0:T(8,128)(2,1)S(1)}, u32[]{:S(2)}, u32[]{:S(2)}) collective-permute-start(bf16[96,256]{1,0:T(8,128)(2,1)S(1)} %get-tuple-element.56), channel_id=1, source_target_pairs={{0,2},{1,3},{2,0},{3,1},{4,6},{5,7},{6,4},{7,5},{8,10},{9,11},{10,... | collective-permute-start | bytes 147464 | tf_op jit(solution)/shard_map/ppermute | solution.py:284
  13.7 5.0 %collective-permute-start.4 = (bf16[96,256]{1,0:T(8,128)(2,1)S(1)}, bf16[96,256]{1,0:T(8,128)(2,1)S(1)}, u32[]{:S(2)}, u32[]{:S(2)}) collective-permute-start(bf16[96,256]{1,0:T(8,128)(2,1)S(1)} %get-tuple-element.52), channel_id=1, source_target_pairs={{0,3},{1,2},{2,1},{3,0},{4,7},{5,6},{6,5},{7,4},{8,11},{9,10},{10,... | collective-permute-start | bytes 147464 | tf_op jit(solution)/shard_map/ppermute | solution.py:284
  14.4 4.3 %collective-permute-start.5 = (bf16[96,256]{1,0:T(8,128)(2,1)S(1)}, bf16[96,256]{1,0:T(8,128)(2,1)S(1)}, u32[]{:S(2)}, u32[]{:S(2)}) collective-permute-start(bf16[96,256]{1,0:T(8,128)(2,1)S(1)} %get-tuple-element.53), channel_id=1, source_target_pairs={{0,1},{1,0},{2,3},{3,2},{4,6},{5,7},{6,4},{7,5},{8,10},{9,11},{10,... | collective-permute-start | bytes 147464 | tf_op jit(solution)/shard_map/ppermute | solution.py:284
  15.4 4.1 %collective-permute-start.6 = (bf16[96,256]{1,0:T(8,128)(2,1)S(1)}, bf16[96,256]{1,0:T(8,128)(2,1)S(1)}, u32[]{:S(2)}, u32[]{:S(2)}) collective-permute-start(bf16[96,256]{1,0:T(8,128)(2,1)S(1)} %get-tuple-element.54), channel_id=1, source_target_pairs={{0,1},{1,0},{2,3},{3,2},{4,7},{5,6},{6,5},{7,4},{8,11},{9,10},{10,... | collective-permute-start | bytes 147464 | tf_op jit(solution)/shard_map/ppermute | solution.py:284

commit v8 on v7

--- a/solution.py
+++ b/solution.py
@@ -198,7 +198,7 @@
 
 def fold_kernel(count, scale, width, stage, *refs):
     come, rot_ref, old, new = refs[:-7], refs[-7], refs[-6:-3], refs[-3:]
-    me = lax.axis_index("pb")
+    me, z, _ = place(count)
     rest = (count // PLANE - 1) * KB
 
     def run(block):
@@ -223,41 +223,58 @@
 
         fold(jnp.concatenate(parts, axis=0), masks, scale, width, block, rot_ref, old, save)
 
-    run(1)
+    if stage < 3:
+        run(1)
     if stage == 0:
         pl.when(me >= 1)(lambda: run(0))
-
-
-def last_kernel(count, scale, width, third_ref, early2_ref, early3_ref, rot_ref, *refs):
-    old, out_ref = refs[:3], refs[3]
+    if stage == 3:
+        pl.when(z >= 1)(lambda: run(1))
+
+
+def last_kernel(count, scale, width, third_ref, second_early_ref, third_early_ref, rot_ref, *refs):
+    old, out_ref, done_ref, sems = refs[:3], refs[3], refs[4], refs[5]
     _, z, _ = place(count)
     half = out_ref.shape[0] // 2
     dim = rot_ref.shape[2]
+
+    def piece(block, step):
+        rows, cols = pl.ds(block * half, half), pl.ds(step * (width // half) * dim, width // half * dim)
+        return pltpu.make_async_copy(done_ref.at[rows, cols], out_ref.at[rows, cols], sems.at[block, step])
 
     def finish(block, step, l, acc):
         done = acc / l
         for h in range(width // half):
             head = step * (width // half) + h
-            out_ref[block * half : (block + 1) * half, head * dim : (head + 1) * dim] = (
-                done[:, h * half : (h + 1) * half].T.astype(out_ref.dtype)
+            done_ref[block * half : (block + 1) * half, head * dim : (head + 1) * dim] = (
+                done[:, h * half : (h + 1) * half].T.astype(done_ref.dtype)
             )
+        piece(block, step).start()
 
     def add(block):
-        masks = usable(count, block, PLANE - 1)[1:]
-        kv = third_ref[...]
+        kv, masks = third_ref[...], usable(count, block, PLANE - 1)[1:]
         if block == 0:
-            kv = jnp.concatenate([early2_ref[...], early3_ref[...]], axis=0)
+            kv = jnp.concatenate([second_early_ref[...], third_early_ref[...]], axis=0)
             masks = usable(count, block, 2)[1:] + masks
         fold(kv, masks, scale, width, block, rot_ref, old, lambda step, m, l, acc: finish(block, step, l, acc))
 
-    add(1)
-    pl.when(z >= 1)(lambda: add(0))
+    def close(block):
+        for step in range(rot_ref.shape[1] // width):
+            cols = slice(step * width, (step + 1) * width)
+            finish(block, step, old[1][block, :, cols], old[2][block, :, cols])
+
+    @pl.when(z >= 1)
+    def _():
+        close(1)
+        add(0)
 
     @pl.when(z < 1)
     def _():
+        close(0)
+        add(1)
+
+    for block in range(2):
         for step in range(rot_ref.shape[1] // width):
-            cols = slice(step * width, (step + 1) * width)
-            finish(0, step, old[1][0, :, cols], old[2][0, :, cols])
+            piece(block, step).wait()
 
 
 def per_device(queries, keys, values, basis, picks):
@@ -266,7 +283,7 @@
     count = lax.axis_size("pb")
     planes = count // PLANE
     wide = queries.shape[1] // dim * half
-    width = 2 * half
+    width = 4 * half
     scale = dim**-0.5 * math.log2(math.e)
     vmem = pl.BlockSpec(memory_space=pltpu.VMEM)
     params = pltpu.CompilerParams(vmem_limit_bytes=VMEM_BYTES)
@@ -360,11 +377,13 @@
 
     state = folded(state, 0, [moved[0], moved[1], over, side, kv])
     state = folded(state, 2, [moved[2]])
+    state = folded(state, 3, [moved[3]])
     return pl.pallas_call(
         functools.partial(last_kernel, count, scale, width),
         out_shape=jax.ShapeDtypeStruct(queries.shape, bf16),
         in_specs=[vmem] * 7,
-        out_specs=vmem,
+        out_specs=pl.BlockSpec(memory_space=pl.ANY),
+        scratch_shapes=[pltpu.VMEM(queries.shape, bf16), pltpu.SemaphoreType.DMA((2, wide // width))],
         compiler_params=params,
         cost_estimate=cost(half),
         name="last",

time: 21.7 us -> 21.1 us (0.972)
  the two profiles are of different devices: /device:TPU:13 before, /device:TPU:0 now
where the time goes in v8:
time: 21.1 us; the launch traced here: 20.7 us
  starting transfers between devices  12.4 us (59%)
  Pallas kernels  4.28 us (20%)
  waiting for transfers between devices  3.04 us (14%)
  other arithmetic  0.89 us (4%)
    ppermute x9, starting transfers between devices, permute(): return lax.ppermute(value, 'pb', pairs)  10.9 us
    ppermute x9, waiting for transfers between devices, permute(): return lax.ppermute(value, 'pb', pairs)  2.07 us
    pallas_call x3, Pallas kernels, folded(): pl.pallas_call(functools.partial(fold_kernel, count, scale, width, stage)...  1.53 us
    ppermute x1, starting transfers between devices, per_device(): side = lax.ppermute(side, ('grp', 'pb'), pairs)  1.52 us
    pallas_call x1, Pallas kernels, per_device(): pl.pallas_call(functools.partial(last_kernel, count, scale, width), out_s...  1.26 us
    pallas_call x1, Pallas kernels, per_device(): pl.pallas_call(functools.partial(near_kernel, scale, width), out_shape=[j...  0.98 us
    ppermute x1, waiting for transfers between devices, per_device(): side = lax.ppermute(side, ('grp', 'pb'), pairs)  0.98 us
    concatenate x1, other arithmetic, per_device(): jnp.concatenate([keys, values])  0.89 us
  transfers between devices with their start and end apart: 10, of which 4 were waited for; matrix products, arithmetic and copies ran while one was open for 0% of the time, Pallas kernels for 13%

profile of v8, /device:TPU:0, one launch (start us, length us, event | category | flops | bytes accessed | tf_op | source)
XLA Modules:
  0.0 20.7 jit_solution(10568616527817222811)
XLA Ops:
  0.0 0.9 %pad_maximum_fusion.both_ref = bf16[512,128]{1,0:T(8,128)(2,1)S(1)} fusion(bf16[256,128]{1,0:T(8,128)(2,1)} %param.7, bf16[256,128]{1,0:T(8,128)(2,1)} %param.6), kind=kLoop, calls=%fused_computation | loop fusion | flops 262144 | bytes 262144 | tf_op jit(solution)/shard_map/concatenate | solution.py:319
  0.9 0.0 copy-start
  0.9 0.0 copy-start.1
  0.9 0.4 %pack.1 = (bf16[256,256]{1,0:T(8,128)(2,1)S(1)}, s32[24,128]{1,0:T(8,128)S(1)}, bf16[64,256]{1,0:T(8,128)(2,1)S(1)}, bf16[128,256]{1,0:T(8,128)(2,1)S(1)}, bf16[...) custom-call(s32[16,32]{1,0:T(8,128)S(1)} %bitcast.1, ...), custom_call_target="tpu_custom_call" | custom-call | flops 4000000000 | bytes 1000000 | tf_op jit(solution)/shard_map/pack/pallas_call | solution.py:310
  1.3 3.1 %collective-permute-start.1 = (bf16[128,256]{1,0:T(8,128)(2,1)S(1)}, bf16[128,256]{1,0:T(8,128)(2,1)S(1)}, u32[]{:S(2)}, u32[]{:S(2)}) collective-permute-start(bf16[128,256]{1,0:T(8,128)(2,1)S(1)} %get-tuple-element.45), channel_id=1, source_target_pairs={{0,4},{1,5},{2,6},{3,7},{4,8},{5,9},{6,10},{7,11},{8,12},{9,13},{1... | collective-permute-start | bytes 196616 | tf_op jit(solution)/shard_map/ppermute | solution.py:301
  4.4 2.6 %collective-permute-start.2 = (bf16[128,256]{1,0:T(8,128)(2,1)S(1)}, bf16[128,256]{1,0:T(8,128)(2,1)S(1)}, u32[]{:S(2)}, u32[]{:S(2)}) collective-permute-start(bf16[128,256]{1,0:T(8,128)(2,1)S(1)} %get-tuple-element.46), channel_id=1, source_target_pairs={{0,8},{1,9},{2,10},{3,11},{4,12},{5,13},{6,14},{7,15},{8,0},{9,1},... | collective-permute-start | bytes 196616 | tf_op jit(solution)/shard_map/ppermute | solution.py:301
  7.0 1.3 %collective-permute-start.3 = (bf16[128,256]{1,0:T(8,128)(2,1)S(1)}, bf16[128,256]{1,0:T(8,128)(2,1)S(1)}, u32[]{:S(2)}, u32[]{:S(2)}) collective-permute-start(bf16[128,256]{1,0:T(8,128)(2,1)S(1)} %get-tuple-element.47), channel_id=1, source_target_pairs={{0,12},{1,13},{2,14},{3,15},{4,0},{5,1},{6,2},{7,3},{8,4},{9,5},{1... | collective-permute-start | bytes 196616 | tf_op jit(solution)/shard_map/ppermute | solution.py:301
  8.4 1.5 %collective-permute-start = (bf16[128,256]{1,0:T(8,128)(2,1)S(1)}, bf16[128,256]{1,0:T(8,128)(2,1)S(1)}, u32[]{:S(2)}, u32[]{:S(2)}) collective-permute-start(bf16[128,256]{1,0:T(8,128)(2,1)S(1)} %get-tuple-element.43), channel_id=1, source_target_pairs={{0,2},{1,3},{2,0},{3,1},{4,6},{5,7},{6,4},{7,5},{8,10},{9,11},{10,... | collective-permute-start | bytes 196616 | tf_op jit(solution)/shard_map/ppermute | solution.py:301
  9.9 1.5 %collective-permute-start.8 = (bf16[128,256]{1,0:T(8,128)(2,1)S(1)}, bf16[128,256]{1,0:T(8,128)(2,1)S(1)}, u32[]{:S(2)}, u32[]{:S(2)}) collective-permute-start(bf16[128,256]{1,0:T(8,128)(2,1)S(1)} %get-tuple-element.62), channel_id=1, source_target_pairs={{1,2},{2,1},{3,4},{4,3},{5,6},{6,5},{7,8},{8,7},{9,10},{10,9},{11,... | collective-permute-start | bytes 196616 | tf_op jit(solution)/shard_map/ppermute | solution.py:341
  11.4 1.0 %near.1 = (bf16[2,1024,128]{2,1,0:T(8,128)(2,1)S(1)}, f32[2,1,1024]{2,1,0:T(1,128)S(1)}, f32[2,1,1024]{2,1,0:T(1,128)S(1)}, f32[2,128,1024]{2,1,0:T(8,128)S(1)}) custom-call(bf16[256,1024]{1,0:T(8,128)(2,1)S(1)} %copy-done, bf16[128,128]{1,0:T(8,128)(2,1)S(1)} %copy-done.1, bf16[256,256]{1,0:T(8,128)(2,1)S(1)} %get-tuple-element.44.kv_ref.refs_4_), custom_call_target="tpu_custom_call" | custom-call | flops 134217728 | bytes 4000000 | tf_op jit(solution)/shard_map/near/pallas_call | solution.py:325
  12.4 0.0 collective-permute-done.1.refs_0_
  12.4 0.6 %collective-permute-done.over_ref.refs_2_ = bf16[128,256]{1,0:T(8,128)(2,1)S(1)} collective-permute-done((bf16[128,256]{1,0:T(8,128)(2,1)S(1)}, bf16[128,256]{1,0:T(8,128)(2,1)S(1)}, u32[]{:S(2)}, u32[]{:S(2)}) %collective-permute-start) | collective-permute-done | bytes 65568 | tf_op jit(solution)/shard_map/ppermute | solution.py:301
  13.0 0.1 select.1
  13.1 1.0 %collective-permute-done.8.refs_3_ = bf16[128,256]{1,0:T(8,128)(2,1)S(1)} collective-permute-done((bf16[128,256]{1,0:T(8,128)(2,1)S(1)}, bf16[128,256]{1,0:T(8,128)(2,1)S(1)}, u32[]{:S(2)}, u32[]{:S(2)}) %collective-permute-start.8) | collective-permute-done | bytes 65568 | tf_op jit(solution)/shard_map/ppermute | solution.py:341
  14.1 1.6 %collective-permute-start.7 = (bf16[96,256]{1,0:T(8,128)(2,1)S(1)}, bf16[96,256]{1,0:T(8,128)(2,1)S(1)}, u32[]{:S(2)}, u32[]{:S(2)}) collective-permute-start(bf16[96,256]{1,0:T(8,128)(2,1)S(1)} %get-tuple-element.59), channel_id=1, source_target_pairs={{0,2},{1,3},{2,0},{3,1},{4,6},{5,7},{6,4},{7,5},{8,10},{9,11},{10,... | collective-permute-start | bytes 147464 | tf_op jit(solution)/shard_map/ppermute | solution.py:301
  15.8 0.2 %collective-permute-start.4 = (bf16[96,256]{1,0:T(8,128)(2,1)S(1)}, bf16[96,256]{1,0:T(8,128)(2,1)S(1)}, u32[]{:S(2)}, u32[]{:S(2)}) collective-permute-start(bf16[96,256]{1,0:T(8,128)(2,1)S(1)} %get-tuple-element.55), channel_id=1, source_target_pairs={{0,3},{1,2},{2,1},{3,0},{4,7},{5,6},{6,5},{7,4},{8,11},{9,10},{10,... | collective-permute-start | bytes 147464 | tf_op jit(solution)/shard_map/ppermute | solution.py:301
  16.0 0.3 %collective-permute-start.5 = (bf16[96,256]{1,0:T(8,128)(2,1)S(1)}, bf16[96,256]{1,0:T(8,128)(2,1)S(1)}, u32[]{:S(2)}, u32[]{:S(2)}) collective-permute-start(bf16[96,256]{1,0:T(8,128)(2,1)S(1)} %get-tuple-element.56), channel_id=1, source_target_pairs={{0,1},{1,0},{2,3},{3,2},{4,6},{5,7},{6,4},{7,5},{8,10},{9,11},{10,... | collective-permute-start | bytes 147464 | tf_op jit(solution)/shard_map/ppermute | solution.py:301
  16.3 0.2 %collective-permute-start.6 = (bf16[96,256]{1,0:T(8,128)(2,1)S(1)}, bf16[96,256]{1,0:T(8,128)(2,1)S(1)}, u32[]{:S(2)}, u32[]{:S(2)}) collective-permute-start(bf16[96,256]{1,0:T(8,128)(2,1)S(1)} %get-tuple-element.57), channel_id=1, source_target_pairs={{0,1},{1,0},{2,3},{3,2},{4,7},{5,6},{6,5},{7,4},{8,11},{9,10},{10,... | collective-permute-start | bytes 147464 | tf_op jit(solution)/shard_map/ppermute | solution.py:301
  16.5 1.0 %fold0.1 = (f32[2,1,1024]{2,1,0:T(1,128)S(1)}, f32[2,1,1024]{2,1,0:T(1,128)S(1)}, f32[2,128,1024]{2,1,0:T(8,128)S(1)}) custom-call(bf16[224,256]{1,0:T(8,128)(2,1)S(1)} %get-tuple-element.60.refs_0_, bf16[416,256]{1,0:T(8,128)(2,1)S(1)} %collective-permute-done.9.refs_1_, ...), custom_call_target="tpu_custom_call", output_to_operand_aliasing={{0}: (6, {}), {1}: (7, {}), {2}: (8, {})} | custom-call | flops 134217728 | bytes 4000000 | tf_op jit(solution)/shard_map/fold0/pallas_call | solution.py:367
  17.5 0.8 %collective-permute-done.7.refs_0_ = bf16[96,256]{1,0:T(8,128)(2,1)S(1)} collective-permute-done((bf16[96,256]{1,0:T(8,128)(2,1)S(1)}, bf16[96,256]{1,0:T(8,128)(2,1)S(1)}, u32[]{:S(2)}, u32[]{:S(2)}) %collective-permute-start.7) | collective-permute-done | bytes 49184 | tf_op jit(solution)/shard_map/ppermute | solution.py:301
  18.3 0.6 %fold2.1 = (f32[2,1,1024]{2,1,0:T(1,128)S(1)}, f32[2,1,1024]{2,1,0:T(1,128)S(1)}, f32[2,128,1024]{2,1,0:T(8,128)S(1)}) custom-call(bf16[96,256]{1,0:T(8,128)(2,1)S(1)} %collective-permute-done.7.refs_0_, bf16[2,1024,128]{2,1,0:T(8,128)(2,1)S(1)} %get-tuple-element.58.refs_5_.refs_1_.rot_ref, ...), custom_call_target="tpu_custom_call", output_to_operand_aliasing={{0}: (2, {}), {1}: (3, {}), {2}: (4, {})} | custom-call | flops 134217728 | bytes 4000000 | tf_op jit(solution)/shard_map/fold2/pallas_call | solution.py:367
  18.8 0.6 %collective-permute-done.4.refs_0_.third_ref = bf16[96,256]{1,0:T(8,128)(2,1)S(1)} collective-permute-done((bf16[96,256]{1,0:T(8,128)(2,1)S(1)}, bf16[96,256]{1,0:T(8,128)(2,1)S(1)}, u32[]{:S(2)}, u32[]{:S(2)}) %collective-permute-start.4) | collective-permute-done | bytes 49184 | tf_op jit(solution)/shard_map/ppermute | solution.py:301
  19.5 0.0 collective-permute-done.5.second_early_ref
  19.5 1.3 %last.1 = bf16[256,1024]{1,0:T(8,128)(2,1)} custom-call(bf16[96,256]{1,0:T(8,128)(2,1)S(1)} %collective-permute-done.4.refs_0_.third_ref, bf16[96,256]{1,0:T(8,128)(2,1)S(1)} %collective-permute-done.5.second_early_ref, bf16[96,256]{1,0:T(8,128)(2,1)S(1)} %collective-permute-done.6.third_early_ref, ...), custom_call_target="tpu_custom_call" | custom-call | flops 134217728 | bytes 4000000 | tf_op jit(solution)/shard_map/last/pallas_call | solution.py:381
  (10 shorter events, 0.0 us)
Async XLA Ops:
  0.0 0.9 %copy-start.2 = (s32[32,16]{0,1:T(8,128)S(1)}, s32[32,16]{0,1:T(8,128)}, u32[]{:S(2)}) copy-start(s32[32,16]{0,1:T(8,128)} %param.9) | copy-start | bytes 6148
  0.9 10.5 %copy-start = (bf16[256,1024]{1,0:T(8,128)(2,1)S(1)}, bf16[256,1024]{1,0:T(8,128)(2,1)}, u32[]{:S(2)}) copy-start(bf16[256,1024]{1,0:T(8,128)(2,1)} %q_ref.1) | copy-start | bytes 1572868
  0.9 10.5 %copy-start.1 = (bf16[128,128]{1,0:T(8,128)(2,1)S(1)}, bf16[128,128]{1,0:T(8,128)(2,1)}, u32[]{:S(2)}) copy-start(bf16[128,128]{1,0:T(8,128)(2,1)} %basis_ref.1) | copy-start | bytes 98308
  1.3 11.0 %collective-permute-start.1 = (bf16[128,256]{1,0:T(8,128)(2,1)S(1)}, bf16[128,256]{1,0:T(8,128)(2,1)S(1)}, u32[]{:S(2)}, u32[]{:S(2)}) collective-permute-start(bf16[128,256]{1,0:T(8,128)(2,1)S(1)} %get-tuple-element.45), channel_id=1, source_target_pairs={{0,4},{1,5},{2,6},{3,7},{4,8},{5,9},{6,10},{7,11},{8,12},{9,13},{1... | collective-permute-start | bytes 196616 | tf_op jit(solution)/shard_map/ppermute | solution.py:301
  4.4 8.0 %collective-permute-start.2 = (bf16[128,256]{1,0:T(8,128)(2,1)S(1)}, bf16[128,256]{1,0:T(8,128)(2,1)S(1)}, u32[]{:S(2)}, u32[]{:S(2)}) collective-permute-start(bf16[128,256]{1,0:T(8,128)(2,1)S(1)} %get-tuple-element.46), channel_id=1, source_target_pairs={{0,8},{1,9},{2,10},{3,11},{4,12},{5,13},{6,14},{7,15},{8,0},{9,1},... | collective-permute-start | bytes 196616 | tf_op jit(solution)/shard_map/ppermute | solution.py:301
  7.0 5.4 %collective-permute-start.3 = (bf16[128,256]{1,0:T(8,128)(2,1)S(1)}, bf16[128,256]{1,0:T(8,128)(2,1)S(1)}, u32[]{:S(2)}, u32[]{:S(2)}) collective-permute-start(bf16[128,256]{1,0:T(8,128)(2,1)S(1)} %get-tuple-element.47), channel_id=1, source_target_pairs={{0,12},{1,13},{2,14},{3,15},{4,0},{5,1},{6,2},{7,3},{8,4},{9,5},{1... | collective-permute-start | bytes 196616 | tf_op jit(solution)/shard_map/ppermute | solution.py:301
  8.4 4.7 %collective-permute-start = (bf16[128,256]{1,0:T(8,128)(2,1)S(1)}, bf16[128,256]{1,0:T(8,128)(2,1)S(1)}, u32[]{:S(2)}, u32[]{:S(2)}) collective-permute-start(bf16[128,256]{1,0:T(8,128)(2,1)S(1)} %get-tuple-element.43), channel_id=1, source_target_pairs={{0,2},{1,3},{2,0},{3,1},{4,6},{5,7},{6,4},{7,5},{8,10},{9,11},{10,... | collective-permute-start | bytes 196616 | tf_op jit(solution)/shard_map/ppermute | solution.py:301
  9.9 4.3 %collective-permute-start.8 = (bf16[128,256]{1,0:T(8,128)(2,1)S(1)}, bf16[128,256]{1,0:T(8,128)(2,1)S(1)}, u32[]{:S(2)}, u32[]{:S(2)}) collective-permute-start(bf16[128,256]{1,0:T(8,128)(2,1)S(1)} %get-tuple-element.62), channel_id=1, source_target_pairs={{1,2},{2,1},{3,4},{4,3},{5,6},{6,5},{7,8},{8,7},{9,10},{10,9},{11,... | collective-permute-start | bytes 196616 | tf_op jit(solution)/shard_map/ppermute | solution.py:341
  14.1 2.4 %collective-permute-start.9 = (bf16[416,256]{1,0:T(8,128)(2,1)S(1)}, bf16[416,256]{1,0:T(8,128)(2,1)S(1)}, u32[]{:S(2)}, u32[]{:S(2)}) collective-permute-start(bf16[416,256]{1,0:T(8,128)(2,1)S(1)} %get-tuple-element.63), channel_id=1, source_target_pairs={{0,1},{1,0},{2,3},{3,2},{4,5},{5,4},{6,7},{7,6},{8,9},{9,8},{10,11... | collective-permute-start | bytes 638984 | tf_op jit(solution)/shard_map/ppermute | solution.py:301
  14.1 4.2 %collective-permute-start.7 = (bf16[96,256]{1,0:T(8,128)(2,1)S(1)}, bf16[96,256]{1,0:T(8,128)(2,1)S(1)}, u32[]{:S(2)}, u32[]{:S(2)}) collective-permute-start(bf16[96,256]{1,0:T(8,128)(2,1)S(1)} %get-tuple-element.59), channel_id=1, source_target_pairs={{0,2},{1,3},{2,0},{3,1},{4,6},{5,7},{6,4},{7,5},{8,10},{9,11},{10,... | collective-permute-start | bytes 147464 | tf_op jit(solution)/shard_map/ppermute | solution.py:301
  15.8 3.7 %collective-permute-start.4 = (bf16[96,256]{1,0:T(8,128)(2,1)S(1)}, bf16[96,256]{1,0:T(8,128)(2,1)S(1)}, u32[]{:S(2)}, u32[]{:S(2)}) collective-permute-start(bf16[96,256]{1,0:T(8,128)(2,1)S(1)} %get-tuple-element.55), channel_id=1, source_target_pairs={{0,3},{1,2},{2,1},{3,0},{4,7},{5,6},{6,5},{7,4},{8,11},{9,10},{10,... | collective-permute-start | bytes 147464 | tf_op jit(solution)/shard_map/ppermute | solution.py:301
  16.0 3.5 %collective-permute-start.5 = (bf16[96,256]{1,0:T(8,128)(2,1)S(1)}, bf16[96,256]{1,0:T(8,128)(2,1)S(1)}, u32[]{:S(2)}, u32[]{:S(2)}) collective-permute-start(bf16[96,256]{1,0:T(8,128)(2,1)S(1)} %get-tuple-element.56), channel_id=1, source_target_pairs={{0,1},{1,0},{2,3},{3,2},{4,6},{5,7},{6,4},{7,5},{8,10},{9,11},{10,... | collective-permute-start | bytes 147464 | tf_op jit(solution)/shard_map/ppermute | solution.py:301
  16.3 3.2 %collective-permute-start.6 = (bf16[96,256]{1,0:T(8,128)(2,1)S(1)}, bf16[96,256]{1,0:T(8,128)(2,1)S(1)}, u32[]{:S(2)}, u32[]{:S(2)}) collective-permute-start(bf16[96,256]{1,0:T(8,128)(2,1)S(1)} %get-tuple-element.57), channel_id=1, source_target_pairs={{0,1},{1,0},{2,3},{3,2},{4,7},{5,6},{6,5},{7,4},{8,11},{9,10},{10,... | collective-permute-start | bytes 147464 | tf_op jit(solution)/shard_map/ppermute | solution.py:301

commit v9 on v8

--- a/solution.py
+++ b/solution.py
@@ -47,38 +47,25 @@
     return value
 
 
-def pack_kernel(count, picks_ref, both_ref, *refs):
+def index_kernel(count, picks_ref, out_ref, table_ref):
     planes = count // PLANE
-    kv_ref, table_ref, own_ref, over_ref, side_ref, packet_refs = *refs[:5], refs[5:]
     me, z, r = place(count)
-    dim = both_ref.shape[1]
-    total = both_ref.shape[0] // 2 // KB
-    per_half = total // 2
-    for part in range(2):
-        kv_ref[:, part * dim : (part + 1) * dim] = both_ref[part * total * KB : (part + 1) * total * KB]
-    wanted, down = [], []
+    dim = out_ref.shape[1]
+    wanted, up_of = [], []
     for j in range(1, planes):
         up = z + j < planes
         to = jnp.where(up, 0, (z + j - planes) * PLANE)
         wanted += [(me, 2 * count - 1 - (to + t)) for t in range(PLANE)]
-        down += [up] * PLANE
+        up_of += [(up, t) for t in range(PLANE)]
     for m in (0, 1):
         wanted.append((me, 2 * count - 1 - (z * PLANE + (r ^ m))))
     for m in (2, 3):
         dest = z * PLANE + (r ^ m)
         wanted += [(me, 2 * count - 1 - dest), (me, dest)]
     index = splat(picks_ref, wanted, dim)
-    for part in range(2):
-        cols = slice(part * dim, (part + 1) * dim)
-        subs = [both_ref[at(part * total + t)] for t in range(total)]
-        for g, up in enumerate(down):
-            j, t = g // PLANE, g % PLANE
-            packet_refs[j][at(t), cols] = jnp.where(up, subs[t], chosen(index[g : g + 1], subs))
-        for g in range(6):
-            ref, t = (own_ref, g) if g < 2 else (over_ref, g - 2)
-            ref[at(t), cols] = chosen(index[len(down) + g : len(down) + g + 1], subs)
-        for t in range(per_half):
-            side_ref[at(t), cols] = jnp.where(me % 2 == 1, subs[t], subs[per_half + t])
+    for g in range(len(wanted)):
+        row = index[g : g + 1]
+        out_ref[g : g + 1] = jnp.where(up_of[g][0], up_of[g][1], row) if g < len(up_of) else row
     wanted, fixed = [], []
     for j in range(1, planes):
         up = z >= j
@@ -92,28 +79,46 @@
         table_ref[g : g + 1] = jnp.where(up, index[g : g + 1], other)
 
 
-def select_kernel(count, table_ref, own_ref, over_ref, kv_ref, *refs):
+def halves(both_ref):
+    dim = both_ref.shape[1]
+    total = both_ref.shape[0] // 2 // KB
+    for part in range(2):
+        yield slice(part * dim, (part + 1) * dim), [both_ref[at(part * total + t)] for t in range(total)]
+
+
+def pack_kernel(index_ref, both_ref, *packet_refs):
+    for cols, subs in halves(both_ref):
+        for g in range(len(packet_refs) * PLANE):
+            packet_refs[g // PLANE][at(g % PLANE), cols] = chosen(index_ref[g : g + 1], subs)
+
+
+def pack_own_kernel(first, index_ref, both_ref, kv_ref, own_ref, beside_ref, over_ref, side_ref):
+    odd = lax.axis_index("pb") % 2 == 1
+    for cols, subs in halves(both_ref):
+        for t, value in enumerate(subs):
+            kv_ref[at(t), cols] = value
+        per_half = len(subs) // 2
+        for g in range(6):
+            ref, t = ((own_ref, 0), (beside_ref, per_half))[g] if g < 2 else (over_ref, g - 2)
+            ref[at(t), cols] = chosen(index_ref[first + g : first + g + 1], subs)
+        for t in range(per_half):
+            side_ref[at(t), cols] = jnp.where(odd, subs[t], subs[per_half + t])
+            beside_ref[at(t), cols] = jnp.where(odd, subs[per_half + t], subs[t])
+
+
+def select_kernel(count, table_ref, own_ref, *refs):
     planes = count // PLANE
-    packet_refs, moved_refs, early_refs = refs[: planes - 1], refs[planes - 1 : planes + 3], refs[planes + 3 :]
+    packet_refs, moved_refs = refs[: planes - 1], refs[planes - 1 :]
     dim = table_ref.shape[1]
-    per_half = kv_ref.shape[0] // 2 // KB
-    for m in (0, 1):
-        moved_refs[m][at(0)] = own_ref[at(m)]
-    moved_refs[1][(2 * planes - 1) * KB : (2 * planes + 1) * KB] = over_ref[2 * KB :]
-    for t in range(per_half):
-        moved_refs[1][at(2 * planes + 1 + t)] = kv_ref[sub(lax.axis_index("pb") % 2 * per_half + t)]
+    moved_refs[0][at(0)] = own_ref[...]
     for j, packet in enumerate(packet_refs, 1):
         for part in (slice(0, dim), slice(dim, 2 * dim)):
             choices = [packet[at(t), part] for t in range(PLANE)]
             for m, ref in enumerate(moved_refs):
                 row = ((j - 1) * PLANE + m) * 2
-                first = j - (m > 1)
+                first = j - (m > 0)
                 ref[at(first), part] = chosen(table_ref[row : row + 1], choices)
-                early = chosen(table_ref[row + 1 : row + 2], choices)
-                if m < 2:
-                    ref[at(first + planes - 1), part] = early
-                else:
-                    early_refs[m - 2][at(first), part] = early
+                ref[at(first + planes - 1), part] = chosen(table_ref[row + 1 : row + 2], choices)
 
 
 def usable(count, block, m):
@@ -204,18 +209,22 @@
     def run(block):
         masks = [usable(count, block, m) for m in range(PLANE)]
         if stage == 0:
-            mine_ref, next_ref, over_ref, side_ref, kv_ref = come
-            half = side_ref.shape[0]
+            mine_ref, next_ref, beside_ref, over_ref, passed_ref, side_ref, kv_ref = come
+            half = kv_ref.shape[0] // 2
             far = slice(0, rest + KB) if block == 1 else slice(rest + KB, 2 * rest + KB)
-            side = side_ref[...]
+            side = side_ref[:half]
             if block == 1:
                 side = jnp.where(me == count - 1, kv_ref[:half], side)
-            third = 2 * rest + (2 - block) * KB
-            parts = [mine_ref[far], next_ref[far], over_ref[at(1 - block)], next_ref[third : third + KB]]
-            parts.append(jnp.where(me % 2 == block, side, next_ref[2 * rest + 3 * KB :]))
-            masks = masks[0][1 - block :] + masks[1][1 - block :] + masks[2][:1] + masks[3][:1] + [None] * (half // KB)
+            near = slice(0, rest) if block == 1 else slice(rest, 2 * rest)
+            parts = [mine_ref[far], next_ref[near], over_ref[at(1 - block)], passed_ref[at(1 - block)]]
+            masks = masks[0][1 - block :] + masks[1][1:] + masks[2][:1] + masks[3][:1]
+            if block == 1:
+                parts.append(beside_ref[half:])
+                masks.append(None)
+            parts.append(jnp.where(me % 2 == block, side, beside_ref[:half]))
+            masks += [None] * (half // KB)
         else:
-            parts, masks = [come[0][...]], masks[stage][1:]
+            parts, masks = [come[0][(1 - block) * rest : (2 - block) * rest]], masks[stage][1:]
 
         def save(step, m, l, acc):
             for ref, value in zip(new, (m, l, acc), strict=True):
@@ -223,15 +232,11 @@
 
         fold(jnp.concatenate(parts, axis=0), masks, scale, width, block, rot_ref, old, save)
 
-    if stage < 3:
-        run(1)
-    if stage == 0:
-        pl.when(me >= 1)(lambda: run(0))
-    if stage == 3:
-        pl.when(z >= 1)(lambda: run(1))
-
-
-def last_kernel(count, scale, width, third_ref, second_early_ref, third_early_ref, rot_ref, *refs):
+    run(1)
+    pl.when(me >= 1 if stage == 0 else z >= 1)(lambda: run(0))
+
+
+def last_kernel(count, scale, width, third_ref, rot_ref, *refs):
     old, out_ref, done_ref, sems = refs[:3], refs[3], refs[4], refs[5]
     _, z, _ = place(count)
     half = out_ref.shape[0] // 2
@@ -251,26 +256,18 @@
         piece(block, step).start()
 
     def add(block):
-        kv, masks = third_ref[...], usable(count, block, PLANE - 1)[1:]
-        if block == 0:
-            kv = jnp.concatenate([second_early_ref[...], third_early_ref[...]], axis=0)
-            masks = usable(count, block, 2)[1:] + masks
+        rest = third_ref.shape[0] // 2
+        kv, masks = third_ref[(1 - block) * rest : (2 - block) * rest], usable(count, block, PLANE - 1)[1:]
         fold(kv, masks, scale, width, block, rot_ref, old, lambda step, m, l, acc: finish(block, step, l, acc))
 
-    def close(block):
+    @pl.when(z < 1)
+    def _():
         for step in range(rot_ref.shape[1] // width):
             cols = slice(step * width, (step + 1) * width)
-            finish(block, step, old[1][block, :, cols], old[2][block, :, cols])
-
-    @pl.when(z >= 1)
-    def _():
-        close(1)
-        add(0)
-
-    @pl.when(z < 1)
-    def _():
-        close(0)
-        add(1)
+            finish(0, step, old[1][0, :, cols], old[2][0, :, cols])
+
+    add(1)
+    pl.when(z >= 1)(lambda: add(0))
 
     for block in range(2):
         for step in range(rot_ref.shape[1] // width):
@@ -306,17 +303,34 @@
         )
 
     per_half = half // KB
-    table = jax.ShapeDtypeStruct(((planes - 1) * PLANE * 2, dim), jnp.int32)
-    kv, table, own, over, side, *packets = pl.pallas_call(
-        functools.partial(pack_kernel, count),
-        out_shape=[rows(2 * per_half), table, rows(2), rows(4), rows(per_half)]
-        + [rows(PLANE)] * (planes - 1),
+    z_rows = (planes - 1) * PLANE
+    both, by_source = lax.optimization_barrier((jnp.concatenate([keys, values]), picks.T))
+    index, table = pl.pallas_call(
+        functools.partial(index_kernel, count),
+        out_shape=[jax.ShapeDtypeStruct((n, dim), jnp.int32) for n in (z_rows + 6, 2 * z_rows)],
+        in_specs=[vmem],
+        out_specs=[vmem] * 2,
+        compiler_params=params,
+        cost_estimate=pl.CostEstimate(flops=4_000_000_000, bytes_accessed=1_000_000, transcendentals=0),
+        name="index",
+    )(by_source)
+    packets = pl.pallas_call(
+        pack_kernel,
+        out_shape=[rows(PLANE)] * (planes - 1),
         in_specs=[vmem] * 2,
-        out_specs=[vmem] * (4 + planes),
+        out_specs=[vmem] * (planes - 1),
         compiler_params=params,
-        cost_estimate=pl.CostEstimate(flops=4000000000, bytes_accessed=1_000_000, transcendentals=0),
+        cost_estimate=pl.CostEstimate(flops=4_000_000_000, bytes_accessed=1_000_000, transcendentals=0),
         name="pack",
-    )(picks.T, jnp.concatenate([keys, values]))
+    )(index, both)
+    kv, own, beside, over, side = pl.pallas_call(
+        functools.partial(pack_own_kernel, z_rows),
+        out_shape=[rows(2 * per_half), rows(1), rows(per_half + 1), rows(4 + 0), rows(per_half + 0)],
+        in_specs=[vmem] * 2,
+        out_specs=[vmem] * 5,
+        compiler_params=params,
+        name="pack_own",
+    )(index, both)
 
     packets = [
         permute(packet, [(s, (s + j * PLANE) % count) for s in range(count)]) for j, packet in enumerate(packets, 1)
@@ -343,23 +357,20 @@
     def swap(value, m):
         return permute(value, [(s, s ^ m) for s in range(count)])
 
-    sizes = [2 * planes - 1, 2 * planes + 1 + per_half, planes - 1, planes - 1, planes - 1, planes - 1]
+    sizes = [2 * planes - 1, 2 * planes - 2, 2 * planes - 2, 2 * planes - 2]
     moved = list(
         pl.pallas_call(
             functools.partial(select_kernel, count),
             out_shape=[rows(size) for size in sizes],
-            in_specs=[vmem] * (planes + 3),
+            in_specs=[vmem] * (planes + 1),
             out_specs=[vmem] * len(sizes),
             compiler_params=params,
             name="select",
-        )(table, own, over, kv, *packets)
+        )(table, own, *packets)
     )
-    moved[1], side = lax.optimization_barrier((moved[1], side))
     for m in (1, 2, 3):
         moved[m] = swap(moved[m], m)
-    for i in range(PLANE, len(moved)):
-        m = PLANE - len(moved) + i
-        moved[i] = permute(moved[i], [(s, s ^ (m if s >= PLANE else 1)) for s in range(count)])
+    beside, passed = swap(beside, 1), swap(over[2 * KB : 4 * KB], 1)
 
     rotated, *state = near
 
@@ -375,19 +386,18 @@
             name=f"fold{stage}",
         )(*messages, rotated, *state)
 
-    state = folded(state, 0, [moved[0], moved[1], over, side, kv])
+    state = folded(state, 0, [moved[0], moved[1], beside, over, passed, side, kv])
     state = folded(state, 2, [moved[2]])
-    state = folded(state, 3, [moved[3]])
     return pl.pallas_call(
         functools.partial(last_kernel, count, scale, width),
         out_shape=jax.ShapeDtypeStruct(queries.shape, bf16),
-        in_specs=[vmem] * 7,
+        in_specs=[vmem] * 5,
         out_specs=pl.BlockSpec(memory_space=pl.ANY),
         scratch_shapes=[pltpu.VMEM(queries.shape, bf16), pltpu.SemaphoreType.DMA((2, wide // width))],
         compiler_params=params,
         cost_estimate=cost(half),
         name="last",
-    )(*moved[3:], rotated, *state)
+    )(moved[3], rotated, *state)
 
 
 def solution(mesh):

time: 21.1 us -> 21 us (level); the launches traced: 20.7 us -> 20.8 us
  starting transfers between devices: 12.4 us -> 13.2 us
  waiting for transfers between devices: 3.04 us -> 2.32 us
    ppermute x1, waiting for transfers between devices: 0.98 us -> 0.01 us  [per_device(): side = lax.ppermute(side, ('grp', 'pb'), pairs)]
    ppermute x9, starting transfers between devices: 10.9 us -> 11.6 us  [permute(): return lax.ppermute(value, 'pb', pairs)]
    ppermute x9, waiting for transfers between devices: 2.07 us -> 2.31 us  [permute(): return lax.ppermute(value, 'pb', pairs)]
    pallas_call x3 -> x2, Pallas kernels: 1.53 us -> 1.53 us  [folded(): pl.pallas_call(functools.partial(fold_kernel, count, scale, width, stage)...]
  transfers between devices with their start and end apart: 10 -> 10, of which waited for: 4 -> 3; matrix products, arithmetic and copies ran while one was open for 0% -> 0% of each run, Pallas kernels for 13% -> 13%
where the time goes in v9:
time: 21 us; the launch traced here: 20.8 us
  starting transfers between devices  13.2 us (63%)
  Pallas kernels  4.35 us (21%)
  waiting for transfers between devices  2.32 us (11%)
  other arithmetic  0.89 us (4%)
    ppermute x9, starting transfers between devices, permute(): return lax.ppermute(value, 'pb', pairs)  11.6 us
    ppermute x9, waiting for transfers between devices, permute(): return lax.ppermute(value, 'pb', pairs)  2.31 us
    pallas_call x2, Pallas kernels, folded(): pl.pallas_call(functools.partial(fold_kernel, count, scale, width, stage)...  1.53 us
    ppermute x1, starting transfers between devices, per_device(): side = lax.ppermute(side, ('grp', 'pb'), pairs)  1.52 us
    pallas_call x1, Pallas kernels, per_device(): pl.pallas_call(functools.partial(last_kernel, count, scale, width), out_s...  1.38 us
    pallas_call x1, Pallas kernels, per_device(): pl.pallas_call(functools.partial(near_kernel, scale, width), out_shape=[j...  0.98 us
    concatenate x1, other arithmetic, per_device(): jnp.concatenate([keys, values])  0.89 us
  transfers between devices with their start and end apart: 10, of which 3 were waited for; matrix products, arithmetic and copies ran while one was open for 0% of the time, Pallas kernels for 13%

profile of v9, /device:TPU:0, one launch (start us, length us, event | category | flops | bytes accessed | tf_op | source)
XLA Modules:
  0.0 20.8 jit_solution(13176097688750183249)
XLA Ops:
  0.0 0.9 %pad_maximum_fusion.both_ref = bf16[512,128]{1,0:T(8,128)(2,1)S(1)} fusion(bf16[256,128]{1,0:T(8,128)(2,1)} %param.7, bf16[256,128]{1,0:T(8,128)(2,1)} %param.6), kind=kLoop, calls=%fused_computation | loop fusion | flops 262144 | bytes 262144 | tf_op jit(solution)/shard_map/concatenate | solution.py:307
  0.9 0.1 index.1
  1.0 0.0 copy-start
  1.1 0.1 pack.1
  1.2 3.1 %collective-permute-start = (bf16[128,256]{1,0:T(8,128)(2,1)S(1)}, bf16[128,256]{1,0:T(8,128)(2,1)S(1)}, u32[]{:S(2)}, u32[]{:S(2)}) collective-permute-start(bf16[128,256]{1,0:T(8,128)(2,1)S(1)} %get-tuple-element.43), channel_id=1, source_target_pairs={{0,4},{1,5},{2,6},{3,7},{4,8},{5,9},{6,10},{7,11},{8,12},{9,13},{1... | collective-permute-start | bytes 196616 | tf_op jit(solution)/shard_map/ppermute | solution.py:298
  4.3 2.6 %collective-permute-start.1 = (bf16[128,256]{1,0:T(8,128)(2,1)S(1)}, bf16[128,256]{1,0:T(8,128)(2,1)S(1)}, u32[]{:S(2)}, u32[]{:S(2)}) collective-permute-start(bf16[128,256]{1,0:T(8,128)(2,1)S(1)} %get-tuple-element.44), channel_id=1, source_target_pairs={{0,8},{1,9},{2,10},{3,11},{4,12},{5,13},{6,14},{7,15},{8,0},{9,1},... | collective-permute-start | bytes 196616 | tf_op jit(solution)/shard_map/ppermute | solution.py:298
  6.9 1.3 %collective-permute-start.2 = (bf16[128,256]{1,0:T(8,128)(2,1)S(1)}, bf16[128,256]{1,0:T(8,128)(2,1)S(1)}, u32[]{:S(2)}, u32[]{:S(2)}) collective-permute-start(bf16[128,256]{1,0:T(8,128)(2,1)S(1)} %get-tuple-element.45), channel_id=1, source_target_pairs={{0,12},{1,13},{2,14},{3,15},{4,0},{5,1},{6,2},{7,3},{8,4},{9,5},{1... | collective-permute-start | bytes 196616 | tf_op jit(solution)/shard_map/ppermute | solution.py:298
  8.2 0.1 pack_own.1
  8.3 1.6 %collective-permute-start.7 = (bf16[128,256]{1,0:T(8,128)(2,1)S(1)}, bf16[128,256]{1,0:T(8,128)(2,1)S(1)}, u32[]{:S(2)}, u32[]{:S(2)}) collective-permute-start(bf16[128,256]{1,0:T(8,128)(2,1)S(1)} %get-tuple-element.60), channel_id=1, source_target_pairs={{0,2},{1,3},{2,0},{3,1},{4,6},{5,7},{6,4},{7,5},{8,10},{9,11},{10,... | collective-permute-start | bytes 196616 | tf_op jit(solution)/shard_map/ppermute | solution.py:298
  9.9 1.5 %collective-permute-start.9 = (bf16[128,256]{1,0:T(8,128)(2,1)S(1)}, bf16[128,256]{1,0:T(8,128)(2,1)S(1)}, u32[]{:S(2)}, u32[]{:S(2)}) collective-permute-start(bf16[128,256]{1,0:T(8,128)(2,1)S(1)} %get-tuple-element.61), channel_id=1, source_target_pairs={{1,2},{2,1},{3,4},{4,3},{5,6},{6,5},{7,8},{8,7},{9,10},{10,9},{11,... | collective-permute-start | bytes 196616 | tf_op jit(solution)/shard_map/ppermute | solution.py:355
  11.4 1.0 %near.1 = (bf16[2,1024,128]{2,1,0:T(8,128)(2,1)S(1)}, f32[2,1,1024]{2,1,0:T(1,128)S(1)}, f32[2,1,1024]{2,1,0:T(1,128)S(1)}, f32[2,128,1024]{2,1,0:T(8,128)S(1)}) custom-call(bf16[256,1024]{1,0:T(8,128)(2,1)S(1)} %copy-done, bf16[128,128]{1,0:T(8,128)(2,1)S(1)} %copy-done.1, bf16[256,256]{1,0:T(8,128)(2,1)S(1)} %get-tuple-element.46.kv_ref.refs_6_), custom_call_target="tpu_custom_call" | custom-call | flops 134217728 | bytes 4000000 | tf_op jit(solution)/shard_map/near/pallas_call | solution.py:339
  12.4 0.0 collective-permute-done.refs_0_
  12.4 0.1 select.1
  12.5 0.1 collective-permute-start.5
  12.6 0.8 %collective-permute-start.4 = (bf16[192,256]{1,0:T(8,128)(2,1)S(1)}, bf16[192,256]{1,0:T(8,128)(2,1)S(1)}, u32[]{:S(2)}, u32[]{:S(2)}) collective-permute-start(bf16[192,256]{1,0:T(8,128)(2,1)S(1)} %get-tuple-element.56), channel_id=1, source_target_pairs={{0,2},{1,3},{2,0},{3,1},{4,6},{5,7},{6,4},{7,5},{8,10},{9,11},{10,... | collective-permute-start | bytes 294920 | tf_op jit(solution)/shard_map/ppermute | solution.py:298
  13.4 0.2 collective-permute-start.6
  13.5 1.3 %collective-permute-start.3 = (bf16[192,256]{1,0:T(8,128)(2,1)S(1)}, bf16[192,256]{1,0:T(8,128)(2,1)S(1)}, u32[]{:S(2)}, u32[]{:S(2)}) collective-permute-start(bf16[192,256]{1,0:T(8,128)(2,1)S(1)} %get-tuple-element.54), channel_id=1, source_target_pairs={{0,3},{1,2},{2,1},{3,0},{4,7},{5,6},{6,5},{7,4},{8,11},{9,10},{10,... | collective-permute-start | bytes 294920 | tf_op jit(solution)/shard_map/ppermute | solution.py:298
  14.8 0.8 %collective-permute-start.8 = (bf16[64,256]{1,0:T(8,128)(2,1)S(1)}, bf16[64,256]{1,0:T(8,128)(2,1)S(1)}, u32[]{:S(2)}, u32[]{:S(2)}) collective-permute-start(bf16[64,256]{1,0:T(8,128)(2,1)S(1)} %slice.4), channel_id=1, source_target_pairs={{0,1},{1,0},{2,3},{3,2},{4,5},{5,4},{6,7},{7,6},{8,9},{9,8},{10,11... | collective-permute-start | bytes 98312 | tf_op jit(solution)/shard_map/ppermute | solution.py:298
  15.6 0.9 %collective-permute-done.8.refs_4_ = bf16[64,256]{1,0:T(8,128)(2,1)S(1)} collective-permute-done((bf16[64,256]{1,0:T(8,128)(2,1)S(1)}, bf16[64,256]{1,0:T(8,128)(2,1)S(1)}, u32[]{:S(2)}, u32[]{:S(2)}) %collective-permute-start.8) | collective-permute-done | bytes 32800 | tf_op jit(solution)/shard_map/ppermute | solution.py:298
  16.5 1.0 %fold0.1 = (f32[2,1,1024]{2,1,0:T(1,128)S(1)}, f32[2,1,1024]{2,1,0:T(1,128)S(1)}, f32[2,128,1024]{2,1,0:T(8,128)S(1)}) custom-call(bf16[224,256]{1,0:T(8,128)(2,1)S(1)} %get-tuple-element.57.refs_0_, bf16[192,256]{1,0:T(8,128)(2,1)S(1)} %collective-permute-done.5.refs_1_, ...), custom_call_target="tpu_custom_call", output_to_operand_aliasing={{0}: (8, {}), {1}: (9, {}), {2}: (10, {})} | custom-call | flops 134217728 | bytes 4000000 | tf_op jit(solution)/shard_map/fold0/pallas_call | solution.py:378
  17.5 0.8 %collective-permute-done.4.refs_0_ = bf16[192,256]{1,0:T(8,128)(2,1)S(1)} collective-permute-done((bf16[192,256]{1,0:T(8,128)(2,1)S(1)}, bf16[192,256]{1,0:T(8,128)(2,1)S(1)}, u32[]{:S(2)}, u32[]{:S(2)}) %collective-permute-start.4) | collective-permute-done | bytes 98336 | tf_op jit(solution)/shard_map/ppermute | solution.py:298
  18.3 0.6 %fold2.1 = (f32[2,1,1024]{2,1,0:T(1,128)S(1)}, f32[2,1,1024]{2,1,0:T(1,128)S(1)}, f32[2,128,1024]{2,1,0:T(8,128)S(1)}) custom-call(bf16[192,256]{1,0:T(8,128)(2,1)S(1)} %collective-permute-done.4.refs_0_, bf16[2,1024,128]{2,1,0:T(8,128)(2,1)S(1)} %get-tuple-element.55.refs_7_.refs_1_.rot_ref, ...), custom_call_target="tpu_custom_call", output_to_operand_aliasing={{0}: (2, {}), {1}: (3, {}), {2}: (4, {})} | custom-call | flops 134217728 | bytes 4000000 | tf_op jit(solution)/shard_map/fold2/pallas_call | solution.py:378
  18.8 0.6 %collective-permute-done.3.third_ref = bf16[192,256]{1,0:T(8,128)(2,1)S(1)} collective-permute-done((bf16[192,256]{1,0:T(8,128)(2,1)S(1)}, bf16[192,256]{1,0:T(8,128)(2,1)S(1)}, u32[]{:S(2)}, u32[]{:S(2)}) %collective-permute-start.3) | collective-permute-done | bytes 98336 | tf_op jit(solution)/shard_map/ppermute | solution.py:298
  19.5 1.4 %last.1 = bf16[256,1024]{1,0:T(8,128)(2,1)} custom-call(bf16[192,256]{1,0:T(8,128)(2,1)S(1)} %collective-permute-done.3.third_ref, bf16[2,1024,128]{2,1,0:T(8,128)(2,1)S(1)} %get-tuple-element.55.refs_7_.refs_1_.rot_ref, f32[2,1,1024]{2,1,0:T(1,128)S(1)} %get-tuple-element.68.refs_0_, f32[2,1,1024]{2,1,0:T(1,128)S(1)} %get-tuple-element.69.refs_1_, ...), custom_call_target="tpu_custom_call" | custom-call | flops 134217728 | bytes 4000000 | tf_op jit(solution)/shard_map/last/pallas_call | solution.py:391
  (12 shorter events, 0.0 us)
Async XLA Ops:
  0.0 0.9 %copy-start.2 = (s32[32,16]{0,1:T(8,128)S(1)}, s32[32,16]{0,1:T(8,128)}, u32[]{:S(2)}) copy-start(s32[32,16]{0,1:T(8,128)} %param.9) | copy-start | bytes 6148
  1.0 10.3 %copy-start = (bf16[256,1024]{1,0:T(8,128)(2,1)S(1)}, bf16[256,1024]{1,0:T(8,128)(2,1)}, u32[]{:S(2)}) copy-start(bf16[256,1024]{1,0:T(8,128)(2,1)} %q_ref.1) | copy-start | bytes 1572868
  1.2 11.2 %collective-permute-start = (bf16[128,256]{1,0:T(8,128)(2,1)S(1)}, bf16[128,256]{1,0:T(8,128)(2,1)S(1)}, u32[]{:S(2)}, u32[]{:S(2)}) collective-permute-start(bf16[128,256]{1,0:T(8,128)(2,1)S(1)} %get-tuple-element.43), channel_id=1, source_target_pairs={{0,4},{1,5},{2,6},{3,7},{4,8},{5,9},{6,10},{7,11},{8,12},{9,13},{1... | collective-permute-start | bytes 196616 | tf_op jit(solution)/shard_map/ppermute | solution.py:298
  4.3 8.1 %collective-permute-start.1 = (bf16[128,256]{1,0:T(8,128)(2,1)S(1)}, bf16[128,256]{1,0:T(8,128)(2,1)S(1)}, u32[]{:S(2)}, u32[]{:S(2)}) collective-permute-start(bf16[128,256]{1,0:T(8,128)(2,1)S(1)} %get-tuple-element.44), channel_id=1, source_target_pairs={{0,8},{1,9},{2,10},{3,11},{4,12},{5,13},{6,14},{7,15},{8,0},{9,1},... | collective-permute-start | bytes 196616 | tf_op jit(solution)/shard_map/ppermute | solution.py:298
  6.9 4.5 %copy-start.1 = (bf16[128,128]{1,0:T(8,128)(2,1)S(1)}, bf16[128,128]{1,0:T(8,128)(2,1)}, u32[]{:S(2)}) copy-start(bf16[128,128]{1,0:T(8,128)(2,1)} %basis_ref.1) | copy-start | bytes 98308
  6.9 5.5 %collective-permute-start.2 = (bf16[128,256]{1,0:T(8,128)(2,1)S(1)}, bf16[128,256]{1,0:T(8,128)(2,1)S(1)}, u32[]{:S(2)}, u32[]{:S(2)}) collective-permute-start(bf16[128,256]{1,0:T(8,128)(2,1)S(1)} %get-tuple-element.45), channel_id=1, source_target_pairs={{0,12},{1,13},{2,14},{3,15},{4,0},{5,1},{6,2},{7,3},{8,4},{9,5},{1... | collective-permute-start | bytes 196616 | tf_op jit(solution)/shard_map/ppermute | solution.py:298
  8.3 5.2 %collective-permute-start.7 = (bf16[128,256]{1,0:T(8,128)(2,1)S(1)}, bf16[128,256]{1,0:T(8,128)(2,1)S(1)}, u32[]{:S(2)}, u32[]{:S(2)}) collective-permute-start(bf16[128,256]{1,0:T(8,128)(2,1)S(1)} %get-tuple-element.60), channel_id=1, source_target_pairs={{0,2},{1,3},{2,0},{3,1},{4,6},{5,7},{6,4},{7,5},{8,10},{9,11},{10,... | collective-permute-start | bytes 196616 | tf_op jit(solution)/shard_map/ppermute | solution.py:298
  9.9 5.0 %collective-permute-start.9 = (bf16[128,256]{1,0:T(8,128)(2,1)S(1)}, bf16[128,256]{1,0:T(8,128)(2,1)S(1)}, u32[]{:S(2)}, u32[]{:S(2)}) collective-permute-start(bf16[128,256]{1,0:T(8,128)(2,1)S(1)} %get-tuple-element.61), channel_id=1, source_target_pairs={{1,2},{2,1},{3,4},{4,3},{5,6},{6,5},{7,8},{8,7},{9,10},{10,9},{11,... | collective-permute-start | bytes 196616 | tf_op jit(solution)/shard_map/ppermute | solution.py:355
  12.5 4.0 %collective-permute-start.5 = (bf16[192,256]{1,0:T(8,128)(2,1)S(1)}, bf16[192,256]{1,0:T(8,128)(2,1)S(1)}, u32[]{:S(2)}, u32[]{:S(2)}) collective-permute-start(bf16[192,256]{1,0:T(8,128)(2,1)S(1)} %get-tuple-element.58), channel_id=1, source_target_pairs={{0,1},{1,0},{2,3},{3,2},{4,5},{5,4},{6,7},{7,6},{8,9},{9,8},{10,11... | collective-permute-start | bytes 294920 | tf_op jit(solution)/shard_map/ppermute | solution.py:298
  12.6 5.7 %collective-permute-start.4 = (bf16[192,256]{1,0:T(8,128)(2,1)S(1)}, bf16[192,256]{1,0:T(8,128)(2,1)S(1)}, u32[]{:S(2)}, u32[]{:S(2)}) collective-permute-start(bf16[192,256]{1,0:T(8,128)(2,1)S(1)} %get-tuple-element.56), channel_id=1, source_target_pairs={{0,2},{1,3},{2,0},{3,1},{4,6},{5,7},{6,4},{7,5},{8,10},{9,11},{10,... | collective-permute-start | bytes 294920 | tf_op jit(solution)/shard_map/ppermute | solution.py:298
  13.4 2.3 %collective-permute-start.6 = (bf16[160,256]{1,0:T(8,128)(2,1)S(1)}, bf16[160,256]{1,0:T(8,128)(2,1)S(1)}, u32[]{:S(2)}, u32[]{:S(2)}) collective-permute-start(bf16[160,256]{1,0:T(8,128)(2,1)S(1)} %get-tuple-element.59), channel_id=1, source_target_pairs={{0,1},{1,0},{2,3},{3,2},{4,5},{5,4},{6,7},{7,6},{8,9},{9,8},{10,11... | collective-permute-start | bytes 245768 | tf_op jit(solution)/shard_map/ppermute | solution.py:298
  13.5 5.9 %collective-permute-start.3 = (bf16[192,256]{1,0:T(8,128)(2,1)S(1)}, bf16[192,256]{1,0:T(8,128)(2,1)S(1)}, u32[]{:S(2)}, u32[]{:S(2)}) collective-permute-start(bf16[192,256]{1,0:T(8,128)(2,1)S(1)} %get-tuple-element.54), channel_id=1, source_target_pairs={{0,3},{1,2},{2,1},{3,0},{4,7},{5,6},{6,5},{7,4},{8,11},{9,10},{10,... | collective-permute-start | bytes 294920 | tf_op jit(solution)/shard_map/ppermute | solution.py:298
  14.8 1.7 %collective-permute-start.8 = (bf16[64,256]{1,0:T(8,128)(2,1)S(1)}, bf16[64,256]{1,0:T(8,128)(2,1)S(1)}, u32[]{:S(2)}, u32[]{:S(2)}) collective-permute-start(bf16[64,256]{1,0:T(8,128)(2,1)S(1)} %slice.4), channel_id=1, source_target_pairs={{0,1},{1,0},{2,3},{3,2},{4,5},{5,4},{6,7},{7,6},{8,9},{9,8},{10,11... | collective-permute-start | bytes 98312 | tf_op jit(solution)/shard_map/ppermute | solution.py:298

commit v10 on v9

--- a/solution.py
+++ b/solution.py
@@ -173,21 +173,25 @@
         attend_all(steps, score, v_t, carried.__getitem__, save if last == total else keep)
 
 
-def near_kernel(scale, width, q_ref, basis_ref, kv_ref, rot_ref, m_ref, l_ref, acc_ref):
+def rotate_kernel(q_ref, basis_ref, rot_ref):
     dim = basis_ref.shape[0]
     half = q_ref.shape[0] // 2
-    heads = q_ref.shape[1] // dim
     basis = basis_ref[...]
+    for block in range(2):
+        for h in range(q_ref.shape[1] // dim):
+            q = q_ref[block * half : (block + 1) * half, h * dim : (h + 1) * dim]
+            q = jnp.dot(q, basis, preferred_element_type=jnp.float32)
+            rot_ref[block, h * half : (h + 1) * half, :] = q.astype(rot_ref.dtype)
+
+
+def near_kernel(scale, width, kv_ref, rot_ref, *state_refs):
+    dim = rot_ref.shape[2]
+    half = kv_ref.shape[0] // 2
     key_row = lax.broadcasted_iota(jnp.int32, (half, width), 0)
     query = lax.broadcasted_iota(jnp.int32, (half, width), 1) % half
     causal = key_row <= query
     for block in range(2):
         rows = slice(block * half, (block + 1) * half)
-        for h in range(heads):
-            q = jnp.dot(q_ref[rows, h * dim : (h + 1) * dim], basis, preferred_element_type=jnp.float32)
-            rot_ref[block, h * half : (h + 1) * half, :] = q.astype(jnp.bfloat16)
-    for block in range(2):
-        rows = slice(block * half, (block + 1) * half)
         k, v_t = kv_ref[rows, :dim], kv_ref[rows, dim:].T
 
         def score(step, block=block, k=k):
@@ -195,10 +199,10 @@
             return jnp.where(causal, s, NEG)
 
         def save(step, m, l, acc, block=block):
-            for ref, value in zip((m_ref, l_ref, acc_ref), (m, l, acc), strict=True):
+            for ref, value in zip(state_refs, (m, l, acc), strict=True):
                 ref[block, :, step * width : (step + 1) * width] = value
 
-        attend_all(heads * half // width, score, v_t, None, save)
+        attend_all(rot_ref.shape[1] // width, score, v_t, None, save)
 
 
 def fold_kernel(count, scale, width, stage, *refs):
@@ -236,7 +240,7 @@
     pl.when(me >= 1 if stage == 0 else z >= 1)(lambda: run(0))
 
 
-def last_kernel(count, scale, width, third_ref, rot_ref, *refs):
+def last_kernel(count, scale, width, second_ref, third_ref, rot_ref, *refs):
     old, out_ref, done_ref, sems = refs[:3], refs[3], refs[4], refs[5]
     _, z, _ = place(count)
     half = out_ref.shape[0] // 2
@@ -257,7 +261,9 @@
 
     def add(block):
         rest = third_ref.shape[0] // 2
-        kv, masks = third_ref[(1 - block) * rest : (2 - block) * rest], usable(count, block, PLANE - 1)[1:]
+        part = slice((1 - block) * rest, (2 - block) * rest)
+        kv = jnp.concatenate([second_ref[part], third_ref[part]], axis=0)
+        masks = usable(count, block, 2)[1:] + usable(count, block, PLANE - 1)[1:]
         fold(kv, masks, scale, width, block, rot_ref, old, lambda step, m, l, acc: finish(block, step, l, acc))
 
     @pl.when(z < 1)
@@ -336,16 +342,16 @@
         permute(packet, [(s, (s + j * PLANE) % count) for s in range(count)]) for j, packet in enumerate(packets, 1)
     ]
 
-    near = pl.pallas_call(
-        functools.partial(near_kernel, scale, width),
-        out_shape=[jax.ShapeDtypeStruct((2, wide, dim), bf16)] + shapes,
-        in_specs=[vmem] * 3,
-        out_specs=[vmem] * 4,
-        compiler_params=params,
-        cost_estimate=cost(half),
-        name="near",
-    )(queries, basis, kv)
-    packets, near = lax.optimization_barrier((packets, near))
+    rotated = pl.pallas_call(
+        rotate_kernel,
+        out_shape=jax.ShapeDtypeStruct((2, wide, dim), bf16),
+        in_specs=[vmem] * 2,
+        out_specs=vmem,
+        compiler_params=params,
+        cost_estimate=pl.CostEstimate(flops=4 * wide * dim * dim, bytes_accessed=2_000_000, transcendentals=0),
+        name="rotate",
+    )(queries, basis)
+    packets, rotated = lax.optimization_barrier((packets, rotated))
     over = permute(over, [(s, s ^ 2) for s in range(count)])
     groups = lax.axis_size("grp")
     pairs = []
@@ -372,7 +378,15 @@
         moved[m] = swap(moved[m], m)
     beside, passed = swap(beside, 1), swap(over[2 * KB : 4 * KB], 1)
 
-    rotated, *state = near
+    state = pl.pallas_call(
+        functools.partial(near_kernel, scale, width),
+        out_shape=shapes,
+        in_specs=[vmem] * 2,
+        out_specs=[vmem] * 3,
+        compiler_params=params,
+        cost_estimate=cost(half),
+        name="near",
+    )(kv, rotated)
 
     def folded(state, stage, messages):
         return pl.pallas_call(
@@ -387,17 +401,16 @@
         )(*messages, rotated, *state)
 
     state = folded(state, 0, [moved[0], moved[1], beside, over, passed, side, kv])
-    state = folded(state, 2, [moved[2]])
     return pl.pallas_call(
         functools.partial(last_kernel, count, scale, width),
         out_shape=jax.ShapeDtypeStruct(queries.shape, bf16),
-        in_specs=[vmem] * 5,
+        in_specs=[vmem] * 6,
         out_specs=pl.BlockSpec(memory_space=pl.ANY),
         scratch_shapes=[pltpu.VMEM(queries.shape, bf16), pltpu.SemaphoreType.DMA((2, wide // width))],
         compiler_params=params,
         cost_estimate=cost(half),
         name="last",
-    )(moved[3], rotated, *state)
+    )(moved[2], moved[3], rotated, *state)
 
 
 def solution(mesh):

time: 21 us -> 20.4 us (0.971)
  starting transfers between devices: 13.2 us -> 12.5 us
  waiting for transfers between devices: 2.32 us -> 2.64 us
  Pallas kernels: 4.35 us -> 4.08 us
    ppermute x9, starting transfers between devices: 11.6 us -> 11 us  [permute(): return lax.ppermute(value, 'pb', pairs)]
    pallas_call x2 -> x1, Pallas kernels: 1.53 us -> 0.98 us  [folded(): pl.pallas_call(functools.partial(fold_kernel, count, scale, width, stage)...]
    ppermute x9, waiting for transfers between devices: 2.31 us -> 2.64 us  [permute(): return lax.ppermute(value, 'pb', pairs)]
    pallas_call x1 -> x2, Pallas kernels: 0.98 us -> 1.15 us  [the longest x1 0.85 us: per_device(): pl.pallas_call(functools.partial(near_kernel, scale, width), out_shape=sh...]
  transfers between devices with their start and end apart: 10 -> 10, of which waited for: 3 -> 3; matrix products, arithmetic and copies ran while one was open for 0% -> 0% of each run, Pallas kernels for 13% -> 11%
where the time goes in v10:
time: 20.4 us; the launch traced here: 20.3 us
  starting transfers between devices  12.5 us (61%)
  Pallas kernels  4.08 us (20%)
  waiting for transfers between devices  2.64 us (13%)
  other arithmetic  0.89 us (4%)
    ppermute x9, starting transfers between devices, permute(): return lax.ppermute(value, 'pb', pairs)  11 us
    ppermute x9, waiting for transfers between devices, permute(): return lax.ppermute(value, 'pb', pairs)  2.64 us
    ppermute x1, starting transfers between devices, per_device(): side = lax.ppermute(side, ('grp', 'pb'), pairs)  1.52 us
    pallas_call x1, Pallas kernels, per_device(): pl.pallas_call(functools.partial(last_kernel, count, scale, width), out_s...  1.5 us
    pallas_call x1, Pallas kernels, folded(): pl.pallas_call(functools.partial(fold_kernel, count, scale, width, stage)...  0.98 us
    concatenate x1, other arithmetic, per_device(): jnp.concatenate([keys, values])  0.89 us
    pallas_call x1, Pallas kernels, per_device(): pl.pallas_call(functools.partial(near_kernel, scale, width), out_shape=sh...  0.85 us
  transfers between devices with their start and end apart: 10, of which 3 were waited for; matrix products, arithmetic and copies ran while one was open for 0% of the time, Pallas kernels for 11%

profile of v10, /device:TPU:0, one launch (start us, length us, event | category | flops | bytes accessed | tf_op | source)
XLA Modules:
  0.0 20.3 jit_solution(7239690914930293155)
XLA Ops:
  0.0 0.9 %pad_maximum_fusion.both_ref = bf16[512,128]{1,0:T(8,128)(2,1)S(1)} fusion(bf16[256,128]{1,0:T(8,128)(2,1)} %param.7, bf16[256,128]{1,0:T(8,128)(2,1)} %param.6), kind=kLoop, calls=%fused_computation | loop fusion | flops 262144 | bytes 262144 | tf_op jit(solution)/shard_map/concatenate | solution.py:313
  0.9 0.1 index.1
  1.0 0.0 copy-start
  1.1 0.1 pack.1
  1.2 3.1 %collective-permute-start = (bf16[128,256]{1,0:T(8,128)(2,1)S(1)}, bf16[128,256]{1,0:T(8,128)(2,1)S(1)}, u32[]{:S(2)}, u32[]{:S(2)}) collective-permute-start(bf16[128,256]{1,0:T(8,128)(2,1)S(1)} %get-tuple-element.36), channel_id=1, source_target_pairs={{0,4},{1,5},{2,6},{3,7},{4,8},{5,9},{6,10},{7,11},{8,12},{9,13},{1... | collective-permute-start | bytes 196616 | tf_op jit(solution)/shard_map/ppermute | solution.py:304
  4.3 2.6 %collective-permute-start.1 = (bf16[128,256]{1,0:T(8,128)(2,1)S(1)}, bf16[128,256]{1,0:T(8,128)(2,1)S(1)}, u32[]{:S(2)}, u32[]{:S(2)}) collective-permute-start(bf16[128,256]{1,0:T(8,128)(2,1)S(1)} %get-tuple-element.37), channel_id=1, source_target_pairs={{0,8},{1,9},{2,10},{3,11},{4,12},{5,13},{6,14},{7,15},{8,0},{9,1},... | collective-permute-start | bytes 196616 | tf_op jit(solution)/shard_map/ppermute | solution.py:304
  6.9 1.3 %collective-permute-start.2 = (bf16[128,256]{1,0:T(8,128)(2,1)S(1)}, bf16[128,256]{1,0:T(8,128)(2,1)S(1)}, u32[]{:S(2)}, u32[]{:S(2)}) collective-permute-start(bf16[128,256]{1,0:T(8,128)(2,1)S(1)} %get-tuple-element.38), channel_id=1, source_target_pairs={{0,12},{1,13},{2,14},{3,15},{4,0},{5,1},{6,2},{7,3},{8,4},{9,5},{1... | collective-permute-start | bytes 196616 | tf_op jit(solution)/shard_map/ppermute | solution.py:304
  8.2 0.1 pack_own.1
  8.3 1.6 %collective-permute-start.7 = (bf16[128,256]{1,0:T(8,128)(2,1)S(1)}, bf16[128,256]{1,0:T(8,128)(2,1)S(1)}, u32[]{:S(2)}, u32[]{:S(2)}) collective-permute-start(bf16[128,256]{1,0:T(8,128)(2,1)S(1)} %get-tuple-element.48), channel_id=1, source_target_pairs={{0,2},{1,3},{2,0},{3,1},{4,6},{5,7},{6,4},{7,5},{8,10},{9,11},{10,... | collective-permute-start | bytes 196616 | tf_op jit(solution)/shard_map/ppermute | solution.py:304
  9.9 1.5 %collective-permute-start.9 = (bf16[128,256]{1,0:T(8,128)(2,1)S(1)}, bf16[128,256]{1,0:T(8,128)(2,1)S(1)}, u32[]{:S(2)}, u32[]{:S(2)}) collective-permute-start(bf16[128,256]{1,0:T(8,128)(2,1)S(1)} %get-tuple-element.49), channel_id=1, source_target_pairs={{1,2},{2,1},{3,4},{4,3},{5,6},{6,5},{7,8},{8,7},{9,10},{10,9},{11,... | collective-permute-start | bytes 196616 | tf_op jit(solution)/shard_map/ppermute | solution.py:361
  11.4 0.3 %rotate.1.rot_ref.refs_7_ = bf16[2,1024,128]{2,1,0:T(8,128)(2,1)S(1)} custom-call(bf16[256,1024]{1,0:T(8,128)(2,1)S(1)} %copy-done, bf16[128,128]{1,0:T(8,128)(2,1)S(1)} %copy-done.1), custom_call_target="tpu_custom_call" | custom-call | flops 67108864 | bytes 2000000 | tf_op jit(solution)/shard_map/rotate/pallas_call | solution.py:345
  11.7 0.0 collective-permute-done.refs_0_
  11.7 0.1 select.1
  11.8 0.1 collective-permute-start.5
  11.9 1.4 %collective-permute-start.3 = (bf16[192,256]{1,0:T(8,128)(2,1)S(1)}, bf16[192,256]{1,0:T(8,128)(2,1)S(1)}, u32[]{:S(2)}, u32[]{:S(2)}) collective-permute-start(bf16[192,256]{1,0:T(8,128)(2,1)S(1)} %get-tuple-element.42), channel_id=1, source_target_pairs={{0,2},{1,3},{2,0},{3,1},{4,6},{5,7},{6,4},{7,5},{8,10},{9,11},{10,... | collective-permute-start | bytes 294920 | tf_op jit(solution)/shard_map/ppermute | solution.py:304
  13.4 0.4 %collective-permute-start.4 = (bf16[192,256]{1,0:T(8,128)(2,1)S(1)}, bf16[192,256]{1,0:T(8,128)(2,1)S(1)}, u32[]{:S(2)}, u32[]{:S(2)}) collective-permute-start(bf16[192,256]{1,0:T(8,128)(2,1)S(1)} %get-tuple-element.43), channel_id=1, source_target_pairs={{0,3},{1,2},{2,1},{3,0},{4,7},{5,6},{6,5},{7,4},{8,11},{9,10},{10,... | collective-permute-start | bytes 294920 | tf_op jit(solution)/shard_map/ppermute | solution.py:304
  13.8 0.3 %collective-permute-start.6 = (bf16[160,256]{1,0:T(8,128)(2,1)S(1)}, bf16[160,256]{1,0:T(8,128)(2,1)S(1)}, u32[]{:S(2)}, u32[]{:S(2)}) collective-permute-start(bf16[160,256]{1,0:T(8,128)(2,1)S(1)} %get-tuple-element.47), channel_id=1, source_target_pairs={{0,1},{1,0},{2,3},{3,2},{4,5},{5,4},{6,7},{7,6},{8,9},{9,8},{10,11... | collective-permute-start | bytes 245768 | tf_op jit(solution)/shard_map/ppermute | solution.py:304
  14.1 0.2 collective-permute-start.8
  14.3 0.9 %near.1 = (f32[2,1,1024]{2,1,0:T(1,128)S(1)}, f32[2,1,1024]{2,1,0:T(1,128)S(1)}, f32[2,128,1024]{2,1,0:T(8,128)S(1)}) custom-call(bf16[256,256]{1,0:T(8,128)(2,1)S(1)} %get-tuple-element.50.kv_ref.refs_6_, bf16[2,1024,128]{2,1,0:T(8,128)(2,1)S(1)} %rotate.1.rot_ref.refs_7_), custom_call_target="tpu_custom_call" | custom-call | flops 134217728 | bytes 4000000 | tf_op jit(solution)/shard_map/near/pallas_call | solution.py:381
  15.2 0.2 collective-permute-done.8.refs_4_
  15.3 1.0 %fold0.1 = (f32[2,1,1024]{2,1,0:T(1,128)S(1)}, f32[2,1,1024]{2,1,0:T(1,128)S(1)}, f32[2,128,1024]{2,1,0:T(8,128)S(1)}) custom-call(bf16[224,256]{1,0:T(8,128)(2,1)S(1)} %get-tuple-element.45.refs_0_, bf16[192,256]{1,0:T(8,128)(2,1)S(1)} %collective-permute-done.5.refs_1_, ...), custom_call_target="tpu_custom_call", output_to_operand_aliasing={{0}: (8, {}), {1}: (9, {}), {2}: (10, {})} | custom-call | flops 134217728 | bytes 4000000 | tf_op jit(solution)/shard_map/fold0/pallas_call | solution.py:392
  16.3 1.2 %collective-permute-done.3.second_ref = bf16[192,256]{1,0:T(8,128)(2,1)S(1)} collective-permute-done((bf16[192,256]{1,0:T(8,128)(2,1)S(1)}, bf16[192,256]{1,0:T(8,128)(2,1)S(1)}, u32[]{:S(2)}, u32[]{:S(2)}) %collective-permute-start.3) | collective-permute-done | bytes 98336 | tf_op jit(solution)/shard_map/ppermute | solution.py:304
  17.6 1.2 %collective-permute-done.4.third_ref = bf16[192,256]{1,0:T(8,128)(2,1)S(1)} collective-permute-done((bf16[192,256]{1,0:T(8,128)(2,1)S(1)}, bf16[192,256]{1,0:T(8,128)(2,1)S(1)}, u32[]{:S(2)}, u32[]{:S(2)}) %collective-permute-start.4) | collective-permute-done | bytes 98336 | tf_op jit(solution)/shard_map/ppermute | solution.py:304
  18.8 1.5 %last.1 = bf16[256,1024]{1,0:T(8,128)(2,1)} custom-call(bf16[192,256]{1,0:T(8,128)(2,1)S(1)} %collective-permute-done.3.second_ref, bf16[192,256]{1,0:T(8,128)(2,1)S(1)} %collective-permute-done.4.third_ref, bf16[2,1024,128]{2,1,0:T(8,128)(2,1)S(1)} %rotate.1.rot_ref.refs_7_, f32[2,1,1024]{2,1,0:T(1,128)S(1)} %get-tuple-element.54.refs_0_, ...), custom_call_target="tpu_custom_call" | custom-call | flops 134217728 | bytes 4000000 | tf_op jit(solution)/shard_map/last/pallas_call | solution.py:404
  (12 shorter events, 0.0 us)
Async XLA Ops:
  0.0 0.9 %copy-start.2 = (s32[32,16]{0,1:T(8,128)S(1)}, s32[32,16]{0,1:T(8,128)}, u32[]{:S(2)}) copy-start(s32[32,16]{0,1:T(8,128)} %param.9) | copy-start | bytes 6148
  1.0 10.3 %copy-start = (bf16[256,1024]{1,0:T(8,128)(2,1)S(1)}, bf16[256,1024]{1,0:T(8,128)(2,1)}, u32[]{:S(2)}) copy-start(bf16[256,1024]{1,0:T(8,128)(2,1)} %q_ref.1) | copy-start | bytes 1572868
  1.2 10.5 %collective-permute-start = (bf16[128,256]{1,0:T(8,128)(2,1)S(1)}, bf16[128,256]{1,0:T(8,128)(2,1)S(1)}, u32[]{:S(2)}, u32[]{:S(2)}) collective-permute-start(bf16[128,256]{1,0:T(8,128)(2,1)S(1)} %get-tuple-element.36), channel_id=1, source_target_pairs={{0,4},{1,5},{2,6},{3,7},{4,8},{5,9},{6,10},{7,11},{8,12},{9,13},{1... | collective-permute-start | bytes 196616 | tf_op jit(solution)/shard_map/ppermute | solution.py:304
  4.3 7.4 %collective-permute-start.1 = (bf16[128,256]{1,0:T(8,128)(2,1)S(1)}, bf16[128,256]{1,0:T(8,128)(2,1)S(1)}, u32[]{:S(2)}, u32[]{:S(2)}) collective-permute-start(bf16[128,256]{1,0:T(8,128)(2,1)S(1)} %get-tuple-element.37), channel_id=1, source_target_pairs={{0,8},{1,9},{2,10},{3,11},{4,12},{5,13},{6,14},{7,15},{8,0},{9,1},... | collective-permute-start | bytes 196616 | tf_op jit(solution)/shard_map/ppermute | solution.py:304
  6.9 4.5 %copy-start.1 = (bf16[128,128]{1,0:T(8,128)(2,1)S(1)}, bf16[128,128]{1,0:T(8,128)(2,1)}, u32[]{:S(2)}) copy-start(bf16[128,128]{1,0:T(8,128)(2,1)} %basis_ref.1) | copy-start | bytes 98308
  6.9 4.9 %collective-permute-start.2 = (bf16[128,256]{1,0:T(8,128)(2,1)S(1)}, bf16[128,256]{1,0:T(8,128)(2,1)S(1)}, u32[]{:S(2)}, u32[]{:S(2)}) collective-permute-start(bf16[128,256]{1,0:T(8,128)(2,1)S(1)} %get-tuple-element.38), channel_id=1, source_target_pairs={{0,12},{1,13},{2,14},{3,15},{4,0},{5,1},{6,2},{7,3},{8,4},{9,5},{1... | collective-permute-start | bytes 196616 | tf_op jit(solution)/shard_map/ppermute | solution.py:304
  8.3 5.5 %collective-permute-start.7 = (bf16[128,256]{1,0:T(8,128)(2,1)S(1)}, bf16[128,256]{1,0:T(8,128)(2,1)S(1)}, u32[]{:S(2)}, u32[]{:S(2)}) collective-permute-start(bf16[128,256]{1,0:T(8,128)(2,1)S(1)} %get-tuple-element.48), channel_id=1, source_target_pairs={{0,2},{1,3},{2,0},{3,1},{4,6},{5,7},{6,4},{7,5},{8,10},{9,11},{10,... | collective-permute-start | bytes 196616 | tf_op jit(solution)/shard_map/ppermute | solution.py:304
  9.9 4.3 %collective-permute-start.9 = (bf16[128,256]{1,0:T(8,128)(2,1)S(1)}, bf16[128,256]{1,0:T(8,128)(2,1)S(1)}, u32[]{:S(2)}, u32[]{:S(2)}) collective-permute-start(bf16[128,256]{1,0:T(8,128)(2,1)S(1)} %get-tuple-element.49), channel_id=1, source_target_pairs={{1,2},{2,1},{3,4},{4,3},{5,6},{6,5},{7,8},{8,7},{9,10},{10,9},{11,... | collective-permute-start | bytes 196616 | tf_op jit(solution)/shard_map/ppermute | solution.py:361
  11.8 3.5 %collective-permute-start.5 = (bf16[192,256]{1,0:T(8,128)(2,1)S(1)}, bf16[192,256]{1,0:T(8,128)(2,1)S(1)}, u32[]{:S(2)}, u32[]{:S(2)}) collective-permute-start(bf16[192,256]{1,0:T(8,128)(2,1)S(1)} %get-tuple-element.46), channel_id=1, source_target_pairs={{0,1},{1,0},{2,3},{3,2},{4,5},{5,4},{6,7},{7,6},{8,9},{9,8},{10,11... | collective-permute-start | bytes 294920 | tf_op jit(solution)/shard_map/ppermute | solution.py:304
  11.9 5.7 %collective-permute-start.3 = (bf16[192,256]{1,0:T(8,128)(2,1)S(1)}, bf16[192,256]{1,0:T(8,128)(2,1)S(1)}, u32[]{:S(2)}, u32[]{:S(2)}) collective-permute-start(bf16[192,256]{1,0:T(8,128)(2,1)S(1)} %get-tuple-element.42), channel_id=1, source_target_pairs={{0,2},{1,3},{2,0},{3,1},{4,6},{5,7},{6,4},{7,5},{8,10},{9,11},{10,... | collective-permute-start | bytes 294920 | tf_op jit(solution)/shard_map/ppermute | solution.py:304
  13.4 5.4 %collective-permute-start.4 = (bf16[192,256]{1,0:T(8,128)(2,1)S(1)}, bf16[192,256]{1,0:T(8,128)(2,1)S(1)}, u32[]{:S(2)}, u32[]{:S(2)}) collective-permute-start(bf16[192,256]{1,0:T(8,128)(2,1)S(1)} %get-tuple-element.43), channel_id=1, source_target_pairs={{0,3},{1,2},{2,1},{3,0},{4,7},{5,6},{6,5},{7,4},{8,11},{9,10},{10,... | collective-permute-start | bytes 294920 | tf_op jit(solution)/shard_map/ppermute | solution.py:304
  13.8 1.4 %collective-permute-start.6 = (bf16[160,256]{1,0:T(8,128)(2,1)S(1)}, bf16[160,256]{1,0:T(8,128)(2,1)S(1)}, u32[]{:S(2)}, u32[]{:S(2)}) collective-permute-start(bf16[160,256]{1,0:T(8,128)(2,1)S(1)} %get-tuple-element.47), channel_id=1, source_target_pairs={{0,1},{1,0},{2,3},{3,2},{4,5},{5,4},{6,7},{7,6},{8,9},{9,8},{10,11... | collective-permute-start | bytes 245768 | tf_op jit(solution)/shard_map/ppermute | solution.py:304
  14.1 1.2 %collective-permute-start.8 = (bf16[64,256]{1,0:T(8,128)(2,1)S(1)}, bf16[64,256]{1,0:T(8,128)(2,1)S(1)}, u32[]{:S(2)}, u32[]{:S(2)}) collective-permute-start(bf16[64,256]{1,0:T(8,128)(2,1)S(1)} %slice.4), channel_id=1, source_target_pairs={{0,1},{1,0},{2,3},{3,2},{4,5},{5,4},{6,7},{7,6},{8,9},{9,8},{10,11... | collective-permute-start | bytes 98312 | tf_op jit(solution)/shard_map/ppermute | solution.py:304

commit v11 on v10

--- a/solution.py
+++ b/solution.py
@@ -240,23 +240,38 @@
     pl.when(me >= 1 if stage == 0 else z >= 1)(lambda: run(0))
 
 
-def last_kernel(count, scale, width, second_ref, third_ref, rot_ref, *refs):
+def put_heads(ref, first, half, step, l, acc):
+    dim, width = acc.shape
+    done = acc / l
+    for h in range(width // half):
+        head = step * (width // half) + h
+        ref[first : first + half, head * dim : (head + 1) * dim] = done[:, h * half : (h + 1) * half].T.astype(ref.dtype)
+
+
+def close_kernel(width, l_ref, acc_ref, first_ref):
+    half = first_ref.shape[0]
+    _, z, _ = place(lax.axis_size("pb"))
+
+    @pl.when(z < 1)
+    def _():
+        for step in range(acc_ref.shape[2] // width):
+            cols = slice(step * width, (step + 1) * width)
+            put_heads(first_ref, 0, half, step, l_ref[0, :, cols], acc_ref[0, :, cols])
+
+
+def last_kernel(count, scale, width, second_ref, third_ref, first_ref, rot_ref, *refs):
     old, out_ref, done_ref, sems = refs[:3], refs[3], refs[4], refs[5]
     _, z, _ = place(count)
     half = out_ref.shape[0] // 2
     dim = rot_ref.shape[2]
 
-    def piece(block, step):
+    def piece(block, step, ready=None):
         rows, cols = pl.ds(block * half, half), pl.ds(step * (width // half) * dim, width // half * dim)
-        return pltpu.make_async_copy(done_ref.at[rows, cols], out_ref.at[rows, cols], sems.at[block, step])
+        source = done_ref.at[rows, cols] if ready is None else ready.at[:, cols]
+        return pltpu.make_async_copy(source, out_ref.at[rows, cols], sems.at[block, step])
 
     def finish(block, step, l, acc):
-        done = acc / l
-        for h in range(width // half):
-            head = step * (width // half) + h
-            done_ref[block * half : (block + 1) * half, head * dim : (head + 1) * dim] = (
-                done[:, h * half : (h + 1) * half].T.astype(done_ref.dtype)
-            )
+        put_heads(done_ref, block * half, half, step, l, acc)
         piece(block, step).start()
 
     def add(block):
@@ -269,8 +284,7 @@
     @pl.when(z < 1)
     def _():
         for step in range(rot_ref.shape[1] // width):
-            cols = slice(step * width, (step + 1) * width)
-            finish(0, step, old[1][0, :, cols], old[2][0, :, cols])
+            piece(0, step, first_ref).start()
 
     add(1)
     pl.when(z >= 1)(lambda: add(0))
@@ -351,7 +365,6 @@
         cost_estimate=pl.CostEstimate(flops=4 * wide * dim * dim, bytes_accessed=2_000_000, transcendentals=0),
         name="rotate",
     )(queries, basis)
-    packets, rotated = lax.optimization_barrier((packets, rotated))
     over = permute(over, [(s, s ^ 2) for s in range(count)])
     groups = lax.axis_size("grp")
     pairs = []
@@ -401,16 +414,24 @@
         )(*messages, rotated, *state)
 
     state = folded(state, 0, [moved[0], moved[1], beside, over, passed, side, kv])
+    first = pl.pallas_call(
+        functools.partial(close_kernel, width),
+        out_shape=jax.ShapeDtypeStruct((half, queries.shape[1]), bf16),
+        in_specs=[vmem] * 2,
+        out_specs=vmem,
+        compiler_params=params,
+        name="close",
+    )(*state[1:])
     return pl.pallas_call(
         functools.partial(last_kernel, count, scale, width),
         out_shape=jax.ShapeDtypeStruct(queries.shape, bf16),
-        in_specs=[vmem] * 6,
+        in_specs=[vmem] * 7,
         out_specs=pl.BlockSpec(memory_space=pl.ANY),
         scratch_shapes=[pltpu.VMEM(queries.shape, bf16), pltpu.SemaphoreType.DMA((2, wide // width))],
         compiler_params=params,
         cost_estimate=cost(half),
         name="last",
-    )(moved[2], moved[3], rotated, *state)
+    )(moved[2], moved[3], first, rotated, *state)
 
 
 def solution(mesh):

time: 20.4 us -> 20.2 us (level)
  waiting for transfers between devices: 2.64 us -> 2.24 us
  local copies, waits for them, and re-layouts: 0.02 us -> 0.25 us
    ppermute x9, waiting for transfers between devices: 2.64 us -> 2.1 us  [permute(): return lax.ppermute(value, 'pb', pairs)]
    unnamed x6, local copies, waits for them, and re-layouts: 0.01 us -> 0.25 us
  transfers between devices with their start and end apart: 10 -> 10, of which waited for: 3 -> 4; matrix products, arithmetic and copies ran while one was open for 0% -> 0% of each run, Pallas kernels for 11% -> 12%
where the time goes in v11:
time: 20.2 us; the launch traced here: 20 us
  starting transfers between devices  12.4 us (61%)
  Pallas kernels  4.09 us (20%)
  waiting for transfers between devices  2.24 us (11%)
  other arithmetic  0.89 us (4%)
  local copies, waits for them, and re-layouts  0.25 us (1%)
    ppermute x9, starting transfers between devices, permute(): return lax.ppermute(value, 'pb', pairs)  10.9 us
    ppermute x9, waiting for transfers between devices, permute(): return lax.ppermute(value, 'pb', pairs)  2.1 us
    ppermute x1, starting transfers between devices, per_device(): side = lax.ppermute(side, ('grp', 'pb'), pairs)  1.52 us
    pallas_call x1, Pallas kernels, per_device(): pl.pallas_call(functools.partial(last_kernel, count, scale, width), out_s...  1.35 us
    pallas_call x1, Pallas kernels, folded(): pl.pallas_call(functools.partial(fold_kernel, count, scale, width, stage)...  0.98 us
    concatenate x1, other arithmetic, per_device(): jnp.concatenate([keys, values])  0.89 us
    pallas_call x1, Pallas kernels, per_device(): pl.pallas_call(functools.partial(near_kernel, scale, width), out_shape=sh...  0.86 us
  transfers between devices with their start and end apart: 10, of which 4 were waited for; matrix products, arithmetic and copies ran while one was open for 0% of the time, Pallas kernels for 12%

profile of v11, /device:TPU:0, one launch (start us, length us, event | category | flops | bytes accessed | tf_op | source)
XLA Modules:
  0.0 20.0 jit_solution(2634460929100419141)
XLA Ops:
  0.0 0.9 %pad_maximum_fusion.both_ref = bf16[512,128]{1,0:T(8,128)(2,1)S(1)} fusion(bf16[256,128]{1,0:T(8,128)(2,1)} %param.7, bf16[256,128]{1,0:T(8,128)(2,1)} %param.6), kind=kLoop, calls=%fused_computation | loop fusion | flops 262144 | bytes 262144 | tf_op jit(solution)/shard_map/concatenate | solution.py:327
  0.9 0.1 index.1
  1.1 0.1 pack.1
  1.2 3.1 %collective-permute-start = (bf16[128,256]{1,0:T(8,128)(2,1)S(1)}, bf16[128,256]{1,0:T(8,128)(2,1)S(1)}, u32[]{:S(2)}, u32[]{:S(2)}) collective-permute-start(bf16[128,256]{1,0:T(8,128)(2,1)S(1)} %get-tuple-element.32), channel_id=1, source_target_pairs={{0,4},{1,5},{2,6},{3,7},{4,8},{5,9},{6,10},{7,11},{8,12},{9,13},{1... | collective-permute-start | bytes 196616 | tf_op jit(solution)/shard_map/ppermute | solution.py:318
  4.3 2.6 %collective-permute-start.1 = (bf16[128,256]{1,0:T(8,128)(2,1)S(1)}, bf16[128,256]{1,0:T(8,128)(2,1)S(1)}, u32[]{:S(2)}, u32[]{:S(2)}) collective-permute-start(bf16[128,256]{1,0:T(8,128)(2,1)S(1)} %get-tuple-element.33), channel_id=1, source_target_pairs={{0,8},{1,9},{2,10},{3,11},{4,12},{5,13},{6,14},{7,15},{8,0},{9,1},... | collective-permute-start | bytes 196616 | tf_op jit(solution)/shard_map/ppermute | solution.py:318
  6.9 1.3 %collective-permute-start.2 = (bf16[128,256]{1,0:T(8,128)(2,1)S(1)}, bf16[128,256]{1,0:T(8,128)(2,1)S(1)}, u32[]{:S(2)}, u32[]{:S(2)}) collective-permute-start(bf16[128,256]{1,0:T(8,128)(2,1)S(1)} %get-tuple-element.34), channel_id=1, source_target_pairs={{0,12},{1,13},{2,14},{3,15},{4,0},{5,1},{6,2},{7,3},{8,4},{9,5},{1... | collective-permute-start | bytes 196616 | tf_op jit(solution)/shard_map/ppermute | solution.py:318
  8.2 0.1 pack_own.1
  8.3 1.6 %collective-permute-start.7 = (bf16[128,256]{1,0:T(8,128)(2,1)S(1)}, bf16[128,256]{1,0:T(8,128)(2,1)S(1)}, u32[]{:S(2)}, u32[]{:S(2)}) collective-permute-start(bf16[128,256]{1,0:T(8,128)(2,1)S(1)} %get-tuple-element.40), channel_id=1, source_target_pairs={{0,2},{1,3},{2,0},{3,1},{4,6},{5,7},{6,4},{7,5},{8,10},{9,11},{10,... | collective-permute-start | bytes 196616 | tf_op jit(solution)/shard_map/ppermute | solution.py:318
  9.9 1.5 %collective-permute-start.9 = (bf16[128,256]{1,0:T(8,128)(2,1)S(1)}, bf16[128,256]{1,0:T(8,128)(2,1)S(1)}, u32[]{:S(2)}, u32[]{:S(2)}) collective-permute-start(bf16[128,256]{1,0:T(8,128)(2,1)S(1)} %get-tuple-element.41), channel_id=1, source_target_pairs={{1,2},{2,1},{3,4},{4,3},{5,6},{6,5},{7,8},{8,7},{9,10},{10,9},{11,... | collective-permute-start | bytes 196616 | tf_op jit(solution)/shard_map/ppermute | solution.py:374
  11.4 0.2 collective-permute-done.2.refs_2_
  11.6 0.1 select.1
  11.7 0.1 collective-permute-start.5
  11.8 1.6 %collective-permute-start.3 = (bf16[192,256]{1,0:T(8,128)(2,1)S(1)}, bf16[192,256]{1,0:T(8,128)(2,1)S(1)}, u32[]{:S(2)}, u32[]{:S(2)}) collective-permute-start(bf16[192,256]{1,0:T(8,128)(2,1)S(1)} %get-tuple-element.35), channel_id=1, source_target_pairs={{0,2},{1,3},{2,0},{3,1},{4,6},{5,7},{6,4},{7,5},{8,10},{9,11},{10,... | collective-permute-start | bytes 294920 | tf_op jit(solution)/shard_map/ppermute | solution.py:318
  13.4 0.3 %collective-permute-start.4 = (bf16[192,256]{1,0:T(8,128)(2,1)S(1)}, bf16[192,256]{1,0:T(8,128)(2,1)S(1)}, u32[]{:S(2)}, u32[]{:S(2)}) collective-permute-start(bf16[192,256]{1,0:T(8,128)(2,1)S(1)} %get-tuple-element.36), channel_id=1, source_target_pairs={{0,3},{1,2},{2,1},{3,0},{4,7},{5,6},{6,5},{7,4},{8,11},{9,10},{10,... | collective-permute-start | bytes 294920 | tf_op jit(solution)/shard_map/ppermute | solution.py:318
  13.6 0.3 %collective-permute-start.6 = (bf16[160,256]{1,0:T(8,128)(2,1)S(1)}, bf16[160,256]{1,0:T(8,128)(2,1)S(1)}, u32[]{:S(2)}, u32[]{:S(2)}) collective-permute-start(bf16[160,256]{1,0:T(8,128)(2,1)S(1)} %get-tuple-element.39), channel_id=1, source_target_pairs={{0,1},{1,0},{2,3},{3,2},{4,5},{5,4},{6,7},{7,6},{8,9},{9,8},{10,11... | collective-permute-start | bytes 245768 | tf_op jit(solution)/shard_map/ppermute | solution.py:318
  14.0 0.1 collective-permute-done.9.refs_5_
  14.2 0.2 %copy-done.1 = bf16[128,128]{1,0:T(8,128)(2,1)S(1)} copy-done((bf16[128,128]{1,0:T(8,128)(2,1)S(1)}, bf16[128,128]{1,0:T(8,128)(2,1)}, u32[]{:S(2)}) %copy-start.1) | copy-done | bytes 32792
  14.4 0.3 %rotate.1.rot_ref.refs_7_ = bf16[2,1024,128]{2,1,0:T(8,128)(2,1)S(1)} custom-call(bf16[256,1024]{1,0:T(8,128)(2,1)S(1)} %copy-done, bf16[128,128]{1,0:T(8,128)(2,1)S(1)} %copy-done.1), custom_call_target="tpu_custom_call" | custom-call | flops 67108864 | bytes 2000000 | tf_op jit(solution)/shard_map/rotate/pallas_call | solution.py:359
  14.7 0.9 %near.1 = (f32[2,1,1024]{2,1,0:T(1,128)S(1)}, f32[2,1,1024]{2,1,0:T(1,128)S(1)}, f32[2,128,1024]{2,1,0:T(8,128)S(1)}) custom-call(bf16[256,256]{1,0:T(8,128)(2,1)S(1)} %get-tuple-element.42.kv_ref.refs_6_, bf16[2,1024,128]{2,1,0:T(8,128)(2,1)S(1)} %rotate.1.rot_ref.refs_7_), custom_call_target="tpu_custom_call" | custom-call | flops 134217728 | bytes 4000000 | tf_op jit(solution)/shard_map/near/pallas_call | solution.py:394
  15.6 1.0 %fold0.1 = (f32[2,1,1024]{2,1,0:T(1,128)S(1)}, f32[2,1,1024]{2,1,0:T(1,128)S(1)}, f32[2,128,1024]{2,1,0:T(8,128)S(1)}) custom-call(bf16[224,256]{1,0:T(8,128)(2,1)S(1)} %get-tuple-element.37.refs_0_, bf16[192,256]{1,0:T(8,128)(2,1)S(1)} %collective-permute-done.5.refs_1_, ...), custom_call_target="tpu_custom_call", output_to_operand_aliasing={{0}: (8, {}), {1}: (9, {}), {2}: (10, {})} | custom-call | flops 134217728 | bytes 4000000 | tf_op jit(solution)/shard_map/fold0/pallas_call | solution.py:405
  16.6 0.2 close.1.first_ref
  16.7 0.7 %collective-permute-done.3.second_ref = bf16[192,256]{1,0:T(8,128)(2,1)S(1)} collective-permute-done((bf16[192,256]{1,0:T(8,128)(2,1)S(1)}, bf16[192,256]{1,0:T(8,128)(2,1)S(1)}, u32[]{:S(2)}, u32[]{:S(2)}) %collective-permute-start.3) | collective-permute-done | bytes 98336 | tf_op jit(solution)/shard_map/ppermute | solution.py:318
  17.4 1.2 %collective-permute-done.4.third_ref = bf16[192,256]{1,0:T(8,128)(2,1)S(1)} collective-permute-done((bf16[192,256]{1,0:T(8,128)(2,1)S(1)}, bf16[192,256]{1,0:T(8,128)(2,1)S(1)}, u32[]{:S(2)}, u32[]{:S(2)}) %collective-permute-start.4) | collective-permute-done | bytes 98336 | tf_op jit(solution)/shard_map/ppermute | solution.py:318
  18.6 1.3 %last.1 = bf16[256,1024]{1,0:T(8,128)(2,1)} custom-call(bf16[192,256]{1,0:T(8,128)(2,1)S(1)} %collective-permute-done.3.second_ref, bf16[192,256]{1,0:T(8,128)(2,1)S(1)} %collective-permute-done.4.third_ref, bf16[128,1024]{1,0:T(8,128)(2,1)S(1)} %close.1.first_ref, bf16[2,1024,128]{2,1,0:T(8,128)(2,1)S(1)} %rotate.1.rot_ref.refs_7_, ...), custom_call_target="tpu_custom_call" | custom-call | flops 134217728 | bytes 4000000 | tf_op jit(solution)/shard_map/last/pallas_call | solution.py:425
  (13 shorter events, 0.1 us)
Async XLA Ops:
  0.0 0.9 %copy-start.2 = (s32[32,16]{0,1:T(8,128)S(1)}, s32[32,16]{0,1:T(8,128)}, u32[]{:S(2)}) copy-start(s32[32,16]{0,1:T(8,128)} %param.9) | copy-start | bytes 6148
  1.0 13.1 %copy-start = (bf16[256,1024]{1,0:T(8,128)(2,1)S(1)}, bf16[256,1024]{1,0:T(8,128)(2,1)}, u32[]{:S(2)}) copy-start(bf16[256,1024]{1,0:T(8,128)(2,1)} %q_ref.1) | copy-start | bytes 1572868
  1.2 10.2 %collective-permute-start = (bf16[128,256]{1,0:T(8,128)(2,1)S(1)}, bf16[128,256]{1,0:T(8,128)(2,1)S(1)}, u32[]{:S(2)}, u32[]{:S(2)}) collective-permute-start(bf16[128,256]{1,0:T(8,128)(2,1)S(1)} %get-tuple-element.32), channel_id=1, source_target_pairs={{0,4},{1,5},{2,6},{3,7},{4,8},{5,9},{6,10},{7,11},{8,12},{9,13},{1... | collective-permute-start | bytes 196616 | tf_op jit(solution)/shard_map/ppermute | solution.py:318
  4.3 7.1 %collective-permute-start.1 = (bf16[128,256]{1,0:T(8,128)(2,1)S(1)}, bf16[128,256]{1,0:T(8,128)(2,1)S(1)}, u32[]{:S(2)}, u32[]{:S(2)}) collective-permute-start(bf16[128,256]{1,0:T(8,128)(2,1)S(1)} %get-tuple-element.33), channel_id=1, source_target_pairs={{0,8},{1,9},{2,10},{3,11},{4,12},{5,13},{6,14},{7,15},{8,0},{9,1},... | collective-permute-start | bytes 196616 | tf_op jit(solution)/shard_map/ppermute | solution.py:318
  6.9 4.7 %collective-permute-start.2 = (bf16[128,256]{1,0:T(8,128)(2,1)S(1)}, bf16[128,256]{1,0:T(8,128)(2,1)S(1)}, u32[]{:S(2)}, u32[]{:S(2)}) collective-permute-start(bf16[128,256]{1,0:T(8,128)(2,1)S(1)} %get-tuple-element.34), channel_id=1, source_target_pairs={{0,12},{1,13},{2,14},{3,15},{4,0},{5,1},{6,2},{7,3},{8,4},{9,5},{1... | collective-permute-start | bytes 196616 | tf_op jit(solution)/shard_map/ppermute | solution.py:318
  8.3 5.3 %collective-permute-start.7 = (bf16[128,256]{1,0:T(8,128)(2,1)S(1)}, bf16[128,256]{1,0:T(8,128)(2,1)S(1)}, u32[]{:S(2)}, u32[]{:S(2)}) collective-permute-start(bf16[128,256]{1,0:T(8,128)(2,1)S(1)} %get-tuple-element.40), channel_id=1, source_target_pairs={{0,2},{1,3},{2,0},{3,1},{4,6},{5,7},{6,4},{7,5},{8,10},{9,11},{10,... | collective-permute-start | bytes 196616 | tf_op jit(solution)/shard_map/ppermute | solution.py:318
  9.9 4.3 %collective-permute-start.9 = (bf16[128,256]{1,0:T(8,128)(2,1)S(1)}, bf16[128,256]{1,0:T(8,128)(2,1)S(1)}, u32[]{:S(2)}, u32[]{:S(2)}) collective-permute-start(bf16[128,256]{1,0:T(8,128)(2,1)S(1)} %get-tuple-element.41), channel_id=1, source_target_pairs={{1,2},{2,1},{3,4},{4,3},{5,6},{6,5},{7,8},{8,7},{9,10},{10,9},{11,... | collective-permute-start | bytes 196616 | tf_op jit(solution)/shard_map/ppermute | solution.py:374
  11.7 3.9 %collective-permute-start.5 = (bf16[192,256]{1,0:T(8,128)(2,1)S(1)}, bf16[192,256]{1,0:T(8,128)(2,1)S(1)}, u32[]{:S(2)}, u32[]{:S(2)}) collective-permute-start(bf16[192,256]{1,0:T(8,128)(2,1)S(1)} %get-tuple-element.38), channel_id=1, source_target_pairs={{0,1},{1,0},{2,3},{3,2},{4,5},{5,4},{6,7},{7,6},{8,9},{9,8},{10,11... | collective-permute-start | bytes 294920 | tf_op jit(solution)/shard_map/ppermute | solution.py:318
  11.8 5.7 %collective-permute-start.3 = (bf16[192,256]{1,0:T(8,128)(2,1)S(1)}, bf16[192,256]{1,0:T(8,128)(2,1)S(1)}, u32[]{:S(2)}, u32[]{:S(2)}) collective-permute-start(bf16[192,256]{1,0:T(8,128)(2,1)S(1)} %get-tuple-element.35), channel_id=1, source_target_pairs={{0,2},{1,3},{2,0},{3,1},{4,6},{5,7},{6,4},{7,5},{8,10},{9,11},{10,... | collective-permute-start | bytes 294920 | tf_op jit(solution)/shard_map/ppermute | solution.py:318
  13.4 5.3 %collective-permute-start.4 = (bf16[192,256]{1,0:T(8,128)(2,1)S(1)}, bf16[192,256]{1,0:T(8,128)(2,1)S(1)}, u32[]{:S(2)}, u32[]{:S(2)}) collective-permute-start(bf16[192,256]{1,0:T(8,128)(2,1)S(1)} %get-tuple-element.36), channel_id=1, source_target_pairs={{0,3},{1,2},{2,1},{3,0},{4,7},{5,6},{6,5},{7,4},{8,11},{9,10},{10,... | collective-permute-start | bytes 294920 | tf_op jit(solution)/shard_map/ppermute | solution.py:318
  13.6 0.8 %copy-start.1 = (bf16[128,128]{1,0:T(8,128)(2,1)S(1)}, bf16[128,128]{1,0:T(8,128)(2,1)}, u32[]{:S(2)}) copy-start(bf16[128,128]{1,0:T(8,128)(2,1)} %basis_ref.1) | copy-start | bytes 98308
  13.6 1.9 %collective-permute-start.6 = (bf16[160,256]{1,0:T(8,128)(2,1)S(1)}, bf16[160,256]{1,0:T(8,128)(2,1)S(1)}, u32[]{:S(2)}, u32[]{:S(2)}) collective-permute-start(bf16[160,256]{1,0:T(8,128)(2,1)S(1)} %get-tuple-element.39), channel_id=1, source_target_pairs={{0,1},{1,0},{2,3},{3,2},{4,5},{5,4},{6,7},{7,6},{8,9},{9,8},{10,11... | collective-permute-start | bytes 245768 | tf_op jit(solution)/shard_map/ppermute | solution.py:318
  14.1 1.4 %collective-permute-start.8 = (bf16[64,256]{1,0:T(8,128)(2,1)S(1)}, bf16[64,256]{1,0:T(8,128)(2,1)S(1)}, u32[]{:S(2)}, u32[]{:S(2)}) collective-permute-start(bf16[64,256]{1,0:T(8,128)(2,1)S(1)} %slice.4), channel_id=1, source_target_pairs={{0,1},{1,0},{2,3},{3,2},{4,5},{5,4},{6,7},{7,6},{8,9},{9,8},{10,11... | collective-permute-start | bytes 98312 | tf_op jit(solution)/shard_map/ppermute | solution.py:318

commit v12 on v11

--- a/solution.py
+++ b/solution.py
@@ -108,7 +108,7 @@
 
 def select_kernel(count, table_ref, own_ref, *refs):
     planes = count // PLANE
-    packet_refs, moved_refs = refs[: planes - 1], refs[planes - 1 :]
+    packet_refs, moved_refs, early_ref = refs[: planes - 1], refs[planes - 1 : planes + 3], refs[planes + 3]
     dim = table_ref.shape[1]
     moved_refs[0][at(0)] = own_ref[...]
     for j, packet in enumerate(packet_refs, 1):
@@ -118,7 +118,11 @@
                 row = ((j - 1) * PLANE + m) * 2
                 first = j - (m > 0)
                 ref[at(first), part] = chosen(table_ref[row : row + 1], choices)
-                ref[at(first + planes - 1), part] = chosen(table_ref[row + 1 : row + 2], choices)
+                early = chosen(table_ref[row + 1 : row + 2], choices)
+                if m < PLANE - 1:
+                    ref[at(first + planes - 1), part] = early
+                else:
+                    early_ref[at(first), part] = early
 
 
 def usable(count, block, m):
@@ -210,7 +214,7 @@
     me, z, _ = place(count)
     rest = (count // PLANE - 1) * KB
 
-    def run(block):
+    def run(block, light=False):
         masks = [usable(count, block, m) for m in range(PLANE)]
         if stage == 0:
             mine_ref, next_ref, beside_ref, over_ref, passed_ref, side_ref, kv_ref = come
@@ -225,6 +229,8 @@
             if block == 1:
                 parts.append(beside_ref[half:])
                 masks.append(None)
+            if light:
+                parts, masks = parts[2:], masks[2 * rest // KB :]
             parts.append(jnp.where(me % 2 == block, side, beside_ref[:half]))
             masks += [None] * (half // KB)
         else:
@@ -237,7 +243,9 @@
         fold(jnp.concatenate(parts, axis=0), masks, scale, width, block, rot_ref, old, save)
 
     run(1)
-    pl.when(me >= 1 if stage == 0 else z >= 1)(lambda: run(0))
+    pl.when(z >= 1)(lambda: run(0))
+    if stage == 0:
+        pl.when((z < 1) & (me >= 1))(lambda: run(0, True))
 
 
 def put_heads(ref, first, half, step, l, acc):
@@ -259,7 +267,7 @@
             put_heads(first_ref, 0, half, step, l_ref[0, :, cols], acc_ref[0, :, cols])
 
 
-def last_kernel(count, scale, width, second_ref, third_ref, first_ref, rot_ref, *refs):
+def last_kernel(count, scale, width, second_ref, third_ref, early_ref, first_ref, rot_ref, *refs):
     old, out_ref, done_ref, sems = refs[:3], refs[3], refs[4], refs[5]
     _, z, _ = place(count)
     half = out_ref.shape[0] // 2
@@ -275,9 +283,10 @@
         piece(block, step).start()
 
     def add(block):
-        rest = third_ref.shape[0] // 2
+        rest = third_ref.shape[0]
         part = slice((1 - block) * rest, (2 - block) * rest)
-        kv = jnp.concatenate([second_ref[part], third_ref[part]], axis=0)
+        third = third_ref if block == 1 else early_ref
+        kv = jnp.concatenate([second_ref[part], third[...]], axis=0)
         masks = usable(count, block, 2)[1:] + usable(count, block, PLANE - 1)[1:]
         fold(kv, masks, scale, width, block, rot_ref, old, lambda step, m, l, acc: finish(block, step, l, acc))
 
@@ -365,6 +374,7 @@
         cost_estimate=pl.CostEstimate(flops=4 * wide * dim * dim, bytes_accessed=2_000_000, transcendentals=0),
         name="rotate",
     )(queries, basis)
+    packets, rotated = lax.optimization_barrier((packets, rotated))
     over = permute(over, [(s, s ^ 2) for s in range(count)])
     groups = lax.axis_size("grp")
     pairs = []
@@ -376,7 +386,7 @@
     def swap(value, m):
         return permute(value, [(s, s ^ m) for s in range(count)])
 
-    sizes = [2 * planes - 1, 2 * planes - 2, 2 * planes - 2, 2 * planes - 2]
+    sizes = [2 * planes - 1, 2 * planes - 2, 2 * planes - 2, planes - 1, planes - 1]
     moved = list(
         pl.pallas_call(
             functools.partial(select_kernel, count),
@@ -389,6 +399,7 @@
     )
     for m in (1, 2, 3):
         moved[m] = swap(moved[m], m)
+    early = permute(moved[PLANE], [(s, s ^ (PLANE - 1 if s >= PLANE else 1)) for s in range(count)])
     beside, passed = swap(beside, 1), swap(over[2 * KB : 4 * KB], 1)
 
     state = pl.pallas_call(
@@ -425,13 +436,13 @@
     return pl.pallas_call(
         functools.partial(last_kernel, count, scale, width),
         out_shape=jax.ShapeDtypeStruct(queries.shape, bf16),
-        in_specs=[vmem] * 7,
+        in_specs=[vmem] * 8,
         out_specs=pl.BlockSpec(memory_space=pl.ANY),
         scratch_shapes=[pltpu.VMEM(queries.shape, bf16), pltpu.SemaphoreType.DMA((2, wide // width))],
         compiler_params=params,
         cost_estimate=cost(half),
         name="last",
-    )(moved[2], moved[3], first, rotated, *state)
+    )(moved[2], moved[3], early, first, rotated, *state)
 
 
 def solution(mesh):

time: 20.2 us -> 20 us (0.990)
  the two profiles are of different devices: /device:TPU:0 before, /device:TPU:1 now
where the time goes in v12:
time: 20 us; the launch traced here: 19.8 us
  starting transfers between devices  13.9 us (70%)
  Pallas kernels  4.79 us (24%)
  other arithmetic  0.89 us (4%)
    ppermute x10, starting transfers between devices, permute(): return lax.ppermute(value, 'pb', pairs)  13.2 us
    pallas_call x1, Pallas kernels, folded(): pl.pallas_call(functools.partial(fold_kernel, count, scale, width, stage)...  1.67 us
    pallas_call x1, Pallas kernels, per_device(): pl.pallas_call(functools.partial(last_kernel, count, scale, width), out_s...  1.35 us
    concatenate x1, other arithmetic, per_device(): jnp.concatenate([keys, values])  0.89 us
    pallas_call x1, Pallas kernels, per_device(): pl.pallas_call(functools.partial(near_kernel, scale, width), out_shape=sh...  0.86 us
    ppermute x1, starting transfers between devices, per_device(): side = lax.ppermute(side, ('grp', 'pb'), pairs)  0.67 us
  transfers between devices with their start and end apart: 11, of which 1 were waited for; matrix products, arithmetic and copies ran while one was open for 0% of the time, Pallas kernels for 16%

profile of v12, /device:TPU:1, one launch (start us, length us, event | category | flops | bytes accessed | tf_op | source)
XLA Modules:
  0.0 19.8 jit_solution(3333083639533697869)
XLA Ops:
  0.0 0.9 %pad_maximum_fusion.both_ref = bf16[512,128]{1,0:T(8,128)(2,1)S(1)} fusion(bf16[256,128]{1,0:T(8,128)(2,1)} %param.7, bf16[256,128]{1,0:T(8,128)(2,1)} %param.6), kind=kLoop, calls=%fused_computation | loop fusion | flops 262144 | bytes 262144 | tf_op jit(solution)/shard_map/concatenate | solution.py:336
  0.9 0.1 index.1
  1.0 0.0 copy-start
  1.1 0.1 pack.1
  1.2 2.2 %collective-permute-start = (bf16[128,256]{1,0:T(8,128)(2,1)S(1)}, bf16[128,256]{1,0:T(8,128)(2,1)S(1)}, u32[]{:S(2)}, u32[]{:S(2)}) collective-permute-start(bf16[128,256]{1,0:T(8,128)(2,1)S(1)} %get-tuple-element.37), channel_id=1, source_target_pairs={{0,4},{1,5},{2,6},{3,7},{4,8},{5,9},{6,10},{7,11},{8,12},{9,13},{1... | collective-permute-start | bytes 196616 | tf_op jit(solution)/shard_map/ppermute | solution.py:327
  3.4 2.3 %collective-permute-start.1 = (bf16[128,256]{1,0:T(8,128)(2,1)S(1)}, bf16[128,256]{1,0:T(8,128)(2,1)S(1)}, u32[]{:S(2)}, u32[]{:S(2)}) collective-permute-start(bf16[128,256]{1,0:T(8,128)(2,1)S(1)} %get-tuple-element.38), channel_id=1, source_target_pairs={{0,8},{1,9},{2,10},{3,11},{4,12},{5,13},{6,14},{7,15},{8,0},{9,1},... | collective-permute-start | bytes 196616 | tf_op jit(solution)/shard_map/ppermute | solution.py:327
  5.7 1.1 %collective-permute-start.2 = (bf16[128,256]{1,0:T(8,128)(2,1)S(1)}, bf16[128,256]{1,0:T(8,128)(2,1)S(1)}, u32[]{:S(2)}, u32[]{:S(2)}) collective-permute-start(bf16[128,256]{1,0:T(8,128)(2,1)S(1)} %get-tuple-element.39), channel_id=1, source_target_pairs={{0,12},{1,13},{2,14},{3,15},{4,0},{5,1},{6,2},{7,3},{8,4},{9,5},{1... | collective-permute-start | bytes 196616 | tf_op jit(solution)/shard_map/ppermute | solution.py:327
  6.7 0.1 pack_own.1
  6.8 1.6 %collective-permute-start.7 = (bf16[160,256]{1,0:T(8,128)(2,1)S(1)}, bf16[160,256]{1,0:T(8,128)(2,1)S(1)}, u32[]{:S(2)}, u32[]{:S(2)}) collective-permute-start(bf16[160,256]{1,0:T(8,128)(2,1)S(1)} %get-tuple-element.48), channel_id=1, source_target_pairs={{0,1},{1,0},{2,3},{3,2},{4,5},{5,4},{6,7},{7,6},{8,9},{9,8},{10,11... | collective-permute-start | bytes 245768 | tf_op jit(solution)/shard_map/ppermute | solution.py:327
  8.4 1.2 %collective-permute-start.8 = (bf16[128,256]{1,0:T(8,128)(2,1)S(1)}, bf16[128,256]{1,0:T(8,128)(2,1)S(1)}, u32[]{:S(2)}, u32[]{:S(2)}) collective-permute-start(bf16[128,256]{1,0:T(8,128)(2,1)S(1)} %get-tuple-element.49), channel_id=1, source_target_pairs={{0,2},{1,3},{2,0},{3,1},{4,6},{5,7},{6,4},{7,5},{8,10},{9,11},{10,... | collective-permute-start | bytes 196616 | tf_op jit(solution)/shard_map/ppermute | solution.py:327
  9.7 0.0 collective-permute-done.refs_0_
  9.7 0.7 %collective-permute-start.10 = (bf16[128,256]{1,0:T(8,128)(2,1)S(1)}, bf16[128,256]{1,0:T(8,128)(2,1)S(1)}, u32[]{:S(2)}, u32[]{:S(2)}) collective-permute-start(bf16[128,256]{1,0:T(8,128)(2,1)S(1)} %get-tuple-element.50), channel_id=1, source_target_pairs={{1,2},{2,1},{3,4},{4,3},{5,6},{6,5},{7,8},{8,7},{9,10},{10,9},{11,... | collective-permute-start | bytes 196616 | tf_op jit(solution)/shard_map/ppermute | solution.py:384
  10.3 0.3 %rotate.1.rot_ref.refs_7_ = bf16[2,1024,128]{2,1,0:T(8,128)(2,1)S(1)} custom-call(bf16[256,1024]{1,0:T(8,128)(2,1)S(1)} %copy-done, bf16[128,128]{1,0:T(8,128)(2,1)S(1)} %copy-done.1), custom_call_target="tpu_custom_call" | custom-call | flops 67108864 | bytes 2000000 | tf_op jit(solution)/shard_map/rotate/pallas_call | solution.py:368
  10.6 0.1 collective-permute-done.1.refs_1_
  10.7 0.0 collective-permute-done.2.refs_2_
  10.7 0.1 select.1
  10.8 1.2 %collective-permute-start.6 = (bf16[192,256]{1,0:T(8,128)(2,1)S(1)}, bf16[192,256]{1,0:T(8,128)(2,1)S(1)}, u32[]{:S(2)}, u32[]{:S(2)}) collective-permute-start(bf16[192,256]{1,0:T(8,128)(2,1)S(1)} %get-tuple-element.47), channel_id=1, source_target_pairs={{0,1},{1,0},{2,3},{3,2},{4,5},{5,4},{6,7},{7,6},{8,9},{9,8},{10,11... | collective-permute-start | bytes 294920 | tf_op jit(solution)/shard_map/ppermute | solution.py:327
  12.0 1.0 %collective-permute-start.3 = (bf16[192,256]{1,0:T(8,128)(2,1)S(1)}, bf16[192,256]{1,0:T(8,128)(2,1)S(1)}, u32[]{:S(2)}, u32[]{:S(2)}) collective-permute-start(bf16[192,256]{1,0:T(8,128)(2,1)S(1)} %get-tuple-element.43), channel_id=1, source_target_pairs={{0,2},{1,3},{2,0},{3,1},{4,6},{5,7},{6,4},{7,5},{8,10},{9,11},{10,... | collective-permute-start | bytes 294920 | tf_op jit(solution)/shard_map/ppermute | solution.py:327
  13.1 2.1 %collective-permute-start.4 = (bf16[96,256]{1,0:T(8,128)(2,1)S(1)}, bf16[96,256]{1,0:T(8,128)(2,1)S(1)}, u32[]{:S(2)}, u32[]{:S(2)}) collective-permute-start(bf16[96,256]{1,0:T(8,128)(2,1)S(1)} %get-tuple-element.44), channel_id=1, source_target_pairs={{0,3},{1,2},{2,1},{3,0},{4,7},{5,6},{6,5},{7,4},{8,11},{9,10},{10,... | collective-permute-start | bytes 147464 | tf_op jit(solution)/shard_map/ppermute | solution.py:327
  15.2 0.5 %collective-permute-start.9 = (bf16[64,256]{1,0:T(8,128)(2,1)S(1)}, bf16[64,256]{1,0:T(8,128)(2,1)S(1)}, u32[]{:S(2)}, u32[]{:S(2)}) collective-permute-start(bf16[64,256]{1,0:T(8,128)(2,1)S(1)} %slice.4), channel_id=1, source_target_pairs={{0,1},{1,0},{2,3},{3,2},{4,5},{5,4},{6,7},{7,6},{8,9},{9,8},{10,11... | collective-permute-start | bytes 98312 | tf_op jit(solution)/shard_map/ppermute | solution.py:327
  15.7 0.9 %near.1 = (f32[2,1,1024]{2,1,0:T(1,128)S(1)}, f32[2,1,1024]{2,1,0:T(1,128)S(1)}, f32[2,128,1024]{2,1,0:T(8,128)S(1)}) custom-call(bf16[256,256]{1,0:T(8,128)(2,1)S(1)} %get-tuple-element.51.kv_ref.refs_6_, bf16[2,1024,128]{2,1,0:T(8,128)(2,1)S(1)} %rotate.1.rot_ref.refs_7_), custom_call_target="tpu_custom_call" | custom-call | flops 134217728 | bytes 4000000 | tf_op jit(solution)/shard_map/near/pallas_call | solution.py:405
  16.6 1.7 %fold0.1 = (f32[2,1,1024]{2,1,0:T(1,128)S(1)}, f32[2,1,1024]{2,1,0:T(1,128)S(1)}, f32[2,128,1024]{2,1,0:T(8,128)S(1)}) custom-call(bf16[224,256]{1,0:T(8,128)(2,1)S(1)} %get-tuple-element.46.refs_0_, bf16[192,256]{1,0:T(8,128)(2,1)S(1)} %collective-permute-done.6.refs_1_, ...), custom_call_target="tpu_custom_call", output_to_operand_aliasing={{0}: (8, {}), {1}: (9, {}), {2}: (10, {})} | custom-call | flops 134217728 | bytes 4000000 | tf_op jit(solution)/shard_map/fold0/pallas_call | solution.py:416
  18.3 0.2 close.1.first_ref
  18.5 1.4 %last.1 = bf16[256,1024]{1,0:T(8,128)(2,1)} custom-call(bf16[192,256]{1,0:T(8,128)(2,1)S(1)} %collective-permute-done.3.second_ref, bf16[96,256]{1,0:T(8,128)(2,1)S(1)} %collective-permute-done.4.third_ref, bf16[96,256]{1,0:T(8,128)(2,1)S(1)} %collective-permute-done.5.early_ref, bf16[128,1024]{1,0:T(8,128)(2,1)S(1)} %close.1.first_ref, ...), custom_call_target="tpu_custom_call" | custom-call | flops 134217728 | bytes 4000000 | tf_op jit(solution)/shard_map/last/pallas_call | solution.py:436
  (15 shorter events, 0.0 us)
Async XLA Ops:
  0.0 0.9 %copy-start.2 = (s32[32,16]{0,1:T(8,128)S(1)}, s32[32,16]{0,1:T(8,128)}, u32[]{:S(2)}) copy-start(s32[32,16]{0,1:T(8,128)} %param.9) | copy-start | bytes 6148
  1.0 9.3 %copy-start = (bf16[256,1024]{1,0:T(8,128)(2,1)S(1)}, bf16[256,1024]{1,0:T(8,128)(2,1)}, u32[]{:S(2)}) copy-start(bf16[256,1024]{1,0:T(8,128)(2,1)} %q_ref.1) | copy-start | bytes 1572868
  1.2 8.5 %collective-permute-start = (bf16[128,256]{1,0:T(8,128)(2,1)S(1)}, bf16[128,256]{1,0:T(8,128)(2,1)S(1)}, u32[]{:S(2)}, u32[]{:S(2)}) collective-permute-start(bf16[128,256]{1,0:T(8,128)(2,1)S(1)} %get-tuple-element.37), channel_id=1, source_target_pairs={{0,4},{1,5},{2,6},{3,7},{4,8},{5,9},{6,10},{7,11},{8,12},{9,13},{1... | collective-permute-start | bytes 196616 | tf_op jit(solution)/shard_map/ppermute | solution.py:327
  3.4 7.3 %collective-permute-start.1 = (bf16[128,256]{1,0:T(8,128)(2,1)S(1)}, bf16[128,256]{1,0:T(8,128)(2,1)S(1)}, u32[]{:S(2)}, u32[]{:S(2)}) collective-permute-start(bf16[128,256]{1,0:T(8,128)(2,1)S(1)} %get-tuple-element.38), channel_id=1, source_target_pairs={{0,8},{1,9},{2,10},{3,11},{4,12},{5,13},{6,14},{7,15},{8,0},{9,1},... | collective-permute-start | bytes 196616 | tf_op jit(solution)/shard_map/ppermute | solution.py:327
  5.7 4.7 %copy-start.1 = (bf16[128,128]{1,0:T(8,128)(2,1)S(1)}, bf16[128,128]{1,0:T(8,128)(2,1)}, u32[]{:S(2)}) copy-start(bf16[128,128]{1,0:T(8,128)(2,1)} %basis_ref.1) | copy-start | bytes 98308
  5.7 5.0 %collective-permute-start.2 = (bf16[128,256]{1,0:T(8,128)(2,1)S(1)}, bf16[128,256]{1,0:T(8,128)(2,1)S(1)}, u32[]{:S(2)}, u32[]{:S(2)}) collective-permute-start(bf16[128,256]{1,0:T(8,128)(2,1)S(1)} %get-tuple-element.39), channel_id=1, source_target_pairs={{0,12},{1,13},{2,14},{3,15},{4,0},{5,1},{6,2},{7,3},{8,4},{9,5},{1... | collective-permute-start | bytes 196616 | tf_op jit(solution)/shard_map/ppermute | solution.py:327
  6.8 8.4 %collective-permute-start.7 = (bf16[160,256]{1,0:T(8,128)(2,1)S(1)}, bf16[160,256]{1,0:T(8,128)(2,1)S(1)}, u32[]{:S(2)}, u32[]{:S(2)}) collective-permute-start(bf16[160,256]{1,0:T(8,128)(2,1)S(1)} %get-tuple-element.48), channel_id=1, source_target_pairs={{0,1},{1,0},{2,3},{3,2},{4,5},{5,4},{6,7},{7,6},{8,9},{9,8},{10,11... | collective-permute-start | bytes 245768 | tf_op jit(solution)/shard_map/ppermute | solution.py:327
  8.4 4.7 %collective-permute-start.8 = (bf16[128,256]{1,0:T(8,128)(2,1)S(1)}, bf16[128,256]{1,0:T(8,128)(2,1)S(1)}, u32[]{:S(2)}, u32[]{:S(2)}) collective-permute-start(bf16[128,256]{1,0:T(8,128)(2,1)S(1)} %get-tuple-element.49), channel_id=1, source_target_pairs={{0,2},{1,3},{2,0},{3,1},{4,6},{5,7},{6,4},{7,5},{8,10},{9,11},{10,... | collective-permute-start | bytes 196616 | tf_op jit(solution)/shard_map/ppermute | solution.py:327
  9.7 5.5 %collective-permute-start.10 = (bf16[128,256]{1,0:T(8,128)(2,1)S(1)}, bf16[128,256]{1,0:T(8,128)(2,1)S(1)}, u32[]{:S(2)}, u32[]{:S(2)}) collective-permute-start(bf16[128,256]{1,0:T(8,128)(2,1)S(1)} %get-tuple-element.50), channel_id=1, source_target_pairs={{1,2},{2,1},{3,4},{4,3},{5,6},{6,5},{7,8},{8,7},{9,10},{10,9},{11,... | collective-permute-start | bytes 196616 | tf_op jit(solution)/shard_map/ppermute | solution.py:384
  10.8 5.8 %collective-permute-start.6 = (bf16[192,256]{1,0:T(8,128)(2,1)S(1)}, bf16[192,256]{1,0:T(8,128)(2,1)S(1)}, u32[]{:S(2)}, u32[]{:S(2)}) collective-permute-start(bf16[192,256]{1,0:T(8,128)(2,1)S(1)} %get-tuple-element.47), channel_id=1, source_target_pairs={{0,1},{1,0},{2,3},{3,2},{4,5},{5,4},{6,7},{7,6},{8,9},{9,8},{10,11... | collective-permute-start | bytes 294920 | tf_op jit(solution)/shard_map/ppermute | solution.py:327
  12.0 6.4 %collective-permute-start.3 = (bf16[192,256]{1,0:T(8,128)(2,1)S(1)}, bf16[192,256]{1,0:T(8,128)(2,1)S(1)}, u32[]{:S(2)}, u32[]{:S(2)}) collective-permute-start(bf16[192,256]{1,0:T(8,128)(2,1)S(1)} %get-tuple-element.43), channel_id=1, source_target_pairs={{0,2},{1,3},{2,0},{3,1},{4,6},{5,7},{6,4},{7,5},{8,10},{9,11},{10,... | collective-permute-start | bytes 294920 | tf_op jit(solution)/shard_map/ppermute | solution.py:327
  13.1 5.4 %collective-permute-start.4 = (bf16[96,256]{1,0:T(8,128)(2,1)S(1)}, bf16[96,256]{1,0:T(8,128)(2,1)S(1)}, u32[]{:S(2)}, u32[]{:S(2)}) collective-permute-start(bf16[96,256]{1,0:T(8,128)(2,1)S(1)} %get-tuple-element.44), channel_id=1, source_target_pairs={{0,3},{1,2},{2,1},{3,0},{4,7},{5,6},{6,5},{7,4},{8,11},{9,10},{10,... | collective-permute-start | bytes 147464 | tf_op jit(solution)/shard_map/ppermute | solution.py:327
  15.2 3.2 %collective-permute-start.5 = (bf16[96,256]{1,0:T(8,128)(2,1)S(1)}, bf16[96,256]{1,0:T(8,128)(2,1)S(1)}, u32[]{:S(2)}, u32[]{:S(2)}) collective-permute-start(bf16[96,256]{1,0:T(8,128)(2,1)S(1)} %get-tuple-element.45), channel_id=1, source_target_pairs={{0,1},{1,0},{2,3},{3,2},{4,7},{5,6},{6,5},{7,4},{8,11},{9,10},{10,... | collective-permute-start | bytes 147464 | tf_op jit(solution)/shard_map/ppermute | solution.py:327
  15.2 1.4 %collective-permute-start.9 = (bf16[64,256]{1,0:T(8,128)(2,1)S(1)}, bf16[64,256]{1,0:T(8,128)(2,1)S(1)}, u32[]{:S(2)}, u32[]{:S(2)}) collective-permute-start(bf16[64,256]{1,0:T(8,128)(2,1)S(1)} %slice.4), channel_id=1, source_target_pairs={{0,1},{1,0},{2,3},{3,2},{4,5},{5,4},{6,7},{7,6},{8,9},{9,8},{10,11... | collective-permute-start | bytes 98312 | tf_op jit(solution)/shard_map/ppermute | solution.py:327

commit v13 on v12

--- a/solution.py
+++ b/solution.py
@@ -214,7 +214,7 @@
     me, z, _ = place(count)
     rest = (count // PLANE - 1) * KB
 
-    def run(block, light=False):
+    def run(block, light=False, one=False):
         masks = [usable(count, block, m) for m in range(PLANE)]
         if stage == 0:
             mine_ref, next_ref, beside_ref, over_ref, passed_ref, side_ref, kv_ref = come
@@ -231,6 +231,9 @@
                 masks.append(None)
             if light:
                 parts, masks = parts[2:], masks[2 * rest // KB :]
+            if one:
+                parts[:2] = [part[:KB] for part in parts[:2]]
+                masks = [masks[0], masks[rest // KB]] + masks[2 * rest // KB :]
             parts.append(jnp.where(me % 2 == block, side, beside_ref[:half]))
             masks += [None] * (half // KB)
         else:
@@ -243,8 +246,9 @@
         fold(jnp.concatenate(parts, axis=0), masks, scale, width, block, rot_ref, old, save)
 
     run(1)
-    pl.when(z >= 1)(lambda: run(0))
+    pl.when(z >= 2)(lambda: run(0))
     if stage == 0:
+        pl.when(z == 1)(lambda: run(0, one=True))
         pl.when((z < 1) & (me >= 1))(lambda: run(0, True))
 
 
@@ -282,12 +286,15 @@
         put_heads(done_ref, block * half, half, step, l, acc)
         piece(block, step).start()
 
-    def add(block):
+    def add(block, one=False):
         rest = third_ref.shape[0]
         part = slice((1 - block) * rest, (2 - block) * rest)
         third = third_ref if block == 1 else early_ref
         kv = jnp.concatenate([second_ref[part], third[...]], axis=0)
         masks = usable(count, block, 2)[1:] + usable(count, block, PLANE - 1)[1:]
+        if one:
+            kv = jnp.concatenate([kv[:KB], kv[rest : rest + KB]], axis=0)
+            masks = [masks[0], masks[rest // KB]]
         fold(kv, masks, scale, width, block, rot_ref, old, lambda step, m, l, acc: finish(block, step, l, acc))
 
     @pl.when(z < 1)
@@ -296,7 +303,8 @@
             piece(0, step, first_ref).start()
 
     add(1)
-    pl.when(z >= 1)(lambda: add(0))
+    pl.when(z == 1)(lambda: add(0, one=True))
+    pl.when(z >= 2)(lambda: add(0))
 
     for block in range(2):
         for step in range(rot_ref.shape[1] // width):

time: 20 us -> 20 us (level)
  no operation moved by 1% of the time
where the time goes in v13:
time: 20 us; the launch traced here: 19.8 us
  starting transfers between devices  13.9 us (70%)
  Pallas kernels  4.79 us (24%)
  other arithmetic  0.89 us (4%)
    ppermute x10, starting transfers between devices, permute(): return lax.ppermute(value, 'pb', pairs)  13.2 us
    pallas_call x1, Pallas kernels, folded(): pl.pallas_call(functools.partial(fold_kernel, count, scale, width, stage)...  1.67 us
    pallas_call x1, Pallas kernels, per_device(): pl.pallas_call(functools.partial(last_kernel, count, scale, width), out_s...  1.35 us
    concatenate x1, other arithmetic, per_device(): jnp.concatenate([keys, values])  0.89 us
    pallas_call x1, Pallas kernels, per_device(): pl.pallas_call(functools.partial(near_kernel, scale, width), out_shape=sh...  0.86 us
    ppermute x1, starting transfers between devices, per_device(): side = lax.ppermute(side, ('grp', 'pb'), pairs)  0.67 us
  transfers between devices with their start and end apart: 11, of which 1 were waited for; matrix products, arithmetic and copies ran while one was open for 0% of the time, Pallas kernels for 16%

profile of v13, /device:TPU:1, one launch (start us, length us, event | category | flops | bytes accessed | tf_op | source)
XLA Modules:
  0.0 19.8 jit_solution(6921910912943078557)
XLA Ops:
  0.0 0.9 %pad_maximum_fusion.both_ref = bf16[512,128]{1,0:T(8,128)(2,1)S(1)} fusion(bf16[256,128]{1,0:T(8,128)(2,1)} %param.7, bf16[256,128]{1,0:T(8,128)(2,1)} %param.6), kind=kLoop, calls=%fused_computation | loop fusion | flops 262144 | bytes 262144 | tf_op jit(solution)/shard_map/concatenate | solution.py:344
  0.9 0.1 index.1
  1.0 0.0 copy-start
  1.1 0.1 pack.1
  1.2 2.2 %collective-permute-start = (bf16[128,256]{1,0:T(8,128)(2,1)S(1)}, bf16[128,256]{1,0:T(8,128)(2,1)S(1)}, u32[]{:S(2)}, u32[]{:S(2)}) collective-permute-start(bf16[128,256]{1,0:T(8,128)(2,1)S(1)} %get-tuple-element.37), channel_id=1, source_target_pairs={{0,4},{1,5},{2,6},{3,7},{4,8},{5,9},{6,10},{7,11},{8,12},{9,13},{1... | collective-permute-start | bytes 196616 | tf_op jit(solution)/shard_map/ppermute | solution.py:335
  3.4 2.3 %collective-permute-start.1 = (bf16[128,256]{1,0:T(8,128)(2,1)S(1)}, bf16[128,256]{1,0:T(8,128)(2,1)S(1)}, u32[]{:S(2)}, u32[]{:S(2)}) collective-permute-start(bf16[128,256]{1,0:T(8,128)(2,1)S(1)} %get-tuple-element.38), channel_id=1, source_target_pairs={{0,8},{1,9},{2,10},{3,11},{4,12},{5,13},{6,14},{7,15},{8,0},{9,1},... | collective-permute-start | bytes 196616 | tf_op jit(solution)/shard_map/ppermute | solution.py:335
  5.7 1.1 %collective-permute-start.2 = (bf16[128,256]{1,0:T(8,128)(2,1)S(1)}, bf16[128,256]{1,0:T(8,128)(2,1)S(1)}, u32[]{:S(2)}, u32[]{:S(2)}) collective-permute-start(bf16[128,256]{1,0:T(8,128)(2,1)S(1)} %get-tuple-element.39), channel_id=1, source_target_pairs={{0,12},{1,13},{2,14},{3,15},{4,0},{5,1},{6,2},{7,3},{8,4},{9,5},{1... | collective-permute-start | bytes 196616 | tf_op jit(solution)/shard_map/ppermute | solution.py:335
  6.7 0.1 pack_own.1
  6.8 1.6 %collective-permute-start.7 = (bf16[160,256]{1,0:T(8,128)(2,1)S(1)}, bf16[160,256]{1,0:T(8,128)(2,1)S(1)}, u32[]{:S(2)}, u32[]{:S(2)}) collective-permute-start(bf16[160,256]{1,0:T(8,128)(2,1)S(1)} %get-tuple-element.48), channel_id=1, source_target_pairs={{0,1},{1,0},{2,3},{3,2},{4,5},{5,4},{6,7},{7,6},{8,9},{9,8},{10,11... | collective-permute-start | bytes 245768 | tf_op jit(solution)/shard_map/ppermute | solution.py:335
  8.4 1.2 %collective-permute-start.8 = (bf16[128,256]{1,0:T(8,128)(2,1)S(1)}, bf16[128,256]{1,0:T(8,128)(2,1)S(1)}, u32[]{:S(2)}, u32[]{:S(2)}) collective-permute-start(bf16[128,256]{1,0:T(8,128)(2,1)S(1)} %get-tuple-element.49), channel_id=1, source_target_pairs={{0,2},{1,3},{2,0},{3,1},{4,6},{5,7},{6,4},{7,5},{8,10},{9,11},{10,... | collective-permute-start | bytes 196616 | tf_op jit(solution)/shard_map/ppermute | solution.py:335
  9.7 0.0 collective-permute-done.refs_0_
  9.7 0.7 %collective-permute-start.10 = (bf16[128,256]{1,0:T(8,128)(2,1)S(1)}, bf16[128,256]{1,0:T(8,128)(2,1)S(1)}, u32[]{:S(2)}, u32[]{:S(2)}) collective-permute-start(bf16[128,256]{1,0:T(8,128)(2,1)S(1)} %get-tuple-element.50), channel_id=1, source_target_pairs={{1,2},{2,1},{3,4},{4,3},{5,6},{6,5},{7,8},{8,7},{9,10},{10,9},{11,... | collective-permute-start | bytes 196616 | tf_op jit(solution)/shard_map/ppermute | solution.py:392
  10.3 0.3 %rotate.1.rot_ref.refs_7_ = bf16[2,1024,128]{2,1,0:T(8,128)(2,1)S(1)} custom-call(bf16[256,1024]{1,0:T(8,128)(2,1)S(1)} %copy-done, bf16[128,128]{1,0:T(8,128)(2,1)S(1)} %copy-done.1), custom_call_target="tpu_custom_call" | custom-call | flops 67108864 | bytes 2000000 | tf_op jit(solution)/shard_map/rotate/pallas_call | solution.py:376
  10.6 0.1 collective-permute-done.1.refs_1_
  10.7 0.0 collective-permute-done.2.refs_2_
  10.7 0.1 select.1
  10.8 1.2 %collective-permute-start.6 = (bf16[192,256]{1,0:T(8,128)(2,1)S(1)}, bf16[192,256]{1,0:T(8,128)(2,1)S(1)}, u32[]{:S(2)}, u32[]{:S(2)}) collective-permute-start(bf16[192,256]{1,0:T(8,128)(2,1)S(1)} %get-tuple-element.47), channel_id=1, source_target_pairs={{0,1},{1,0},{2,3},{3,2},{4,5},{5,4},{6,7},{7,6},{8,9},{9,8},{10,11... | collective-permute-start | bytes 294920 | tf_op jit(solution)/shard_map/ppermute | solution.py:335
  12.0 1.0 %collective-permute-start.3 = (bf16[192,256]{1,0:T(8,128)(2,1)S(1)}, bf16[192,256]{1,0:T(8,128)(2,1)S(1)}, u32[]{:S(2)}, u32[]{:S(2)}) collective-permute-start(bf16[192,256]{1,0:T(8,128)(2,1)S(1)} %get-tuple-element.43), channel_id=1, source_target_pairs={{0,2},{1,3},{2,0},{3,1},{4,6},{5,7},{6,4},{7,5},{8,10},{9,11},{10,... | collective-permute-start | bytes 294920 | tf_op jit(solution)/shard_map/ppermute | solution.py:335
  13.1 2.1 %collective-permute-start.4 = (bf16[96,256]{1,0:T(8,128)(2,1)S(1)}, bf16[96,256]{1,0:T(8,128)(2,1)S(1)}, u32[]{:S(2)}, u32[]{:S(2)}) collective-permute-start(bf16[96,256]{1,0:T(8,128)(2,1)S(1)} %get-tuple-element.44), channel_id=1, source_target_pairs={{0,3},{1,2},{2,1},{3,0},{4,7},{5,6},{6,5},{7,4},{8,11},{9,10},{10,... | collective-permute-start | bytes 147464 | tf_op jit(solution)/shard_map/ppermute | solution.py:335
  15.2 0.5 %collective-permute-start.9 = (bf16[64,256]{1,0:T(8,128)(2,1)S(1)}, bf16[64,256]{1,0:T(8,128)(2,1)S(1)}, u32[]{:S(2)}, u32[]{:S(2)}) collective-permute-start(bf16[64,256]{1,0:T(8,128)(2,1)S(1)} %slice.4), channel_id=1, source_target_pairs={{0,1},{1,0},{2,3},{3,2},{4,5},{5,4},{6,7},{7,6},{8,9},{9,8},{10,11... | collective-permute-start | bytes 98312 | tf_op jit(solution)/shard_map/ppermute | solution.py:335
  15.7 0.9 %near.1 = (f32[2,1,1024]{2,1,0:T(1,128)S(1)}, f32[2,1,1024]{2,1,0:T(1,128)S(1)}, f32[2,128,1024]{2,1,0:T(8,128)S(1)}) custom-call(bf16[256,256]{1,0:T(8,128)(2,1)S(1)} %get-tuple-element.51.kv_ref.refs_6_, bf16[2,1024,128]{2,1,0:T(8,128)(2,1)S(1)} %rotate.1.rot_ref.refs_7_), custom_call_target="tpu_custom_call" | custom-call | flops 134217728 | bytes 4000000 | tf_op jit(solution)/shard_map/near/pallas_call | solution.py:413
  16.6 1.7 %fold0.1 = (f32[2,1,1024]{2,1,0:T(1,128)S(1)}, f32[2,1,1024]{2,1,0:T(1,128)S(1)}, f32[2,128,1024]{2,1,0:T(8,128)S(1)}) custom-call(bf16[224,256]{1,0:T(8,128)(2,1)S(1)} %get-tuple-element.46.refs_0_, bf16[192,256]{1,0:T(8,128)(2,1)S(1)} %collective-permute-done.6.refs_1_, ...), custom_call_target="tpu_custom_call", output_to_operand_aliasing={{0}: (8, {}), {1}: (9, {}), {2}: (10, {})} | custom-call | flops 134217728 | bytes 4000000 | tf_op jit(solution)/shard_map/fold0/pallas_call | solution.py:424
  18.3 0.2 close.1.first_ref
  18.5 1.4 %last.1 = bf16[256,1024]{1,0:T(8,128)(2,1)} custom-call(bf16[192,256]{1,0:T(8,128)(2,1)S(1)} %collective-permute-done.3.second_ref, bf16[96,256]{1,0:T(8,128)(2,1)S(1)} %collective-permute-done.4.third_ref, bf16[96,256]{1,0:T(8,128)(2,1)S(1)} %collective-permute-done.5.early_ref, bf16[128,1024]{1,0:T(8,128)(2,1)S(1)} %close.1.first_ref, ...), custom_call_target="tpu_custom_call" | custom-call | flops 134217728 | bytes 4000000 | tf_op jit(solution)/shard_map/last/pallas_call | solution.py:444
  (15 shorter events, 0.0 us)
Async XLA Ops:
  0.0 0.9 %copy-start.2 = (s32[32,16]{0,1:T(8,128)S(1)}, s32[32,16]{0,1:T(8,128)}, u32[]{:S(2)}) copy-start(s32[32,16]{0,1:T(8,128)} %param.9) | copy-start | bytes 6148
  1.0 9.3 %copy-start = (bf16[256,1024]{1,0:T(8,128)(2,1)S(1)}, bf16[256,1024]{1,0:T(8,128)(2,1)}, u32[]{:S(2)}) copy-start(bf16[256,1024]{1,0:T(8,128)(2,1)} %q_ref.1) | copy-start | bytes 1572868
  1.2 8.5 %collective-permute-start = (bf16[128,256]{1,0:T(8,128)(2,1)S(1)}, bf16[128,256]{1,0:T(8,128)(2,1)S(1)}, u32[]{:S(2)}, u32[]{:S(2)}) collective-permute-start(bf16[128,256]{1,0:T(8,128)(2,1)S(1)} %get-tuple-element.37), channel_id=1, source_target_pairs={{0,4},{1,5},{2,6},{3,7},{4,8},{5,9},{6,10},{7,11},{8,12},{9,13},{1... | collective-permute-start | bytes 196616 | tf_op jit(solution)/shard_map/ppermute | solution.py:335
  3.4 7.3 %collective-permute-start.1 = (bf16[128,256]{1,0:T(8,128)(2,1)S(1)}, bf16[128,256]{1,0:T(8,128)(2,1)S(1)}, u32[]{:S(2)}, u32[]{:S(2)}) collective-permute-start(bf16[128,256]{1,0:T(8,128)(2,1)S(1)} %get-tuple-element.38), channel_id=1, source_target_pairs={{0,8},{1,9},{2,10},{3,11},{4,12},{5,13},{6,14},{7,15},{8,0},{9,1},... | collective-permute-start | bytes 196616 | tf_op jit(solution)/shard_map/ppermute | solution.py:335
  5.7 4.7 %copy-start.1 = (bf16[128,128]{1,0:T(8,128)(2,1)S(1)}, bf16[128,128]{1,0:T(8,128)(2,1)}, u32[]{:S(2)}) copy-start(bf16[128,128]{1,0:T(8,128)(2,1)} %basis_ref.1) | copy-start | bytes 98308
  5.7 5.0 %collective-permute-start.2 = (bf16[128,256]{1,0:T(8,128)(2,1)S(1)}, bf16[128,256]{1,0:T(8,128)(2,1)S(1)}, u32[]{:S(2)}, u32[]{:S(2)}) collective-permute-start(bf16[128,256]{1,0:T(8,128)(2,1)S(1)} %get-tuple-element.39), channel_id=1, source_target_pairs={{0,12},{1,13},{2,14},{3,15},{4,0},{5,1},{6,2},{7,3},{8,4},{9,5},{1... | collective-permute-start | bytes 196616 | tf_op jit(solution)/shard_map/ppermute | solution.py:335
  6.8 8.4 %collective-permute-start.7 = (bf16[160,256]{1,0:T(8,128)(2,1)S(1)}, bf16[160,256]{1,0:T(8,128)(2,1)S(1)}, u32[]{:S(2)}, u32[]{:S(2)}) collective-permute-start(bf16[160,256]{1,0:T(8,128)(2,1)S(1)} %get-tuple-element.48), channel_id=1, source_target_pairs={{0,1},{1,0},{2,3},{3,2},{4,5},{5,4},{6,7},{7,6},{8,9},{9,8},{10,11... | collective-permute-start | bytes 245768 | tf_op jit(solution)/shard_map/ppermute | solution.py:335
  8.4 4.7 %collective-permute-start.8 = (bf16[128,256]{1,0:T(8,128)(2,1)S(1)}, bf16[128,256]{1,0:T(8,128)(2,1)S(1)}, u32[]{:S(2)}, u32[]{:S(2)}) collective-permute-start(bf16[128,256]{1,0:T(8,128)(2,1)S(1)} %get-tuple-element.49), channel_id=1, source_target_pairs={{0,2},{1,3},{2,0},{3,1},{4,6},{5,7},{6,4},{7,5},{8,10},{9,11},{10,... | collective-permute-start | bytes 196616 | tf_op jit(solution)/shard_map/ppermute | solution.py:335
  9.7 5.5 %collective-permute-start.10 = (bf16[128,256]{1,0:T(8,128)(2,1)S(1)}, bf16[128,256]{1,0:T(8,128)(2,1)S(1)}, u32[]{:S(2)}, u32[]{:S(2)}) collective-permute-start(bf16[128,256]{1,0:T(8,128)(2,1)S(1)} %get-tuple-element.50), channel_id=1, source_target_pairs={{1,2},{2,1},{3,4},{4,3},{5,6},{6,5},{7,8},{8,7},{9,10},{10,9},{11,... | collective-permute-start | bytes 196616 | tf_op jit(solution)/shard_map/ppermute | solution.py:392
  10.8 5.8 %collective-permute-start.6 = (bf16[192,256]{1,0:T(8,128)(2,1)S(1)}, bf16[192,256]{1,0:T(8,128)(2,1)S(1)}, u32[]{:S(2)}, u32[]{:S(2)}) collective-permute-start(bf16[192,256]{1,0:T(8,128)(2,1)S(1)} %get-tuple-element.47), channel_id=1, source_target_pairs={{0,1},{1,0},{2,3},{3,2},{4,5},{5,4},{6,7},{7,6},{8,9},{9,8},{10,11... | collective-permute-start | bytes 294920 | tf_op jit(solution)/shard_map/ppermute | solution.py:335
  12.0 6.4 %collective-permute-start.3 = (bf16[192,256]{1,0:T(8,128)(2,1)S(1)}, bf16[192,256]{1,0:T(8,128)(2,1)S(1)}, u32[]{:S(2)}, u32[]{:S(2)}) collective-permute-start(bf16[192,256]{1,0:T(8,128)(2,1)S(1)} %get-tuple-element.43), channel_id=1, source_target_pairs={{0,2},{1,3},{2,0},{3,1},{4,6},{5,7},{6,4},{7,5},{8,10},{9,11},{10,... | collective-permute-start | bytes 294920 | tf_op jit(solution)/shard_map/ppermute | solution.py:335
  13.1 5.4 %collective-permute-start.4 = (bf16[96,256]{1,0:T(8,128)(2,1)S(1)}, bf16[96,256]{1,0:T(8,128)(2,1)S(1)}, u32[]{:S(2)}, u32[]{:S(2)}) collective-permute-start(bf16[96,256]{1,0:T(8,128)(2,1)S(1)} %get-tuple-element.44), channel_id=1, source_target_pairs={{0,3},{1,2},{2,1},{3,0},{4,7},{5,6},{6,5},{7,4},{8,11},{9,10},{10,... | collective-permute-start | bytes 147464 | tf_op jit(solution)/shard_map/ppermute | solution.py:335
  15.2 3.2 %collective-permute-start.5 = (bf16[96,256]{1,0:T(8,128)(2,1)S(1)}, bf16[96,256]{1,0:T(8,128)(2,1)S(1)}, u32[]{:S(2)}, u32[]{:S(2)}) collective-permute-start(bf16[96,256]{1,0:T(8,128)(2,1)S(1)} %get-tuple-element.45), channel_id=1, source_target_pairs={{0,1},{1,0},{2,3},{3,2},{4,7},{5,6},{6,5},{7,4},{8,11},{9,10},{10,... | collective-permute-start | bytes 147464 | tf_op jit(solution)/shard_map/ppermute | solution.py:335
  15.2 1.4 %collective-permute-start.9 = (bf16[64,256]{1,0:T(8,128)(2,1)S(1)}, bf16[64,256]{1,0:T(8,128)(2,1)S(1)}, u32[]{:S(2)}, u32[]{:S(2)}) collective-permute-start(bf16[64,256]{1,0:T(8,128)(2,1)S(1)} %slice.4), channel_id=1, source_target_pairs={{0,1},{1,0},{2,3},{3,2},{4,5},{5,4},{6,7},{7,6},{8,9},{9,8},{10,11... | collective-permute-start | bytes 98312 | tf_op jit(solution)/shard_map/ppermute | solution.py:335

commit v14 on v13

--- a/solution.py
+++ b/solution.py
@@ -317,7 +317,7 @@
     count = lax.axis_size("pb")
     planes = count // PLANE
     wide = queries.shape[1] // dim * half
-    width = 4 * half
+    width = 2 * half
     scale = dim**-0.5 * math.log2(math.e)
     vmem = pl.BlockSpec(memory_space=pltpu.VMEM)
     params = pltpu.CompilerParams(vmem_limit_bytes=VMEM_BYTES)

time: 20 us -> 19.9 us (level)
  transfers between devices with their start and end apart: 11 -> 11, of which waited for: 1 -> 2; matrix products, arithmetic and copies ran while one was open for 0% -> 0% of each run, Pallas kernels for 16% -> 16%
where the time goes in v14:
time: 19.9 us; the launch traced here: 19.8 us
  starting transfers between devices  13.9 us (70%)
  Pallas kernels  4.71 us (24%)
  other arithmetic  0.89 us (4%)
    ppermute x10, starting transfers between devices, permute(): return lax.ppermute(value, 'pb', pairs)  13.2 us
    pallas_call x1, Pallas kernels, folded(): pl.pallas_call(functools.partial(fold_kernel, count, scale, width, stage)...  1.64 us
    pallas_call x1, Pallas kernels, per_device(): pl.pallas_call(functools.partial(last_kernel, count, scale, width), out_s...  1.35 us
    concatenate x1, other arithmetic, per_device(): jnp.concatenate([keys, values])  0.89 us
    pallas_call x1, Pallas kernels, per_device(): pl.pallas_call(functools.partial(near_kernel, scale, width), out_shape=sh...  0.8 us
    ppermute x1, starting transfers between devices, per_device(): side = lax.ppermute(side, ('grp', 'pb'), pairs)  0.67 us
  transfers between devices with their start and end apart: 11, of which 2 were waited for; matrix products, arithmetic and copies ran while one was open for 0% of the time, Pallas kernels for 16%

profile of v14, /device:TPU:1, one launch (start us, length us, event | category | flops | bytes accessed | tf_op | source)
XLA Modules:
  0.0 19.8 jit_solution(8335327423911735058)
XLA Ops:
  0.0 0.9 %pad_maximum_fusion.both_ref = bf16[512,128]{1,0:T(8,128)(2,1)S(1)} fusion(bf16[256,128]{1,0:T(8,128)(2,1)} %param.7, bf16[256,128]{1,0:T(8,128)(2,1)} %param.6), kind=kLoop, calls=%fused_computation | loop fusion | flops 262144 | bytes 262144 | tf_op jit(solution)/shard_map/concatenate | solution.py:344
  0.9 0.1 index.1
  1.0 0.0 copy-start
  1.1 0.1 pack.1
  1.2 2.2 %collective-permute-start = (bf16[128,256]{1,0:T(8,128)(2,1)S(1)}, bf16[128,256]{1,0:T(8,128)(2,1)S(1)}, u32[]{:S(2)}, u32[]{:S(2)}) collective-permute-start(bf16[128,256]{1,0:T(8,128)(2,1)S(1)} %get-tuple-element.37), channel_id=1, source_target_pairs={{0,4},{1,5},{2,6},{3,7},{4,8},{5,9},{6,10},{7,11},{8,12},{9,13},{1... | collective-permute-start | bytes 196616 | tf_op jit(solution)/shard_map/ppermute | solution.py:335
  3.4 2.3 %collective-permute-start.1 = (bf16[128,256]{1,0:T(8,128)(2,1)S(1)}, bf16[128,256]{1,0:T(8,128)(2,1)S(1)}, u32[]{:S(2)}, u32[]{:S(2)}) collective-permute-start(bf16[128,256]{1,0:T(8,128)(2,1)S(1)} %get-tuple-element.38), channel_id=1, source_target_pairs={{0,8},{1,9},{2,10},{3,11},{4,12},{5,13},{6,14},{7,15},{8,0},{9,1},... | collective-permute-start | bytes 196616 | tf_op jit(solution)/shard_map/ppermute | solution.py:335
  5.7 1.1 %collective-permute-start.2 = (bf16[128,256]{1,0:T(8,128)(2,1)S(1)}, bf16[128,256]{1,0:T(8,128)(2,1)S(1)}, u32[]{:S(2)}, u32[]{:S(2)}) collective-permute-start(bf16[128,256]{1,0:T(8,128)(2,1)S(1)} %get-tuple-element.39), channel_id=1, source_target_pairs={{0,12},{1,13},{2,14},{3,15},{4,0},{5,1},{6,2},{7,3},{8,4},{9,5},{1... | collective-permute-start | bytes 196616 | tf_op jit(solution)/shard_map/ppermute | solution.py:335
  6.7 0.1 pack_own.1
  6.8 1.6 %collective-permute-start.7 = (bf16[160,256]{1,0:T(8,128)(2,1)S(1)}, bf16[160,256]{1,0:T(8,128)(2,1)S(1)}, u32[]{:S(2)}, u32[]{:S(2)}) collective-permute-start(bf16[160,256]{1,0:T(8,128)(2,1)S(1)} %get-tuple-element.48), channel_id=1, source_target_pairs={{0,1},{1,0},{2,3},{3,2},{4,5},{5,4},{6,7},{7,6},{8,9},{9,8},{10,11... | collective-permute-start | bytes 245768 | tf_op jit(solution)/shard_map/ppermute | solution.py:335
  8.4 1.2 %collective-permute-start.8 = (bf16[128,256]{1,0:T(8,128)(2,1)S(1)}, bf16[128,256]{1,0:T(8,128)(2,1)S(1)}, u32[]{:S(2)}, u32[]{:S(2)}) collective-permute-start(bf16[128,256]{1,0:T(8,128)(2,1)S(1)} %get-tuple-element.49), channel_id=1, source_target_pairs={{0,2},{1,3},{2,0},{3,1},{4,6},{5,7},{6,4},{7,5},{8,10},{9,11},{10,... | collective-permute-start | bytes 196616 | tf_op jit(solution)/shard_map/ppermute | solution.py:335
  9.7 0.0 collective-permute-done.refs_0_
  9.7 0.7 %collective-permute-start.10 = (bf16[128,256]{1,0:T(8,128)(2,1)S(1)}, bf16[128,256]{1,0:T(8,128)(2,1)S(1)}, u32[]{:S(2)}, u32[]{:S(2)}) collective-permute-start(bf16[128,256]{1,0:T(8,128)(2,1)S(1)} %get-tuple-element.50), channel_id=1, source_target_pairs={{1,2},{2,1},{3,4},{4,3},{5,6},{6,5},{7,8},{8,7},{9,10},{10,9},{11,... | collective-permute-start | bytes 196616 | tf_op jit(solution)/shard_map/ppermute | solution.py:392
  10.3 0.3 %rotate.1.rot_ref.refs_7_ = bf16[2,1024,128]{2,1,0:T(8,128)(2,1)S(1)} custom-call(bf16[256,1024]{1,0:T(8,128)(2,1)S(1)} %copy-done, bf16[128,128]{1,0:T(8,128)(2,1)S(1)} %copy-done.1), custom_call_target="tpu_custom_call" | custom-call | flops 67108864 | bytes 2000000 | tf_op jit(solution)/shard_map/rotate/pallas_call | solution.py:376
  10.6 0.1 collective-permute-done.1.refs_1_
  10.7 0.1 select.1
  10.8 1.2 %collective-permute-start.6 = (bf16[192,256]{1,0:T(8,128)(2,1)S(1)}, bf16[192,256]{1,0:T(8,128)(2,1)S(1)}, u32[]{:S(2)}, u32[]{:S(2)}) collective-permute-start(bf16[192,256]{1,0:T(8,128)(2,1)S(1)} %get-tuple-element.47), channel_id=1, source_target_pairs={{0,1},{1,0},{2,3},{3,2},{4,5},{5,4},{6,7},{7,6},{8,9},{9,8},{10,11... | collective-permute-start | bytes 294920 | tf_op jit(solution)/shard_map/ppermute | solution.py:335
  12.0 1.0 %collective-permute-start.3 = (bf16[192,256]{1,0:T(8,128)(2,1)S(1)}, bf16[192,256]{1,0:T(8,128)(2,1)S(1)}, u32[]{:S(2)}, u32[]{:S(2)}) collective-permute-start(bf16[192,256]{1,0:T(8,128)(2,1)S(1)} %get-tuple-element.43), channel_id=1, source_target_pairs={{0,2},{1,3},{2,0},{3,1},{4,6},{5,7},{6,4},{7,5},{8,10},{9,11},{10,... | collective-permute-start | bytes 294920 | tf_op jit(solution)/shard_map/ppermute | solution.py:335
  13.1 2.1 %collective-permute-start.4 = (bf16[96,256]{1,0:T(8,128)(2,1)S(1)}, bf16[96,256]{1,0:T(8,128)(2,1)S(1)}, u32[]{:S(2)}, u32[]{:S(2)}) collective-permute-start(bf16[96,256]{1,0:T(8,128)(2,1)S(1)} %get-tuple-element.44), channel_id=1, source_target_pairs={{0,3},{1,2},{2,1},{3,0},{4,7},{5,6},{6,5},{7,4},{8,11},{9,10},{10,... | collective-permute-start | bytes 147464 | tf_op jit(solution)/shard_map/ppermute | solution.py:335
  15.2 0.5 %collective-permute-start.9 = (bf16[64,256]{1,0:T(8,128)(2,1)S(1)}, bf16[64,256]{1,0:T(8,128)(2,1)S(1)}, u32[]{:S(2)}, u32[]{:S(2)}) collective-permute-start(bf16[64,256]{1,0:T(8,128)(2,1)S(1)} %slice.4), channel_id=1, source_target_pairs={{0,1},{1,0},{2,3},{3,2},{4,5},{5,4},{6,7},{7,6},{8,9},{9,8},{10,11... | collective-permute-start | bytes 98312 | tf_op jit(solution)/shard_map/ppermute | solution.py:335
  15.7 0.8 %near.1 = (f32[2,1,1024]{2,1,0:T(1,128)S(1)}, f32[2,1,1024]{2,1,0:T(1,128)S(1)}, f32[2,128,1024]{2,1,0:T(8,128)S(1)}) custom-call(bf16[256,256]{1,0:T(8,128)(2,1)S(1)} %get-tuple-element.51.kv_ref.refs_6_, bf16[2,1024,128]{2,1,0:T(8,128)(2,1)S(1)} %rotate.1.rot_ref.refs_7_), custom_call_target="tpu_custom_call" | custom-call | flops 134217728 | bytes 4000000 | tf_op jit(solution)/shard_map/near/pallas_call | solution.py:413
  16.5 0.1 collective-permute-done.9.refs_4_
  16.6 1.6 %fold0.1 = (f32[2,1,1024]{2,1,0:T(1,128)S(1)}, f32[2,1,1024]{2,1,0:T(1,128)S(1)}, f32[2,128,1024]{2,1,0:T(8,128)S(1)}) custom-call(bf16[224,256]{1,0:T(8,128)(2,1)S(1)} %get-tuple-element.46.refs_0_, bf16[192,256]{1,0:T(8,128)(2,1)S(1)} %collective-permute-done.6.refs_1_, ...), custom_call_target="tpu_custom_call", output_to_operand_aliasing={{0}: (8, {}), {1}: (9, {}), {2}: (10, {})} | custom-call | flops 134217728 | bytes 4000000 | tf_op jit(solution)/shard_map/fold0/pallas_call | solution.py:424
  18.2 0.2 close.1.first_ref
  18.4 1.3 %last.1 = bf16[256,1024]{1,0:T(8,128)(2,1)} custom-call(bf16[192,256]{1,0:T(8,128)(2,1)S(1)} %collective-permute-done.3.second_ref, bf16[96,256]{1,0:T(8,128)(2,1)S(1)} %collective-permute-done.4.third_ref, bf16[96,256]{1,0:T(8,128)(2,1)S(1)} %collective-permute-done.5.early_ref, bf16[128,1024]{1,0:T(8,128)(2,1)S(1)} %close.1.first_ref, ...), custom_call_target="tpu_custom_call" | custom-call | flops 134217728 | bytes 4000000 | tf_op jit(solution)/shard_map/last/pallas_call | solution.py:444
  (15 shorter events, 0.0 us)
Async XLA Ops:
  0.0 0.9 %copy-start.2 = (s32[32,16]{0,1:T(8,128)S(1)}, s32[32,16]{0,1:T(8,128)}, u32[]{:S(2)}) copy-start(s32[32,16]{0,1:T(8,128)} %param.9) | copy-start | bytes 6148
  1.0 9.3 %copy-start = (bf16[256,1024]{1,0:T(8,128)(2,1)S(1)}, bf16[256,1024]{1,0:T(8,128)(2,1)}, u32[]{:S(2)}) copy-start(bf16[256,1024]{1,0:T(8,128)(2,1)} %q_ref.1) | copy-start | bytes 1572868
  1.2 8.5 %collective-permute-start = (bf16[128,256]{1,0:T(8,128)(2,1)S(1)}, bf16[128,256]{1,0:T(8,128)(2,1)S(1)}, u32[]{:S(2)}, u32[]{:S(2)}) collective-permute-start(bf16[128,256]{1,0:T(8,128)(2,1)S(1)} %get-tuple-element.37), channel_id=1, source_target_pairs={{0,4},{1,5},{2,6},{3,7},{4,8},{5,9},{6,10},{7,11},{8,12},{9,13},{1... | collective-permute-start | bytes 196616 | tf_op jit(solution)/shard_map/ppermute | solution.py:335
  3.4 7.3 %collective-permute-start.1 = (bf16[128,256]{1,0:T(8,128)(2,1)S(1)}, bf16[128,256]{1,0:T(8,128)(2,1)S(1)}, u32[]{:S(2)}, u32[]{:S(2)}) collective-permute-start(bf16[128,256]{1,0:T(8,128)(2,1)S(1)} %get-tuple-element.38), channel_id=1, source_target_pairs={{0,8},{1,9},{2,10},{3,11},{4,12},{5,13},{6,14},{7,15},{8,0},{9,1},... | collective-permute-start | bytes 196616 | tf_op jit(solution)/shard_map/ppermute | solution.py:335
  5.7 4.7 %copy-start.1 = (bf16[128,128]{1,0:T(8,128)(2,1)S(1)}, bf16[128,128]{1,0:T(8,128)(2,1)}, u32[]{:S(2)}) copy-start(bf16[128,128]{1,0:T(8,128)(2,1)} %basis_ref.1) | copy-start | bytes 98308
  5.7 5.0 %collective-permute-start.2 = (bf16[128,256]{1,0:T(8,128)(2,1)S(1)}, bf16[128,256]{1,0:T(8,128)(2,1)S(1)}, u32[]{:S(2)}, u32[]{:S(2)}) collective-permute-start(bf16[128,256]{1,0:T(8,128)(2,1)S(1)} %get-tuple-element.39), channel_id=1, source_target_pairs={{0,12},{1,13},{2,14},{3,15},{4,0},{5,1},{6,2},{7,3},{8,4},{9,5},{1... | collective-permute-start | bytes 196616 | tf_op jit(solution)/shard_map/ppermute | solution.py:335
  6.8 8.4 %collective-permute-start.7 = (bf16[160,256]{1,0:T(8,128)(2,1)S(1)}, bf16[160,256]{1,0:T(8,128)(2,1)S(1)}, u32[]{:S(2)}, u32[]{:S(2)}) collective-permute-start(bf16[160,256]{1,0:T(8,128)(2,1)S(1)} %get-tuple-element.48), channel_id=1, source_target_pairs={{0,1},{1,0},{2,3},{3,2},{4,5},{5,4},{6,7},{7,6},{8,9},{9,8},{10,11... | collective-permute-start | bytes 245768 | tf_op jit(solution)/shard_map/ppermute | solution.py:335
  8.4 4.7 %collective-permute-start.8 = (bf16[128,256]{1,0:T(8,128)(2,1)S(1)}, bf16[128,256]{1,0:T(8,128)(2,1)S(1)}, u32[]{:S(2)}, u32[]{:S(2)}) collective-permute-start(bf16[128,256]{1,0:T(8,128)(2,1)S(1)} %get-tuple-element.49), channel_id=1, source_target_pairs={{0,2},{1,3},{2,0},{3,1},{4,6},{5,7},{6,4},{7,5},{8,10},{9,11},{10,... | collective-permute-start | bytes 196616 | tf_op jit(solution)/shard_map/ppermute | solution.py:335
  9.7 5.5 %collective-permute-start.10 = (bf16[128,256]{1,0:T(8,128)(2,1)S(1)}, bf16[128,256]{1,0:T(8,128)(2,1)S(1)}, u32[]{:S(2)}, u32[]{:S(2)}) collective-permute-start(bf16[128,256]{1,0:T(8,128)(2,1)S(1)} %get-tuple-element.50), channel_id=1, source_target_pairs={{1,2},{2,1},{3,4},{4,3},{5,6},{6,5},{7,8},{8,7},{9,10},{10,9},{11,... | collective-permute-start | bytes 196616 | tf_op jit(solution)/shard_map/ppermute | solution.py:392
  10.8 5.8 %collective-permute-start.6 = (bf16[192,256]{1,0:T(8,128)(2,1)S(1)}, bf16[192,256]{1,0:T(8,128)(2,1)S(1)}, u32[]{:S(2)}, u32[]{:S(2)}) collective-permute-start(bf16[192,256]{1,0:T(8,128)(2,1)S(1)} %get-tuple-element.47), channel_id=1, source_target_pairs={{0,1},{1,0},{2,3},{3,2},{4,5},{5,4},{6,7},{7,6},{8,9},{9,8},{10,11... | collective-permute-start | bytes 294920 | tf_op jit(solution)/shard_map/ppermute | solution.py:335
  12.0 6.4 %collective-permute-start.3 = (bf16[192,256]{1,0:T(8,128)(2,1)S(1)}, bf16[192,256]{1,0:T(8,128)(2,1)S(1)}, u32[]{:S(2)}, u32[]{:S(2)}) collective-permute-start(bf16[192,256]{1,0:T(8,128)(2,1)S(1)} %get-tuple-element.43), channel_id=1, source_target_pairs={{0,2},{1,3},{2,0},{3,1},{4,6},{5,7},{6,4},{7,5},{8,10},{9,11},{10,... | collective-permute-start | bytes 294920 | tf_op jit(solution)/shard_map/ppermute | solution.py:335
  13.1 5.3 %collective-permute-start.4 = (bf16[96,256]{1,0:T(8,128)(2,1)S(1)}, bf16[96,256]{1,0:T(8,128)(2,1)S(1)}, u32[]{:S(2)}, u32[]{:S(2)}) collective-permute-start(bf16[96,256]{1,0:T(8,128)(2,1)S(1)} %get-tuple-element.44), channel_id=1, source_target_pairs={{0,3},{1,2},{2,1},{3,0},{4,7},{5,6},{6,5},{7,4},{8,11},{9,10},{10,... | collective-permute-start | bytes 147464 | tf_op jit(solution)/shard_map/ppermute | solution.py:335
  15.2 3.2 %collective-permute-start.5 = (bf16[96,256]{1,0:T(8,128)(2,1)S(1)}, bf16[96,256]{1,0:T(8,128)(2,1)S(1)}, u32[]{:S(2)}, u32[]{:S(2)}) collective-permute-start(bf16[96,256]{1,0:T(8,128)(2,1)S(1)} %get-tuple-element.45), channel_id=1, source_target_pairs={{0,1},{1,0},{2,3},{3,2},{4,7},{5,6},{6,5},{7,4},{8,11},{9,10},{10,... | collective-permute-start | bytes 147464 | tf_op jit(solution)/shard_map/ppermute | solution.py:335
  15.2 1.4 %collective-permute-start.9 = (bf16[64,256]{1,0:T(8,128)(2,1)S(1)}, bf16[64,256]{1,0:T(8,128)(2,1)S(1)}, u32[]{:S(2)}, u32[]{:S(2)}) collective-permute-start(bf16[64,256]{1,0:T(8,128)(2,1)S(1)} %slice.4), channel_id=1, source_target_pairs={{0,1},{1,0},{2,3},{3,2},{4,5},{5,4},{6,7},{7,6},{8,9},{9,8},{10,11... | collective-permute-start | bytes 98312 | tf_op jit(solution)/shard_map/ppermute | solution.py:335
